TPU v7x, 32 devices: a whole 2x2x4 slice. The times are simulated.
32 devices in a mesh: grp: 4 (over y, core), dev: 8 (over z, x).
Axes of the slice: x: 2, y: 2, z: 4, core: 2. Of those that a mesh axis runs over, the one named last changes fastest.
Arguments:
- row_panel: bfloat16 [8, 512, 512], P('grp', 'dev'), may hold values from -3 to 3
- col_near: bfloat16 [32, 512, 512], P('dev', 'grp'), may hold values from -3 to 3
- col_far: bfloat16 [32, 2, 48, 512], P('dev', None, 'grp'), may hold values from -0.4375 to 0.4375
- near_tiles: bfloat16 [256, 512, 512], P(('grp', 'dev')), may hold values from -6 to 6
- near_rows: int32 [32, 8], P(('grp', 'dev')), may hold values from 0 to 1, as said below
- near_cols: int32 [32, 8], replicated, may hold values from 0 to 31, as said below
- far_tiles: bfloat16 [256, 2, 48, 512], P(('grp', 'dev')), may hold values from -6 to 6
- far_rows: int32 [32, 8], P(('grp', 'dev')), may hold values from 0 to 1, as said below
- far_cols: int32 [32, 8], replicated, may hold values from 0 to 31, as said below
Outputs:
- near_out: bfloat16 [256, 512, 512], P(('grp', 'dev'))
- far_out: bfloat16 [256, 48, 512], P(('grp', 'dev'))
Inputs may be any that keep to these rules, and one draw needn't show every extreme that they name: `near_rows`: for every row group and every slot s, the 8 devices of the group hold in their near slot s every near tile of that group whose column lies in bucket s (columns s * 4 to (s + 1) * 4 - 1), each exactly once. near_cols[f, s] lies in bucket s, from s * 4 to (s + 1) * 4 - 1. `far_rows`: for every row group and every slot s, the 8 devices of the group hold in their far slot s every far tile of that group whose column lies in bucket s, each exactly once. far_cols[f, s] lies in bucket s, from s * 4 to (s + 1) * 4 - 1.
All inputs are finite; a program needn't handle non-finite values.
Results may differ from a plain program's by a relative error of at most 0.001.
Values may be sent and summed in bfloat16 or wider, within the bound.
No kernel may reach another device: no remote copies, remote signals or barrier semaphores. Data moves between devices by JAX's collectives and lax.ppermute only.
A program may use at most 128 MiB of HBM per device.

v0:
```python
import jax
import jax.numpy as jnp
from jax import lax
from jax.sharding import PartitionSpec as P


def shards(
    row_panel, col_near, col_far, near_tiles, near_rows, near_cols, far_tiles, far_rows, far_cols
):
    own_index = lax.axis_index("dev")
    group_index = lax.axis_index("grp")
    dev_count = lax.axis_size("dev")
    per_bucket = col_near.shape[0]
    row_tiles = lax.all_gather(row_panel, "dev", axis=1, tiled=True)
    group_near = lax.dynamic_slice_in_dim(near_cols, group_index * dev_count, dev_count, 0)
    group_far = lax.dynamic_slice_in_dim(far_cols, group_index * dev_count, dev_count, 0)
    bucket_near, bucket_far = (
        lax.all_gather(col_near, "grp", axis=1, tiled=True),
        lax.all_gather(col_far, "grp", axis=2, tiled=True),
    )
    near_pick = (
        lax.dynamic_index_in_dim(group_near, own_index, 1, keepdims=False) - own_index * per_bucket
    )
    near_outgoing = jnp.take(bucket_near, near_pick, axis=0)
    near_panel = lax.all_to_all(near_outgoing, "dev", split_axis=0, concat_axis=0, tiled=True)
    far_every = lax.all_gather(bucket_far, "dev", axis=0, tiled=True)
    own_far = lax.dynamic_index_in_dim(group_far, own_index, 0, keepdims=False)
    far_panel = jnp.take(far_every, own_far, axis=0)
    near_left = jnp.take(row_tiles, near_rows[0], axis=0)
    near_product = jnp.einsum(
        "sik,sjk->sij", near_left, near_panel, preferred_element_type=jnp.float32
    )
    near_out = (near_tiles.astype(jnp.float32) - near_product).astype(jnp.bfloat16)
    far_left = jnp.take(row_tiles, far_rows[0], axis=0)
    basis = far_tiles[:, 0]
    x_trans = jnp.einsum("sqi,sik->sqk", basis, far_left, preferred_element_type=jnp.float32)
    small = jnp.einsum(
        "sak,sqk->saq",
        far_panel[:, 1].astype(jnp.float32),
        x_trans,
        precision=lax.Precision.HIGHEST,
    )
    update = jnp.einsum(
        "saq,saj->sqj", small, far_panel[:, 0].astype(jnp.float32), precision=lax.Precision.HIGHEST
    )
    far_out = (far_tiles[:, 1].astype(jnp.float32) - update).astype(jnp.bfloat16)
    return (near_out, far_out)


def solution(mesh):
    placed = (
        P("grp", "dev", None),
        P("dev", "grp", None),
        P("dev", None, "grp", None),
        P(("grp", "dev"), None, None),
        P(("grp", "dev"), None),
        P(),
        P(("grp", "dev"), None, None, None),
        P(("grp", "dev"), None),
        P(),
    )
    return jax.shard_map(
        shards,
        mesh=mesh,
        in_specs=placed,
        out_specs=(P(("grp", "dev"), None, None), P(("grp", "dev"), None, None)),
        check_vma=False,
    )
```

profile of v0, /device:TPU:0, one launch (start us, length us, event | category | flops | bytes accessed | tf_op | source)
XLA Modules:
  0.0 221.4 jit_solution(2212394341272282627)
XLA Ops:
  7.2 0.0 copy-start
  7.2 0.0 all-gather.6.cloned.1.call-start
  7.2 0.7 all-gather.6.cloned.1.call-update
  7.9 0.0 all-gather.4.cloned.1.call-start
  8.0 0.7 all-gather.4.cloned.1.call-update
  8.7 0.8 and_bitcast_fusion
  9.5 25.4 %all-gather.6.cloned.1.call-done = bf16[4,512,512]{2,1,0:T(8,128)(2,1)} async-done(((bf16[4,128,512]{2,1,0:T(8,128)(2,1)}), bf16[4,512,512]{2,1,0:T(8,128)(2,1)}) %all-gather.6.cloned.1.call-update) | async-done | bytes 2097168 | tf_op jit(solution)/shard_map/all_gather | solution.py:18
  34.9 4.4 %gather_fusion = bf16[8,512,512]{2,1,0:T(8,128)(2,1)} fusion(bf16[4,512,512]{2,1,0:T(8,128)(2,1)} %all-gather.6.cloned.1.call-done, s32[1024]{0:T(1024)S(1)} %pad_clamp_fusion.2), kind=kCustom, calls=%fused_computation.2 | custom fusion | bytes 8388640 | tf_op jit(solution)/shard_map/jit(_take)/gather | solution.py:24
  39.3 4.7 %broadcast_select_fusion = bf16[8,512,512]{2,1,0:T(8,128)(2,1)} fusion(bf16[8,512,512]{2,1,0:T(8,128)(2,1)} %gather_fusion, pred[8]{0:T(512)(128)(4,1)S(1)} %get-tuple-element.3), kind=kLoop, calls=%fused_computation.11 | loop fusion | flops 2097152 | bytes 8388616 | tf_op jit(solution)/shard_map/jit(_take)/select_n | solution.py:24
  44.0 0.0 copy-start.3
  44.0 0.0 copy-start.4
  44.0 0.0 copy-start.5
  44.0 5.6 %all-to-all-start = ((bf16[8,512,512]{2,1,0:T(8,128)(2,1)}), bf16[8,512,512]{2,1,0:T(8,128)(2,1)}, u32[]{:S(2)}, u32[]{:S(2)}) async-start(bf16[8,512,512]{2,1,0:T(8,128)(2,1)} %broadcast_select_fusion), calls=%async_computation | async-start | bytes 8388608 | tf_op jit(solution)/shard_map/all_to_all | solution.py:25
  49.6 0.0 all-gather.8.cloned.1.call-start
  49.7 0.0 copy-done.3
  49.7 0.1 copy.16
  49.7 6.2 %all_gather.14 = bf16[4,2,48,512]{3,0,1,2:T(4,128)(2,1)S(1)} all-gather(bf16[4,2,12,512]{3,0,1,2:T(4,128)(2,1)S(1)} %copy.16), channel_id=1, replica_groups=mesh['grp'=4,'dev'=8] {'grp'}, dimensions={2}, use_global_device_ids=true | all-gather | bytes 491520 | tf_op jit(solution)/shard_map/all_gather | solution.py:19
  55.9 0.9 copy.17
  56.8 0.0 all-gather.8.cloned.1.call-update
  56.8 0.0 copy-done
  56.8 0.2 dynamic-slice_reduce_fusion
  57.0 0.0 copy-done.4
  57.1 0.0 copy-done.5
  57.2 77.5 %all-gather.4.cloned.1.call-done = bf16[2,512,512]{2,1,0:T(8,128)(2,1)} async-done(((bf16[2,64,512]{2,1,0:T(8,128)(2,1)}), bf16[2,512,512]{2,1,0:T(8,128)(2,1)}) %all-gather.4.cloned.1.call-update) | async-done | bytes 1048592 | tf_op jit(solution)/shard_map/all_gather | solution.py:14
  134.7 0.0 copy-start.1
  134.7 4.1 %gather_fusion.3 = bf16[8,512,512]{2,1,0:T(8,128)(2,1)} fusion(bf16[2,512,512]{2,1,0:T(8,128)(2,1)} %all-gather.4.cloned.1.call-done, s32[1024]{0:T(1024)S(1)} %pad_clamp_fusion), kind=kCustom, calls=%fused_computation.1.clone | custom fusion | bytes 8388640 | tf_op jit(solution)/shard_map/jit(_take)/gather | solution.py:34
  138.8 0.0 copy-done.1
  138.8 0.0 copy-start.2
  138.8 2.8 %gather_fusion.2 = bf16[8,512,512]{2,1,0:T(8,128)(2,1)} fusion(bf16[2,512,512]{2,1,0:T(8,128)(2,1)S(1)} %copy-done.1, s32[1024]{0:T(1024)S(1)} %pad_clamp_fusion.3), kind=kCustom, calls=%fused_computation.clone | custom fusion | bytes 8388640 | tf_op jit(solution)/shard_map/jit(_take)/gather | solution.py:29
  141.5 0.0 copy-done.2
  141.5 3.4 %fusion = f32[8,512,48]{1,2,0:T(8,128)S(1)} fusion(bf16[8,512,512]{2,1,0:T(8,128)(2,1)} %gather_fusion.3, pred[8]{0:T(512)(128)(4,1)S(1)} %compare_and_fusion, bf16[8,2,48,512]{3,2,1,0:T(8,128)(2,1)S(1)} %copy-done.2), kind=kOutput, calls=%fused_computation.5 | convolution fusion | flops 203423744 | bytes 5374464 | tf_op jit(solution)/shard_map/sqi,sik->sqk/dot_general | solution.py:36
  145.0 56.5 %all-gather.8.cloned.1.call-done = bf16[32,2,48,512]{3,2,1,0:T(8,128)(2,1)} async-done(((bf16[4,2,48,512]{3,2,1,0:T(8,128)(2,1)}), bf16[32,2,48,512]{3,2,1,0:T(8,128)(2,1)}) %all-gather.8.cloned.1.call-update) | async-done | bytes 3145744 | tf_op jit(solution)/shard_map/all_gather | solution.py:26
  201.4 2.5 %gather_fusion.1 = bf16[8,2,48,512]{3,2,1,0:T(8,128)(2,1)S(1)} fusion(bf16[32,2,48,512]{3,2,1,0:T(8,128)(2,1)} %all-gather.8.cloned.1.call-done, s32[1024]{0:T(1024)S(1)} %pad_clamp_fusion.1), kind=kCustom, calls=%fused_computation.3 | custom fusion | bytes 1572896 | tf_op jit(solution)/shard_map/jit(_take)/gather | solution.py:28
  203.9 0.1 copy_select_fusion
  204.1 0.5 fusion.11
  204.6 1.2 fusion.10
  205.8 0.0 all-to-all-done
  205.8 9.1 %subtract_convert_fusion = bf16[8,512,512]{2,1,0:T(8,128)(2,1)} fusion(bf16[8,512,512]{2,1,0:T(8,128)(2,1)} %param.14, bf16[8,512,512]{2,1,0:T(8,128)(2,1)} %all-to-all-done, bf16[8,512,512]{2,1,0:T(8,128)(2,1)} %gather_fusion.2, pred[8]{0:T(512)(128)(4,1)S(1)} %compare_and_fusion.1), kind=kOutput, calls=%fused_computation.4 | convolution fusion | flops 2155872256 | bytes 16777224 | tf_op jit(solution)/shard_map/sik,sjk->sij/dot_general | solution.py:30
  (10 shorter events, 0.1 us)
Async XLA Ops:
  7.2 49.7 %copy-start = (s32[32,8]{0,1:T(8,128)S(1)}, s32[32,8]{0,1:T(8,128)}, u32[]{:S(2)}) copy-start(s32[32,8]{0,1:T(8,128)} %param.19) | copy-start | bytes 3076
  7.2 27.7 %all-gather.6.cloned.1.call-start = ((), (), s32[]{:S(2)}) async-start(), calls=%async_computation.2 | async-start | bytes 2621440 | tf_op jit(solution)/shard_map/all_gather | solution.py:18
  7.9 126.8 %all-gather.4.cloned.1.call-start = ((), (), s32[]{:S(2)}) async-start(), calls=%async_computation.1 | async-start | bytes 1179648 | tf_op jit(solution)/shard_map/all_gather | solution.py:14
  44.0 5.7 %copy-start.3 = (bf16[4,2,12,512]{3,1,2,0:T(2,128)(2,1)S(1)}, bf16[4,2,12,512]{3,1,2,0:T(2,128)(2,1)}, u32[]{:S(2)}) copy-start(bf16[4,2,12,512]{3,1,2,0:T(2,128)(2,1)} %param.13) | copy-start | bytes 294916
  44.0 13.1 %copy-start.4 = (s32[1,8]{1,0:T(1,128)S(1)}, s32[1,8]{1,0:T(1,128)}, u32[]{:S(2)}) copy-start(s32[1,8]{1,0:T(1,128)} %param.18) | copy-start | bytes 100
  44.0 13.1 %copy-start.5 = (s32[1,8]{1,0:T(1,128)S(1)}, s32[1,8]{1,0:T(1,128)}, u32[]{:S(2)}) copy-start(s32[1,8]{1,0:T(1,128)} %param.15) | copy-start | bytes 100
  44.0 161.8 %all-to-all-start = ((bf16[8,512,512]{2,1,0:T(8,128)(2,1)}), bf16[8,512,512]{2,1,0:T(8,128)(2,1)}, u32[]{:S(2)}, u32[]{:S(2)}) async-start(bf16[8,512,512]{2,1,0:T(8,128)(2,1)} %broadcast_select_fusion), calls=%async_computation | async-start | bytes 8388608 | tf_op jit(solution)/shard_map/all_to_all | solution.py:25
  49.6 151.8 %all-gather.8.cloned.1.call-start = ((), (), s32[]{:S(2)}) async-start(), calls=%async_computation.3 | async-start | bytes 3538944 | tf_op jit(solution)/shard_map/all_gather | solution.py:26
  134.7 4.1 %copy-start.1 = (bf16[2,512,512]{2,1,0:T(8,128)(2,1)S(1)}, bf16[2,512,512]{2,1,0:T(8,128)(2,1)}, u32[]{:S(2)}) copy-start(bf16[2,512,512]{2,1,0:T(8,128)(2,1)} %all-gather.4.cloned.1.call-done) | copy-start | bytes 3145732
  138.8 2.8 %copy-start.2 = (bf16[8,2,48,512]{3,2,1,0:T(8,128)(2,1)S(1)}, bf16[8,2,48,512]{3,2,1,0:T(8,128)(2,1)}, u32[]{:S(2)}) copy-start(bf16[8,2,48,512]{3,2,1,0:T(8,128)(2,1)} %param.17) | copy-start | bytes 2359300
Sparse Core Ops, SparseCore 0:
  9.6 25.2 all-gather.5
  37.1 97.5 all-gather.3
  137.4 63.9 all-gather.7
where the time goes:
time: 222 us; the launch traced here: 221 us
  waiting for transfers between devices  161 us (73%)
  local copies, waits for them, and re-layouts  14.9 us (7%)
  matrix products  14.2 us (6%)
  between operations  13.9 us (6%)
  blocking collectives  6.19 us (3%)
  starting transfers between devices  5.76 us (3%)
  other arithmetic  5.64 us (3%)
    all_gather x1, waiting for transfers between devices, shards(): row_tiles = lax.all_gather(row_panel, 'dev', axis=1, tiled=True)  77.5 us
    all_gather x1, waiting for transfers between devices, shards(): far_every = lax.all_gather(bucket_far, 'dev', axis=0, tiled=True)  56.5 us
    all_gather x1, waiting for transfers between devices, shards(): lax.all_gather(col_near, 'grp', axis=1, tiled=True)  25.4 us
    dot_general x1, matrix products, shards(): jnp.einsum('sik,sjk->sij', near_left, near_panel, preferred_element_type=...  9.06 us
    all_gather x1, blocking collectives, shards(): lax.all_gather(col_far, 'grp', axis=2, tiled=True)  6.19 us
    all_to_all x1, starting transfers between devices, shards(): lax.all_to_all(near_outgoing, 'dev', split_axis=0, concat_axis=0, tiled=T...  5.64 us
    select_n x1, other arithmetic, shards(): near_outgoing = jnp.take(bucket_near, near_pick, axis=0)  4.66 us
  transfers between devices with their start and end apart: 4, of which 3 were waited for; matrix products, arithmetic and copies ran while one was open for 12% of the time, Pallas kernels for 0%

commit v1 on v0

v1 whole, which is shorter than its diff:
```python
import jax
import jax.numpy as jnp
from jax import lax
from jax.sharding import Mesh, PartitionSpec as P

OUTER = 4
PLANE = ("gy", "core", "inner")


def shards(
    row_panel, col_near, col_far, near_tiles, near_rows, near_cols, far_tiles, far_rows, far_cols
):
    inner_size = lax.axis_size("inner")
    outer_size = lax.axis_size("outer")
    groups = lax.axis_size("gy") * lax.axis_size("core")
    dev_count = inner_size * outer_size
    per_bucket = col_near.shape[0]
    outer, inner = lax.axis_index("outer"), lax.axis_index("inner")
    order = col_near.shape[2]
    quarter = col_near.shape[1]
    rank = col_far.shape[2] * groups

    def wanted(cols):
        table = cols.reshape(groups, outer_size, inner_size, outer_size, inner_size)
        table = lax.dynamic_index_in_dim(table, outer, 1, keepdims=False)
        table = lax.dynamic_index_in_dim(table, inner, 3, keepdims=False)
        return table.reshape(groups * inner_size, outer_size) % per_bucket

    line = jnp.arange(outer_size, dtype=jnp.int32) * per_bucket
    near_line = lax.all_gather(col_near, "outer", axis=0, tiled=True)
    near_send = jnp.take(near_line, wanted(near_cols) + line, axis=0)
    near_got = lax.all_to_all(near_send, PLANE, split_axis=0, concat_axis=0, tiled=True)

    far_line = lax.all_gather(col_far, "outer", axis=0, tiled=True)
    far_send = jnp.take(far_line, wanted(far_cols) + line, axis=0)
    far_got = lax.all_to_all(far_send, PLANE, split_axis=0, concat_axis=0, tiled=True)

    row_tiles = lax.all_gather(row_panel, ("outer", "inner"), axis=1, tiled=True)

    near_got = near_got.reshape(groups, inner_size, outer_size, quarter, order)
    near_panel = jnp.transpose(near_got, (2, 1, 0, 3, 4)).reshape(dev_count, order, order)
    far_got = far_got.reshape(groups, inner_size, outer_size, 2, rank // groups, order)
    far_panel = jnp.transpose(far_got, (2, 1, 3, 0, 4, 5)).reshape(dev_count, 2, rank, order)

    near_left = jnp.take(row_tiles, near_rows[0], axis=0)
    near_product = jnp.einsum(
        "sik,sjk->sij", near_left, near_panel, preferred_element_type=jnp.float32
    )
    near_out = (near_tiles.astype(jnp.float32) - near_product).astype(jnp.bfloat16)
    far_left = jnp.take(row_tiles, far_rows[0], axis=0)
    basis = far_tiles[:, 0]
    x_trans = jnp.einsum("sqi,sik->sqk", basis, far_left, preferred_element_type=jnp.float32)
    small = jnp.einsum(
        "sak,sqk->saq",
        far_panel[:, 1].astype(jnp.float32),
        x_trans,
        precision=lax.Precision.HIGHEST,
    )
    update = jnp.einsum(
        "saq,saj->sqj", small, far_panel[:, 0].astype(jnp.float32), precision=lax.Precision.HIGHEST
    )
    far_out = (far_tiles[:, 1].astype(jnp.float32) - update).astype(jnp.bfloat16)
    return (near_out, far_out)


def solution(mesh):
    groups, dev_count = mesh.shape["grp"], mesh.shape["dev"]
    fine = Mesh(
        mesh.devices.reshape(groups // 2, 2, OUTER, dev_count // OUTER),
        ("gy", "core", "outer", "inner"),
    )
    grp, dev = ("gy", "core"), ("outer", "inner")
    every = grp + dev
    placed = (
        P(grp, dev, None),
        P(dev, grp, None),
        P(dev, None, grp, None),
        P(every, None, None),
        P(every, None),
        P(),
        P(every, None, None, None),
        P(every, None),
        P(),
    )
    return jax.shard_map(
        shards,
        mesh=fine,
        in_specs=placed,
        out_specs=(P(every, None, None), P(every, None, None)),
        check_vma=False,
    )
```

time: 222 us -> 151 us (0.68)
  waiting for transfers between devices: 161 us -> 69.8 us
  blocking collectives: 6.19 us -> 18.4 us
  local copies, waits for them, and re-layouts: 14.9 us -> 22.2 us
  matrix products: 14.2 us -> 9.37 us
  starting transfers between devices: 5.76 us -> 8.59 us
    all_gather x3 -> x2, waiting for transfers between devices: 159 us -> 68.6 us  [the longest x1 44.7 us: shards(): lax.all_gather(row_panel, ('outer', 'inner'), axis=1, tiled=True)]
    all_gather x1, blocking collectives: 6.19 us -> 18.4 us  [shards(): far_line = lax.all_gather(col_far, 'outer', axis=0, tiled=True)]
    dot_general x1, matrix products: 9.06 us -> 4.4 us  [shards(): jnp.einsum('sik,sjk->sij', near_left, near_panel, preferred_element_type=...]
    transpose x0 -> x2, local copies, waits for them, and re-layouts: none -> 3.29 us  [the longest x1 2.68 us: shards(): jnp.transpose(near_got, (2, 1, 0, 3, 4)).reshape(dev_count, order, order)]
    all_to_all x1 -> x2, starting transfers between devices: 5.64 us -> 8.51 us  [the longest x1 4.7 us: shards(): lax.all_to_all(near_send, PLANE, split_axis=0, concat_axis=0, tiled=True)]
    select_n x4 -> x3, other arithmetic: 4.81 us -> 6.35 us  [the longest x1 4.67 us: shards(): near_send = jnp.take(near_line, wanted(near_cols) + line, axis=0)]
  transfers between devices with their start and end apart: 4 -> 4, of which waited for: 3 -> 2; matrix products, arithmetic and copies ran while one was open for 12% -> 19% of each run, Pallas kernels for 0% -> 0%
where the time goes in v1:
time: 151 us; the launch traced here: 150 us
  waiting for transfers between devices  69.8 us (46%)
  local copies, waits for them, and re-layouts  22.2 us (15%)
  blocking collectives  18.4 us (12%)
  between operations  15.6 us (10%)
  matrix products  9.37 us (6%)
  starting transfers between devices  8.59 us (6%)
  other arithmetic  6.41 us (4%)
    all_gather x1, waiting for transfers between devices, shards(): lax.all_gather(row_panel, ('outer', 'inner'), axis=1, tiled=True)  44.7 us
    all_gather x1, waiting for transfers between devices, shards(): near_line = lax.all_gather(col_near, 'outer', axis=0, tiled=True)  23.9 us
    all_gather x1, blocking collectives, shards(): far_line = lax.all_gather(col_far, 'outer', axis=0, tiled=True)  18.4 us
    all_to_all x1, starting transfers between devices, shards(): lax.all_to_all(near_send, PLANE, split_axis=0, concat_axis=0, tiled=True)  4.7 us
    select_n x1, other arithmetic, shards(): near_send = jnp.take(near_line, wanted(near_cols) + line, axis=0)  4.67 us
    gather x1, local copies, waits for them, and re-layouts, shards(): near_send = jnp.take(near_line, wanted(near_cols) + line, axis=0)  4.42 us
    dot_general x1, matrix products, shards(): jnp.einsum('sik,sjk->sij', near_left, near_panel, preferred_element_type=...  4.4 us
    gather x1, local copies, waits for them, and re-layouts, shards(): far_left = jnp.take(row_tiles, far_rows[0], axis=0)  4.09 us
  transfers between devices with their start and end apart: 4, of which 2 were waited for; matrix products, arithmetic and copies ran while one was open for 19% of the time, Pallas kernels for 0%

profile of v1, /device:TPU:0, one launch (start us, length us, event | category | flops | bytes accessed | tf_op | source)
XLA Modules:
  0.0 150.4 jit_solution(17052459012647926991)
XLA Ops:
  8.0 0.0 all-gather.5.cloned.1.call-start
  8.0 0.7 all-gather.5.cloned.1.call-update
  8.7 0.8 reshape.239
  9.5 0.8 reshape.244
  10.4 0.1 copy.32
  10.5 0.1 copy.36
  10.6 0.1 reshape.276
  10.7 18.4 %all_gather.11 = bf16[16,2,12,512]{3,1,2,0:T(2,128)(2,1)S(1)} all-gather(bf16[4,2,12,512]{3,1,2,0:T(2,128)(2,1)} %param.13), channel_id=1, replica_groups=mesh['gy'=2,'core'=2,'outer'=4,'inner'=2] {'outer'}, dimensions={0}, use_global_device_ids=true | all-gather | bytes 491520 | tf_op jit(solution)/shard_map/all_gather | solution.py:34
  29.2 2.1 %gather_fusion.1 = bf16[32,2,12,512]{3,1,2,0:T(2,128)(2,1)S(1)} fusion(bf16[16,2,12,512]{3,1,2,0:T(2,128)(2,1)S(1)} %all_gather.11, s32[1024]{0:T(1024)S(1)} %pad_clamp_fusion.1), kind=kCustom, calls=%fused_computation.3 | custom fusion | bytes 1572992 | tf_op jit(solution)/shard_map/jit(_take)/gather | solution.py:35
  31.3 1.7 %broadcast_select_fusion.1 = bf16[8,4,2,12,512]{4,2,3,1,0:T(2,128)(2,1)} fusion(bf16[8,4,2,12,512]{4,2,3,1,0:T(2,128)(2,1)S(1)} %bitcast.51, pred[8,4]{1,0:T(8,128)(4,1)S(1)} %get-tuple-element.5), kind=kLoop, calls=%fused_computation.14 | loop fusion | flops 393216 | bytes 1572896 | tf_op jit(solution)/shard_map/jit(_take)/select_n | solution.py:35
  33.0 3.8 %all-to-all-start.1 = ((bf16[8,4,2,12,512]{4,2,3,1,0:T(2,128)(2,1)}), bf16[8,4,2,12,512]{4,2,3,1,0:T(2,128)(2,1)S(1)}, u32[]{:S(2)}, u32[]{:S(2)}) async-start(bf16[8,4,2,12,512]{4,2,3,1,0:T(2,128)(2,1)} %broadcast_select_fusion.1), calls=%async_computation.1 | async-start | bytes 1572864 | tf_op jit(solution)/shard_map/all_to_all | solution.py:36
  36.8 0.1 reshape.268
  36.9 23.9 %all-gather.5.cloned.1.call-done = bf16[16,128,512]{2,1,0:T(8,128)(2,1)} async-done(((bf16[4,128,512]{2,1,0:T(8,128)(2,1)}), bf16[16,128,512]{2,1,0:T(8,128)(2,1)}) %all-gather.5.cloned.1.call-update) | async-done | bytes 2097168 | tf_op jit(solution)/shard_map/all_gather | solution.py:30
  60.8 4.4 %gather_fusion = bf16[32,128,512]{2,1,0:T(8,128)(2,1)} fusion(bf16[16,128,512]{2,1,0:T(8,128)(2,1)} %all-gather.5.cloned.1.call-done, s32[1024]{0:T(1024)S(1)} %pad_clamp_fusion.2), kind=kCustom, calls=%fused_computation.2 | custom fusion | bytes 8388736 | tf_op jit(solution)/shard_map/jit(_take)/gather | solution.py:31
  65.2 4.7 %broadcast_select_fusion = bf16[8,4,128,512]{3,2,1,0:T(8,128)(2,1)} fusion(bf16[8,4,128,512]{3,2,1,0:T(8,128)(2,1)} %bitcast.49, pred[8,4]{1,0:T(8,128)(4,1)S(1)} %get-tuple-element.6), kind=kLoop, calls=%fused_computation.11 | loop fusion | flops 2097152 | bytes 8388640 | tf_op jit(solution)/shard_map/jit(_take)/select_n | solution.py:31
  69.9 0.0 copy-start.3
  69.9 0.0 copy-start.4
  69.9 0.0 all-to-all-done.1
  69.9 4.7 %all-to-all-start = ((bf16[8,4,128,512]{3,2,1,0:T(8,128)(2,1)}), bf16[8,4,128,512]{3,2,1,0:T(8,128)(2,1)}, u32[]{:S(2)}, u32[]{:S(2)}) async-start(bf16[8,4,128,512]{3,2,1,0:T(8,128)(2,1)} %broadcast_select_fusion), calls=%async_computation | async-start | bytes 8388608 | tf_op jit(solution)/shard_map/all_to_all | solution.py:32
  74.6 0.0 all-gather.3.cloned.1.call-start
  74.6 0.5 all-gather.3.cloned.1.call-update
  75.2 0.0 copy-done.3
  75.2 0.0 copy-done.4
  75.3 0.6 copy.38
  75.9 1.4 fusion.26
  77.3 44.7 %all-gather.3.cloned.1.call-done = bf16[2,512,512]{2,1,0:T(8,128)(2,1)} async-done(((bf16[2,64,512]{2,1,0:T(8,128)(2,1)}), bf16[2,512,512]{2,1,0:T(8,128)(2,1)}) %all-gather.3.cloned.1.call-update) | async-done | bytes 1048592 | tf_op jit(solution)/shard_map/all_gather | solution.py:38
  122.0 0.0 copy-start
  122.0 4.1 %gather_fusion.3 = bf16[8,512,512]{2,1,0:T(8,128)(2,1)} fusion(bf16[2,512,512]{2,1,0:T(8,128)(2,1)} %all-gather.3.cloned.1.call-done, s32[1024]{0:T(1024)S(1)} %pad_clamp_fusion), kind=kCustom, calls=%fused_computation.1.clone | custom fusion | bytes 8388640 | tf_op jit(solution)/shard_map/jit(_take)/gather | solution.py:50
  126.1 0.0 copy-done
  126.1 0.0 copy-start.2
  126.1 2.8 %gather_fusion.2 = bf16[8,512,512]{2,1,0:T(8,128)(2,1)} fusion(bf16[2,512,512]{2,1,0:T(8,128)(2,1)S(1)} %copy-done, s32[1024]{0:T(1024)S(1)} %pad_clamp_fusion.3), kind=kCustom, calls=%fused_computation.clone | custom fusion | bytes 8388640 | tf_op jit(solution)/shard_map/jit(_take)/gather | solution.py:45
  128.9 0.0 copy-done.2
  128.9 3.2 %fusion = f32[8,512,48]{1,2,0:T(8,128)S(1)} fusion(bf16[8,512,512]{2,1,0:T(8,128)(2,1)} %gather_fusion.3, pred[8]{0:T(512)(128)(4,1)S(1)} %get-tuple-element.11, bf16[8,2,48,512]{3,2,1,0:T(8,128)(2,1)S(1)} %copy-done.2), kind=kOutput, calls=%fused_computation.5 | convolution fusion | flops 203423744 | bytes 5374464 | tf_op jit(solution)/shard_map/sqi,sik->sqk/dot_general | solution.py:52
  132.1 0.5 fusion.12
  132.6 1.2 fusion.10
  133.8 0.0 all-to-all-done
  133.8 0.0 copy-start.1
  133.9 0.0 copy-start.5
  133.9 2.7 %copy.34 = bf16[4,2,4,128,512]{4,3,2,1,0:T(8,128)(2,1)S(1)} copy(bf16[4,2,4,128,512]{4,3,0,1,2:T(8,128)(2,1)} %bitcast.5) | data formatting | bytes 8388608 | tf_op jit(solution)/shard_map/transpose | solution.py:41
  136.5 0.8 copy-done.1
  137.3 1.3 copy-done.5
  138.6 4.4 %subtract_convert_fusion = bf16[8,512,512]{2,1,0:T(8,128)(2,1)} fusion(bf16[8,512,512]{2,1,0:T(8,128)(2,1)S(1)} %copy-done.5, bf16[8,512,512]{2,1,0:T(8,128)(2,1)S(1)} %bitcast.52, bf16[8,512,512]{2,1,0:T(8,128)(2,1)S(1)} %copy-done.1, pred[8]{0:T(512)(128)(4,1)S(1)} %get-tuple-element.12), kind=kOutput, calls=%fused_computation.4 | convolution fusion | flops 2155872256 | bytes 16777224 | tf_op jit(solution)/shard_map/sik,sjk->sij/dot_general | solution.py:46
  (10 shorter events, 0.1 us)
Async XLA Ops:
  8.0 52.8 %all-gather.5.cloned.1.call-start = ((), (), s32[]{:S(2)}) async-start(), calls=%async_computation.3 | async-start | bytes 2621440 | tf_op jit(solution)/shard_map/all_gather | solution.py:30
  33.0 36.9 %all-to-all-start.1 = ((bf16[8,4,2,12,512]{4,2,3,1,0:T(2,128)(2,1)}), bf16[8,4,2,12,512]{4,2,3,1,0:T(2,128)(2,1)S(1)}, u32[]{:S(2)}, u32[]{:S(2)}) async-start(bf16[8,4,2,12,512]{4,2,3,1,0:T(2,128)(2,1)} %broadcast_select_fusion.1), calls=%async_computation.1 | async-start | bytes 1572864 | tf_op jit(solution)/shard_map/all_to_all | solution.py:36
  69.9 5.3 %copy-start.3 = (s32[1,8]{1,0:T(1,128)S(1)}, s32[1,8]{1,0:T(1,128)}, u32[]{:S(2)}) copy-start(s32[1,8]{1,0:T(1,128)} %param.18) | copy-start | bytes 100
  69.9 5.3 %copy-start.4 = (s32[1,8]{1,0:T(1,128)S(1)}, s32[1,8]{1,0:T(1,128)}, u32[]{:S(2)}) copy-start(s32[1,8]{1,0:T(1,128)} %param.15) | copy-start | bytes 100
  69.9 64.0 %all-to-all-start = ((bf16[8,4,128,512]{3,2,1,0:T(8,128)(2,1)}), bf16[8,4,128,512]{3,2,1,0:T(8,128)(2,1)}, u32[]{:S(2)}, u32[]{:S(2)}) async-start(bf16[8,4,128,512]{3,2,1,0:T(8,128)(2,1)} %broadcast_select_fusion), calls=%async_computation | async-start | bytes 8388608 | tf_op jit(solution)/shard_map/all_to_all | solution.py:32
  74.6 47.4 %all-gather.3.cloned.1.call-start = ((), (), s32[]{:S(2)}) async-start(), calls=%async_computation.2 | async-start | bytes 1179648 | tf_op jit(solution)/shard_map/all_gather | solution.py:38
  122.0 4.1 %copy-start = (bf16[2,512,512]{2,1,0:T(8,128)(2,1)S(1)}, bf16[2,512,512]{2,1,0:T(8,128)(2,1)}, u32[]{:S(2)}) copy-start(bf16[2,512,512]{2,1,0:T(8,128)(2,1)} %all-gather.3.cloned.1.call-done) | copy-start | bytes 3145732
  126.1 2.8 %copy-start.2 = (bf16[8,2,48,512]{3,2,1,0:T(8,128)(2,1)S(1)}, bf16[8,2,48,512]{3,2,1,0:T(8,128)(2,1)}, u32[]{:S(2)}) copy-start(bf16[8,2,48,512]{3,2,1,0:T(8,128)(2,1)} %param.17) | copy-start | bytes 2359300
  133.8 3.5 %copy-start.1 = (bf16[8,512,512]{2,1,0:T(8,128)(2,1)S(1)}, bf16[8,512,512]{2,1,0:T(8,128)(2,1)}, u32[]{:S(2)}) copy-start(bf16[8,512,512]{2,1,0:T(8,128)(2,1)} %gather_fusion.2) | copy-start | bytes 12582916
  133.9 4.7 %copy-start.5 = (bf16[8,512,512]{2,1,0:T(8,128)(2,1)S(1)}, bf16[8,512,512]{2,1,0:T(8,128)(2,1)}, u32[]{:S(2)}) copy-start(bf16[8,512,512]{2,1,0:T(8,128)(2,1)} %param.14) | copy-start | bytes 12582916
Sparse Core Ops, SparseCore 0:
  10.4 50.3 all-gather.4
Sparse Core Ops, SparseCore 1:
  77.3 44.6 all-gather.2

commit v2 on v1

v2 whole, which is shorter than its diff:
```python
import functools

import jax
import jax.numpy as jnp
from jax import lax
from jax.experimental import pallas as pl
from jax.experimental.pallas import tpu as pltpu
from jax.sharding import Mesh, PartitionSpec as P

OUTER = 4
PLANE = ("gy", "core", "inner")
ROW_ALIGN = 16
VMEM_LIMIT = 48 * 1024 * 1024


def pack_kernel(dims, meta, near_cols, far_cols, *refs):
    groups, inner_size, per_bucket, quarter, far_rows, row_count = dims
    sources, (out, rows_out, sems) = refs[:-3], refs[-3:]
    which, outer, inner, bucket_outer = meta[0], meta[1], meta[2], meta[3]
    bucket = bucket_outer * inner_size + inner
    far_at = per_bucket * quarter
    rows_at = far_at + per_bucket * far_rows
    for k, source in enumerate(sources):

        @pl.when(which == k)
        def _(source=source):
            copies = []
            for g in range(groups):
                for x in range(inner_size):
                    at = g * inner_size + x
                    device = (g * OUTER + outer) * inner_size + x
                    near = near_cols[device, bucket] - bucket * per_bucket
                    far = far_cols[device, bucket] - bucket * per_bucket
                    copies.append(
                        pltpu.make_async_copy(
                            source.at[pl.ds(pl.multiple_of(near * quarter, ROW_ALIGN), quarter)],
                            out.at[at, pl.ds(0, quarter)],
                            sems.at[2 * at],
                        )
                    )
                    copies.append(
                        pltpu.make_async_copy(
                            source.at[
                                pl.ds(pl.multiple_of(far_at + far * far_rows, ROW_ALIGN), far_rows)
                            ],
                            out.at[at, pl.ds(quarter, far_rows)],
                            sems.at[2 * at + 1],
                        )
                    )
            copies.append(
                pltpu.make_async_copy(
                    source.at[pl.ds(rows_at, row_count)],
                    rows_out,
                    sems.at[2 * groups * inner_size],
                )
            )
            for copy in copies:
                copy.start()
            for copy in copies:
                copy.wait()


def pack(dims, meta, near_cols, far_cols, sources):
    groups, inner_size, per_bucket, quarter, far_rows, row_count = dims
    order = sources[0].shape[1]
    wanted = groups * inner_size
    moved = wanted * (quarter + far_rows) * order * 2
    return pl.pallas_call(
        functools.partial(pack_kernel, dims),
        grid_spec=pltpu.PrefetchScalarGridSpec(
            num_scalar_prefetch=3,
            grid=(),
            in_specs=[pl.BlockSpec(memory_space=pl.ANY)] * len(sources),
            out_specs=[pl.BlockSpec(memory_space=pl.ANY)] * 2,
            scratch_shapes=[pltpu.SemaphoreType.DMA((2 * wanted + 1,))],
        ),
        out_shape=[
            jax.ShapeDtypeStruct((wanted, quarter + far_rows, order), jnp.bfloat16),
            jax.ShapeDtypeStruct((row_count, order), jnp.bfloat16),
        ],
        cost_estimate=pl.CostEstimate(flops=0, bytes_accessed=2 * moved, transcendentals=0),
    )(meta, near_cols, far_cols, *sources)


def split_dot(exact, wide, dimensions):
    high = wide.astype(jnp.bfloat16)
    low = (wide - high.astype(jnp.float32)).astype(jnp.bfloat16)
    return lax.dot_general(
        exact, high, dimensions, preferred_element_type=jnp.float32
    ) + lax.dot_general(exact, low, dimensions, preferred_element_type=jnp.float32)


def update_kernel(dims, meta, near_rows, far_rows, near_tile, far_tile, *refs):
    groups, inner_size, quarter, far_half, shard = dims
    got = refs[:OUTER]
    shards_in = refs[OUTER : OUTER + OUTER * inner_size]
    near_out, far_out, lefts, panel, factor_p, factor_q = refs[OUTER + OUTER * inner_size :]
    row_group = lefts.shape[0]
    inner = meta[OUTER]
    step = pl.program_id(0)
    chunk = step // inner_size
    x = step % inner_size

    @pl.when(step == 0)
    def _():
        for n in range(OUTER):
            for k in range(inner_size):
                owner = meta[n] * inner_size + (inner + k) % inner_size
                for r in range(row_group):
                    lefts[r, pl.ds(pl.multiple_of(owner * shard, ROW_ALIGN), shard), :] = shards_in[
                        n * inner_size + k
                    ][r * shard : (r + 1) * shard, :]

    for n in range(OUTER):

        @pl.when(chunk == n)
        def _(n=n):
            for g in range(groups):
                at = g * inner_size + x
                panel[g * quarter : (g + 1) * quarter, :] = got[n][at, 0:quarter, :]
                middle = quarter + far_half
                factor_p[g * far_half : (g + 1) * far_half, :] = got[n][at, quarter:middle, :]
                factor_q[g * far_half : (g + 1) * far_half, :] = got[n][
                    at, middle : middle + far_half, :
                ]

    slot = meta[chunk] * inner_size + x
    across = (((1,), (1,)), ((), ()))
    product = lax.dot_general(
        lefts[near_rows[slot]], panel[...], across, preferred_element_type=jnp.float32
    )
    near_out[0] = (near_tile[0].astype(jnp.float32) - product).astype(jnp.bfloat16)
    x_trans = jnp.dot(
        far_tile[0, 0], lefts[far_rows[slot]], preferred_element_type=jnp.float32
    )
    small = split_dot(factor_q[...], x_trans, across)
    update = split_dot(factor_p[...], small, (((0,), (0,)), ((), ())))
    far_out[0] = (far_tile[0, 1].astype(jnp.float32) - update.T).astype(jnp.bfloat16)


def update(dims, meta, near_rows, far_rows, near_tiles, far_tiles, got, shards_in):
    groups, inner_size, quarter, far_half, shard = dims
    slots, order = near_tiles.shape[0], near_tiles.shape[1]
    rank = far_tiles.shape[2]

    def at_slot(*rest):
        def index(step, meta, near_rows, far_rows):
            return (meta[step // inner_size] * inner_size + step % inner_size,) + rest

        return index

    whole = pl.BlockSpec(memory_space=pltpu.VMEM)
    row_group = shards_in[0].shape[0] // shard
    return pl.pallas_call(
        functools.partial(update_kernel, dims),
        grid_spec=pltpu.PrefetchScalarGridSpec(
            num_scalar_prefetch=3,
            grid=(slots,),
            in_specs=[
                pl.BlockSpec((1, order, order), at_slot(0, 0)),
                pl.BlockSpec((1, 2, rank, order), at_slot(0, 0, 0)),
            ]
            + [whole] * (len(got) + len(shards_in)),
            out_specs=[
                pl.BlockSpec((1, order, order), at_slot(0, 0)),
                pl.BlockSpec((1, rank, order), at_slot(0, 0)),
            ],
            scratch_shapes=[
                pltpu.VMEM((row_group, order, order), jnp.bfloat16),
                pltpu.VMEM((order, order), jnp.bfloat16),
                pltpu.VMEM((groups * far_half, order), jnp.bfloat16),
                pltpu.VMEM((groups * far_half, order), jnp.bfloat16),
            ],
        ),
        out_shape=[
            jax.ShapeDtypeStruct(near_tiles.shape, jnp.bfloat16),
            jax.ShapeDtypeStruct((slots, rank, order), jnp.bfloat16),
        ],
        compiler_params=pltpu.CompilerParams(vmem_limit_bytes=VMEM_LIMIT),
        cost_estimate=pl.CostEstimate(
            flops=2 * slots * order * order * (order + 4 * rank),
            bytes_accessed=3 * slots * order * order * 2,
            transcendentals=0,
        ),
    )(meta, near_rows, far_rows, near_tiles, far_tiles, *got, *shards_in)


def shards(
    row_panel, col_near, col_far, near_tiles, near_rows, near_cols, far_tiles, far_rows, far_cols
):
    inner_size = lax.axis_size("inner")
    groups = lax.axis_size("gy") * lax.axis_size("core")
    outer, inner = lax.axis_index("outer"), lax.axis_index("inner")
    per_bucket, quarter, order = col_near.shape
    row_group, shard = row_panel.shape[:2]
    far_part = col_far.shape[2]
    far_half = -(-far_part // ROW_ALIGN) * ROW_ALIGN
    row_count = row_group * shard

    far_padded = jnp.pad(col_far, ((0, 0), (0, 0), (0, far_half - far_part), (0, 0)))
    own = jnp.concatenate(
        [
            col_near.reshape(per_bucket * quarter, order),
            far_padded.reshape(per_bucket * 2 * far_half, order),
            row_panel.reshape(row_count, order),
        ],
        axis=0,
    )

    def along(value, pairs):
        return lax.ppermute(value, "outer", pairs)

    up1 = along(own, [(0, 1), (1, 2), (2, 3)])
    down1 = along(own, [(3, 2), (2, 1), (1, 0)])
    up2 = along(up1, [(1, 2), (2, 3)])
    down2 = along(down1, [(2, 1), (1, 0)])
    relay = jnp.where(outer == 1, down2, up2)
    last = along(relay, [(1, 0), (2, 3)])

    def choose(*by_outer):
        return jnp.asarray(by_outer, jnp.int32)[outer]

    plan = [
        ((own,), jnp.int32(0), outer),
        ((up1, down1), choose(1, 0, 0, 0), choose(1, 0, 1, 2)),
        ((up2, down1, down2), choose(2, 1, 1, 0), choose(2, 2, 3, 1)),
        ((last, down2, up2), choose(0, 1, 2, 0), choose(3, 3, 0, 0)),
    ]
    dims = (groups, inner_size, per_bucket, quarter, 2 * far_half, row_count)
    got, shards_in = [], []
    for sources, which, bucket_outer in plan:
        meta = jnp.stack([which, outer, inner, bucket_outer])
        send, rows = pack(dims, meta, near_cols, far_cols, sources)
        got.append(lax.all_to_all(send, PLANE, split_axis=0, concat_axis=0, tiled=True))
        shards_in.append(rows)
        for k in range(1, inner_size):
            turn = [((i + k) % inner_size, i) for i in range(inner_size)]
            shards_in.append(lax.ppermute(rows, "inner", turn))
    meta = jnp.stack([bucket_outer for _, _, bucket_outer in plan] + [inner])
    return tuple(
        update(
            (groups, inner_size, quarter, far_half, shard),
            meta,
            near_rows[0],
            far_rows[0],
            near_tiles,
            far_tiles,
            got,
            shards_in,
        )
    )


def solution(mesh):
    groups, dev_count = mesh.shape["grp"], mesh.shape["dev"]
    fine = Mesh(
        mesh.devices.reshape(groups // 2, 2, OUTER, dev_count // OUTER),
        ("gy", "core", "outer", "inner"),
    )
    grp, dev = ("gy", "core"), ("outer", "inner")
    every = grp + dev
    placed = (
        P(grp, dev, None),
        P(dev, grp, None),
        P(dev, None, grp, None),
        P(every, None, None),
        P(every, None),
        P(),
        P(every, None, None, None),
        P(every, None),
        P(),
    )
    return jax.shard_map(
        shards,
        mesh=fine,
        in_specs=placed,
        out_specs=(P(every, None, None), P(every, None, None)),
        check_vma=False,
    )
```

time: 151 us -> 326 us (2.16)
  Pallas kernels: 0 us -> 197 us
  starting transfers between devices: 8.59 us -> 33.1 us
  blocking collectives: 18.4 us -> 0 us
  between operations: 15.6 us -> 0.91 us
  matrix products: 9.37 us -> 0 us
  local copies, waits for them, and re-layouts: 22.2 us -> 13.9 us
    pallas_call x0 -> x5, Pallas kernels: none -> 197 us  [the longest x4 185 us: pack(): pl.pallas_call(functools.partial(pack_kernel, dims), grid_spec=pltpu.Pref...]
    ppermute x0 -> x9, waiting for transfers between devices: none -> 70.4 us  [the longest x5 48 us: along(): return lax.ppermute(value, 'outer', pairs)]
    all_gather x2 -> x0, waiting for transfers between devices: 68.6 us -> none  [the longest x1 44.7 us: shards(): lax.all_gather(row_panel, ('outer', 'inner'), axis=1, tiled=True)]
    all_gather x1 -> x0, blocking collectives: 18.4 us -> none  [shards(): far_line = lax.all_gather(col_far, 'outer', axis=0, tiled=True)]
    ppermute x0 -> x9, starting transfers between devices: none -> 15 us  [the longest x5 10.8 us: along(): return lax.ppermute(value, 'outer', pairs)]
    gather x4 -> x0, local copies, waits for them, and re-layouts: 13.4 us -> none  [the longest x1 4.42 us: shards(): near_send = jnp.take(near_line, wanted(near_cols) + line, axis=0)]
    all_to_all x2 -> x4, starting transfers between devices: 8.51 us -> 18.1 us  [shards(): lax.all_to_all(send, PLANE, split_axis=0, concat_axis=0, tiled=True)]
    dot_general x4 -> x0, matrix products: 9.37 us -> none  [the longest x1 4.4 us: shards(): jnp.einsum('sik,sjk->sij', near_left, near_panel, preferred_element_type=...]
  transfers between devices with their start and end apart: 4 -> 13, of which waited for: 2 -> 8; matrix products, arithmetic and copies ran while one was open for 19% -> 4% of each run, Pallas kernels for 0% -> 43%
where the time goes in v2:
time: 326 us; the launch traced here: 325 us
  Pallas kernels  197 us (60%)
  waiting for transfers between devices  70.4 us (22%)
  starting transfers between devices  33.1 us (10%)
  local copies, waits for them, and re-layouts  13.9 us (4%)
  other arithmetic  8.93 us (3%)
    pallas_call x4, Pallas kernels, pack(): pl.pallas_call(functools.partial(pack_kernel, dims), grid_spec=pltpu.Pref...  185 us
    ppermute x5, waiting for transfers between devices, along(): return lax.ppermute(value, 'outer', pairs)  48 us
    ppermute x4, waiting for transfers between devices, shards(): shards_in.append(lax.ppermute(rows, 'inner', turn))  22.4 us
    all_to_all x4, starting transfers between devices, shards(): lax.all_to_all(send, PLANE, split_axis=0, concat_axis=0, tiled=True)  18.1 us
    pallas_call x1, Pallas kernels, update(): pl.pallas_call(functools.partial(update_kernel, dims), grid_spec=pltpu.Pr...  12.8 us
    ppermute x5, starting transfers between devices, along(): return lax.ppermute(value, 'outer', pairs)  10.8 us
    unnamed x39, local copies, waits for them, and re-layouts  8.2 us
  transfers between devices with their start and end apart: 13, of which 8 were waited for; matrix products, arithmetic and copies ran while one was open for 4% of the time, Pallas kernels for 43%

profile of v2, /device:TPU:0, one launch (start us, length us, event | category | flops | bytes accessed | tf_op | source)
XLA Modules:
  0.0 324.7 jit_solution(8436349553198685209)
XLA Ops:
  0.6 1.4 copy.18.near_cols
  2.0 1.4 copy.19.far_cols
  3.4 0.9 copy.26
  4.3 0.6 pad_add_fusion.meta
  4.9 2.0 pad_maximum_fusion.refs_0_
  6.9 46.1 %shard_map.158 = (bf16[8,160,512]{2,1,0:T(8,128)(2,1)}, bf16[128,512]{1,0:T(8,128)(2,1)}) custom-call(s32[4]{0:T(128)} %pad_add_fusion.meta, s32[32,8]{1,0:T(8,128)} %copy.18.near_cols, s32[32,8]{1,0:T(8,128)} %copy.19.far_cols, bf16[768,512]{1,0:T(8,128)(2,1)} %pad_maximum_fusion.refs_0_), custom_call_target="tpu_custom_call" | custom-call | bytes 2621440 | tf_op jit(solution)/shard_map/pallas_call | solution.py:68
  53.1 0.0 copy-start.17
  53.1 0.0 copy-start.16
  53.1 5.3 %all-to-all-start = ((bf16[8,160,512]{2,1,0:T(8,128)(2,1)}), bf16[8,160,512]{2,1,0:T(8,128)(2,1)S(1)}, u32[]{:S(2)}, u32[]{:S(2)}) async-start(bf16[8,160,512]{2,1,0:T(8,128)(2,1)} %get-tuple-element.10), calls=%async_computation | async-start | bytes 2621440 | tf_op jit(solution)/shard_map/all_to_all | solution.py:234
  58.5 1.3 collective-permute-start.1
  59.8 5.4 %collective-permute-start = (bf16[768,512]{1,0:T(8,128)(2,1)S(1)}, bf16[768,512]{1,0:T(8,128)(2,1)}, u32[]{:S(2)}, u32[]{:S(2)}) collective-permute-start(bf16[768,512]{1,0:T(8,128)(2,1)S(1)} %copy-done.9), channel_id=1, source_target_pairs={{0,2},{2,4},{4,6},{1,3},{3,5},{5,7},{8,10},{10,12},{12,14},{9,11},... | collective-permute-start | bytes 2359304 | tf_op jit(solution)/shard_map/ppermute | solution.py:211
  65.2 0.6 dynamic_slice.18
  65.8 0.6 dynamic_slice.21
  66.4 1.8 pad_add_fusion.1.meta
  68.2 12.1 %collective-permute-done.1.refs_1_ = bf16[768,512]{1,0:T(8,128)(2,1)S(1)} collective-permute-done((bf16[768,512]{1,0:T(8,128)(2,1)S(1)}, bf16[768,512]{1,0:T(8,128)(2,1)S(1)}, u32[]{:S(2)}, u32[]{:S(2)}) %collective-permute-start.1) | collective-permute-done | bytes 786464 | tf_op jit(solution)/shard_map/ppermute | solution.py:211
  80.3 1.2 collective-permute-done.refs_0_
  81.5 46.2 %shard_map.159 = (bf16[8,160,512]{2,1,0:T(8,128)(2,1)}, bf16[128,512]{1,0:T(8,128)(2,1)}) custom-call(s32[4]{0:T(128)} %pad_add_fusion.1.meta, s32[32,8]{1,0:T(8,128)} %copy.18.near_cols, s32[32,8]{1,0:T(8,128)} %copy.19.far_cols, bf16[768,512]{1,0:T(8,128)(2,1)} %collective-permute-done.refs_0_, bf16[768,512]{1,0:T(8,128)(2,1)} %copy-done.10), custom_call_target="tpu_custom_call" | custom-call | bytes 2621440 | tf_op jit(solution)/shard_map/pallas_call | solution.py:68
  127.7 4.0 %all-to-all-start.1 = ((bf16[8,160,512]{2,1,0:T(8,128)(2,1)}), bf16[8,160,512]{2,1,0:T(8,128)(2,1)S(1)}, u32[]{:S(2)}, u32[]{:S(2)}) async-start(bf16[8,160,512]{2,1,0:T(8,128)(2,1)} %get-tuple-element.11), calls=%async_computation.1 | async-start | bytes 2621440 | tf_op jit(solution)/shard_map/all_to_all | solution.py:234
  131.7 1.3 collective-permute-start.3
  133.0 1.5 collective-permute-start.2
  134.5 0.6 dynamic_slice.20
  135.2 0.6 dynamic_slice.23
  135.7 0.7 dynamic_slice.19
  136.4 0.6 dynamic_slice.22
  137.0 3.2 pad_add_fusion.2
  140.2 14.4 %collective-permute-done.3.refs_2_.refs_1_ = bf16[768,512]{1,0:T(8,128)(2,1)S(1)} collective-permute-done((bf16[768,512]{1,0:T(8,128)(2,1)}, bf16[768,512]{1,0:T(8,128)(2,1)S(1)}, u32[]{:S(2)}, u32[]{:S(2)}) %collective-permute-start.3) | collective-permute-done | bytes 786464 | tf_op jit(solution)/shard_map/ppermute | solution.py:211
  154.6 0.9 copy-done.7
  155.5 46.2 %shard_map.160 = (bf16[8,160,512]{2,1,0:T(8,128)(2,1)}, bf16[128,512]{1,0:T(8,128)(2,1)}) custom-call(s32[4]{0:T(128)} %get-tuple-element.18.meta, s32[32,8]{1,0:T(8,128)} %copy.18.near_cols, s32[32,8]{1,0:T(8,128)} %copy.19.far_cols, bf16[768,512]{1,0:T(8,128)(2,1)} %collective-permute-done.2.refs_0_.refs_2_, bf16[768,512]{1,0:T(8,128)(2,1)} %copy-done.10, ...), custom_call_target="tpu_custom_call" | custom-call | bytes 2621440 | tf_op jit(solution)/shard_map/pallas_call | solution.py:68
  201.7 4.4 %all-to-all-start.2 = ((bf16[8,160,512]{2,1,0:T(8,128)(2,1)}), bf16[8,160,512]{2,1,0:T(8,128)(2,1)}, u32[]{:S(2)}, u32[]{:S(2)}) async-start(bf16[8,160,512]{2,1,0:T(8,128)(2,1)} %get-tuple-element.12), calls=%async_computation.2 | async-start | bytes 2621440 | tf_op jit(solution)/shard_map/all_to_all | solution.py:234
  206.1 1.2 broadcast_select_fusion
  207.3 1.3 collective-permute-start.4
  208.6 20.4 %collective-permute-done.4.refs_0_ = bf16[768,512]{1,0:T(8,128)(2,1)S(1)} collective-permute-done((bf16[768,512]{1,0:T(8,128)(2,1)S(1)}, bf16[768,512]{1,0:T(8,128)(2,1)S(1)}, u32[]{:S(2)}, u32[]{:S(2)}) %collective-permute-start.4) | collective-permute-done | bytes 786464 | tf_op jit(solution)/shard_map/ppermute | solution.py:211
  229.0 0.9 copy-done.11
  229.9 46.2 %shard_map.161 = (bf16[8,160,512]{2,1,0:T(8,128)(2,1)}, bf16[128,512]{1,0:T(8,128)(2,1)}) custom-call(s32[4]{0:T(128)} %get-tuple-element.19.meta, s32[32,8]{1,0:T(8,128)} %copy.18.near_cols, s32[32,8]{1,0:T(8,128)} %copy.19.far_cols, bf16[768,512]{1,0:T(8,128)(2,1)} %copy-done.11, bf16[768,512]{1,0:T(8,128)(2,1)} %copy-done.7, ...), custom_call_target="tpu_custom_call" | custom-call | bytes 2621440 | tf_op jit(solution)/shard_map/pallas_call | solution.py:68
  276.2 4.4 %all-to-all-start.3 = ((bf16[8,160,512]{2,1,0:T(8,128)(2,1)}), bf16[8,160,512]{2,1,0:T(8,128)(2,1)}, u32[]{:S(2)}, u32[]{:S(2)}) async-start(bf16[8,160,512]{2,1,0:T(8,128)(2,1)} %get-tuple-element.13), calls=%async_computation.3 | async-start | bytes 2621440 | tf_op jit(solution)/shard_map/all_to_all | solution.py:234
  280.6 1.9 collective-permute-start.5
  282.5 0.2 collective-permute-start.6
  282.7 1.8 collective-permute-start.7
  284.5 0.2 collective-permute-start.8
  284.7 2.0 stack.32.meta
  286.7 14.4 %collective-permute-done.5.refs_5_ = bf16[128,512]{1,0:T(8,128)(2,1)} collective-permute-done((bf16[128,512]{1,0:T(8,128)(2,1)S(1)}, bf16[128,512]{1,0:T(8,128)(2,1)}, u32[]{:S(2)}, u32[]{:S(2)}) %collective-permute-start.5) | collective-permute-done | bytes 131104 | tf_op jit(solution)/shard_map/ppermute | solution.py:238
  301.2 2.8 collective-permute-done.6.refs_7_
  304.0 2.8 collective-permute-done.7.refs_9_
  306.8 2.3 collective-permute-done.8.refs_11_
  309.1 0.9 copy-done.2
  310.0 0.9 copy-done.3
  310.9 0.9 copy-done.4
  311.8 12.8 %shard_map.162 = (bf16[8,512,512]{2,1,0:T(8,128)(2,1)}, bf16[8,48,512]{2,1,0:T(8,128)(2,1)}) custom-call(s32[5]{0:T(128)S(1)} %stack.32.meta, s32[8]{0:T(128)S(1)} %bitcast.7, s32[8]{0:T(128)S(1)} %bitcast.8, bf16[8,512,512]{2,1,0:T(8,128)(2,1)} %near_tile.1, bf16[8,2,48,512]{3,2,1,0:T(8,128)(2,1)S(1)} %copy-done, ...), custom_call_target="tpu_custom_call" | custom-call | flops 2952790016 | bytes 12582912 | tf_op jit(solution)/shard_map/pallas_call | solution.py:154
  (35 shorter events, 0.1 us)
Async XLA Ops:
  53.1 5.4 %copy-start.9 = (bf16[768,512]{1,0:T(8,128)(2,1)S(1)}, bf16[768,512]{1,0:T(8,128)(2,1)}, u32[]{:S(2)}) copy-start(bf16[768,512]{1,0:T(8,128)(2,1)} %pad_maximum_fusion.refs_0_) | copy-start | bytes 2359300
  53.1 12.1 %copy-start.17 = (s32[4]{0:T(128)S(1)}, s32[4]{0:T(128)}, u32[]{:S(2)}) copy-start(s32[4]{0:T(128)} %constant.31.clone) | copy-start | bytes 52
  53.1 12.7 %copy-start.16 = (s32[4]{0:T(128)S(1)}, s32[4]{0:T(128)}, u32[]{:S(2)}) copy-start(s32[4]{0:T(128)} %constant.30.clone) | copy-start | bytes 52
  53.1 74.5 %all-to-all-start = ((bf16[8,160,512]{2,1,0:T(8,128)(2,1)}), bf16[8,160,512]{2,1,0:T(8,128)(2,1)S(1)}, u32[]{:S(2)}, u32[]{:S(2)}) async-start(bf16[8,160,512]{2,1,0:T(8,128)(2,1)} %get-tuple-element.10), calls=%async_computation | async-start | bytes 2621440 | tf_op jit(solution)/shard_map/all_to_all | solution.py:234
  58.5 21.8 %collective-permute-start.1 = (bf16[768,512]{1,0:T(8,128)(2,1)S(1)}, bf16[768,512]{1,0:T(8,128)(2,1)S(1)}, u32[]{:S(2)}, u32[]{:S(2)}) collective-permute-start(bf16[768,512]{1,0:T(8,128)(2,1)S(1)} %copy-done.9), channel_id=1, source_target_pairs={{6,4},{4,2},{2,0},{7,5},{5,3},{3,1},{14,12},{12,10},{10,8},{15,13}... | collective-permute-start | bytes 2359304 | tf_op jit(solution)/shard_map/ppermute | solution.py:211
  59.8 21.7 %collective-permute-start = (bf16[768,512]{1,0:T(8,128)(2,1)S(1)}, bf16[768,512]{1,0:T(8,128)(2,1)}, u32[]{:S(2)}, u32[]{:S(2)}) collective-permute-start(bf16[768,512]{1,0:T(8,128)(2,1)S(1)} %copy-done.9), channel_id=1, source_target_pairs={{0,2},{2,4},{4,6},{1,3},{3,5},{5,7},{8,10},{10,12},{12,14},{9,11},... | collective-permute-start | bytes 2359304 | tf_op jit(solution)/shard_map/ppermute | solution.py:211
  80.3 1.2 copy-start.10
  127.7 6.9 %copy-start.15 = (s32[4]{0:T(128)S(1)}, s32[4]{0:T(128)}, u32[]{:S(2)}) copy-start(s32[4]{0:T(128)} %constant.35.clone) | copy-start | bytes 52
  127.7 7.5 %copy-start.14 = (s32[4]{0:T(128)S(1)}, s32[4]{0:T(128)}, u32[]{:S(2)}) copy-start(s32[4]{0:T(128)} %constant.34.clone) | copy-start | bytes 52
  127.7 8.1 %copy-start.13 = (s32[4]{0:T(128)S(1)}, s32[4]{0:T(128)}, u32[]{:S(2)}) copy-start(s32[4]{0:T(128)} %constant.33.clone) | copy-start | bytes 52
  127.7 8.7 %copy-start.12 = (s32[4]{0:T(128)S(1)}, s32[4]{0:T(128)}, u32[]{:S(2)}) copy-start(s32[4]{0:T(128)} %constant.32.clone) | copy-start | bytes 52
  127.7 74.0 %all-to-all-start.1 = ((bf16[8,160,512]{2,1,0:T(8,128)(2,1)}), bf16[8,160,512]{2,1,0:T(8,128)(2,1)S(1)}, u32[]{:S(2)}, u32[]{:S(2)}) async-start(bf16[8,160,512]{2,1,0:T(8,128)(2,1)} %get-tuple-element.11), calls=%async_computation.1 | async-start | bytes 2621440 | tf_op jit(solution)/shard_map/all_to_all | solution.py:234
  131.7 22.9 %collective-permute-start.3 = (bf16[768,512]{1,0:T(8,128)(2,1)}, bf16[768,512]{1,0:T(8,128)(2,1)S(1)}, u32[]{:S(2)}, u32[]{:S(2)}) collective-permute-start(bf16[768,512]{1,0:T(8,128)(2,1)} %copy-done.10), channel_id=1, source_target_pairs={{4,2},{2,0},{5,3},{3,1},{12,10},{10,8},{13,11},{11,9},{20,18},{18,... | collective-permute-start | bytes 2359304 | tf_op jit(solution)/shard_map/ppermute | solution.py:211
  133.0 21.6 %collective-permute-start.2 = (bf16[768,512]{1,0:T(8,128)(2,1)}, bf16[768,512]{1,0:T(8,128)(2,1)}, u32[]{:S(2)}, u32[]{:S(2)}) collective-permute-start(bf16[768,512]{1,0:T(8,128)(2,1)} %collective-permute-done.refs_0_), channel_id=1, source_target_pairs={{2,4},{4,6},{3,5},{5,7},{10,12},{12,14},{11,13},{13,15},{18,20},{2... | collective-permute-start | bytes 2359304 | tf_op jit(solution)/shard_map/ppermute | solution.py:211
  154.6 0.9 copy-start.7
  201.7 4.4 %copy-start.8 = (bf16[768,512]{1,0:T(8,128)(2,1)S(1)}, bf16[768,512]{1,0:T(8,128)(2,1)}, u32[]{:S(2)}) copy-start(bf16[768,512]{1,0:T(8,128)(2,1)} %copy-done.7) | copy-start | bytes 2359300
  201.7 74.4 %all-to-all-start.2 = ((bf16[8,160,512]{2,1,0:T(8,128)(2,1)}), bf16[8,160,512]{2,1,0:T(8,128)(2,1)}, u32[]{:S(2)}, u32[]{:S(2)}) async-start(bf16[8,160,512]{2,1,0:T(8,128)(2,1)} %get-tuple-element.12), calls=%async_computation.2 | async-start | bytes 2621440 | tf_op jit(solution)/shard_map/all_to_all | solution.py:234
  207.3 21.7 %collective-permute-start.4 = (bf16[768,512]{1,0:T(8,128)(2,1)S(1)}, bf16[768,512]{1,0:T(8,128)(2,1)S(1)}, u32[]{:S(2)}, u32[]{:S(2)}) collective-permute-start(bf16[768,512]{1,0:T(8,128)(2,1)S(1)} %broadcast_select_fusion), channel_id=1, source_target_pairs={{2,0},{4,6},{3,1},{5,7},{10,8},{12,14},{11,9},{13,15},{18,16},{20,... | collective-permute-start | bytes 2359304 | tf_op jit(solution)/shard_map/ppermute | solution.py:211
  229.0 0.9 copy-start.11
  276.1 4.5 %copy-start.1 = (bf16[128,512]{1,0:T(8,128)(2,1)S(1)}, bf16[128,512]{1,0:T(8,128)(2,1)}, u32[]{:S(2)}) copy-start(bf16[128,512]{1,0:T(8,128)(2,1)} %get-tuple-element.14.refs_4_) | copy-start | bytes 393220
  276.1 33.0 %copy-start = (bf16[8,2,48,512]{3,2,1,0:T(8,128)(2,1)S(1)}, bf16[8,2,48,512]{3,2,1,0:T(8,128)(2,1)}, u32[]{:S(2)}) copy-start(bf16[8,2,48,512]{3,2,1,0:T(8,128)(2,1)} %far_tile.1) | copy-start | bytes 2359300
  276.1 33.0 %copy-start.5 = (s32[1,8]{1,0:T(1,128)S(1)}, s32[1,8]{1,0:T(1,128)}, u32[]{:S(2)}) copy-start(s32[1,8]{1,0:T(1,128)} %param.19) | copy-start | bytes 100
  276.1 33.0 %copy-start.6 = (s32[1,8]{1,0:T(1,128)S(1)}, s32[1,8]{1,0:T(1,128)}, u32[]{:S(2)}) copy-start(s32[1,8]{1,0:T(1,128)} %param.22) | copy-start | bytes 100
  276.2 33.0 %all-to-all-start.3 = ((bf16[8,160,512]{2,1,0:T(8,128)(2,1)}), bf16[8,160,512]{2,1,0:T(8,128)(2,1)}, u32[]{:S(2)}, u32[]{:S(2)}) async-start(bf16[8,160,512]{2,1,0:T(8,128)(2,1)} %get-tuple-element.13), calls=%async_computation.3 | async-start | bytes 2621440 | tf_op jit(solution)/shard_map/all_to_all | solution.py:234
  280.6 20.6 %collective-permute-start.5 = (bf16[128,512]{1,0:T(8,128)(2,1)S(1)}, bf16[128,512]{1,0:T(8,128)(2,1)}, u32[]{:S(2)}, u32[]{:S(2)}) collective-permute-start(bf16[128,512]{1,0:T(8,128)(2,1)S(1)} %copy-done.1), channel_id=1, source_target_pairs={{1,0},{0,1},{3,2},{2,3},{5,4},{4,5},{7,6},{6,7},{9,8},{8,9},{11,10... | collective-permute-start | bytes 393224 | tf_op jit(solution)/shard_map/ppermute | solution.py:238
  282.5 21.5 %collective-permute-start.6 = (bf16[128,512]{1,0:T(8,128)(2,1)}, bf16[128,512]{1,0:T(8,128)(2,1)}, u32[]{:S(2)}, u32[]{:S(2)}) collective-permute-start(bf16[128,512]{1,0:T(8,128)(2,1)} %get-tuple-element.15.refs_6_), channel_id=1, source_target_pairs={{1,0},{0,1},{3,2},{2,3},{5,4},{4,5},{7,6},{6,7},{9,8},{8,9},{11,10... | collective-permute-start | bytes 393224 | tf_op jit(solution)/shard_map/ppermute | solution.py:238
  282.7 24.1 %collective-permute-start.7 = (bf16[128,512]{1,0:T(8,128)(2,1)}, bf16[128,512]{1,0:T(8,128)(2,1)}, u32[]{:S(2)}, u32[]{:S(2)}) collective-permute-start(bf16[128,512]{1,0:T(8,128)(2,1)} %get-tuple-element.16.refs_8_), channel_id=1, source_target_pairs={{1,0},{0,1},{3,2},{2,3},{5,4},{4,5},{7,6},{6,7},{9,8},{8,9},{11,10... | collective-permute-start | bytes 393224 | tf_op jit(solution)/shard_map/ppermute | solution.py:238
  284.5 24.6 %collective-permute-start.8 = (bf16[128,512]{1,0:T(8,128)(2,1)}, bf16[128,512]{1,0:T(8,128)(2,1)}, u32[]{:S(2)}, u32[]{:S(2)}) collective-permute-start(bf16[128,512]{1,0:T(8,128)(2,1)} %get-tuple-element.17.refs_10_), channel_id=1, source_target_pairs={{1,0},{0,1},{3,2},{2,3},{5,4},{4,5},{7,6},{6,7},{9,8},{8,9},{11,10... | collective-permute-start | bytes 393224 | tf_op jit(solution)/shard_map/ppermute | solution.py:238
  309.1 0.9 copy-start.2
  310.0 0.9 copy-start.3
  310.9 0.9 copy-start.4

commit v3 on v1

v3 whole, which is shorter than its diff:
```python
import functools

import jax
import jax.numpy as jnp
from jax import lax
from jax.experimental import pallas as pl
from jax.experimental.pallas import tpu as pltpu
from jax.sharding import Mesh, PartitionSpec as P

OUTER = 4
PLANE = ("gy", "core", "inner")
ROW_ALIGN = 16
VMEM_LIMIT = 40 * 1024 * 1024
CHUNK_OWNER = ((0, 1, 2, 3), (1, 0, 1, 2), (2, 2, 3, 1), (3, 3, 0, 0))
CHUNK_SOURCE = ((0, 0, 0, 0), (1, 0, 0, 0), (2, 1, 1, 0), (0, 1, 1, 0))
VMEM = pl.BlockSpec(memory_space=pltpu.VMEM)
SMEM = pl.BlockSpec(memory_space=pltpu.SMEM)


class Sizes:
    def __init__(self, groups, inner, per_bucket, quarter, far_half, shard):
        self.groups, self.inner, self.per_bucket = groups, inner, per_bucket
        self.quarter, self.far_half, self.shard = quarter, far_half, shard
        self.far = 2 * far_half
        self.slots = OUTER * inner
        self.wanted = groups * inner
        self.stride = 2 * self.wanted + 2
        self.near_rows_at = OUTER * self.stride
        self.far_rows_at = self.near_rows_at + self.slots
        self.inner_at = self.far_rows_at + self.slots
        self.table = self.inner_at + 1

    def owner_at(self, n):
        return n * self.stride + 2 * self.wanted

    def source_at(self, n):
        return n * self.stride + 2 * self.wanted + 1


def by_position(values, position):
    result = jnp.int32(values[0])
    for k in range(1, len(values)):
        result = jnp.where(position == k, jnp.int32(values[k]), result)
    return result


def table_kernel(sizes, place, near_cols, far_cols, near_rows, far_rows, table):
    outer, inner = place[0], place[1]
    table[sizes.inner_at] = inner
    for n in range(OUTER):
        owner = by_position(CHUNK_OWNER[n], outer)
        table[sizes.owner_at(n)] = owner
        table[sizes.source_at(n)] = by_position(CHUNK_SOURCE[n], outer)
        bucket = owner * sizes.inner + inner
        for g in range(sizes.groups):
            for x in range(sizes.inner):
                at = g * sizes.inner + x
                device = (g * OUTER + outer) * sizes.inner + x
                first = bucket * sizes.per_bucket
                table[n * sizes.stride + at] = near_cols[bucket, device] - first
                table[n * sizes.stride + sizes.wanted + at] = far_cols[bucket, device] - first
    for s in range(sizes.slots):
        table[sizes.near_rows_at + s] = near_rows[0, s]
        table[sizes.far_rows_at + s] = far_rows[0, s]


def make_table(sizes, place, near_cols, far_cols, near_rows, far_rows):
    return pl.pallas_call(
        functools.partial(table_kernel, sizes),
        in_specs=[SMEM] * 5,
        out_specs=SMEM,
        out_shape=jax.ShapeDtypeStruct((sizes.table,), jnp.int32),
    )(place, near_cols.T, far_cols.T, near_rows, far_rows)


def pack_kernel(sizes, n, table, *refs):
    sources, out = refs[:-1], refs[-1]
    quarter, far = sizes.quarter, sizes.far
    far_at = sizes.per_bucket * quarter
    for k, source in enumerate(sources):

        @pl.when(table[sizes.source_at(n)] == k)
        def _(source=source):
            for at in range(sizes.wanted):
                near_pick = table[n * sizes.stride + at] * quarter
                far_pick = far_at + table[n * sizes.stride + sizes.wanted + at] * far
                out[at, 0:quarter, :] = source[
                    pl.ds(pl.multiple_of(near_pick, ROW_ALIGN), quarter), :
                ]
                out[at, quarter : quarter + far, :] = source[
                    pl.ds(pl.multiple_of(far_pick, ROW_ALIGN), far), :
                ]


def pack(sizes, n, table, sources):
    order = sources[0].shape[1]
    shape = (sizes.wanted, sizes.quarter + sizes.far, order)
    return pl.pallas_call(
        functools.partial(pack_kernel, sizes, n),
        in_specs=[SMEM] + [VMEM] * len(sources),
        out_specs=VMEM,
        out_shape=jax.ShapeDtypeStruct(shape, jnp.bfloat16),
        compiler_params=pltpu.CompilerParams(vmem_limit_bytes=VMEM_LIMIT),
        cost_estimate=pl.CostEstimate(
            flops=0, bytes_accessed=4 * shape[0] * shape[1] * shape[2], transcendentals=0
        ),
    )(table, *sources)


def lefts_kernel(sizes, table, *refs):
    parts, lefts = refs[:-1], refs[-1]
    shard = sizes.shard
    inner = table[sizes.inner_at]
    for k, part in enumerate(parts):
        x = lax.rem(inner + k, sizes.inner)
        for z in range(OUTER):
            at = pl.multiple_of((z * sizes.inner + x) * shard, ROW_ALIGN)
            for r in range(lefts.shape[0]):
                lefts[r, pl.ds(at, shard), :] = part[z, r]


def make_lefts(sizes, table, parts):
    row_group, shard, order = parts[0].shape[1:]
    return pl.pallas_call(
        functools.partial(lefts_kernel, sizes),
        in_specs=[SMEM] + [VMEM] * len(parts),
        out_specs=VMEM,
        out_shape=jax.ShapeDtypeStruct((row_group, order, order), jnp.bfloat16),
        compiler_params=pltpu.CompilerParams(vmem_limit_bytes=VMEM_LIMIT),
    )(table, *parts)


def update_kernel(sizes, n, table, near_tile, far_tile, lefts, got, *refs):
    near_out, far_out, panel, factor_p, factor_q = refs[-5:]
    x = pl.program_id(0)
    slot = table[sizes.owner_at(n)] * sizes.inner + x
    quarter, half = sizes.quarter, sizes.far_half
    for g in range(sizes.groups):
        at = g * sizes.inner + x
        panel[g * quarter : (g + 1) * quarter, :] = got[at, 0:quarter, :]
        factor_p[g * half : (g + 1) * half, :] = got[at, quarter : quarter + half, :]
        factor_q[g * half : (g + 1) * half, :] = got[at, quarter + half : quarter + 2 * half, :]
    across = (((1,), (1,)), ((), ()))
    product = lax.dot_general(
        lefts[table[sizes.near_rows_at + slot]],
        panel[...],
        across,
        preferred_element_type=jnp.float32,
    )
    near_out[0] = (near_tile[0].astype(jnp.float32) - product).astype(jnp.bfloat16)

    def halves(value):
        high = value.astype(jnp.bfloat16)
        return high, (value - high.astype(jnp.float32)).astype(jnp.bfloat16)

    x_trans = jnp.dot(
        far_tile[0, 0],
        lefts[table[sizes.far_rows_at + slot]],
        preferred_element_type=jnp.float32,
    )
    factors = factor_q[...]
    small = sum(
        lax.dot_general(part, factors, across, preferred_element_type=jnp.float32)
        for part in halves(x_trans)
    )
    factors = factor_p[...]
    change = sum(
        jnp.dot(part, factors, preferred_element_type=jnp.float32) for part in halves(small)
    )
    far_out[0] = (far_tile[0, 1].astype(jnp.float32) - change).astype(jnp.bfloat16)


def update(sizes, n, table, near_tiles, far_tiles, lefts, got, before):
    slots, order = near_tiles.shape[:2]
    rank = far_tiles.shape[2]

    def at_slot(*rest):
        return lambda x, table: (table[sizes.owner_at(n)] * sizes.inner + x,) + rest

    whole = pl.BlockSpec(memory_space=pltpu.VMEM)
    kept = pl.BlockSpec(memory_space=pl.ANY)
    return pl.pallas_call(
        functools.partial(update_kernel, sizes, n),
        grid_spec=pltpu.PrefetchScalarGridSpec(
            num_scalar_prefetch=1,
            grid=(sizes.inner,),
            in_specs=[
                pl.BlockSpec((1, order, order), at_slot(0, 0)),
                pl.BlockSpec((1, 2, rank, order), at_slot(0, 0, 0)),
                whole,
                whole,
            ]
            + [kept] * len(before),
            out_specs=[
                pl.BlockSpec((1, order, order), at_slot(0, 0)),
                pl.BlockSpec((1, rank, order), at_slot(0, 0)),
            ],
            scratch_shapes=[
                pltpu.VMEM((order, order), jnp.bfloat16),
                pltpu.VMEM((sizes.groups * sizes.far_half, order), jnp.bfloat16),
                pltpu.VMEM((sizes.groups * sizes.far_half, order), jnp.bfloat16),
            ],
        ),
        out_shape=[
            jax.ShapeDtypeStruct(near_tiles.shape, jnp.bfloat16),
            jax.ShapeDtypeStruct((slots, rank, order), jnp.bfloat16),
        ],
        input_output_aliases={5 + k: k for k in range(len(before))},
        compiler_params=pltpu.CompilerParams(vmem_limit_bytes=VMEM_LIMIT),
        cost_estimate=pl.CostEstimate(
            flops=2 * sizes.inner * order * order * (order + 4 * rank),
            bytes_accessed=4 * sizes.inner * order * order * 2,
            transcendentals=0,
        ),
    )(table, near_tiles, far_tiles, lefts, got, *before)


def shards(
    row_panel, col_near, col_far, near_tiles, near_rows, near_cols, far_tiles, far_rows, far_cols
):
    inner_size = lax.axis_size("inner")
    groups = lax.axis_size("gy") * lax.axis_size("core")
    outer, inner = lax.axis_index("outer"), lax.axis_index("inner")
    per_bucket, quarter, order = col_near.shape
    row_group, shard = row_panel.shape[:2]
    far_part = col_far.shape[2]
    far_half = -(-far_part // ROW_ALIGN) * ROW_ALIGN
    sizes = Sizes(groups, inner_size, per_bucket, quarter, far_half, shard)

    rows_line = lax.all_to_all(
        jnp.broadcast_to(row_panel, (OUTER,) + row_panel.shape),
        "outer",
        split_axis=0,
        concat_axis=0,
        tiled=True,
    )
    far_padded = jnp.pad(col_far, ((0, 0), (0, 0), (0, far_half - far_part), (0, 0)))
    own = jnp.concatenate(
        [
            col_near.reshape(per_bucket * quarter, order),
            far_padded.reshape(per_bucket * 2 * far_half, order),
        ],
        axis=0,
    )

    def along(value, pairs):
        return lax.ppermute(value, "outer", pairs)

    up1 = along(own, [(0, 1), (1, 2), (2, 3)])
    down1 = along(own, [(3, 2), (2, 1), (1, 0)])
    up2 = along(up1, [(1, 2), (2, 3)])
    down2 = along(down1, [(2, 1), (1, 0)])
    relay = jnp.where(outer == 1, down2, up2)
    last = along(relay, [(1, 0), (2, 3)])
    chunks = [(own,), (up1, down1), (up2, down1, down2), (last, relay)]

    row_parts = [rows_line]
    for k in range(1, inner_size):
        turn = [((i + k) % inner_size, i) for i in range(inner_size)]
        row_parts.append(lax.ppermute(rows_line, "inner", turn))

    table = make_table(
        sizes, jnp.stack([outer, inner]), near_cols, far_cols, near_rows, far_rows
    )
    lefts = make_lefts(sizes, table, row_parts)
    outs = ()
    for n, sources in enumerate(chunks):
        send = pack(sizes, n, table, sources)
        got = lax.all_to_all(send, PLANE, split_axis=0, concat_axis=0, tiled=True)
        outs = update(sizes, n, table, near_tiles, far_tiles, lefts, got, outs)
    return tuple(outs)


def solution(mesh):
    groups, dev_count = mesh.shape["grp"], mesh.shape["dev"]
    fine = Mesh(
        mesh.devices.reshape(groups // 2, 2, OUTER, dev_count // OUTER),
        ("gy", "core", "outer", "inner"),
    )
    grp, dev = ("gy", "core"), ("outer", "inner")
    every = grp + dev
    placed = (
        P(grp, dev, None),
        P(dev, grp, None),
        P(dev, None, grp, None),
        P(every, None, None),
        P(every, None),
        P(),
        P(every, None, None, None),
        P(every, None),
        P(),
    )
    return jax.shard_map(
        shards,
        mesh=fine,
        in_specs=placed,
        out_specs=(P(every, None, None), P(every, None, None)),
        check_vma=False,
    )
```

time: 151 us -> 155 us (1.026)
  starting transfers between devices: 8.59 us -> 33 us
  Pallas kernels: 0 us -> 20.3 us
  blocking collectives: 18.4 us -> 0 us
  waiting for transfers between devices: 69.8 us -> 86.5 us
  between operations: 15.6 us -> 0.84 us
  local copies, waits for them, and re-layouts: 22.2 us -> 11.9 us
  matrix products: 9.37 us -> 0 us
  other arithmetic: 6.41 us -> 1.79 us
    ppermute x0 -> x6, waiting for transfers between devices: none -> 76.4 us  [the longest x5 49.8 us: along(): return lax.ppermute(value, 'outer', pairs)]
    all_gather x2 -> x0, waiting for transfers between devices: 68.6 us -> none  [the longest x1 44.7 us: shards(): lax.all_gather(row_panel, ('outer', 'inner'), axis=1, tiled=True)]
    pallas_call x0 -> x10, Pallas kernels: none -> 20.3 us  [the longest x4 13 us: update(): pl.pallas_call(functools.partial(update_kernel, sizes, n), grid_spec=pltp...]
    all_gather x1 -> x0, blocking collectives: 18.4 us -> none  [shards(): far_line = lax.all_gather(col_far, 'outer', axis=0, tiled=True)]
    all_to_all x2 -> x5, starting transfers between devices: 8.51 us -> 22 us  [the longest x4 15.7 us: shards(): got = lax.all_to_all(send, PLANE, split_axis=0, concat_axis=0, tiled=True)]
    gather x4 -> x0, local copies, waits for them, and re-layouts: 13.4 us -> none  [the longest x1 4.42 us: shards(): near_send = jnp.take(near_line, wanted(near_cols) + line, axis=0)]
    ppermute x0 -> x6, starting transfers between devices: none -> 11 us  [the longest x5 9.14 us: along(): return lax.ppermute(value, 'outer', pairs)]
    all_to_all x2 -> x5, waiting for transfers between devices: 0.01 us -> 10.2 us  [the longest x1 10.2 us: shards(): lax.all_to_all(jnp.broadcast_to(row_panel, (OUTER,) + row_panel.shape), '...]
  transfers between devices with their start and end apart: 4 -> 11, of which waited for: 2 -> 6; matrix products, arithmetic and copies ran while one was open for 19% -> 1% of each run, Pallas kernels for 0% -> 10%
where the time goes in v3:
time: 155 us; the launch traced here: 154 us
  waiting for transfers between devices  86.5 us (56%)
  starting transfers between devices  33 us (21%)
  Pallas kernels  20.3 us (13%)
  local copies, waits for them, and re-layouts  11.9 us (8%)
  other arithmetic  1.79 us (1%)
    ppermute x5, waiting for transfers between devices, along(): return lax.ppermute(value, 'outer', pairs)  49.8 us
    ppermute x1, waiting for transfers between devices, shards(): row_parts.append(lax.ppermute(rows_line, 'inner', turn))  26.5 us
    all_to_all x4, starting transfers between devices, shards(): got = lax.all_to_all(send, PLANE, split_axis=0, concat_axis=0, tiled=True)  15.7 us
    pallas_call x4, Pallas kernels, update(): pl.pallas_call(functools.partial(update_kernel, sizes, n), grid_spec=pltp...  13 us
    all_to_all x1, waiting for transfers between devices, shards(): lax.all_to_all(jnp.broadcast_to(row_panel, (OUTER,) + row_panel.shape), '...  10.2 us
    unnamed x27, local copies, waits for them, and re-layouts  10.1 us
    ppermute x5, starting transfers between devices, along(): return lax.ppermute(value, 'outer', pairs)  9.14 us
    all_to_all x1, starting transfers between devices, shards(): lax.all_to_all(jnp.broadcast_to(row_panel, (OUTER,) + row_panel.shape), '...  6.32 us
  transfers between devices with their start and end apart: 11, of which 6 were waited for; matrix products, arithmetic and copies ran while one was open for 1% of the time, Pallas kernels for 10%

profile of v3, /device:TPU:0, one launch (start us, length us, event | category | flops | bytes accessed | tf_op | source)
XLA Modules:
  0.0 154.4 jit_solution(9083061894867171437)
XLA Ops:
  0.6 1.8 %broadcast_in_dim.3 = bf16[4,2,64,512]{3,2,1,0:T(8,128)(2,1)} broadcast(bf16[2,64,512]{2,1,0:T(8,128)(2,1)} %param.9), dimensions={1,2,3} | broadcast | bytes 655360 | tf_op jit(solution)/shard_map/broadcast_in_dim | solution.py:231
  2.5 6.3 %all-to-all-start = ((bf16[4,2,64,512]{3,2,1,0:T(8,128)(2,1)}), bf16[4,2,64,512]{3,2,1,0:T(8,128)(2,1)}, u32[]{:S(2)}, u32[]{:S(2)}) async-start(bf16[4,2,64,512]{3,2,1,0:T(8,128)(2,1)} %broadcast_in_dim.3), calls=%async_computation | async-start | bytes 1048576 | tf_op jit(solution)/shard_map/all_to_all | solution.py:230
  8.8 0.6 pad_add_fusion.place
  9.4 1.5 shard_map.104.table
  10.9 0.0 copy-start.10
  11.0 0.6 copy-done.10
  11.5 1.7 %shard_map.109 = bf16[8,160,512]{2,1,0:T(8,128)(2,1)} custom-call(s32[89]{0:T(128)S(1)} %copy-done.10, bf16[640,512]{1,0:T(8,128)(2,1)S(1)} %pad_maximum_fusion.refs_0_), custom_call_target="tpu_custom_call" | custom-call | bytes 2621440 | tf_op jit(solution)/shard_map/pallas_call | solution.py:98
  13.2 10.2 %all-to-all-done.refs_0_ = bf16[4,2,64,512]{3,2,1,0:T(8,128)(2,1)} async-done(((bf16[4,2,64,512]{3,2,1,0:T(8,128)(2,1)}), bf16[4,2,64,512]{3,2,1,0:T(8,128)(2,1)}, u32[]{:S(2)}, u32[]{:S(2)}) %all-to-all-start) | async-done | bytes 524320 | tf_op jit(solution)/shard_map/all_to_all | solution.py:230
  23.4 3.7 %all-to-all-start.4 = ((bf16[8,160,512]{2,1,0:T(8,128)(2,1)}), bf16[8,160,512]{2,1,0:T(8,128)(2,1)S(1)}, u32[]{:S(2)}, u32[]{:S(2)}) async-start(bf16[8,160,512]{2,1,0:T(8,128)(2,1)} %shard_map.109), calls=%async_computation.4 | async-start | bytes 2621440 | tf_op jit(solution)/shard_map/all_to_all | solution.py:269
  27.1 1.3 collective-permute-start.1
  28.4 4.6 %collective-permute-start.3 = (bf16[640,512]{1,0:T(8,128)(2,1)S(1)}, bf16[640,512]{1,0:T(8,128)(2,1)S(1)}, u32[]{:S(2)}, u32[]{:S(2)}) collective-permute-start(bf16[640,512]{1,0:T(8,128)(2,1)S(1)} %pad_maximum_fusion.refs_0_), channel_id=1, source_target_pairs={{0,2},{2,4},{4,6},{1,3},{3,5},{5,7},{8,10},{10,12},{12,14},{9,11},... | collective-permute-start | bytes 1966088 | tf_op jit(solution)/shard_map/ppermute | solution.py:247
  33.0 13.1 %collective-permute-done.1.refs_1_ = bf16[640,512]{1,0:T(8,128)(2,1)S(1)} collective-permute-done((bf16[640,512]{1,0:T(8,128)(2,1)S(1)}, bf16[640,512]{1,0:T(8,128)(2,1)S(1)}, u32[]{:S(2)}, u32[]{:S(2)}) %collective-permute-start.1) | collective-permute-done | bytes 655392 | tf_op jit(solution)/shard_map/ppermute | solution.py:247
  46.1 1.2 collective-permute-done.3.refs_0_
  47.3 1.7 %shard_map.108 = bf16[8,160,512]{2,1,0:T(8,128)(2,1)} custom-call(s32[89]{0:T(128)S(1)} %copy-done.10, bf16[640,512]{1,0:T(8,128)(2,1)S(1)} %collective-permute-done.3.refs_0_, bf16[640,512]{1,0:T(8,128)(2,1)S(1)} %collective-permute-done.1.refs_1_), custom_call_target="tpu_custom_call" | custom-call | bytes 2621440 | tf_op jit(solution)/shard_map/pallas_call | solution.py:98
  49.0 0.0 all-to-all-done.4.got
  49.0 1.1 copy-done.7
  50.1 3.8 %all-to-all-start.3 = ((bf16[8,160,512]{2,1,0:T(8,128)(2,1)}), bf16[8,160,512]{2,1,0:T(8,128)(2,1)S(1)}, u32[]{:S(2)}, u32[]{:S(2)}) async-start(bf16[8,160,512]{2,1,0:T(8,128)(2,1)} %shard_map.108), calls=%async_computation.3 | async-start | bytes 2621440 | tf_op jit(solution)/shard_map/all_to_all | solution.py:269
  54.0 1.3 collective-permute-start.2
  55.2 0.7 collective-permute-start.4
  56.0 17.8 %collective-permute-done.2.refs_2_ = bf16[640,512]{1,0:T(8,128)(2,1)S(1)} collective-permute-done((bf16[640,512]{1,0:T(8,128)(2,1)S(1)}, bf16[640,512]{1,0:T(8,128)(2,1)S(1)}, u32[]{:S(2)}, u32[]{:S(2)}) %collective-permute-start.2) | collective-permute-done | bytes 655392 | tf_op jit(solution)/shard_map/ppermute | solution.py:247
  73.7 0.0 collective-permute-done.4.refs_0_
  73.7 0.7 shard_map.107
  74.4 0.0 copy-start.6
  74.4 1.0 copy-done.6
  75.5 0.8 copy-done.9
  76.3 0.0 all-to-all-done.3.got
  76.3 3.8 %all-to-all-start.2 = ((bf16[8,160,512]{2,1,0:T(8,128)(2,1)}), bf16[8,160,512]{2,1,0:T(8,128)(2,1)S(1)}, u32[]{:S(2)}, u32[]{:S(2)}) async-start(bf16[8,160,512]{2,1,0:T(8,128)(2,1)} %copy-done.6), calls=%async_computation.2 | async-start | bytes 2621440 | tf_op jit(solution)/shard_map/all_to_all | solution.py:269
  80.1 1.2 broadcast_select_fusion.refs_1_
  81.3 1.3 collective-permute-start.5
  82.6 17.7 %collective-permute-done.5.refs_0_ = bf16[640,512]{1,0:T(8,128)(2,1)S(1)} collective-permute-done((bf16[640,512]{1,0:T(8,128)(2,1)S(1)}, bf16[640,512]{1,0:T(8,128)(2,1)S(1)}, u32[]{:S(2)}, u32[]{:S(2)}) %collective-permute-start.5) | collective-permute-done | bytes 655392 | tf_op jit(solution)/shard_map/ppermute | solution.py:247
  100.3 0.6 shard_map.106
  101.0 1.1 copy-done.5
  102.0 0.0 all-to-all-done.2.got
  102.0 1.1 copy-done.3
  103.1 4.3 %all-to-all-start.1 = ((bf16[8,160,512]{2,1,0:T(8,128)(2,1)}), bf16[8,160,512]{2,1,0:T(8,128)(2,1)}, u32[]{:S(2)}, u32[]{:S(2)}) async-start(bf16[8,160,512]{2,1,0:T(8,128)(2,1)} %copy-done.5), calls=%async_computation.1 | async-start | bytes 2621440 | tf_op jit(solution)/shard_map/all_to_all | solution.py:269
  107.4 0.0 copy-start.2
  107.4 1.9 %collective-permute-start = (bf16[4,2,64,512]{3,2,1,0:T(8,128)(2,1)}, bf16[4,2,64,512]{3,2,1,0:T(8,128)(2,1)S(1)}, u32[]{:S(2)}, u32[]{:S(2)}) collective-permute-start(bf16[4,2,64,512]{3,2,1,0:T(8,128)(2,1)} %all-to-all-done.refs_0_), channel_id=1, source_target_pairs={{1,0},{0,1},{3,2},{2,3},{5,4},{4,5},{7,6},{6,7},{9,8},{8,9},{11,10... | collective-permute-start | bytes 1572872 | tf_op jit(solution)/shard_map/ppermute | solution.py:260
  109.3 26.5 %collective-permute-done.refs_1_ = bf16[4,2,64,512]{3,2,1,0:T(8,128)(2,1)S(1)} collective-permute-done((bf16[4,2,64,512]{3,2,1,0:T(8,128)(2,1)}, bf16[4,2,64,512]{3,2,1,0:T(8,128)(2,1)S(1)}, u32[]{:S(2)}, u32[]{:S(2)}) %collective-permute-start) | collective-permute-done | bytes 524320 | tf_op jit(solution)/shard_map/ppermute | solution.py:260
  135.8 1.1 shard_map.105.lefts
  137.0 0.0 copy-done.2
  137.0 0.0 copy-start
  137.0 2.2 %copy-done = bf16[8,512,512]{2,1,0:T(8,128)(2,1)S(1)} copy-done((bf16[8,512,512]{2,1,0:T(8,128)(2,1)S(1)}, bf16[8,512,512]{2,1,0:T(8,128)(2,1)}, u32[]{:S(2)}) %copy-start) | copy-done | bytes 4194328
  139.2 2.9 %shard_map.110 = (bf16[8,512,512]{2,1,0:T(8,128)(2,1)}, bf16[8,48,512]{2,1,0:T(8,128)(2,1)}) custom-call(s32[89]{0:T(128)S(1)} %copy-done.10, bf16[8,512,512]{2,1,0:T(8,128)(2,1)S(1)} %copy-done, bf16[8,2,48,512]{3,2,1,0:T(8,128)(2,1)S(1)} %copy-done.2, bf16[2,512,512]{2,1,0:T(8,128)(2,1)S(1)} %shard_map.105.lefts, bf16[8,160,512]{2,1,0:T(8,128)(2,1)S(1)} %copy-done.8), custom_call_target="tpu_custom_call" | custom-call | flops 738197504 | bytes 4194304 | tf_op jit(solution)/shard_map/pallas_call | solution.py:182
  142.1 2.9 %shard_map.111 = (bf16[8,512,512]{2,1,0:T(8,128)(2,1)}, bf16[8,48,512]{2,1,0:T(8,128)(2,1)}) custom-call(s32[89]{0:T(128)S(1)} %copy-done.10, bf16[8,512,512]{2,1,0:T(8,128)(2,1)S(1)} %copy-done, bf16[8,2,48,512]{3,2,1,0:T(8,128)(2,1)S(1)} %copy-done.2, bf16[2,512,512]{2,1,0:T(8,128)(2,1)S(1)} %shard_map.105.lefts, ...), custom_call_target="tpu_custom_call", output_to_operand_aliasing={{0}: (5, {}), {1}: (6, {})} | custom-call | flops 738197504 | bytes 4194304 | tf_op jit(solution)/shard_map/pallas_call | solution.py:182
  145.0 2.9 %shard_map.112 = (bf16[8,512,512]{2,1,0:T(8,128)(2,1)}, bf16[8,48,512]{2,1,0:T(8,128)(2,1)}) custom-call(s32[89]{0:T(128)S(1)} %copy-done.10, bf16[8,512,512]{2,1,0:T(8,128)(2,1)S(1)} %copy-done, bf16[8,2,48,512]{3,2,1,0:T(8,128)(2,1)S(1)} %copy-done.2, bf16[2,512,512]{2,1,0:T(8,128)(2,1)S(1)} %shard_map.105.lefts, ...), custom_call_target="tpu_custom_call", output_to_operand_aliasing={{0}: (5, {}), {1}: (6, {})} | custom-call | flops 738197504 | bytes 4194304 | tf_op jit(solution)/shard_map/pallas_call | solution.py:182
  147.9 0.0 all-to-all-done.1.got
  147.9 2.2 %copy-done.1 = bf16[8,512,512]{2,1,0:T(8,128)(2,1)S(1)} copy-done((bf16[8,512,512]{2,1,0:T(8,128)(2,1)S(1)}, bf16[8,512,512]{2,1,0:T(8,128)(2,1)}, u32[]{:S(2)}) %copy-start.1) | copy-done | bytes 4194328
  150.1 4.2 %shard_map.113 = (bf16[8,512,512]{2,1,0:T(8,128)(2,1)}, bf16[8,48,512]{2,1,0:T(8,128)(2,1)}) custom-call(s32[89]{0:T(128)S(1)} %copy-done.10, bf16[8,512,512]{2,1,0:T(8,128)(2,1)S(1)} %copy-done.1, bf16[8,2,48,512]{3,2,1,0:T(8,128)(2,1)S(1)} %copy-done.2, bf16[2,512,512]{2,1,0:T(8,128)(2,1)S(1)} %shard_map.105.lefts, ...), custom_call_target="tpu_custom_call", output_to_operand_aliasing={{0}: (5, {}), {1}: (6, {})} | custom-call | flops 738197504 | bytes 4194304 | tf_op jit(solution)/shard_map/pallas_call | solution.py:182
  (16 shorter events, 0.1 us)
Async XLA Ops:
  0.6 8.2 %copy-start.12 = (bf16[4,2,12,512]{3,1,2,0:T(2,128)(2,1)S(1)}, bf16[4,2,12,512]{3,1,2,0:T(2,128)(2,1)}, u32[]{:S(2)}) copy-start(bf16[4,2,12,512]{3,1,2,0:T(2,128)(2,1)} %param.11) | copy-start | bytes 294916
  0.6 10.3 %copy-start.11 = (bf16[4,128,512]{2,1,0:T(8,128)(2,1)S(1)}, bf16[4,128,512]{2,1,0:T(8,128)(2,1)}, u32[]{:S(2)}) copy-start(bf16[4,128,512]{2,1,0:T(8,128)(2,1)} %param.10) | copy-start | bytes 1572868
  2.5 20.9 %all-to-all-start = ((bf16[4,2,64,512]{3,2,1,0:T(8,128)(2,1)}), bf16[4,2,64,512]{3,2,1,0:T(8,128)(2,1)}, u32[]{:S(2)}, u32[]{:S(2)}) async-start(bf16[4,2,64,512]{3,2,1,0:T(8,128)(2,1)} %broadcast_in_dim.3), calls=%async_computation | async-start | bytes 1048576 | tf_op jit(solution)/shard_map/all_to_all | solution.py:230
  10.9 0.7 copy-start.10
  23.4 25.6 %all-to-all-start.4 = ((bf16[8,160,512]{2,1,0:T(8,128)(2,1)}), bf16[8,160,512]{2,1,0:T(8,128)(2,1)S(1)}, u32[]{:S(2)}, u32[]{:S(2)}) async-start(bf16[8,160,512]{2,1,0:T(8,128)(2,1)} %shard_map.109), calls=%async_computation.4 | async-start | bytes 2621440 | tf_op jit(solution)/shard_map/all_to_all | solution.py:269
  27.1 19.0 %collective-permute-start.1 = (bf16[640,512]{1,0:T(8,128)(2,1)S(1)}, bf16[640,512]{1,0:T(8,128)(2,1)S(1)}, u32[]{:S(2)}, u32[]{:S(2)}) collective-permute-start(bf16[640,512]{1,0:T(8,128)(2,1)S(1)} %pad_maximum_fusion.refs_0_), channel_id=1, source_target_pairs={{6,4},{4,2},{2,0},{7,5},{5,3},{3,1},{14,12},{12,10},{10,8},{15,13}... | collective-permute-start | bytes 1966088 | tf_op jit(solution)/shard_map/ppermute | solution.py:247
  28.4 18.9 %collective-permute-start.3 = (bf16[640,512]{1,0:T(8,128)(2,1)S(1)}, bf16[640,512]{1,0:T(8,128)(2,1)S(1)}, u32[]{:S(2)}, u32[]{:S(2)}) collective-permute-start(bf16[640,512]{1,0:T(8,128)(2,1)S(1)} %pad_maximum_fusion.refs_0_), channel_id=1, source_target_pairs={{0,2},{2,4},{4,6},{1,3},{3,5},{5,7},{8,10},{10,12},{12,14},{9,11},... | collective-permute-start | bytes 1966088 | tf_op jit(solution)/shard_map/ppermute | solution.py:247
  49.0 1.1 copy-start.7
  50.1 26.2 %all-to-all-start.3 = ((bf16[8,160,512]{2,1,0:T(8,128)(2,1)}), bf16[8,160,512]{2,1,0:T(8,128)(2,1)S(1)}, u32[]{:S(2)}, u32[]{:S(2)}) async-start(bf16[8,160,512]{2,1,0:T(8,128)(2,1)} %shard_map.108), calls=%async_computation.3 | async-start | bytes 2621440 | tf_op jit(solution)/shard_map/all_to_all | solution.py:269
  54.0 19.8 %collective-permute-start.2 = (bf16[640,512]{1,0:T(8,128)(2,1)S(1)}, bf16[640,512]{1,0:T(8,128)(2,1)S(1)}, u32[]{:S(2)}, u32[]{:S(2)}) collective-permute-start(bf16[640,512]{1,0:T(8,128)(2,1)S(1)} %collective-permute-done.1.refs_1_), channel_id=1, source_target_pairs={{4,2},{2,0},{5,3},{3,1},{12,10},{10,8},{13,11},{11,9},{20,18},{18,... | collective-permute-start | bytes 1966088 | tf_op jit(solution)/shard_map/ppermute | solution.py:247
  55.2 18.5 %collective-permute-start.4 = (bf16[640,512]{1,0:T(8,128)(2,1)S(1)}, bf16[640,512]{1,0:T(8,128)(2,1)S(1)}, u32[]{:S(2)}, u32[]{:S(2)}) collective-permute-start(bf16[640,512]{1,0:T(8,128)(2,1)S(1)} %collective-permute-done.3.refs_0_), channel_id=1, source_target_pairs={{2,4},{4,6},{3,5},{5,7},{10,12},{12,14},{11,13},{13,15},{18,20},{2... | collective-permute-start | bytes 1966088 | tf_op jit(solution)/shard_map/ppermute | solution.py:247
  74.4 1.1 copy-start.6
  75.4 0.8 copy-start.9
  76.3 25.8 %all-to-all-start.2 = ((bf16[8,160,512]{2,1,0:T(8,128)(2,1)}), bf16[8,160,512]{2,1,0:T(8,128)(2,1)S(1)}, u32[]{:S(2)}, u32[]{:S(2)}) async-start(bf16[8,160,512]{2,1,0:T(8,128)(2,1)} %copy-done.6), calls=%async_computation.2 | async-start | bytes 2621440 | tf_op jit(solution)/shard_map/all_to_all | solution.py:269
  81.3 19.0 %collective-permute-start.5 = (bf16[640,512]{1,0:T(8,128)(2,1)S(1)}, bf16[640,512]{1,0:T(8,128)(2,1)S(1)}, u32[]{:S(2)}, u32[]{:S(2)}) collective-permute-start(bf16[640,512]{1,0:T(8,128)(2,1)S(1)} %broadcast_select_fusion.refs_1_), channel_id=1, source_target_pairs={{2,0},{4,6},{3,1},{5,7},{10,8},{12,14},{11,9},{13,15},{18,16},{20,... | collective-permute-start | bytes 1966088 | tf_op jit(solution)/shard_map/ppermute | solution.py:247
  101.0 1.1 copy-start.5
  102.0 1.1 copy-start.3
  103.1 44.8 %all-to-all-start.1 = ((bf16[8,160,512]{2,1,0:T(8,128)(2,1)}), bf16[8,160,512]{2,1,0:T(8,128)(2,1)}, u32[]{:S(2)}, u32[]{:S(2)}) async-start(bf16[8,160,512]{2,1,0:T(8,128)(2,1)} %copy-done.5), calls=%async_computation.1 | async-start | bytes 2621440 | tf_op jit(solution)/shard_map/all_to_all | solution.py:269
  107.4 29.6 %copy-start.2 = (bf16[8,2,48,512]{3,2,1,0:T(8,128)(2,1)S(1)}, bf16[8,2,48,512]{3,2,1,0:T(8,128)(2,1)}, u32[]{:S(2)}) copy-start(bf16[8,2,48,512]{3,2,1,0:T(8,128)(2,1)} %far_tile.7) | copy-start | bytes 2359300
  107.4 29.6 %copy-start.8 = (bf16[8,160,512]{2,1,0:T(8,128)(2,1)S(1)}, bf16[8,160,512]{2,1,0:T(8,128)(2,1)}, u32[]{:S(2)}) copy-start(bf16[8,160,512]{2,1,0:T(8,128)(2,1)} %copy-done.7) | copy-start | bytes 3932164
  107.4 28.4 %collective-permute-start = (bf16[4,2,64,512]{3,2,1,0:T(8,128)(2,1)}, bf16[4,2,64,512]{3,2,1,0:T(8,128)(2,1)S(1)}, u32[]{:S(2)}, u32[]{:S(2)}) collective-permute-start(bf16[4,2,64,512]{3,2,1,0:T(8,128)(2,1)} %all-to-all-done.refs_0_), channel_id=1, source_target_pairs={{1,0},{0,1},{3,2},{2,3},{5,4},{4,5},{7,6},{6,7},{9,8},{8,9},{11,10... | collective-permute-start | bytes 1572872 | tf_op jit(solution)/shard_map/ppermute | solution.py:260
  137.0 2.2 %copy-start = (bf16[8,512,512]{2,1,0:T(8,128)(2,1)S(1)}, bf16[8,512,512]{2,1,0:T(8,128)(2,1)}, u32[]{:S(2)}) copy-start(bf16[8,512,512]{2,1,0:T(8,128)(2,1)} %near_tile.7) | copy-start | bytes 12582916
  142.1 2.9 %copy-start.4 = (bf16[8,160,512]{2,1,0:T(8,128)(2,1)S(1)}, bf16[8,160,512]{2,1,0:T(8,128)(2,1)}, u32[]{:S(2)}) copy-start(bf16[8,160,512]{2,1,0:T(8,128)(2,1)} %copy-done.3) | copy-start | bytes 3932164
  147.9 2.2 %copy-start.1 = (bf16[8,512,512]{2,1,0:T(8,128)(2,1)S(1)}, bf16[8,512,512]{2,1,0:T(8,128)(2,1)}, u32[]{:S(2)}) copy-start(bf16[8,512,512]{2,1,0:T(8,128)(2,1)} %near_tile.7) | copy-start | bytes 12582916

commit v4 on v3

v4 whole, which is shorter than its diff:
```python
import functools

import jax
import jax.numpy as jnp
from jax import lax
from jax.experimental import pallas as pl
from jax.experimental.pallas import tpu as pltpu
from jax.sharding import Mesh, PartitionSpec as P

OUTER = 4
PLANE = ("gy", "core", "inner")
ROW_ALIGN = 16
FAR_ALIGN = 8
LANES = 128
VMEM_LIMIT = 16 * 1024 * 1024
UPDATE_VMEM = 56 * 1024 * 1024
CHUNK_OWNER = ((0, 1, 2, 3), (1, 0, 1, 2), (2, 2, 3, 1), (3, 3, 0, 0))
CHUNK_SOURCE = ((0, 0, 0, 0), (1, 0, 0, 0), (2, 1, 1, 0), (0, 1, 1, 0))
CHUNK_SOURCES = (("own",), ("up1", "down1"), ("up2", "down1", "down2"), ("last", "relay"))
PACK_FLOPS = 10**12
TOKEN = jax.ShapeDtypeStruct((8, LANES), jnp.float32)
VMEM = pl.BlockSpec(memory_space=pltpu.VMEM)
SMEM = pl.BlockSpec(memory_space=pltpu.SMEM)
KEPT = pl.BlockSpec(memory_space=pl.ANY)
HBM = pl.BlockSpec(memory_space=pltpu.HBM)


class Sizes:
    def __init__(self, groups, inner, per_bucket, quarter, far, shard):
        self.groups, self.inner, self.per_bucket = groups, inner, per_bucket
        self.quarter, self.far, self.shard = quarter, far, shard
        self.far_all = -(-groups * far // LANES) * LANES
        self.slots = OUTER * inner
        self.wanted = groups * inner
        self.stride = 2 * self.wanted + 2
        self.near_rows_at = OUTER * self.stride
        self.far_rows_at = self.near_rows_at + self.slots
        self.inner_at = self.far_rows_at + self.slots
        self.outer_at = self.inner_at + 1
        self.table = self.outer_at + 1

    def owner_at(self, n):
        return n * self.stride + 2 * self.wanted

    def source_at(self, n):
        return n * self.stride + 2 * self.wanted + 1


def by_position(values, position):
    result = jnp.int32(values[0])
    for k in range(1, len(values)):
        result = jnp.where(position == k, jnp.int32(values[k]), result)
    return result


def table_kernel(sizes, place, near_cols, far_cols, near_rows, far_rows, table):
    outer, inner = place[0], place[1]
    table[sizes.inner_at] = inner
    table[sizes.outer_at] = outer
    for n in range(OUTER):
        owner = by_position(CHUNK_OWNER[n], outer)
        table[sizes.owner_at(n)] = owner
        table[sizes.source_at(n)] = by_position(CHUNK_SOURCE[n], outer)
        bucket = owner * sizes.inner + inner
        for g in range(sizes.groups):
            for x in range(sizes.inner):
                at = g * sizes.inner + x
                device = (g * OUTER + outer) * sizes.inner + x
                first = bucket * sizes.per_bucket
                table[n * sizes.stride + at] = near_cols[bucket, device] - first
                table[n * sizes.stride + sizes.wanted + at] = far_cols[bucket, device] - first
    for s in range(sizes.slots):
        table[sizes.near_rows_at + s] = near_rows[0, s]
        table[sizes.far_rows_at + s] = far_rows[0, s]


def make_table(sizes, place, near_cols, far_cols, near_rows, far_rows):
    return pl.pallas_call(
        functools.partial(table_kernel, sizes),
        in_specs=[SMEM] * 5,
        out_specs=SMEM,
        out_shape=jax.ShapeDtypeStruct((sizes.table,), jnp.int32),
    )(place, near_cols.T, far_cols.T, near_rows, far_rows)


def pack_kernel(sizes, n, table, *refs):
    count = len(CHUNK_SOURCES[n])
    sources, out = refs[:count], refs[-1]
    quarter, far = sizes.quarter, sizes.far
    far_at = sizes.per_bucket * quarter
    for k, source in enumerate(sources):

        @pl.when(table[sizes.source_at(n)] == k)
        def _(source=source):
            for at in range(sizes.wanted):
                near_pick = table[n * sizes.stride + at] * quarter
                out[at, 0:quarter, :] = source[
                    pl.ds(pl.multiple_of(near_pick, ROW_ALIGN), quarter), :
                ]
                far_pick = table[n * sizes.stride + sizes.wanted + at]
                picked = source[far_at : far_at + far, :]
                for j in range(1, sizes.per_bucket):
                    other = source[far_at + j * far : far_at + (j + 1) * far, :]
                    picked = jnp.where(far_pick == j, other, picked)
                out[at, quarter : quarter + far, :] = picked


def pack(sizes, n, table, sources, after):
    order = sources[0].shape[1]
    shape = (sizes.wanted, sizes.quarter + sizes.far, order)
    return pl.pallas_call(
        functools.partial(pack_kernel, sizes, n),
        in_specs=[SMEM] + [VMEM] * len(sources) + [KEPT] * len(after),
        out_specs=VMEM,
        out_shape=jax.ShapeDtypeStruct(shape, jnp.bfloat16),
        compiler_params=pltpu.CompilerParams(vmem_limit_bytes=VMEM_LIMIT),
        cost_estimate=pl.CostEstimate(
            flops=PACK_FLOPS, bytes_accessed=0, transcendentals=0
        ),
    )(table, *sources, *after)


def half_kernel(sizes, table, *refs):
    parts, half, token = refs[:-2], refs[-2], refs[-1]
    token[...] = jnp.zeros_like(token)
    for k, part in enumerate(parts):
        half[lax.rem(table[sizes.outer_at] + OUTER - k, OUTER)] = part[...]


def make_half(sizes, table, parts):
    return pl.pallas_call(
        functools.partial(half_kernel, sizes),
        in_specs=[SMEM] + [VMEM] * len(parts),
        out_specs=[VMEM, VMEM],
        out_shape=[jax.ShapeDtypeStruct((OUTER,) + parts[0].shape, jnp.bfloat16), TOKEN],
        compiler_params=pltpu.CompilerParams(vmem_limit_bytes=VMEM_LIMIT),
        cost_estimate=pl.CostEstimate(flops=0, bytes_accessed=0, transcendentals=0),
    )(table, *parts)


def lefts_kernel(sizes, table, *refs):
    parts, lefts = refs[:-1], refs[-1]
    shard = sizes.shard
    inner = table[sizes.inner_at]
    for k, part in enumerate(parts):
        x = lax.rem(inner + k, sizes.inner)
        for z in range(OUTER):
            at = pl.multiple_of((z * sizes.inner + x) * shard, ROW_ALIGN)
            for r in range(lefts.shape[0]):
                lefts[r, pl.ds(at, shard), :] = part[z, r]


def make_lefts(sizes, table, parts):
    row_group, shard, order = parts[0].shape[1:]
    return pl.pallas_call(
        functools.partial(lefts_kernel, sizes),
        in_specs=[SMEM] + [VMEM] * len(parts),
        out_specs=VMEM,
        out_shape=jax.ShapeDtypeStruct((row_group, order, order), jnp.bfloat16),
        compiler_params=pltpu.CompilerParams(vmem_limit_bytes=VMEM_LIMIT),
        cost_estimate=pl.CostEstimate(flops=0, bytes_accessed=0, transcendentals=0),
    )(table, *parts)


def halves(value):
    high = value.astype(jnp.bfloat16)
    return high, (value - high.astype(jnp.float32)).astype(jnp.bfloat16)


def update_kernel(sizes, n, table, near_tiles, far_tiles, lefts, got, *refs):
    near_out, far_out, token, near, far_in, near_done, far_done, panel, factors, sems = refs[-10:]
    quarter, far = sizes.quarter, sizes.far
    first = table[sizes.owner_at(n)] * sizes.inner
    loads = []
    for x in range(sizes.inner):
        loads.append(
            (
                pltpu.make_async_copy(near_tiles.at[first + x], near.at[x], sems.at[0, x]),
                pltpu.make_async_copy(far_tiles.at[first + x], far_in.at[x], sems.at[1, x]),
            )
        )
        for load in loads[x]:
            load.start()
    token[...] = jnp.zeros_like(token)
    filled = sizes.groups * far
    if filled < sizes.far_all:
        factors[filled:, :] = jnp.zeros_like(factors[filled:, :])
    across = (((1,), (1,)), ((), ()))
    stores = []
    for x in range(sizes.inner):
        for g in range(sizes.groups):
            at = g * sizes.inner + x
            panel[g * quarter : (g + 1) * quarter, :] = got[at, 0:quarter, :]
            factors[g * far : (g + 1) * far, :] = got[at, quarter : quarter + far, :]
        product = lax.dot_general(
            lefts[table[sizes.near_rows_at + first + x]],
            panel[...],
            across,
            preferred_element_type=jnp.float32,
        )
        for load in loads[x]:
            load.wait()
        near_done[x] = (near[x].astype(jnp.float32) - product).astype(jnp.bfloat16)
        stores.append(
            pltpu.make_async_copy(near_done.at[x], near_out.at[first + x], sems.at[2, x])
        )
        stores[-1].start()
        x_trans = jnp.dot(
            far_in[x, 0],
            lefts[table[sizes.far_rows_at + first + x]],
            preferred_element_type=jnp.float32,
        )
        pairs = factors[...]
        small = sum(
            lax.dot_general(part, pairs, across, preferred_element_type=jnp.float32)
            for part in halves(x_trans)
        )
        turned = pltpu.roll(small, sizes.far_all - 1, 1)
        lane = lax.broadcasted_iota(jnp.int32, turned.shape, 1)
        turned = jnp.where(lane % 2 == 0, turned, 0.0)
        change = sum(
            jnp.dot(part, pairs, preferred_element_type=jnp.float32) for part in halves(turned)
        )
        far_done[x] = (far_in[x, 1].astype(jnp.float32) - change).astype(jnp.bfloat16)
        stores.append(
            pltpu.make_async_copy(far_done.at[x], far_out.at[first + x], sems.at[3, x])
        )
        stores[-1].start()
    for store in stores:
        store.wait()


def update(sizes, n, table, near_tiles, far_tiles, lefts, got, before):
    slots, order = near_tiles.shape[:2]
    rank = far_tiles.shape[2]
    return pl.pallas_call(
        functools.partial(update_kernel, sizes, n),
        in_specs=[SMEM, HBM, HBM, VMEM, VMEM] + [HBM] * len(before),
        out_specs=[HBM, HBM, VMEM],
        scratch_shapes=[
            pltpu.VMEM((sizes.inner, order, order), jnp.bfloat16),
            pltpu.VMEM((sizes.inner, 2, rank, order), jnp.bfloat16),
            pltpu.VMEM((sizes.inner, order, order), jnp.bfloat16),
            pltpu.VMEM((sizes.inner, rank, order), jnp.bfloat16),
            pltpu.VMEM((order, order), jnp.bfloat16),
            pltpu.VMEM((sizes.far_all, order), jnp.bfloat16),
            pltpu.SemaphoreType.DMA((4, sizes.inner)),
        ],
        out_shape=[
            jax.ShapeDtypeStruct(near_tiles.shape, jnp.bfloat16),
            jax.ShapeDtypeStruct((slots, rank, order), jnp.bfloat16),
            TOKEN,
        ],
        input_output_aliases={5 + k: k for k in range(len(before))},
        compiler_params=pltpu.CompilerParams(vmem_limit_bytes=UPDATE_VMEM),
        cost_estimate=pl.CostEstimate(flops=0, bytes_accessed=0, transcendentals=0),
    )(table, near_tiles, far_tiles, lefts, got, *before)


def shards(
    row_panel, col_near, col_far, near_tiles, near_rows, near_cols, far_tiles, far_rows, far_cols
):
    inner_size = lax.axis_size("inner")
    groups = lax.axis_size("gy") * lax.axis_size("core")
    outer, inner = lax.axis_index("outer"), lax.axis_index("inner")
    per_bucket, quarter, order = col_near.shape
    row_group, shard = row_panel.shape[:2]
    far_pairs = jnp.swapaxes(col_far, 1, 2).reshape(per_bucket, -1, order)
    far = -(-far_pairs.shape[1] // FAR_ALIGN) * FAR_ALIGN
    far_pairs = jnp.pad(far_pairs, ((0, 0), (0, far - far_pairs.shape[1]), (0, 0)))
    sizes = Sizes(groups, inner_size, per_bucket, quarter, far, shard)

    def along(value, pairs):
        return lax.ppermute(value, "outer", pairs)

    parts = [row_panel]
    for k in range(1, OUTER):
        parts.append(along(row_panel, [(i, (i + k) % OUTER) for i in range(OUTER)]))

    own = jnp.concatenate(
        [col_near.reshape(per_bucket * quarter, order), far_pairs.reshape(per_bucket * far, order)],
        axis=0,
    )
    held = {"own": own}
    held["up1"] = along(own, [(0, 1), (1, 2), (2, 3)])
    held["down1"] = along(own, [(3, 2), (2, 1), (1, 0)])
    held["up2"] = along(held["up1"], [(1, 2), (2, 3)])
    held["down2"] = along(held["down1"], [(2, 1), (1, 0)])
    held["relay"] = jnp.where(outer == 1, held["down2"], held["up2"])
    held["last"] = along(held["relay"], [(1, 0), (2, 3)])

    table = make_table(
        sizes, jnp.stack([outer, inner]), near_cols, far_cols, near_rows, far_rows
    )
    half, half_token = make_half(sizes, table, parts)
    halves = [half]
    for k in range(1, inner_size):
        turn = [((i + k) % inner_size, i) for i in range(inner_size)]
        halves.append(lax.ppermute(half, "inner", turn))
    lefts = make_lefts(sizes, table, halves)

    outs, tokens = (), []
    for n in range(OUTER):
        sources = [held[name] for name in CHUNK_SOURCES[n]]
        after = [half_token] if n == 1 else (tokens[n - 2 : n - 1] if n else [])
        send = pack(sizes, n, table, sources, after)
        got = lax.all_to_all(send, PLANE, split_axis=0, concat_axis=0, tiled=True)
        *outs, token = update(sizes, n, table, near_tiles, far_tiles, lefts, got, outs)
        tokens.append(token)
    return tuple(outs)


def solution(mesh):
    groups, dev_count = mesh.shape["grp"], mesh.shape["dev"]
    fine = Mesh(
        mesh.devices.reshape(groups // 2, 2, OUTER, dev_count // OUTER),
        ("gy", "core", "outer", "inner"),
    )
    grp, dev = ("gy", "core"), ("outer", "inner")
    every = grp + dev
    placed = (
        P(grp, dev, None),
        P(dev, grp, None),
        P(dev, None, grp, None),
        P(every, None, None),
        P(every, None),
        P(),
        P(every, None, None, None),
        P(every, None),
        P(),
    )
    return jax.shard_map(
        shards,
        mesh=fine,
        in_specs=placed,
        out_specs=(P(every, None, None), P(every, None, None)),
        check_vma=False,
    )
```

time: 155 us -> 128 us (0.83)
  waiting for transfers between devices: 86.5 us -> 42.7 us
  Pallas kernels: 20.3 us -> 38.3 us
  local copies, waits for them, and re-layouts: 11.9 us -> 4.26 us
  starting transfers between devices: 33 us -> 36.1 us
  other arithmetic: 1.79 us -> 4.52 us
    ppermute x5 -> x8, waiting for transfers between devices: 49.8 us -> 0.02 us  [along(): return lax.ppermute(value, 'outer', pairs)]
    all_to_all x4, waiting for transfers between devices: 0.01 us -> 23.9 us  [shards(): got = lax.all_to_all(send, PLANE, split_axis=0, concat_axis=0, tiled=True)]
    pallas_call x4 -> x5, Pallas kernels: 13 us -> 25.9 us  [the longest x4 24 us: update(): pl.pallas_call(functools.partial(update_kernel, sizes, n), in_specs=[SMEM...]
    all_to_all x1 -> x0, waiting for transfers between devices: 10.2 us -> none  [shards(): lax.all_to_all(jnp.broadcast_to(row_panel, (OUTER,) + row_panel.shape), '...]
    ppermute x5 -> x8, starting transfers between devices: 9.14 us -> 17.7 us  [along(): return lax.ppermute(value, 'outer', pairs)]
    ppermute x1, waiting for transfers between devices: 26.5 us -> 18.8 us  [shards(): halves.append(lax.ppermute(half, 'inner', turn))]
    unnamed x27 -> x18, local copies, waits for them, and re-layouts: 10.1 us -> 3.32 us
    all_to_all x1 -> x0, starting transfers between devices: 6.32 us -> none  [shards(): lax.all_to_all(jnp.broadcast_to(row_panel, (OUTER,) + row_panel.shape), '...]
  transfers between devices with their start and end apart: 11 -> 13, of which waited for: 6 -> 4; matrix products, arithmetic and copies ran while one was open for 1% -> 4% of each run, Pallas kernels for 10% -> 25%
where the time goes in v4:
time: 128 us; the launch traced here: 127 us
  waiting for transfers between devices  42.7 us (33%)
  Pallas kernels  38.3 us (30%)
  starting transfers between devices  36.1 us (28%)
  other arithmetic  4.52 us (4%)
  local copies, waits for them, and re-layouts  4.26 us (3%)
    pallas_call x4, Pallas kernels, update(): pl.pallas_call(functools.partial(update_kernel, sizes, n), in_specs=[SMEM...  24 us
    all_to_all x4, waiting for transfers between devices, shards(): got = lax.all_to_all(send, PLANE, split_axis=0, concat_axis=0, tiled=True)  23.9 us
    ppermute x1, waiting for transfers between devices, shards(): halves.append(lax.ppermute(half, 'inner', turn))  18.8 us
    ppermute x8, starting transfers between devices, along(): return lax.ppermute(value, 'outer', pairs)  17.7 us
    all_to_all x4, starting transfers between devices, shards(): got = lax.all_to_all(send, PLANE, split_axis=0, concat_axis=0, tiled=True)  16.5 us
    pallas_call x4, Pallas kernels, pack(): pl.pallas_call(functools.partial(pack_kernel, sizes, n), in_specs=[SMEM]...  9.66 us
    unnamed x18, local copies, waits for them, and re-layouts  3.32 us
  transfers between devices with their start and end apart: 13, of which 4 were waited for; matrix products, arithmetic and copies ran while one was open for 4% of the time, Pallas kernels for 25%

profile of v4, /device:TPU:0, one launch (start us, length us, event | category | flops | bytes accessed | tf_op | source)
XLA Modules:
  0.0 126.8 jit_solution(3089499689584024131)
XLA Ops:
  0.6 3.1 %collective-permute-start = (bf16[2,64,512]{2,1,0:T(8,128)(2,1)}, bf16[2,64,512]{2,1,0:T(8,128)(2,1)}, u32[]{:S(2)}, u32[]{:S(2)}) collective-permute-start(bf16[2,64,512]{2,1,0:T(8,128)(2,1)} %refs_0_.1), channel_id=1, source_target_pairs={{0,2},{2,4},{4,6},{6,0},{1,3},{3,5},{5,7},{7,1},{8,10},{10,12},{12... | collective-permute-start | bytes 393224 | tf_op jit(solution)/shard_map/ppermute | solution.py:274
  3.7 2.6 %collective-permute-start.1 = (bf16[2,64,512]{2,1,0:T(8,128)(2,1)}, bf16[2,64,512]{2,1,0:T(8,128)(2,1)}, u32[]{:S(2)}, u32[]{:S(2)}) collective-permute-start(bf16[2,64,512]{2,1,0:T(8,128)(2,1)} %refs_0_.1), channel_id=1, source_target_pairs={{0,4},{2,6},{4,0},{6,2},{1,5},{3,7},{5,1},{7,3},{8,12},{10,14},{12... | collective-permute-start | bytes 393224 | tf_op jit(solution)/shard_map/ppermute | solution.py:274
  6.3 1.3 %collective-permute-start.2 = (bf16[2,64,512]{2,1,0:T(8,128)(2,1)}, bf16[2,64,512]{2,1,0:T(8,128)(2,1)}, u32[]{:S(2)}, u32[]{:S(2)}) collective-permute-start(bf16[2,64,512]{2,1,0:T(8,128)(2,1)} %refs_0_.1), channel_id=1, source_target_pairs={{0,6},{2,0},{4,2},{6,4},{1,7},{3,1},{5,3},{7,5},{8,14},{10,8},{12,... | collective-permute-start | bytes 393224 | tf_op jit(solution)/shard_map/ppermute | solution.py:274
  7.6 0.9 reshape.13
  8.6 1.9 %pad_maximum_fusion.refs_0_ = bf16[608,512]{1,0:T(8,128)(2,1)} fusion(bf16[96,512]{1,0:T(8,128)(2,1)S(1)} %reshape.13, bf16[512,512]{1,0:T(8,128)(2,1)} %bitcast.6), kind=kLoop, calls=%fused_computation | loop fusion | flops 1245184 | bytes 1245184 | tf_op jit(solution)/shard_map/concatenate | solution.py:280
  10.5 1.3 %collective-permute-start.4 = (bf16[608,512]{1,0:T(8,128)(2,1)}, bf16[608,512]{1,0:T(8,128)(2,1)}, u32[]{:S(2)}, u32[]{:S(2)}) collective-permute-start(bf16[608,512]{1,0:T(8,128)(2,1)} %pad_maximum_fusion.refs_0_), channel_id=1, source_target_pairs={{6,4},{4,2},{2,0},{7,5},{5,3},{3,1},{14,12},{12,10},{10,8},{15,13}... | collective-permute-start | bytes 1867784 | tf_op jit(solution)/shard_map/ppermute | solution.py:274
  11.8 5.4 %collective-permute-start.6 = (bf16[608,512]{1,0:T(8,128)(2,1)}, bf16[608,512]{1,0:T(8,128)(2,1)}, u32[]{:S(2)}, u32[]{:S(2)}) collective-permute-start(bf16[608,512]{1,0:T(8,128)(2,1)} %pad_maximum_fusion.refs_0_), channel_id=1, source_target_pairs={{0,2},{2,4},{4,6},{1,3},{3,5},{5,7},{8,10},{10,12},{12,14},{9,11},... | collective-permute-start | bytes 1867784 | tf_op jit(solution)/shard_map/ppermute | solution.py:274
  17.2 0.6 pad_add_fusion.place
  17.8 1.5 %shard_map.104.table = s32[90]{0:T(128)} custom-call(s32[2]{0:T(128)} %pad_add_fusion.place, s32[8,32]{1,0:T(8,128)} %bitcast.8, s32[8,32]{1,0:T(8,128)} %bitcast.9, s32[1,8]{1,0:T(1,128)} %near_rows.1, s32[1,8]{1,0:T(1,128)} %far_rows.1), custom_call_target="tpu_custom_call" | custom-call | tf_op jit(solution)/shard_map/pallas_call | solution.py:78
  19.3 0.6 copy-done.2
  19.9 2.2 %shard_map.108 = bf16[8,152,512]{2,1,0:T(8,128)(2,1)} custom-call(s32[90]{0:T(128)S(1)} %copy-done.2, bf16[608,512]{1,0:T(8,128)(2,1)} %pad_maximum_fusion.refs_0_), custom_call_target="tpu_custom_call" | custom-call | flops 999999995904 | tf_op jit(solution)/shard_map/pallas_call | solution.py:111
  22.1 4.4 %all-to-all-start.1 = ((bf16[8,152,512]{2,1,0:T(8,128)(2,1)}), bf16[8,152,512]{2,1,0:T(8,128)(2,1)}, u32[]{:S(2)}, u32[]{:S(2)}) async-start(bf16[8,152,512]{2,1,0:T(8,128)(2,1)} %shard_map.108), calls=%async_computation.1 | async-start | bytes 2490368 | tf_op jit(solution)/shard_map/all_to_all | solution.py:307
  26.5 0.0 collective-permute-done.refs_1_
  26.5 0.0 collective-permute-done.1.refs_2_
  26.5 0.0 collective-permute-done.2.refs_3_
  26.5 0.0 copy-done.1
  26.5 0.0 copy-done.3
  26.5 1.9 %shard_map.105 = (bf16[4,2,64,512]{3,2,1,0:T(8,128)(2,1)}, f32[8,128]{1,0:T(8,128)S(1)}) custom-call(s32[90]{0:T(128)S(1)} %copy-done.3, bf16[2,64,512]{2,1,0:T(8,128)(2,1)S(1)} %copy-done.1, bf16[2,64,512]{2,1,0:T(8,128)(2,1)} %collective-permute-done.refs_1_, bf16[2,64,512]{2,1,0:T(8,128)(2,1)} %collective-permute-done.1.refs_2_, ...), custom_call_target="tpu_custom_call" | custom-call | tf_op jit(solution)/shard_map/pallas_call | solution.py:131
  28.4 1.9 %collective-permute-start.3 = (bf16[4,2,64,512]{3,2,1,0:T(8,128)(2,1)}, bf16[4,2,64,512]{3,2,1,0:T(8,128)(2,1)}, u32[]{:S(2)}, u32[]{:S(2)}) collective-permute-start(bf16[4,2,64,512]{3,2,1,0:T(8,128)(2,1)} %get-tuple-element.14.refs_0_), channel_id=1, source_target_pairs={{1,0},{0,1},{3,2},{2,3},{5,4},{4,5},{7,6},{6,7},{9,8},{8,9},{11,10... | collective-permute-start | bytes 1572872 | tf_op jit(solution)/shard_map/ppermute | solution.py:299
  30.3 0.0 collective-permute-done.4.refs_1_
  30.3 1.3 %collective-permute-start.5 = (bf16[608,512]{1,0:T(8,128)(2,1)}, bf16[608,512]{1,0:T(8,128)(2,1)}, u32[]{:S(2)}, u32[]{:S(2)}) collective-permute-start(bf16[608,512]{1,0:T(8,128)(2,1)} %collective-permute-done.4.refs_1_), channel_id=1, source_target_pairs={{4,2},{2,0},{5,3},{3,1},{12,10},{10,8},{13,11},{11,9},{20,18},{18,... | collective-permute-start | bytes 1867784 | tf_op jit(solution)/shard_map/ppermute | solution.py:274
  31.6 0.0 collective-permute-done.6.refs_0_
  31.6 1.5 %collective-permute-start.7 = (bf16[608,512]{1,0:T(8,128)(2,1)}, bf16[608,512]{1,0:T(8,128)(2,1)}, u32[]{:S(2)}, u32[]{:S(2)}) collective-permute-start(bf16[608,512]{1,0:T(8,128)(2,1)} %collective-permute-done.6.refs_0_), channel_id=1, source_target_pairs={{2,4},{4,6},{3,5},{5,7},{10,12},{12,14},{11,13},{13,15},{18,20},{2... | collective-permute-start | bytes 1867784 | tf_op jit(solution)/shard_map/ppermute | solution.py:274
  33.1 2.4 %shard_map.107 = bf16[8,152,512]{2,1,0:T(8,128)(2,1)} custom-call(s32[90]{0:T(128)S(1)} %copy-done.3, bf16[608,512]{1,0:T(8,128)(2,1)} %collective-permute-done.6.refs_0_, bf16[608,512]{1,0:T(8,128)(2,1)} %collective-permute-done.4.refs_1_, f32[8,128]{1,0:T(8,128)S(1)} %get-tuple-element.15.refs_2_), custom_call_target="tpu_custom_call" | custom-call | flops 999999995904 | tf_op jit(solution)/shard_map/pallas_call | solution.py:111
  35.5 18.8 %collective-permute-done.3.refs_1_ = bf16[4,2,64,512]{3,2,1,0:T(8,128)(2,1)} collective-permute-done((bf16[4,2,64,512]{3,2,1,0:T(8,128)(2,1)}, bf16[4,2,64,512]{3,2,1,0:T(8,128)(2,1)}, u32[]{:S(2)}, u32[]{:S(2)}) %collective-permute-start.3) | collective-permute-done | bytes 524320 | tf_op jit(solution)/shard_map/ppermute | solution.py:299
  54.3 1.3 %shard_map.106.lefts = bf16[2,512,512]{2,1,0:T(8,128)(2,1)S(1)} custom-call(s32[90]{0:T(128)S(1)} %copy-done.3, bf16[4,2,64,512]{3,2,1,0:T(8,128)(2,1)} %get-tuple-element.14.refs_0_, bf16[4,2,64,512]{3,2,1,0:T(8,128)(2,1)} %collective-permute-done.3.refs_1_), custom_call_target="tpu_custom_call" | custom-call | tf_op jit(solution)/shard_map/pallas_call | solution.py:155
  55.6 1.0 copy-done
  56.6 0.0 all-to-all-done.1.got
  56.6 4.3 %all-to-all-start = ((bf16[8,152,512]{2,1,0:T(8,128)(2,1)}), bf16[8,152,512]{2,1,0:T(8,128)(2,1)}, u32[]{:S(2)}, u32[]{:S(2)}) async-start(bf16[8,152,512]{2,1,0:T(8,128)(2,1)} %shard_map.107), calls=%async_computation | async-start | bytes 2490368 | tf_op jit(solution)/shard_map/all_to_all | solution.py:307
  60.9 6.0 %shard_map.109 = (bf16[8,512,512]{2,1,0:T(8,128)(2,1)}, bf16[8,48,512]{2,1,0:T(8,128)(2,1)}, f32[8,128]{1,0:T(8,128)}) custom-call(s32[90]{0:T(128)} %shard_map.104.table, bf16[8,512,512]{2,1,0:T(8,128)(2,1)} %near_tiles.7, bf16[8,2,48,512]{3,2,1,0:T(8,128)(2,1)} %far_tiles.7, bf16[2,512,512]{2,1,0:T(8,128)(2,1)} %copy-done, ...), custom_call_target="tpu_custom_call" | custom-call | tf_op jit(solution)/shard_map/pallas_call | solution.py:236
  66.9 0.0 collective-permute-done.5.refs_2_
  66.9 0.0 collective-permute-done.7.refs_0_
  66.9 2.0 %broadcast_select_fusion.refs_1_ = bf16[608,512]{1,0:T(8,128)(2,1)} fusion(bf16[608,512]{1,0:T(8,128)(2,1)} %collective-permute-done.5.refs_2_, bf16[608,512]{1,0:T(8,128)(2,1)} %collective-permute-done.7.refs_0_, pred[]{:T(512)S(6)} %eq.3), kind=kLoop, calls=%fused_computation.1 | loop fusion | flops 311296 | bytes 1867777 | tf_op jit(solution)/shard_map/jit(_where)/select_n | solution.py:289
  68.9 1.3 %collective-permute-start.8 = (bf16[608,512]{1,0:T(8,128)(2,1)}, bf16[608,512]{1,0:T(8,128)(2,1)}, u32[]{:S(2)}, u32[]{:S(2)}) collective-permute-start(bf16[608,512]{1,0:T(8,128)(2,1)} %broadcast_select_fusion.refs_1_), channel_id=1, source_target_pairs={{2,0},{4,6},{3,1},{5,7},{10,8},{12,14},{11,9},{13,15},{18,16},{20,... | collective-permute-start | bytes 1867784 | tf_op jit(solution)/shard_map/ppermute | solution.py:274
  70.2 2.6 %shard_map.112 = bf16[8,152,512]{2,1,0:T(8,128)(2,1)} custom-call(s32[90]{0:T(128)S(1)} %copy-done.4, bf16[608,512]{1,0:T(8,128)(2,1)} %collective-permute-done.7.refs_0_, bf16[608,512]{1,0:T(8,128)(2,1)} %collective-permute-done.4.refs_1_, bf16[608,512]{1,0:T(8,128)(2,1)} %collective-permute-done.5.refs_2_, f32[8,128]{1,0:T(8,128)S(1)} %copy-done.6), custom_call_target="tpu_custom_call" | custom-call | flops 999999995904 | tf_op jit(solution)/shard_map/pallas_call | solution.py:111
  72.8 5.1 %all-to-all-done.got = bf16[8,152,512]{2,1,0:T(8,128)(2,1)} async-done(((bf16[8,152,512]{2,1,0:T(8,128)(2,1)}), bf16[8,152,512]{2,1,0:T(8,128)(2,1)}, u32[]{:S(2)}, u32[]{:S(2)}) %all-to-all-start) | async-done | bytes 1245216 | tf_op jit(solution)/shard_map/all_to_all | solution.py:307
  77.9 4.3 %all-to-all-start.3 = ((bf16[8,152,512]{2,1,0:T(8,128)(2,1)}), bf16[8,152,512]{2,1,0:T(8,128)(2,1)}, u32[]{:S(2)}, u32[]{:S(2)}) async-start(bf16[8,152,512]{2,1,0:T(8,128)(2,1)} %shard_map.112), calls=%async_computation.3 | async-start | bytes 2490368 | tf_op jit(solution)/shard_map/all_to_all | solution.py:307
  82.2 0.0 copy-start.5
  82.2 6.0 %shard_map.110 = (bf16[8,512,512]{2,1,0:T(8,128)(2,1)}, bf16[8,48,512]{2,1,0:T(8,128)(2,1)}, f32[8,128]{1,0:T(8,128)}) custom-call(s32[90]{0:T(128)} %shard_map.104.table, bf16[8,512,512]{2,1,0:T(8,128)(2,1)} %near_tiles.7, bf16[8,2,48,512]{3,2,1,0:T(8,128)(2,1)} %far_tiles.7, ...), custom_call_target="tpu_custom_call", output_to_operand_aliasing={{0}: (5, {}), {1}: (6, {})} | custom-call | tf_op jit(solution)/shard_map/pallas_call | solution.py:236
  88.2 0.0 collective-permute-done.8.refs_0_
  88.2 0.7 copy-done.7
  88.9 2.4 %shard_map.111 = bf16[8,152,512]{2,1,0:T(8,128)(2,1)} custom-call(s32[90]{0:T(128)S(1)} %copy-done.5, bf16[608,512]{1,0:T(8,128)(2,1)} %collective-permute-done.8.refs_0_, bf16[608,512]{1,0:T(8,128)(2,1)} %broadcast_select_fusion.refs_1_, f32[8,128]{1,0:T(8,128)S(1)} %copy-done.7), custom_call_target="tpu_custom_call" | custom-call | flops 999999995904 | tf_op jit(solution)/shard_map/pallas_call | solution.py:111
  91.3 7.9 %all-to-all-done.3.got = bf16[8,152,512]{2,1,0:T(8,128)(2,1)} async-done(((bf16[8,152,512]{2,1,0:T(8,128)(2,1)}), bf16[8,152,512]{2,1,0:T(8,128)(2,1)}, u32[]{:S(2)}, u32[]{:S(2)}) %all-to-all-start.3) | async-done | bytes 1245216 | tf_op jit(solution)/shard_map/all_to_all | solution.py:307
  99.2 3.6 %all-to-all-start.2 = ((bf16[8,152,512]{2,1,0:T(8,128)(2,1)}), bf16[8,152,512]{2,1,0:T(8,128)(2,1)S(1)}, u32[]{:S(2)}, u32[]{:S(2)}) async-start(bf16[8,152,512]{2,1,0:T(8,128)(2,1)} %shard_map.111), calls=%async_computation.2 | async-start | bytes 2490368 | tf_op jit(solution)/shard_map/all_to_all | solution.py:307
  102.8 6.0 %shard_map.113 = (bf16[8,512,512]{2,1,0:T(8,128)(2,1)}, bf16[8,48,512]{2,1,0:T(8,128)(2,1)}, f32[8,128]{1,0:T(8,128)}) custom-call(s32[90]{0:T(128)} %shard_map.104.table, bf16[8,512,512]{2,1,0:T(8,128)(2,1)} %near_tiles.7, bf16[8,2,48,512]{3,2,1,0:T(8,128)(2,1)} %far_tiles.7, ...), custom_call_target="tpu_custom_call", output_to_operand_aliasing={{0}: (5, {}), {1}: (6, {})} | custom-call | tf_op jit(solution)/shard_map/pallas_call | solution.py:236
  108.8 11.0 %all-to-all-done.2.got = bf16[8,152,512]{2,1,0:T(8,128)(2,1)S(1)} async-done(((bf16[8,152,512]{2,1,0:T(8,128)(2,1)}), bf16[8,152,512]{2,1,0:T(8,128)(2,1)S(1)}, u32[]{:S(2)}, u32[]{:S(2)}) %all-to-all-start.2) | async-done | bytes 1245216 | tf_op jit(solution)/shard_map/all_to_all | solution.py:307
  119.8 1.1 copy-done.8
  120.8 6.0 %shard_map.114 = (bf16[8,512,512]{2,1,0:T(8,128)(2,1)}, bf16[8,48,512]{2,1,0:T(8,128)(2,1)}, f32[8,128]{1,0:T(8,128)}) custom-call(s32[90]{0:T(128)} %shard_map.104.table, bf16[8,512,512]{2,1,0:T(8,128)(2,1)} %near_tiles.7, bf16[8,2,48,512]{3,2,1,0:T(8,128)(2,1)} %far_tiles.7, ...), custom_call_target="tpu_custom_call", output_to_operand_aliasing={{0}: (5, {}), {1}: (6, {})} | custom-call | tf_op jit(solution)/shard_map/pallas_call | solution.py:236
  (11 shorter events, 0.0 us)
Async XLA Ops:
  0.6 25.8 %collective-permute-start = (bf16[2,64,512]{2,1,0:T(8,128)(2,1)}, bf16[2,64,512]{2,1,0:T(8,128)(2,1)}, u32[]{:S(2)}, u32[]{:S(2)}) collective-permute-start(bf16[2,64,512]{2,1,0:T(8,128)(2,1)} %refs_0_.1), channel_id=1, source_target_pairs={{0,2},{2,4},{4,6},{6,0},{1,3},{3,5},{5,7},{7,1},{8,10},{10,12},{12... | collective-permute-start | bytes 393224 | tf_op jit(solution)/shard_map/ppermute | solution.py:274
  3.7 22.8 %collective-permute-start.1 = (bf16[2,64,512]{2,1,0:T(8,128)(2,1)}, bf16[2,64,512]{2,1,0:T(8,128)(2,1)}, u32[]{:S(2)}, u32[]{:S(2)}) collective-permute-start(bf16[2,64,512]{2,1,0:T(8,128)(2,1)} %refs_0_.1), channel_id=1, source_target_pairs={{0,4},{2,6},{4,0},{6,2},{1,5},{3,7},{5,1},{7,3},{8,12},{10,14},{12... | collective-permute-start | bytes 393224 | tf_op jit(solution)/shard_map/ppermute | solution.py:274
  6.3 20.2 %collective-permute-start.2 = (bf16[2,64,512]{2,1,0:T(8,128)(2,1)}, bf16[2,64,512]{2,1,0:T(8,128)(2,1)}, u32[]{:S(2)}, u32[]{:S(2)}) collective-permute-start(bf16[2,64,512]{2,1,0:T(8,128)(2,1)} %refs_0_.1), channel_id=1, source_target_pairs={{0,6},{2,0},{4,2},{6,4},{1,7},{3,1},{5,3},{7,5},{8,14},{10,8},{12,... | collective-permute-start | bytes 393224 | tf_op jit(solution)/shard_map/ppermute | solution.py:274
  10.5 19.8 %collective-permute-start.4 = (bf16[608,512]{1,0:T(8,128)(2,1)}, bf16[608,512]{1,0:T(8,128)(2,1)}, u32[]{:S(2)}, u32[]{:S(2)}) collective-permute-start(bf16[608,512]{1,0:T(8,128)(2,1)} %pad_maximum_fusion.refs_0_), channel_id=1, source_target_pairs={{6,4},{4,2},{2,0},{7,5},{5,3},{3,1},{14,12},{12,10},{10,8},{15,13}... | collective-permute-start | bytes 1867784 | tf_op jit(solution)/shard_map/ppermute | solution.py:274
  11.8 19.8 %collective-permute-start.6 = (bf16[608,512]{1,0:T(8,128)(2,1)}, bf16[608,512]{1,0:T(8,128)(2,1)}, u32[]{:S(2)}, u32[]{:S(2)}) collective-permute-start(bf16[608,512]{1,0:T(8,128)(2,1)} %pad_maximum_fusion.refs_0_), channel_id=1, source_target_pairs={{0,2},{2,4},{4,6},{1,3},{3,5},{5,7},{8,10},{10,12},{12,14},{9,11},... | collective-permute-start | bytes 1867784 | tf_op jit(solution)/shard_map/ppermute | solution.py:274
  19.2 0.6 copy-start.2
  22.1 4.4 %copy-start.1 = (bf16[2,64,512]{2,1,0:T(8,128)(2,1)S(1)}, bf16[2,64,512]{2,1,0:T(8,128)(2,1)}, u32[]{:S(2)}) copy-start(bf16[2,64,512]{2,1,0:T(8,128)(2,1)} %refs_0_.1) | copy-start | bytes 393220
  22.1 4.4 %copy-start.3 = (s32[90]{0:T(128)S(1)}, s32[90]{0:T(128)}, u32[]{:S(2)}) copy-start(s32[90]{0:T(128)} %shard_map.104.table) | copy-start | bytes 1084
  22.1 34.5 %all-to-all-start.1 = ((bf16[8,152,512]{2,1,0:T(8,128)(2,1)}), bf16[8,152,512]{2,1,0:T(8,128)(2,1)}, u32[]{:S(2)}, u32[]{:S(2)}) async-start(bf16[8,152,512]{2,1,0:T(8,128)(2,1)} %shard_map.108), calls=%async_computation.1 | async-start | bytes 2490368 | tf_op jit(solution)/shard_map/all_to_all | solution.py:307
  28.4 25.9 %collective-permute-start.3 = (bf16[4,2,64,512]{3,2,1,0:T(8,128)(2,1)}, bf16[4,2,64,512]{3,2,1,0:T(8,128)(2,1)}, u32[]{:S(2)}, u32[]{:S(2)}) collective-permute-start(bf16[4,2,64,512]{3,2,1,0:T(8,128)(2,1)} %get-tuple-element.14.refs_0_), channel_id=1, source_target_pairs={{1,0},{0,1},{3,2},{2,3},{5,4},{4,5},{7,6},{6,7},{9,8},{8,9},{11,10... | collective-permute-start | bytes 1572872 | tf_op jit(solution)/shard_map/ppermute | solution.py:299
  30.3 36.6 %collective-permute-start.5 = (bf16[608,512]{1,0:T(8,128)(2,1)}, bf16[608,512]{1,0:T(8,128)(2,1)}, u32[]{:S(2)}, u32[]{:S(2)}) collective-permute-start(bf16[608,512]{1,0:T(8,128)(2,1)} %collective-permute-done.4.refs_1_), channel_id=1, source_target_pairs={{4,2},{2,0},{5,3},{3,1},{12,10},{10,8},{13,11},{11,9},{20,18},{18,... | collective-permute-start | bytes 1867784 | tf_op jit(solution)/shard_map/ppermute | solution.py:274
  31.6 35.3 %collective-permute-start.7 = (bf16[608,512]{1,0:T(8,128)(2,1)}, bf16[608,512]{1,0:T(8,128)(2,1)}, u32[]{:S(2)}, u32[]{:S(2)}) collective-permute-start(bf16[608,512]{1,0:T(8,128)(2,1)} %collective-permute-done.6.refs_0_), channel_id=1, source_target_pairs={{2,4},{4,6},{3,5},{5,7},{10,12},{12,14},{11,13},{13,15},{18,20},{2... | collective-permute-start | bytes 1867784 | tf_op jit(solution)/shard_map/ppermute | solution.py:274
  55.6 1.0 copy-start
  56.6 21.3 %all-to-all-start = ((bf16[8,152,512]{2,1,0:T(8,128)(2,1)}), bf16[8,152,512]{2,1,0:T(8,128)(2,1)}, u32[]{:S(2)}, u32[]{:S(2)}) async-start(bf16[8,152,512]{2,1,0:T(8,128)(2,1)} %shard_map.107), calls=%async_computation | async-start | bytes 2490368 | tf_op jit(solution)/shard_map/all_to_all | solution.py:307
  66.9 3.3 %copy-start.4 = (s32[90]{0:T(128)S(1)}, s32[90]{0:T(128)}, u32[]{:S(2)}) copy-start(s32[90]{0:T(128)} %shard_map.104.table) | copy-start | bytes 1084
  66.9 3.3 %copy-start.6 = (f32[8,128]{1,0:T(8,128)S(1)}, f32[8,128]{1,0:T(8,128)}, u32[]{:S(2)}) copy-start(f32[8,128]{1,0:T(8,128)} %get-tuple-element.19.refs_3_) | copy-start | bytes 12292
  68.9 19.3 %collective-permute-start.8 = (bf16[608,512]{1,0:T(8,128)(2,1)}, bf16[608,512]{1,0:T(8,128)(2,1)}, u32[]{:S(2)}, u32[]{:S(2)}) collective-permute-start(bf16[608,512]{1,0:T(8,128)(2,1)} %broadcast_select_fusion.refs_1_), channel_id=1, source_target_pairs={{2,0},{4,6},{3,1},{5,7},{10,8},{12,14},{11,9},{13,15},{18,16},{20,... | collective-permute-start | bytes 1867784 | tf_op jit(solution)/shard_map/ppermute | solution.py:274
  77.9 21.3 %all-to-all-start.3 = ((bf16[8,152,512]{2,1,0:T(8,128)(2,1)}), bf16[8,152,512]{2,1,0:T(8,128)(2,1)}, u32[]{:S(2)}, u32[]{:S(2)}) async-start(bf16[8,152,512]{2,1,0:T(8,128)(2,1)} %shard_map.112), calls=%async_computation.3 | async-start | bytes 2490368 | tf_op jit(solution)/shard_map/all_to_all | solution.py:307
  82.2 6.0 %copy-start.5 = (s32[90]{0:T(128)S(1)}, s32[90]{0:T(128)}, u32[]{:S(2)}) copy-start(s32[90]{0:T(128)} %shard_map.104.table) | copy-start | bytes 1084
  88.2 0.7 copy-start.7
  99.2 20.5 %all-to-all-start.2 = ((bf16[8,152,512]{2,1,0:T(8,128)(2,1)}), bf16[8,152,512]{2,1,0:T(8,128)(2,1)S(1)}, u32[]{:S(2)}, u32[]{:S(2)}) async-start(bf16[8,152,512]{2,1,0:T(8,128)(2,1)} %shard_map.111), calls=%async_computation.2 | async-start | bytes 2490368 | tf_op jit(solution)/shard_map/all_to_all | solution.py:307
  119.8 1.1 copy-start.8

commit v5 on v3

v5 whole, which is shorter than its diff:
```python
import functools

import jax
import jax.numpy as jnp
from jax import lax
from jax.experimental import pallas as pl
from jax.experimental.pallas import tpu as pltpu
from jax.sharding import Mesh, PartitionSpec as P

OUTER = 4
PLANE = ("gy", "core", "inner")
ROW_ALIGN = 16
FAR_ALIGN = 8
LANES = 128
VMEM_LIMIT = 16 * 1024 * 1024
CHUNK_OWNER = ((0, 1, 2, 3), (1, 0, 3, 2), (2, 2, 1, 1), (3, 3, 0, 0))
CHUNK_SOURCE = ((0, 0, 0, 0), (0, 0, 0, 0), (1, 0, 0, 1), (1, 0, 0, 1))
CHUNK_SOURCES = (("own",), ("pair",), ("middle", "pass2"), ("cross", "pass3"))
PACK_FLOPS = 10**10
UPDATE_FLOPS = 3 * 10**9
VMEM = pl.BlockSpec(memory_space=pltpu.VMEM)
SMEM = pl.BlockSpec(memory_space=pltpu.SMEM)
KEPT = pl.BlockSpec(memory_space=pl.ANY)


class Sizes:
    def __init__(self, groups, inner, per_bucket, quarter, far, shard):
        self.groups, self.inner, self.per_bucket = groups, inner, per_bucket
        self.quarter, self.far, self.shard = quarter, far, shard
        self.far_all = -(-groups * far // LANES) * LANES
        self.slots = OUTER * inner
        self.wanted = groups * inner
        self.stride = 2 * self.wanted + 2
        self.near_rows_at = OUTER * self.stride
        self.far_rows_at = self.near_rows_at + self.slots
        self.inner_at = self.far_rows_at + self.slots
        self.outer_at = self.inner_at + 1
        self.table = self.outer_at + 1

    def owner_at(self, n):
        return n * self.stride + 2 * self.wanted

    def source_at(self, n):
        return n * self.stride + 2 * self.wanted + 1


def by_position(values, position):
    result = jnp.int32(values[0])
    for k in range(1, len(values)):
        result = jnp.where(position == k, jnp.int32(values[k]), result)
    return result


def fill_table(sizes, place, near_cols, far_cols, near_rows, far_rows, table):
    outer, inner = place[0], place[1]
    table[sizes.inner_at] = inner
    table[sizes.outer_at] = outer
    for n in range(OUTER):
        owner = by_position(CHUNK_OWNER[n], outer)
        table[sizes.owner_at(n)] = owner
        table[sizes.source_at(n)] = by_position(CHUNK_SOURCE[n], outer)
        bucket = owner * sizes.inner + inner
        for g in range(sizes.groups):
            for x in range(sizes.inner):
                at = g * sizes.inner + x
                device = (g * OUTER + outer) * sizes.inner + x
                first = bucket * sizes.per_bucket
                table[n * sizes.stride + at] = near_cols[bucket, device] - first
                table[n * sizes.stride + sizes.wanted + at] = far_cols[bucket, device] - first
    for s in range(sizes.slots):
        table[sizes.near_rows_at + s] = near_rows[0, s]
        table[sizes.far_rows_at + s] = far_rows[0, s]


def pack_from(sizes, n, table, source, out):
    quarter, far = sizes.quarter, sizes.far
    far_at = sizes.per_bucket * quarter
    for at in range(sizes.wanted):
        near_pick = table[n * sizes.stride + at] * quarter
        out[at, 0:quarter, :] = source[pl.ds(pl.multiple_of(near_pick, ROW_ALIGN), quarter), :]
        far_pick = table[n * sizes.stride + sizes.wanted + at]
        picked = source[far_at : far_at + far, :]
        for j in range(1, sizes.per_bucket):
            other = source[far_at + j * far : far_at + (j + 1) * far, :]
            picked = jnp.where(far_pick == j, other, picked)
        out[at, quarter : quarter + far, :] = picked


def first_kernel(sizes, place, near_cols, far_cols, near_rows, far_rows, near, pairs, *outs):
    table, own, out = outs
    fill_table(sizes, place, near_cols, far_cols, near_rows, far_rows, table)
    quarter, far = sizes.quarter, sizes.far
    far_at = sizes.per_bucket * quarter
    for j in range(sizes.per_bucket):
        own[j * quarter : (j + 1) * quarter, :] = near[j]
        own[far_at + j * far : far_at + (j + 1) * far, :] = pairs[j]
    pack_from(sizes, 0, table, own, out)


def send_shape(sizes, order):
    return jax.ShapeDtypeStruct((sizes.wanted, sizes.quarter + sizes.far, order), jnp.bfloat16)


def first(sizes, place, near_cols, far_cols, near_rows, far_rows, near, pairs):
    order = near.shape[2]
    rows = sizes.per_bucket * (sizes.quarter + sizes.far)
    return pl.pallas_call(
        functools.partial(first_kernel, sizes),
        in_specs=[SMEM] * 5 + [VMEM] * 2,
        out_specs=[SMEM, VMEM, VMEM],
        out_shape=[
            jax.ShapeDtypeStruct((sizes.table,), jnp.int32),
            jax.ShapeDtypeStruct((rows, order), jnp.bfloat16),
            send_shape(sizes, order),
        ],
        compiler_params=pltpu.CompilerParams(vmem_limit_bytes=VMEM_LIMIT),
        cost_estimate=pl.CostEstimate(flops=0, bytes_accessed=0, transcendentals=0),
    )(place, near_cols.T, far_cols.T, near_rows, far_rows, near, pairs)


def pack_kernel(sizes, n, table, *refs):
    sources, out = refs[: len(CHUNK_SOURCES[n])], refs[-1]
    for k, source in enumerate(sources):

        @pl.when(table[sizes.source_at(n)] == k)
        def _(source=source):
            pack_from(sizes, n, table, source, out)


def pack(sizes, n, table, sources, after):
    return pl.pallas_call(
        functools.partial(pack_kernel, sizes, n),
        in_specs=[SMEM] + [VMEM] * len(sources) + [KEPT] * len(after),
        out_specs=VMEM,
        out_shape=send_shape(sizes, sources[0].shape[1]),
        compiler_params=pltpu.CompilerParams(vmem_limit_bytes=VMEM_LIMIT),
        cost_estimate=pl.CostEstimate(flops=PACK_FLOPS, bytes_accessed=0, transcendentals=0),
    )(table, *sources, *after)


def rows_kernel(after, *refs):
    parts, out, token = refs[:-2], refs[-2], refs[-1]
    for k, part in enumerate(parts):
        out[k] = part[...]
    token[...] = jnp.zeros_like(token)


def join_rows(parts, after):
    return pl.pallas_call(
        rows_kernel,
        in_specs=[KEPT] + [VMEM] * len(parts),
        out_specs=[VMEM, VMEM],
        out_shape=[
            jax.ShapeDtypeStruct((len(parts),) + parts[0].shape, jnp.bfloat16),
            jax.ShapeDtypeStruct((8, LANES), jnp.float32),
        ],
        compiler_params=pltpu.CompilerParams(vmem_limit_bytes=VMEM_LIMIT),
        cost_estimate=pl.CostEstimate(flops=PACK_FLOPS, bytes_accessed=0, transcendentals=0),
    )(after, *parts)


def lefts_kernel(sizes, table, *refs):
    parts, lefts = refs[:-1], refs[-1]
    shard = sizes.shard
    inner, outer = table[sizes.inner_at], table[sizes.outer_at]
    for step, part in enumerate(parts):
        z = lax.rem(outer + OUTER - step, OUTER)
        for k in range(sizes.inner):
            x = lax.rem(inner + k, sizes.inner)
            at = pl.multiple_of((z * sizes.inner + x) * shard, ROW_ALIGN)
            for r in range(lefts.shape[0]):
                lefts[r, pl.ds(at, shard), :] = part[k, r]


def make_lefts(sizes, table, parts):
    row_group, shard, order = parts[0].shape[1:]
    return pl.pallas_call(
        functools.partial(lefts_kernel, sizes),
        in_specs=[SMEM] + [VMEM] * len(parts),
        out_specs=VMEM,
        out_shape=jax.ShapeDtypeStruct((row_group, order, order), jnp.bfloat16),
        compiler_params=pltpu.CompilerParams(vmem_limit_bytes=VMEM_LIMIT),
        cost_estimate=pl.CostEstimate(flops=0, bytes_accessed=0, transcendentals=0),
    )(table, *parts)


def halves(value):
    high = value.astype(jnp.bfloat16)
    return high, (value - high.astype(jnp.float32)).astype(jnp.bfloat16)


def update_kernel(sizes, n, table, near_tile, far_tile, lefts, got, *refs):
    near_out, far_out, panel, factors = refs[-4:]
    x = pl.program_id(0)
    slot = table[sizes.owner_at(n)] * sizes.inner + x
    quarter, far = sizes.quarter, sizes.far
    for g in range(sizes.groups):
        at = g * sizes.inner + x
        panel[g * quarter : (g + 1) * quarter, :] = got[at, 0:quarter, :]
        factors[g * far : (g + 1) * far, :] = got[at, quarter : quarter + far, :]
    filled = sizes.groups * far
    if filled < sizes.far_all:
        factors[filled:, :] = jnp.zeros_like(factors[filled:, :])
    across = (((1,), (1,)), ((), ()))
    product = lax.dot_general(
        lefts[table[sizes.near_rows_at + slot]],
        panel[...],
        across,
        preferred_element_type=jnp.float32,
    )
    near_out[0] = (near_tile[0].astype(jnp.float32) - product).astype(jnp.bfloat16)
    x_trans = jnp.dot(
        far_tile[0, 0],
        lefts[table[sizes.far_rows_at + slot]],
        preferred_element_type=jnp.float32,
    )
    pairs = factors[...]
    small = sum(
        lax.dot_general(part, pairs, across, preferred_element_type=jnp.float32)
        for part in halves(x_trans)
    )
    turned = pltpu.roll(small, sizes.far_all - 1, 1)
    lane = lax.broadcasted_iota(jnp.int32, turned.shape, 1)
    turned = jnp.where(lane % 2 == 0, turned, 0.0)
    change = sum(
        jnp.dot(part, pairs, preferred_element_type=jnp.float32) for part in halves(turned)
    )
    far_out[0] = (far_tile[0, 1].astype(jnp.float32) - change).astype(jnp.bfloat16)


def update(sizes, n, table, near_tiles, far_tiles, lefts, got, before):
    order, rank = near_tiles.shape[1], far_tiles.shape[2]

    def at_slot(*rest):
        return lambda x, table: (table[sizes.owner_at(n)] * sizes.inner + x,) + rest

    return pl.pallas_call(
        functools.partial(update_kernel, sizes, n),
        grid_spec=pltpu.PrefetchScalarGridSpec(
            num_scalar_prefetch=1,
            grid=(sizes.inner,),
            in_specs=[
                pl.BlockSpec((1, order, order), lambda x, table: (x, 0, 0)),
                pl.BlockSpec((1, 2, rank, order), lambda x, table: (x, 0, 0, 0)),
                VMEM,
                VMEM,
            ]
            + [KEPT] * len(before),
            out_specs=[
                pl.BlockSpec((1, order, order), at_slot(0, 0)),
                pl.BlockSpec((1, rank, order), at_slot(0, 0)),
            ],
            scratch_shapes=[
                pltpu.VMEM((order, order), jnp.bfloat16),
                pltpu.VMEM((sizes.far_all, order), jnp.bfloat16),
            ],
        ),
        out_shape=[
            jax.ShapeDtypeStruct((sizes.slots, order, order), jnp.bfloat16),
            jax.ShapeDtypeStruct((sizes.slots, rank, order), jnp.bfloat16),
        ],
        input_output_aliases={5 + k: k for k in range(len(before))},
        compiler_params=pltpu.CompilerParams(vmem_limit_bytes=VMEM_LIMIT),
        cost_estimate=pl.CostEstimate(flops=UPDATE_FLOPS, bytes_accessed=0, transcendentals=0),
    )(table, near_tiles, far_tiles, lefts, got, *before)


def shards(
    row_panel, col_near, col_far, near_tiles, near_rows, near_cols, far_tiles, far_rows, far_cols
):
    inner_size = lax.axis_size("inner")
    groups = lax.axis_size("gy") * lax.axis_size("core")
    outer, inner = lax.axis_index("outer"), lax.axis_index("inner")
    per_bucket, quarter, order = col_near.shape
    row_group, shard = row_panel.shape[:2]
    far_pairs = jnp.swapaxes(col_far, 1, 2).reshape(per_bucket, -1, order)
    far = -(-far_pairs.shape[1] // FAR_ALIGN) * FAR_ALIGN
    far_pairs = jnp.pad(far_pairs, ((0, 0), (0, far - far_pairs.shape[1]), (0, 0)))
    sizes = Sizes(groups, inner_size, per_bucket, quarter, far, shard)

    def along(value, pairs):
        return lax.ppermute(value, "outer", pairs)

    rows = [row_panel]
    for k in range(1, inner_size):
        turn = [((i + k) % inner_size, i) for i in range(inner_size)]
        rows.append(lax.ppermute(row_panel, "inner", turn))

    place = jnp.stack([outer, inner])
    table, own, send = first(
        sizes, place, near_cols, far_cols, near_rows, far_rows, col_near, far_pairs
    )
    held = {"own": own}
    held["pair"] = along(own, [(0, 1), (1, 0), (2, 3), (3, 2)])
    held["middle"] = along(own, [(1, 2), (2, 1)])
    held["cross"] = along(held["pair"], [(1, 2), (2, 1)])
    held["pass2"] = along(held["middle"], [(1, 0), (2, 3)])
    held["pass3"] = along(held["cross"], [(1, 0), (2, 3)])

    got, after = [], []
    for n in range(OUTER):
        if n > 0:
            send = pack(sizes, n, table, [held[name] for name in CHUNK_SOURCES[n]], after)
        got.append(lax.all_to_all(send, PLANE, split_axis=0, concat_axis=0, tiled=True))
        if n == 2:
            line, token = join_rows(rows, got[1])
            after = [token]

    parts = [line]
    for k in range(1, OUTER):
        parts.append(along(line, [(i, (i + k) % OUTER) for i in range(OUTER)]))
    lefts = make_lefts(sizes, table, parts)
    outs = ()
    for n in range(OUTER):
        at = jnp.asarray(CHUNK_OWNER[n], jnp.int32)[outer] * inner_size
        near = lax.dynamic_slice_in_dim(near_tiles, at, inner_size, 0)
        far_pair = lax.dynamic_slice_in_dim(far_tiles, at, inner_size, 0)
        outs = update(sizes, n, table, near, far_pair, lefts, got[n], outs)
    return tuple(outs)


def solution(mesh):
    groups, dev_count = mesh.shape["grp"], mesh.shape["dev"]
    fine = Mesh(
        mesh.devices.reshape(groups // 2, 2, OUTER, dev_count // OUTER),
        ("gy", "core", "outer", "inner"),
    )
    grp, dev = ("gy", "core"), ("outer", "inner")
    every = grp + dev
    placed = (
        P(grp, dev, None),
        P(dev, grp, None),
        P(dev, None, grp, None),
        P(every, None, None),
        P(every, None),
        P(),
        P(every, None, None, None),
        P(every, None),
        P(),
    )
    return jax.shard_map(
        shards,
        mesh=fine,
        in_specs=placed,
        out_specs=(P(every, None, None), P(every, None, None)),
        check_vma=False,
    )
```

time: 155 us -> 122 us (0.79)
  waiting for transfers between devices: 86.5 us -> 37.7 us
  starting transfers between devices: 33 us -> 40.1 us
  local copies, waits for them, and re-layouts: 11.9 us -> 18 us
  between operations: 0.84 us -> 2.77 us
  other arithmetic: 1.79 us -> 0.08 us
  Pallas kernels: 20.3 us -> 22 us
    ppermute x1, waiting for transfers between devices: 26.5 us -> 0.01 us  [shards(): rows.append(lax.ppermute(row_panel, 'inner', turn))]
    ppermute x5 -> x8, waiting for transfers between devices: 49.8 us -> 26.7 us  [along(): return lax.ppermute(value, 'outer', pairs)]
    ppermute x5 -> x8, starting transfers between devices: 9.14 us -> 22.2 us  [along(): return lax.ppermute(value, 'outer', pairs)]
    all_to_all x5 -> x4, starting transfers between devices: 22 us -> 16 us  [shards(): lax.all_to_all(send, PLANE, split_axis=0, concat_axis=0, tiled=True)]
    dynamic_slice x0 -> x5, local copies, waits for them, and re-layouts: none -> 5.13 us  [the longest x1 2.59 us: shards(): near = lax.dynamic_slice_in_dim(near_tiles, at, inner_size, 0)]
    pallas_call x4, Pallas kernels: 13 us -> 15.2 us  [update(): pl.pallas_call(functools.partial(update_kernel, sizes, n), grid_spec=pltp...]
    unnamed x27 -> x38, local copies, waits for them, and re-layouts: 10.1 us -> 12 us
    broadcast_in_dim x1 -> x0, local copies, waits for them, and re-layouts: 1.82 us -> none  [shards(): jnp.broadcast_to(row_panel, (OUTER,) + row_panel.shape)]
  transfers between devices with their start and end apart: 11 -> 13, of which waited for: 6 -> 5; matrix products, arithmetic and copies ran while one was open for 1% -> 4% of each run, Pallas kernels for 10% -> 13%
where the time goes in v5:
time: 122 us; the launch traced here: 121 us
  starting transfers between devices  40.1 us (33%)
  waiting for transfers between devices  37.7 us (31%)
  Pallas kernels  22 us (18%)
  local copies, waits for them, and re-layouts  18 us (15%)
  between operations  2.77 us (2%)
    ppermute x8, waiting for transfers between devices, along(): return lax.ppermute(value, 'outer', pairs)  26.7 us
    ppermute x8, starting transfers between devices, along(): return lax.ppermute(value, 'outer', pairs)  22.2 us
    all_to_all x4, starting transfers between devices, shards(): lax.all_to_all(send, PLANE, split_axis=0, concat_axis=0, tiled=True)  16 us
    pallas_call x4, Pallas kernels, update(): pl.pallas_call(functools.partial(update_kernel, sizes, n), grid_spec=pltp...  15.2 us
    unnamed x38, local copies, waits for them, and re-layouts  12 us
    all_to_all x4, waiting for transfers between devices, shards(): lax.all_to_all(send, PLANE, split_axis=0, concat_axis=0, tiled=True)  11 us
    pallas_call x3, Pallas kernels, pack(): pl.pallas_call(functools.partial(pack_kernel, sizes, n), in_specs=[SMEM]...  3 us
    dynamic_slice x1, local copies, waits for them, and re-layouts, shards(): near = lax.dynamic_slice_in_dim(near_tiles, at, inner_size, 0)  2.59 us
  transfers between devices with their start and end apart: 13, of which 5 were waited for; matrix products, arithmetic and copies ran while one was open for 4% of the time, Pallas kernels for 13%

profile of v5, /device:TPU:0, one launch (start us, length us, event | category | flops | bytes accessed | tf_op | source)
XLA Modules:
  0.0 120.7 jit_solution(17800746405217914571)
XLA Ops:
  0.6 0.9 reshape.15.pairs
  1.6 0.1 pad_add_fusion.place
  1.7 1.0 copy-done.6
  2.7 0.7 copy-done.8
  3.4 0.7 copy-done.9
  4.1 0.7 copy-done.10
  4.7 0.7 copy-done.11
  5.4 1.7 %shard_map.140 = (s32[90]{0:T(128)S(1)}, bf16[608,512]{1,0:T(8,128)(2,1)}, bf16[8,152,512]{2,1,0:T(8,128)(2,1)S(1)}) custom-call(s32[2]{0:T(128)S(1)} %pad_add_fusion.place, s32[8,32]{1,0:T(8,128)S(1)} %bitcast.8, s32[8,32]{1,0:T(8,128)S(1)} %bitcast.9, s32[1,8]{1,0:T(1,128)S(1)} %copy-done.10, s32[1,8]{1,0:T(1,128)S(1)} %copy-done.11, ...), custom_call_target="tpu_custom_call" | custom-call | tf_op jit(solution)/shard_map/pallas_call | solution.py:107
  7.1 1.0 copy-done.3
  8.2 0.7 collective-permute-start.7
  8.9 5.9 %collective-permute-start = (bf16[608,512]{1,0:T(8,128)(2,1)}, bf16[608,512]{1,0:T(8,128)(2,1)S(1)}, u32[]{:S(2)}, u32[]{:S(2)}) collective-permute-start(bf16[608,512]{1,0:T(8,128)(2,1)} %get-tuple-element.14), channel_id=1, source_target_pairs={{0,2},{2,0},{4,6},{6,4},{1,3},{3,1},{5,7},{7,5},{8,10},{10,8},{12,... | collective-permute-start | bytes 1867784 | tf_op jit(solution)/shard_map/ppermute | solution.py:282
  14.7 3.7 %all-to-all-start.3 = ((bf16[8,152,512]{2,1,0:T(8,128)(2,1)}), bf16[8,152,512]{2,1,0:T(8,128)(2,1)S(1)}, u32[]{:S(2)}, u32[]{:S(2)}) async-start(bf16[8,152,512]{2,1,0:T(8,128)(2,1)} %copy-done.3), calls=%async_computation.3 | async-start | bytes 2490368 | tf_op jit(solution)/shard_map/all_to_all | solution.py:304
  18.5 1.3 %collective-permute-start.8 = (bf16[608,512]{1,0:T(8,128)(2,1)S(1)}, bf16[608,512]{1,0:T(8,128)(2,1)}, u32[]{:S(2)}, u32[]{:S(2)}) collective-permute-start(bf16[608,512]{1,0:T(8,128)(2,1)S(1)} %collective-permute-done.7.refs_0_), channel_id=1, source_target_pairs={{2,0},{4,6},{3,1},{5,7},{10,8},{12,14},{11,9},{13,15},{18,16},{20,... | collective-permute-start | bytes 1867784 | tf_op jit(solution)/shard_map/ppermute | solution.py:282
  19.8 8.9 %collective-permute-done.refs_0_ = bf16[608,512]{1,0:T(8,128)(2,1)S(1)} collective-permute-done((bf16[608,512]{1,0:T(8,128)(2,1)}, bf16[608,512]{1,0:T(8,128)(2,1)S(1)}, u32[]{:S(2)}, u32[]{:S(2)}) %collective-permute-start) | collective-permute-done | bytes 622624 | tf_op jit(solution)/shard_map/ppermute | solution.py:282
  28.7 0.8 copy-done.12
  29.5 1.1 copy-done.13
  30.6 0.6 shard_map.141
  31.3 1.0 copy-done
  32.3 3.2 %all-to-all-done.3.got = bf16[8,152,512]{2,1,0:T(8,128)(2,1)S(1)} async-done(((bf16[8,152,512]{2,1,0:T(8,128)(2,1)}), bf16[8,152,512]{2,1,0:T(8,128)(2,1)S(1)}, u32[]{:S(2)}, u32[]{:S(2)}) %all-to-all-start.3) | async-done | bytes 1245216 | tf_op jit(solution)/shard_map/all_to_all | solution.py:304
  35.5 3.6 %all-to-all-start = ((bf16[8,152,512]{2,1,0:T(8,128)(2,1)}), bf16[8,152,512]{2,1,0:T(8,128)(2,1)S(1)}, u32[]{:S(2)}, u32[]{:S(2)}) async-start(bf16[8,152,512]{2,1,0:T(8,128)(2,1)} %copy-done), calls=%async_computation | async-start | bytes 2490368 | tf_op jit(solution)/shard_map/all_to_all | solution.py:304
  39.1 1.9 %collective-permute-start.1 = (bf16[2,64,512]{2,1,0:T(8,128)(2,1)S(1)}, bf16[2,64,512]{2,1,0:T(8,128)(2,1)S(1)}, u32[]{:S(2)}, u32[]{:S(2)}) collective-permute-start(bf16[2,64,512]{2,1,0:T(8,128)(2,1)S(1)} %copy-done.14), channel_id=1, source_target_pairs={{1,0},{0,1},{3,2},{2,3},{5,4},{4,5},{7,6},{6,7},{9,8},{8,9},{11,10... | collective-permute-start | bytes 393224 | tf_op jit(solution)/shard_map/ppermute | solution.py:287
  41.0 0.6 dynamic_slice.36
  42.2 0.6 dynamic_slice.39
  43.5 0.6 dynamic_slice.42
  44.7 1.5 %collective-permute-start.5 = (bf16[608,512]{1,0:T(8,128)(2,1)}, bf16[608,512]{1,0:T(8,128)(2,1)}, u32[]{:S(2)}, u32[]{:S(2)}) collective-permute-start(bf16[608,512]{1,0:T(8,128)(2,1)} %copy-done.12), channel_id=1, source_target_pairs={{2,4},{4,2},{3,5},{5,3},{10,12},{12,10},{11,13},{13,11},{18,20},{2... | collective-permute-start | bytes 1867784 | tf_op jit(solution)/shard_map/ppermute | solution.py:282
  46.2 1.2 shard_map.145
  47.4 1.1 copy-done.2
  48.4 1.3 %collective-permute-start.6 = (bf16[608,512]{1,0:T(8,128)(2,1)}, bf16[608,512]{1,0:T(8,128)(2,1)S(1)}, u32[]{:S(2)}, u32[]{:S(2)}) collective-permute-start(bf16[608,512]{1,0:T(8,128)(2,1)} %collective-permute-done.5.refs_0_), channel_id=1, source_target_pairs={{2,0},{4,6},{3,1},{5,7},{10,8},{12,14},{11,9},{13,15},{18,16},{20,... | collective-permute-start | bytes 1867784 | tf_op jit(solution)/shard_map/ppermute | solution.py:282
  49.7 6.3 %all-to-all-done.after.got = bf16[8,152,512]{2,1,0:T(8,128)(2,1)S(1)} async-done(((bf16[8,152,512]{2,1,0:T(8,128)(2,1)}), bf16[8,152,512]{2,1,0:T(8,128)(2,1)S(1)}, u32[]{:S(2)}, u32[]{:S(2)}) %all-to-all-start) | async-done | bytes 1245216 | tf_op jit(solution)/shard_map/all_to_all | solution.py:304
  56.0 4.3 %all-to-all-start.2 = ((bf16[8,152,512]{2,1,0:T(8,128)(2,1)}), bf16[8,152,512]{2,1,0:T(8,128)(2,1)}, u32[]{:S(2)}, u32[]{:S(2)}) async-start(bf16[8,152,512]{2,1,0:T(8,128)(2,1)} %copy-done.2), calls=%async_computation.2 | async-start | bytes 2490368 | tf_op jit(solution)/shard_map/all_to_all | solution.py:304
  60.3 0.7 shard_map.142
  61.0 8.0 %collective-permute-start.2 = (bf16[2,2,64,512]{3,2,1,0:T(8,128)(2,1)}, bf16[2,2,64,512]{3,2,1,0:T(8,128)(2,1)}, u32[]{:S(2)}, u32[]{:S(2)}) collective-permute-start(bf16[2,2,64,512]{3,2,1,0:T(8,128)(2,1)} %get-tuple-element.15.refs_0_), channel_id=1, source_target_pairs={{0,2},{2,4},{4,6},{6,0},{1,3},{3,5},{5,7},{7,1},{8,10},{10,12},{12... | collective-permute-start | bytes 786440 | tf_op jit(solution)/shard_map/ppermute | solution.py:282
  69.1 0.6 collective-permute-start.3
  69.7 2.9 %collective-permute-start.4 = (bf16[2,2,64,512]{3,2,1,0:T(8,128)(2,1)}, bf16[2,2,64,512]{3,2,1,0:T(8,128)(2,1)}, u32[]{:S(2)}, u32[]{:S(2)}) collective-permute-start(bf16[2,2,64,512]{3,2,1,0:T(8,128)(2,1)} %get-tuple-element.15.refs_0_), channel_id=1, source_target_pairs={{0,6},{2,0},{4,2},{6,4},{1,7},{3,1},{5,3},{7,5},{8,14},{10,8},{12,... | collective-permute-start | bytes 786440 | tf_op jit(solution)/shard_map/ppermute | solution.py:282
  72.7 17.7 %collective-permute-done.6.refs_1_ = bf16[608,512]{1,0:T(8,128)(2,1)S(1)} collective-permute-done((bf16[608,512]{1,0:T(8,128)(2,1)}, bf16[608,512]{1,0:T(8,128)(2,1)S(1)}, u32[]{:S(2)}, u32[]{:S(2)}) %collective-permute-start.6) | collective-permute-done | bytes 622624 | tf_op jit(solution)/shard_map/ppermute | solution.py:282
  90.4 1.2 shard_map.144
  91.6 1.0 copy-done.1
  92.6 4.4 %all-to-all-start.1 = ((bf16[8,152,512]{2,1,0:T(8,128)(2,1)}), bf16[8,152,512]{2,1,0:T(8,128)(2,1)}, u32[]{:S(2)}, u32[]{:S(2)}) async-start(bf16[8,152,512]{2,1,0:T(8,128)(2,1)} %copy-done.1), calls=%async_computation.1 | async-start | bytes 2490368 | tf_op jit(solution)/shard_map/all_to_all | solution.py:304
  97.0 0.8 constant_dynamic-slice_fusion
  97.8 2.6 %constant_dynamic-slice_fusion.1 = (bf16[2,512,512]{2,1,0:T(8,128)(2,1)S(1)}, bf16[2,512,512]{2,1,0:T(8,128)(2,1)S(1)}, bf16[2,512,512]{2,1,0:T(8,128)(2,1)S(1)}, bf16[2,512,512]{2,1,0:T(8,128)(2,1)S(1)}) fusion(bf16[8,512,512]{2,1,0:T(8,128)(2,1)} %param.16, s32[]{:T(128)S(6)} %select_n.26, s32[]{:T(128)S(6)} %select_n.24, s32[]{:T(128)S(6)} %select_n.11, ...), kind=kLoop, calls=%fused_computation.1 | loop fusion | bytes 8388624 | tf_op jit(solution)/shard_map/dynamic_slice | solution.py:316
  100.5 1.3 %shard_map.143.lefts = bf16[2,512,512]{2,1,0:T(8,128)(2,1)S(1)} custom-call(s32[90]{0:T(128)S(1)} %get-tuple-element.13.table, bf16[2,2,64,512]{3,2,1,0:T(8,128)(2,1)} %get-tuple-element.15.refs_0_, bf16[2,2,64,512]{3,2,1,0:T(8,128)(2,1)} %collective-permute-done.2.refs_1_, bf16[2,2,64,512]{3,2,1,0:T(8,128)(2,1)} %collective-permute-done.3.refs_2_, ...), custom_call_target="tpu_custom_call" | custom-call | tf_op jit(solution)/shard_map/pallas_call | solution.py:177
  101.7 3.2 %shard_map.146 = (bf16[8,512,512]{2,1,0:T(8,128)(2,1)}, bf16[8,48,512]{2,1,0:T(8,128)(2,1)}) custom-call(s32[90]{0:T(128)S(1)} %get-tuple-element.13.table, bf16[2,512,512]{2,1,0:T(8,128)(2,1)S(1)} %get-tuple-element.24.near_tile, bf16[2,2,48,512]{3,2,1,0:T(8,128)(2,1)S(1)} %get-tuple-element.28.far_tile, bf16[2,512,512]{2,1,0:T(8,128)(2,1)S(1)} %shard_map.143.lefts, ...), custom_call_target="tpu_custom_call" | custom-call | flops 3000000000 | tf_op jit(solution)/shard_map/pallas_call | solution.py:237
  104.9 3.2 %shard_map.147 = (bf16[8,512,512]{2,1,0:T(8,128)(2,1)}, bf16[8,48,512]{2,1,0:T(8,128)(2,1)}) custom-call(s32[90]{0:T(128)S(1)} %get-tuple-element.13.table, bf16[2,512,512]{2,1,0:T(8,128)(2,1)S(1)} %get-tuple-element.27.near_tile, bf16[2,2,48,512]{3,2,1,0:T(8,128)(2,1)S(1)} %get-tuple-element.31.far_tile, ...), custom_call_target="tpu_custom_call", output_to_operand_aliasing={{0}: (5, {}), {1}: (6, {})} | custom-call | flops 3000000000 | tf_op jit(solution)/shard_map/pallas_call | solution.py:237
  108.1 4.5 %shard_map.148 = (bf16[8,512,512]{2,1,0:T(8,128)(2,1)}, bf16[8,48,512]{2,1,0:T(8,128)(2,1)}) custom-call(s32[90]{0:T(128)S(1)} %get-tuple-element.13.table, bf16[2,512,512]{2,1,0:T(8,128)(2,1)S(1)} %get-tuple-element.25.near_tile, bf16[2,2,48,512]{3,2,1,0:T(8,128)(2,1)S(1)} %get-tuple-element.29.far_tile, ...), custom_call_target="tpu_custom_call", output_to_operand_aliasing={{0}: (5, {}), {1}: (6, {})} | custom-call | flops 3000000000 | tf_op jit(solution)/shard_map/pallas_call | solution.py:237
  112.5 1.5 %all-to-all-done.1.got = bf16[8,152,512]{2,1,0:T(8,128)(2,1)} async-done(((bf16[8,152,512]{2,1,0:T(8,128)(2,1)}), bf16[8,152,512]{2,1,0:T(8,128)(2,1)}, u32[]{:S(2)}, u32[]{:S(2)}) %all-to-all-start.1) | async-done | bytes 1245216 | tf_op jit(solution)/shard_map/all_to_all | solution.py:304
  114.1 1.2 %copy-done.5 = bf16[2,512,512]{2,1,0:T(8,128)(2,1)S(1)} copy-done((bf16[2,512,512]{2,1,0:T(8,128)(2,1)S(1)}, bf16[2,512,512]{2,1,0:T(8,128)(2,1)}, u32[]{:S(2)}) %copy-start.5) | copy-done | bytes 1048600
  115.3 0.9 copy-done.7
  116.2 4.5 %shard_map.149 = (bf16[8,512,512]{2,1,0:T(8,128)(2,1)}, bf16[8,48,512]{2,1,0:T(8,128)(2,1)}) custom-call(s32[90]{0:T(128)S(1)} %get-tuple-element.13.table, bf16[2,512,512]{2,1,0:T(8,128)(2,1)S(1)} %get-tuple-element.26.near_tile, bf16[2,2,48,512]{3,2,1,0:T(8,128)(2,1)S(1)} %copy-done.7, ...), custom_call_target="tpu_custom_call", output_to_operand_aliasing={{0}: (5, {}), {1}: (6, {})} | custom-call | flops 3000000000 | tf_op jit(solution)/shard_map/pallas_call | solution.py:237
  (33 shorter events, 0.1 us)
Async XLA Ops:
  1.7 1.0 copy-start.6
  2.7 0.7 copy-start.8
  3.4 0.7 copy-start.9
  4.1 0.7 copy-start.10
  4.7 0.7 copy-start.11
  7.1 1.1 copy-start.3
  8.2 10.3 %collective-permute-start.7 = (bf16[608,512]{1,0:T(8,128)(2,1)}, bf16[608,512]{1,0:T(8,128)(2,1)S(1)}, u32[]{:S(2)}, u32[]{:S(2)}) collective-permute-start(bf16[608,512]{1,0:T(8,128)(2,1)} %get-tuple-element.14), channel_id=1, source_target_pairs={{2,4},{4,2},{3,5},{5,3},{10,12},{12,10},{11,13},{13,11},{18,20},{2... | collective-permute-start | bytes 1867784 | tf_op jit(solution)/shard_map/ppermute | solution.py:282
  8.9 19.8 %collective-permute-start = (bf16[608,512]{1,0:T(8,128)(2,1)}, bf16[608,512]{1,0:T(8,128)(2,1)S(1)}, u32[]{:S(2)}, u32[]{:S(2)}) collective-permute-start(bf16[608,512]{1,0:T(8,128)(2,1)} %get-tuple-element.14), channel_id=1, source_target_pairs={{0,2},{2,0},{4,6},{6,4},{1,3},{3,1},{5,7},{7,5},{8,10},{10,8},{12,... | collective-permute-start | bytes 1867784 | tf_op jit(solution)/shard_map/ppermute | solution.py:282
  14.7 20.8 %all-to-all-start.3 = ((bf16[8,152,512]{2,1,0:T(8,128)(2,1)}), bf16[8,152,512]{2,1,0:T(8,128)(2,1)S(1)}, u32[]{:S(2)}, u32[]{:S(2)}) async-start(bf16[8,152,512]{2,1,0:T(8,128)(2,1)} %copy-done.3), calls=%async_computation.3 | async-start | bytes 2490368 | tf_op jit(solution)/shard_map/all_to_all | solution.py:304
  18.5 27.7 %collective-permute-start.8 = (bf16[608,512]{1,0:T(8,128)(2,1)S(1)}, bf16[608,512]{1,0:T(8,128)(2,1)}, u32[]{:S(2)}, u32[]{:S(2)}) collective-permute-start(bf16[608,512]{1,0:T(8,128)(2,1)S(1)} %collective-permute-done.7.refs_0_), channel_id=1, source_target_pairs={{2,0},{4,6},{3,1},{5,7},{10,8},{12,14},{11,9},{13,15},{18,16},{20,... | collective-permute-start | bytes 1867784 | tf_op jit(solution)/shard_map/ppermute | solution.py:282
  28.7 0.8 copy-start.12
  29.5 1.1 copy-start.13
  31.2 1.0 copy-start
  32.3 6.8 %copy-start.14 = (bf16[2,64,512]{2,1,0:T(8,128)(2,1)S(1)}, bf16[2,64,512]{2,1,0:T(8,128)(2,1)}, u32[]{:S(2)}) copy-start(bf16[2,64,512]{2,1,0:T(8,128)(2,1)} %refs_0_.1) | copy-start | bytes 393220
  32.3 8.7 %copy-start.18 = (s32[4]{0:T(128)S(1)}, s32[4]{0:T(128)}, u32[]{:S(2)}) copy-start(s32[4]{0:T(128)} %constant.30.clone) | copy-start | bytes 52
  32.3 10.0 %copy-start.17 = (s32[4]{0:T(128)S(1)}, s32[4]{0:T(128)}, u32[]{:S(2)}) copy-start(s32[4]{0:T(128)} %constant.29.clone) | copy-start | bytes 52
  32.3 11.2 %copy-start.16 = (s32[4]{0:T(128)S(1)}, s32[4]{0:T(128)}, u32[]{:S(2)}) copy-start(s32[4]{0:T(128)} %constant.28.clone) | copy-start | bytes 52
  35.5 20.5 %all-to-all-start = ((bf16[8,152,512]{2,1,0:T(8,128)(2,1)}), bf16[8,152,512]{2,1,0:T(8,128)(2,1)S(1)}, u32[]{:S(2)}, u32[]{:S(2)}) async-start(bf16[8,152,512]{2,1,0:T(8,128)(2,1)} %copy-done), calls=%async_computation | async-start | bytes 2490368 | tf_op jit(solution)/shard_map/all_to_all | solution.py:304
  39.1 21.2 %collective-permute-start.1 = (bf16[2,64,512]{2,1,0:T(8,128)(2,1)S(1)}, bf16[2,64,512]{2,1,0:T(8,128)(2,1)S(1)}, u32[]{:S(2)}, u32[]{:S(2)}) collective-permute-start(bf16[2,64,512]{2,1,0:T(8,128)(2,1)S(1)} %copy-done.14), channel_id=1, source_target_pairs={{1,0},{0,1},{3,2},{2,3},{5,4},{4,5},{7,6},{6,7},{9,8},{8,9},{11,10... | collective-permute-start | bytes 393224 | tf_op jit(solution)/shard_map/ppermute | solution.py:287
  44.7 3.8 %collective-permute-start.5 = (bf16[608,512]{1,0:T(8,128)(2,1)}, bf16[608,512]{1,0:T(8,128)(2,1)}, u32[]{:S(2)}, u32[]{:S(2)}) collective-permute-start(bf16[608,512]{1,0:T(8,128)(2,1)} %copy-done.12), channel_id=1, source_target_pairs={{2,4},{4,2},{3,5},{5,3},{10,12},{12,10},{11,13},{13,11},{18,20},{2... | collective-permute-start | bytes 1867784 | tf_op jit(solution)/shard_map/ppermute | solution.py:282
  47.4 1.1 copy-start.2
  48.4 41.9 %collective-permute-start.6 = (bf16[608,512]{1,0:T(8,128)(2,1)}, bf16[608,512]{1,0:T(8,128)(2,1)S(1)}, u32[]{:S(2)}, u32[]{:S(2)}) collective-permute-start(bf16[608,512]{1,0:T(8,128)(2,1)} %collective-permute-done.5.refs_0_), channel_id=1, source_target_pairs={{2,0},{4,6},{3,1},{5,7},{10,8},{12,14},{11,9},{13,15},{18,16},{20,... | collective-permute-start | bytes 1867784 | tf_op jit(solution)/shard_map/ppermute | solution.py:282
  56.0 36.6 %all-to-all-start.2 = ((bf16[8,152,512]{2,1,0:T(8,128)(2,1)}), bf16[8,152,512]{2,1,0:T(8,128)(2,1)}, u32[]{:S(2)}, u32[]{:S(2)}) async-start(bf16[8,152,512]{2,1,0:T(8,128)(2,1)} %copy-done.2), calls=%async_computation.2 | async-start | bytes 2490368 | tf_op jit(solution)/shard_map/all_to_all | solution.py:304
  61.0 39.4 %collective-permute-start.2 = (bf16[2,2,64,512]{3,2,1,0:T(8,128)(2,1)}, bf16[2,2,64,512]{3,2,1,0:T(8,128)(2,1)}, u32[]{:S(2)}, u32[]{:S(2)}) collective-permute-start(bf16[2,2,64,512]{3,2,1,0:T(8,128)(2,1)} %get-tuple-element.15.refs_0_), channel_id=1, source_target_pairs={{0,2},{2,4},{4,6},{6,0},{1,3},{3,5},{5,7},{7,1},{8,10},{10,12},{12... | collective-permute-start | bytes 786440 | tf_op jit(solution)/shard_map/ppermute | solution.py:282
  69.1 31.4 %collective-permute-start.3 = (bf16[2,2,64,512]{3,2,1,0:T(8,128)(2,1)}, bf16[2,2,64,512]{3,2,1,0:T(8,128)(2,1)}, u32[]{:S(2)}, u32[]{:S(2)}) collective-permute-start(bf16[2,2,64,512]{3,2,1,0:T(8,128)(2,1)} %get-tuple-element.15.refs_0_), channel_id=1, source_target_pairs={{0,4},{2,6},{4,0},{6,2},{1,5},{3,7},{5,1},{7,3},{8,12},{10,14},{12... | collective-permute-start | bytes 786440 | tf_op jit(solution)/shard_map/ppermute | solution.py:282
  69.7 30.7 %collective-permute-start.4 = (bf16[2,2,64,512]{3,2,1,0:T(8,128)(2,1)}, bf16[2,2,64,512]{3,2,1,0:T(8,128)(2,1)}, u32[]{:S(2)}, u32[]{:S(2)}) collective-permute-start(bf16[2,2,64,512]{3,2,1,0:T(8,128)(2,1)} %get-tuple-element.15.refs_0_), channel_id=1, source_target_pairs={{0,6},{2,0},{4,2},{6,4},{1,7},{3,1},{5,3},{7,5},{8,14},{10,8},{12,... | collective-permute-start | bytes 786440 | tf_op jit(solution)/shard_map/ppermute | solution.py:282
  91.6 1.0 copy-start.1
  92.6 4.4 %copy-start.15 = (bf16[8,2,48,512]{3,2,1,0:T(8,128)(2,1)S(1)}, bf16[8,2,48,512]{3,2,1,0:T(8,128)(2,1)}, u32[]{:S(2)}) copy-start(bf16[8,2,48,512]{3,2,1,0:T(8,128)(2,1)} %param.19) | copy-start | bytes 2359300
  92.6 21.4 %all-to-all-start.1 = ((bf16[8,152,512]{2,1,0:T(8,128)(2,1)}), bf16[8,152,512]{2,1,0:T(8,128)(2,1)}, u32[]{:S(2)}, u32[]{:S(2)}) async-start(bf16[8,152,512]{2,1,0:T(8,128)(2,1)} %copy-done.1), calls=%async_computation.1 | async-start | bytes 2490368 | tf_op jit(solution)/shard_map/all_to_all | solution.py:304
  101.7 6.3 %copy-start.4 = (bf16[2,512,512]{2,1,0:T(8,128)(2,1)}, bf16[2,512,512]{2,1,0:T(8,128)(2,1)S(1)}, u32[]{:S(2)}) copy-start(bf16[2,512,512]{2,1,0:T(8,128)(2,1)S(1)} %shard_map.143.lefts) | copy-start | bytes 3145732
  114.1 1.2 %copy-start.5 = (bf16[2,512,512]{2,1,0:T(8,128)(2,1)S(1)}, bf16[2,512,512]{2,1,0:T(8,128)(2,1)}, u32[]{:S(2)}) copy-start(bf16[2,512,512]{2,1,0:T(8,128)(2,1)} %copy-done.4) | copy-start | bytes 3145732
  115.3 0.9 copy-start.7

commit v6 on v5

--- a/solution.py
+++ b/solution.py
@@ -13,6 +13,8 @@
 FAR_ALIGN = 8
 LANES = 128
 VMEM_LIMIT = 16 * 1024 * 1024
+WIDE_VMEM = 60 * 1024 * 1024
+HBM = pl.BlockSpec(memory_space=pltpu.HBM)
 CHUNK_OWNER = ((0, 1, 2, 3), (1, 0, 3, 2), (2, 2, 1, 1), (3, 3, 0, 0))
 CHUNK_SOURCE = ((0, 0, 0, 0), (0, 0, 0, 0), (1, 0, 0, 1), (1, 0, 0, 1))
 CHUNK_SOURCES = (("own",), ("pair",), ("middle", "pass2"), ("cross", "pass3"))
@@ -72,9 +74,10 @@
         table[sizes.far_rows_at + s] = far_rows[0, s]
 
 
-def pack_from(sizes, n, table, source, out):
+def pack_from(sizes, n, table, source, out, sent, sems):
     quarter, far = sizes.quarter, sizes.far
     far_at = sizes.per_bucket * quarter
+    copies = []
     for at in range(sizes.wanted):
         near_pick = table[n * sizes.stride + at] * quarter
         out[at, 0:quarter, :] = source[pl.ds(pl.multiple_of(near_pick, ROW_ALIGN), quarter), :]
@@ -84,17 +87,28 @@
             other = source[far_at + j * far : far_at + (j + 1) * far, :]
             picked = jnp.where(far_pick == j, other, picked)
         out[at, quarter : quarter + far, :] = picked
+        copies.append(pltpu.make_async_copy(out.at[at], sent.at[at], sems.at[at]))
+        copies[at].start()
+    for copy in copies:
+        copy.wait()
+
+
+def pack_scratch(sizes, order):
+    return [
+        pltpu.VMEM((sizes.wanted, sizes.quarter + sizes.far, order), jnp.bfloat16),
+        pltpu.SemaphoreType.DMA((sizes.wanted,)),
+    ]
 
 
 def first_kernel(sizes, place, near_cols, far_cols, near_rows, far_rows, near, pairs, *outs):
-    table, own, out = outs
+    table, own, sent, out, sems = outs
     fill_table(sizes, place, near_cols, far_cols, near_rows, far_rows, table)
     quarter, far = sizes.quarter, sizes.far
     far_at = sizes.per_bucket * quarter
     for j in range(sizes.per_bucket):
         own[j * quarter : (j + 1) * quarter, :] = near[j]
         own[far_at + j * far : far_at + (j + 1) * far, :] = pairs[j]
-    pack_from(sizes, 0, table, own, out)
+    pack_from(sizes, 0, table, own, out, sent, sems)
 
 
 def send_shape(sizes, order):
@@ -107,53 +121,56 @@
     return pl.pallas_call(
         functools.partial(first_kernel, sizes),
         in_specs=[SMEM] * 5 + [VMEM] * 2,
-        out_specs=[SMEM, VMEM, VMEM],
+        out_specs=[SMEM, VMEM, HBM],
+        scratch_shapes=pack_scratch(sizes, order),
         out_shape=[
             jax.ShapeDtypeStruct((sizes.table,), jnp.int32),
             jax.ShapeDtypeStruct((rows, order), jnp.bfloat16),
             send_shape(sizes, order),
         ],
-        compiler_params=pltpu.CompilerParams(vmem_limit_bytes=VMEM_LIMIT),
+        compiler_params=pltpu.CompilerParams(vmem_limit_bytes=WIDE_VMEM),
         cost_estimate=pl.CostEstimate(flops=0, bytes_accessed=0, transcendentals=0),
     )(place, near_cols.T, far_cols.T, near_rows, far_rows, near, pairs)
 
 
 def pack_kernel(sizes, n, table, *refs):
-    sources, out = refs[: len(CHUNK_SOURCES[n])], refs[-1]
+    sources, (sent, out, sems, held, held_sem) = refs[: len(CHUNK_SOURCES[n])], refs[-5:]
     for k, source in enumerate(sources):
 
         @pl.when(table[sizes.source_at(n)] == k)
         def _(source=source):
-            pack_from(sizes, n, table, source, out)
+            load = pltpu.make_async_copy(source, held, held_sem.at[0])
+            load.start()
+            load.wait()
+
+    pack_from(sizes, n, table, held, out, sent, sems)
 
 
 def pack(sizes, n, table, sources, after):
+    order = sources[0].shape[1]
     return pl.pallas_call(
         functools.partial(pack_kernel, sizes, n),
-        in_specs=[SMEM] + [VMEM] * len(sources) + [KEPT] * len(after),
-        out_specs=VMEM,
-        out_shape=send_shape(sizes, sources[0].shape[1]),
-        compiler_params=pltpu.CompilerParams(vmem_limit_bytes=VMEM_LIMIT),
+        in_specs=[SMEM] + [HBM] * len(sources) + [KEPT] * len(after),
+        out_specs=HBM,
+        out_shape=send_shape(sizes, order),
+        scratch_shapes=pack_scratch(sizes, order)
+        + [pltpu.VMEM(sources[0].shape, jnp.bfloat16), pltpu.SemaphoreType.DMA((1,))],
+        compiler_params=pltpu.CompilerParams(vmem_limit_bytes=WIDE_VMEM),
         cost_estimate=pl.CostEstimate(flops=PACK_FLOPS, bytes_accessed=0, transcendentals=0),
     )(table, *sources, *after)
 
 
 def rows_kernel(after, *refs):
-    parts, out, token = refs[:-2], refs[-2], refs[-1]
-    for k, part in enumerate(parts):
-        out[k] = part[...]
-    token[...] = jnp.zeros_like(token)
+    for k, part in enumerate(refs[:-1]):
+        refs[-1][k] = part[...]
 
 
 def join_rows(parts, after):
     return pl.pallas_call(
         rows_kernel,
         in_specs=[KEPT] + [VMEM] * len(parts),
-        out_specs=[VMEM, VMEM],
-        out_shape=[
-            jax.ShapeDtypeStruct((len(parts),) + parts[0].shape, jnp.bfloat16),
-            jax.ShapeDtypeStruct((8, LANES), jnp.float32),
-        ],
+        out_specs=VMEM,
+        out_shape=jax.ShapeDtypeStruct((len(parts),) + parts[0].shape, jnp.bfloat16),
         compiler_params=pltpu.CompilerParams(vmem_limit_bytes=VMEM_LIMIT),
         cost_estimate=pl.CostEstimate(flops=PACK_FLOPS, bytes_accessed=0, transcendentals=0),
     )(after, *parts)
@@ -189,15 +206,21 @@
     return high, (value - high.astype(jnp.float32)).astype(jnp.bfloat16)
 
 
-def update_kernel(sizes, n, table, near_tile, far_tile, lefts, got, *refs):
-    near_out, far_out, panel, factors = refs[-4:]
-    x = pl.program_id(0)
-    slot = table[sizes.owner_at(n)] * sizes.inner + x
+def update_kernel(sizes, chunks, table, near_tile, far_tile, lefts, *refs):
+    got, (near_out, far_out, panel, factors) = refs[: len(chunks)], refs[-4:]
+    step = pl.program_id(0)
+    x = step % sizes.inner
+    slot = slot_of(sizes, chunks, step, table)
     quarter, far = sizes.quarter, sizes.far
-    for g in range(sizes.groups):
-        at = g * sizes.inner + x
-        panel[g * quarter : (g + 1) * quarter, :] = got[at, 0:quarter, :]
-        factors[g * far : (g + 1) * far, :] = got[at, quarter : quarter + far, :]
+    for k, part in enumerate(got):
+
+        @pl.when(step // sizes.inner == k)
+        def _(part=part):
+            for g in range(sizes.groups):
+                at = g * sizes.inner + x
+                panel[g * quarter : (g + 1) * quarter, :] = part[at, 0:quarter, :]
+                factors[g * far : (g + 1) * far, :] = part[at, quarter : quarter + far, :]
+
     filled = sizes.groups * far
     if filled < sizes.far_all:
         factors[filled:, :] = jnp.zeros_like(factors[filled:, :])
@@ -228,23 +251,36 @@
     far_out[0] = (far_tile[0, 1].astype(jnp.float32) - change).astype(jnp.bfloat16)
 
 
-def update(sizes, n, table, near_tiles, far_tiles, lefts, got, before):
+def slot_of(sizes, chunks, step, table):
+    k = step // sizes.inner
+    owner = table[sizes.owner_at(chunks[0])]
+    for j in range(1, len(chunks)):
+        owner = jnp.where(k == j, table[sizes.owner_at(chunks[j])], owner)
+    return owner * sizes.inner + step % sizes.inner
+
+
+def update(sizes, chunks, table, near_tiles, far_tiles, lefts, got, before):
     order, rank = near_tiles.shape[1], far_tiles.shape[2]
+    steps = len(chunks) * sizes.inner
 
     def at_slot(*rest):
-        return lambda x, table: (table[sizes.owner_at(n)] * sizes.inner + x,) + rest
-
-    return pl.pallas_call(
-        functools.partial(update_kernel, sizes, n),
+        return lambda step, table: (slot_of(sizes, chunks, step, table),) + rest
+
+    def at_step(*rest):
+        return lambda step, table: (step,) + rest
+
+    place_in = at_slot if near_tiles.shape[0] == sizes.slots else at_step
+    return pl.pallas_call(
+        functools.partial(update_kernel, sizes, chunks),
         grid_spec=pltpu.PrefetchScalarGridSpec(
             num_scalar_prefetch=1,
-            grid=(sizes.inner,),
+            grid=(steps,),
             in_specs=[
-                pl.BlockSpec((1, order, order), lambda x, table: (x, 0, 0)),
-                pl.BlockSpec((1, 2, rank, order), lambda x, table: (x, 0, 0, 0)),
-                VMEM,
+                pl.BlockSpec((1, order, order), place_in(0, 0)),
+                pl.BlockSpec((1, 2, rank, order), place_in(0, 0, 0)),
                 VMEM,
             ]
+            + [VMEM] * len(got)
             + [KEPT] * len(before),
             out_specs=[
                 pl.BlockSpec((1, order, order), at_slot(0, 0)),
@@ -259,10 +295,12 @@
             jax.ShapeDtypeStruct((sizes.slots, order, order), jnp.bfloat16),
             jax.ShapeDtypeStruct((sizes.slots, rank, order), jnp.bfloat16),
         ],
-        input_output_aliases={5 + k: k for k in range(len(before))},
+        input_output_aliases={4 + len(got) + k: k for k in range(len(before))},
         compiler_params=pltpu.CompilerParams(vmem_limit_bytes=VMEM_LIMIT),
-        cost_estimate=pl.CostEstimate(flops=UPDATE_FLOPS, bytes_accessed=0, transcendentals=0),
-    )(table, near_tiles, far_tiles, lefts, got, *before)
+        cost_estimate=pl.CostEstimate(
+            flops=UPDATE_FLOPS * len(chunks), bytes_accessed=0, transcendentals=0
+        ),
+    )(table, near_tiles, far_tiles, lefts, *got, *before)
 
 
 def shards(
@@ -297,25 +335,23 @@
     held["pass2"] = along(held["middle"], [(1, 0), (2, 3)])
     held["pass3"] = along(held["cross"], [(1, 0), (2, 3)])
 
-    got, after = [], []
+    got = []
     for n in range(OUTER):
         if n > 0:
+            after = [held["cross"]] if n == 2 else []
             send = pack(sizes, n, table, [held[name] for name in CHUNK_SOURCES[n]], after)
         got.append(lax.all_to_all(send, PLANE, split_axis=0, concat_axis=0, tiled=True))
-        if n == 2:
-            line, token = join_rows(rows, got[1])
-            after = [token]
-
+
+    line = join_rows(rows, held["pass3"])
     parts = [line]
     for k in range(1, OUTER):
         parts.append(along(line, [(i, (i + k) % OUTER) for i in range(OUTER)]))
     lefts = make_lefts(sizes, table, parts)
-    outs = ()
-    for n in range(OUTER):
-        at = jnp.asarray(CHUNK_OWNER[n], jnp.int32)[outer] * inner_size
-        near = lax.dynamic_slice_in_dim(near_tiles, at, inner_size, 0)
-        far_pair = lax.dynamic_slice_in_dim(far_tiles, at, inner_size, 0)
-        outs = update(sizes, n, table, near, far_pair, lefts, got[n], outs)
+    outs = update(sizes, (0, 1, 2), table, near_tiles, far_tiles, lefts, got[:3], ())
+    at = by_position(CHUNK_OWNER[3], outer) * inner_size
+    near = lax.dynamic_slice_in_dim(near_tiles, at, inner_size, 0)
+    far_pair = lax.dynamic_slice_in_dim(far_tiles, at, inner_size, 0)
+    outs = update(sizes, (3,), table, near, far_pair, lefts, got[3:], outs)
     return tuple(outs)
 
 

time: 122 us -> 107 us (0.88)
  local copies, waits for them, and re-layouts: 18 us -> 9.12 us
  starting transfers between devices: 40.1 us -> 31.4 us
  Pallas kernels: 22 us -> 27.3 us
  between operations: 2.77 us -> 0.8 us
    ppermute x8, waiting for transfers between devices: 26.7 us -> 16.4 us  [along(): return lax.ppermute(value, 'outer', pairs)]
    all_to_all x4, waiting for transfers between devices: 11 us -> 20.3 us  [shards(): lax.all_to_all(send, PLANE, split_axis=0, concat_axis=0, tiled=True)]
    ppermute x8, starting transfers between devices: 22.2 us -> 13.7 us  [along(): return lax.ppermute(value, 'outer', pairs)]
    unnamed x38 -> x18, local copies, waits for them, and re-layouts: 12 us -> 4.47 us
    pallas_call x3, Pallas kernels: 3 us -> 8.62 us  [pack(): pl.pallas_call(functools.partial(pack_kernel, sizes, n), in_specs=[SMEM]...]
    dynamic_slice x3 -> x0, local copies, waits for them, and re-layouts: 1.75 us -> none  [shards(): at = jnp.asarray(CHUNK_OWNER[n], jnp.int32)[outer] * inner_size]
    pallas_call x4 -> x2, Pallas kernels: 15.2 us -> 13.5 us  [update(): pl.pallas_call(functools.partial(update_kernel, sizes, chunks), grid_spec...]
    pallas_call x1, Pallas kernels: 1.73 us -> 3.14 us  [first(): pl.pallas_call(functools.partial(first_kernel, sizes), in_specs=[SMEM] *...]
  transfers between devices with their start and end apart: 13 -> 13, of which waited for: 5 -> 7; matrix products, arithmetic and copies ran while one was open for 4% -> 3% of each run, Pallas kernels for 13% -> 18%
where the time goes in v6:
time: 107 us; the launch traced here: 106 us
  waiting for transfers between devices  36.7 us (34%)
  starting transfers between devices  31.4 us (29%)
  Pallas kernels  27.3 us (26%)
  local copies, waits for them, and re-layouts  9.12 us (9%)
    all_to_all x4, waiting for transfers between devices, shards(): lax.all_to_all(send, PLANE, split_axis=0, concat_axis=0, tiled=True)  20.3 us
    ppermute x8, waiting for transfers between devices, along(): return lax.ppermute(value, 'outer', pairs)  16.4 us
    all_to_all x4, starting transfers between devices, shards(): lax.all_to_all(send, PLANE, split_axis=0, concat_axis=0, tiled=True)  15.8 us
    ppermute x8, starting transfers between devices, along(): return lax.ppermute(value, 'outer', pairs)  13.7 us
    pallas_call x2, Pallas kernels, update(): pl.pallas_call(functools.partial(update_kernel, sizes, chunks), grid_spec...  13.5 us
    pallas_call x3, Pallas kernels, pack(): pl.pallas_call(functools.partial(pack_kernel, sizes, n), in_specs=[SMEM]...  8.62 us
    unnamed x18, local copies, waits for them, and re-layouts  4.47 us
    pallas_call x1, Pallas kernels, first(): pl.pallas_call(functools.partial(first_kernel, sizes), in_specs=[SMEM] *...  3.14 us
  transfers between devices with their start and end apart: 13, of which 7 were waited for; matrix products, arithmetic and copies ran while one was open for 3% of the time, Pallas kernels for 18%

profile of v6, /device:TPU:0, one launch (start us, length us, event | category | flops | bytes accessed | tf_op | source)
XLA Modules:
  0.0 106.0 jit_solution(8826749948717023930)
XLA Ops:
  0.6 1.6 %reshape.7.pairs = bf16[4,24,512]{2,1,0:T(8,128)(2,1)} reshape(bf16[4,12,2,512]{3,2,1,0:T(2,128)(2,1)} %bitcast.5) | data formatting | bytes 196608 | tf_op jit(solution)/shard_map/reshape | solution.py:314
  2.2 0.6 pad_add_fusion.place
  2.8 3.1 %shard_map.104 = (s32[90]{0:T(128)}, bf16[608,512]{1,0:T(8,128)(2,1)}, bf16[8,152,512]{2,1,0:T(8,128)(2,1)}) custom-call(s32[2]{0:T(128)} %pad_add_fusion.place, s32[8,32]{1,0:T(8,128)} %bitcast.6, s32[8,32]{1,0:T(8,128)} %bitcast.7, s32[1,8]{1,0:T(1,128)} %near_rows.1, s32[1,8]{1,0:T(1,128)} %far_rows.1, bf16[4,128,512]{2,1,0:T(8,128)(2,1)} %near.1, ...), custom_call_target="tpu_custom_call" | custom-call | tf_op jit(solution)/shard_map/pallas_call | solution.py:121
  6.0 1.5 %collective-permute-start.7 = (bf16[608,512]{1,0:T(8,128)(2,1)}, bf16[608,512]{1,0:T(8,128)(2,1)}, u32[]{:S(2)}, u32[]{:S(2)}) collective-permute-start(bf16[608,512]{1,0:T(8,128)(2,1)} %get-tuple-element.8), channel_id=1, source_target_pairs={{2,4},{4,2},{3,5},{5,3},{10,12},{12,10},{11,13},{13,11},{18,20},{2... | collective-permute-start | bytes 1867784 | tf_op jit(solution)/shard_map/ppermute | solution.py:320
  7.5 5.1 %collective-permute-start = (bf16[608,512]{1,0:T(8,128)(2,1)}, bf16[608,512]{1,0:T(8,128)(2,1)S(1)}, u32[]{:S(2)}, u32[]{:S(2)}) collective-permute-start(bf16[608,512]{1,0:T(8,128)(2,1)} %get-tuple-element.8), channel_id=1, source_target_pairs={{0,2},{2,0},{4,6},{6,4},{1,3},{3,1},{5,7},{7,5},{8,10},{10,8},{12,... | collective-permute-start | bytes 1867784 | tf_op jit(solution)/shard_map/ppermute | solution.py:320
  12.6 3.7 %all-to-all-start.1 = ((bf16[8,152,512]{2,1,0:T(8,128)(2,1)}), bf16[8,152,512]{2,1,0:T(8,128)(2,1)S(1)}, u32[]{:S(2)}, u32[]{:S(2)}) async-start(bf16[8,152,512]{2,1,0:T(8,128)(2,1)} %get-tuple-element.9), calls=%async_computation.1 | async-start | bytes 2490368 | tf_op jit(solution)/shard_map/all_to_all | solution.py:343
  16.3 0.0 collective-permute-done.7.refs_0_
  16.3 1.3 %collective-permute-start.8 = (bf16[608,512]{1,0:T(8,128)(2,1)}, bf16[608,512]{1,0:T(8,128)(2,1)}, u32[]{:S(2)}, u32[]{:S(2)}) collective-permute-start(bf16[608,512]{1,0:T(8,128)(2,1)} %collective-permute-done.7.refs_0_), channel_id=1, source_target_pairs={{2,0},{4,6},{3,1},{5,7},{10,8},{12,14},{11,9},{13,15},{18,16},{20,... | collective-permute-start | bytes 1867784 | tf_op jit(solution)/shard_map/ppermute | solution.py:320
  17.6 8.9 %collective-permute-done.refs_0_ = bf16[608,512]{1,0:T(8,128)(2,1)S(1)} collective-permute-done((bf16[608,512]{1,0:T(8,128)(2,1)}, bf16[608,512]{1,0:T(8,128)(2,1)S(1)}, u32[]{:S(2)}, u32[]{:S(2)}) %collective-permute-start) | collective-permute-done | bytes 622624 | tf_op jit(solution)/shard_map/ppermute | solution.py:320
  26.5 1.5 %collective-permute-start.1 = (bf16[608,512]{1,0:T(8,128)(2,1)S(1)}, bf16[608,512]{1,0:T(8,128)(2,1)}, u32[]{:S(2)}, u32[]{:S(2)}) collective-permute-start(bf16[608,512]{1,0:T(8,128)(2,1)S(1)} %collective-permute-done.refs_0_), channel_id=1, source_target_pairs={{2,4},{4,2},{3,5},{5,3},{10,12},{12,10},{11,13},{13,11},{18,20},{2... | collective-permute-start | bytes 1867784 | tf_op jit(solution)/shard_map/ppermute | solution.py:320
  28.0 0.0 copy-done.8
  28.0 2.9 %shard_map.108 = bf16[8,152,512]{2,1,0:T(8,128)(2,1)} custom-call(s32[90]{0:T(128)} %get-tuple-element.7.table, bf16[608,512]{1,0:T(8,128)(2,1)} %copy-done.8), custom_call_target="tpu_custom_call" | custom-call | flops 10000000000 | tf_op jit(solution)/shard_map/pallas_call | solution.py:151
  30.9 0.0 copy-start.7
  30.9 2.4 %all-to-all-done.1.refs_0_ = bf16[8,152,512]{2,1,0:T(8,128)(2,1)S(1)} async-done(((bf16[8,152,512]{2,1,0:T(8,128)(2,1)}), bf16[8,152,512]{2,1,0:T(8,128)(2,1)S(1)}, u32[]{:S(2)}, u32[]{:S(2)}) %all-to-all-start.1) | async-done | bytes 1245216 | tf_op jit(solution)/shard_map/all_to_all | solution.py:343
  33.3 3.6 %all-to-all-start.2 = ((bf16[8,152,512]{2,1,0:T(8,128)(2,1)}), bf16[8,152,512]{2,1,0:T(8,128)(2,1)S(1)}, u32[]{:S(2)}, u32[]{:S(2)}) async-start(bf16[8,152,512]{2,1,0:T(8,128)(2,1)} %shard_map.108), calls=%async_computation.2 | async-start | bytes 2490368 | tf_op jit(solution)/shard_map/all_to_all | solution.py:343
  36.9 0.0 copy-done.7
  36.9 1.9 %collective-permute-start.3 = (bf16[2,64,512]{2,1,0:T(8,128)(2,1)S(1)}, bf16[2,64,512]{2,1,0:T(8,128)(2,1)S(1)}, u32[]{:S(2)}, u32[]{:S(2)}) collective-permute-start(bf16[2,64,512]{2,1,0:T(8,128)(2,1)S(1)} %copy-done.7), channel_id=1, source_target_pairs={{1,0},{0,1},{3,2},{2,3},{5,4},{4,5},{7,6},{6,7},{9,8},{8,9},{11,10... | collective-permute-start | bytes 393224 | tf_op jit(solution)/shard_map/ppermute | solution.py:325
  38.8 0.0 collective-permute-done.1.refs_0_.refs_2_
  38.8 1.3 %collective-permute-start.2 = (bf16[608,512]{1,0:T(8,128)(2,1)}, bf16[608,512]{1,0:T(8,128)(2,1)S(1)}, u32[]{:S(2)}, u32[]{:S(2)}) collective-permute-start(bf16[608,512]{1,0:T(8,128)(2,1)} %collective-permute-done.1.refs_0_.refs_2_), channel_id=1, source_target_pairs={{2,0},{4,6},{3,1},{5,7},{10,8},{12,14},{11,9},{13,15},{18,16},{20,... | collective-permute-start | bytes 1867784 | tf_op jit(solution)/shard_map/ppermute | solution.py:320
  40.1 1.6 %collective-permute-done.8.refs_1_ = bf16[608,512]{1,0:T(8,128)(2,1)} collective-permute-done((bf16[608,512]{1,0:T(8,128)(2,1)}, bf16[608,512]{1,0:T(8,128)(2,1)}, u32[]{:S(2)}, u32[]{:S(2)}) %collective-permute-start.8) | collective-permute-done | bytes 622624 | tf_op jit(solution)/shard_map/ppermute | solution.py:320
  41.7 2.9 %shard_map.109 = bf16[8,152,512]{2,1,0:T(8,128)(2,1)} custom-call(s32[90]{0:T(128)} %get-tuple-element.7.table, bf16[608,512]{1,0:T(8,128)(2,1)} %collective-permute-done.7.refs_0_, bf16[608,512]{1,0:T(8,128)(2,1)} %collective-permute-done.8.refs_1_, bf16[608,512]{1,0:T(8,128)(2,1)} %collective-permute-done.1.refs_0_.refs_2_), custom_call_target="tpu_custom_call" | custom-call | flops 10000000000 | tf_op jit(solution)/shard_map/pallas_call | solution.py:151
  44.6 9.3 %all-to-all-done.2.refs_1_ = bf16[8,152,512]{2,1,0:T(8,128)(2,1)S(1)} async-done(((bf16[8,152,512]{2,1,0:T(8,128)(2,1)}), bf16[8,152,512]{2,1,0:T(8,128)(2,1)S(1)}, u32[]{:S(2)}, u32[]{:S(2)}) %all-to-all-start.2) | async-done | bytes 1245216 | tf_op jit(solution)/shard_map/all_to_all | solution.py:343
  53.8 4.3 %all-to-all-start.3 = ((bf16[8,152,512]{2,1,0:T(8,128)(2,1)}), bf16[8,152,512]{2,1,0:T(8,128)(2,1)}, u32[]{:S(2)}, u32[]{:S(2)}) async-start(bf16[8,152,512]{2,1,0:T(8,128)(2,1)} %shard_map.109), calls=%async_computation.3 | async-start | bytes 2490368 | tf_op jit(solution)/shard_map/all_to_all | solution.py:343
  58.1 0.0 collective-permute-done.3.refs_1_
  58.1 1.6 %collective-permute-done.2.after.refs_1_ = bf16[608,512]{1,0:T(8,128)(2,1)S(1)} collective-permute-done((bf16[608,512]{1,0:T(8,128)(2,1)}, bf16[608,512]{1,0:T(8,128)(2,1)S(1)}, u32[]{:S(2)}, u32[]{:S(2)}) %collective-permute-start.2) | collective-permute-done | bytes 622624 | tf_op jit(solution)/shard_map/ppermute | solution.py:320
  59.7 0.8 shard_map.105.refs_0_
  60.5 0.2 copy-done.6
  60.6 2.5 %collective-permute-start.6 = (bf16[2,2,64,512]{3,2,1,0:T(8,128)(2,1)}, bf16[2,2,64,512]{3,2,1,0:T(8,128)(2,1)}, u32[]{:S(2)}, u32[]{:S(2)}) collective-permute-start(bf16[2,2,64,512]{3,2,1,0:T(8,128)(2,1)} %shard_map.105.refs_0_), channel_id=1, source_target_pairs={{0,6},{2,0},{4,2},{6,4},{1,7},{3,1},{5,3},{7,5},{8,14},{10,8},{12,... | collective-permute-start | bytes 786440 | tf_op jit(solution)/shard_map/ppermute | solution.py:320
  63.1 0.0 collective-permute-start.5
  63.1 0.6 collective-permute-start.4
  63.7 2.9 %shard_map.107 = bf16[8,152,512]{2,1,0:T(8,128)(2,1)} custom-call(s32[90]{0:T(128)} %get-tuple-element.7.table, bf16[608,512]{1,0:T(8,128)(2,1)} %collective-permute-done.1.refs_0_.refs_2_, bf16[608,512]{1,0:T(8,128)(2,1)} %copy-done.6), custom_call_target="tpu_custom_call" | custom-call | flops 10000000000 | tf_op jit(solution)/shard_map/pallas_call | solution.py:151
  66.6 8.6 %all-to-all-done.3.refs_2_ = bf16[8,152,512]{2,1,0:T(8,128)(2,1)} async-done(((bf16[8,152,512]{2,1,0:T(8,128)(2,1)}), bf16[8,152,512]{2,1,0:T(8,128)(2,1)}, u32[]{:S(2)}, u32[]{:S(2)}) %all-to-all-start.3) | async-done | bytes 1245216 | tf_op jit(solution)/shard_map/all_to_all | solution.py:343
  75.2 4.3 %all-to-all-start = ((bf16[8,152,512]{2,1,0:T(8,128)(2,1)}), bf16[8,152,512]{2,1,0:T(8,128)(2,1)}, u32[]{:S(2)}, u32[]{:S(2)}) async-start(bf16[8,152,512]{2,1,0:T(8,128)(2,1)} %shard_map.107), calls=%async_computation | async-start | bytes 2490368 | tf_op jit(solution)/shard_map/all_to_all | solution.py:343
  79.4 1.6 %constant_dynamic-slice_fusion.far_tile = bf16[2,2,48,512]{3,2,1,0:T(8,128)(2,1)} fusion(bf16[8,2,48,512]{3,2,1,0:T(8,128)(2,1)} %far_tile.1, s32[]{:T(128)S(6)} %select_n.14), kind=kLoop, calls=%fused_computation.1 | loop fusion | bytes 393220 | tf_op jit(solution)/shard_map/dynamic_slice | solution.py:353
  81.1 1.4 %constant_dynamic-slice_fusion.1.near_tile = bf16[2,512,512]{2,1,0:T(8,128)(2,1)S(1)} fusion(bf16[8,512,512]{2,1,0:T(8,128)(2,1)} %near_tile.1, s32[]{:T(128)S(6)} %select_n.14), kind=kLoop, calls=%fused_computation.2 | loop fusion | bytes 2097156 | tf_op jit(solution)/shard_map/dynamic_slice | solution.py:352
  82.5 0.0 collective-permute-done.6.refs_3_
  82.5 4.3 %collective-permute-done.5.refs_2_ = bf16[2,2,64,512]{3,2,1,0:T(8,128)(2,1)} collective-permute-done((bf16[2,2,64,512]{3,2,1,0:T(8,128)(2,1)}, bf16[2,2,64,512]{3,2,1,0:T(8,128)(2,1)}, u32[]{:S(2)}, u32[]{:S(2)}) %collective-permute-start.5) | collective-permute-done | bytes 262176 | tf_op jit(solution)/shard_map/ppermute | solution.py:320
  86.8 0.0 collective-permute-done.4.refs_1_
  86.8 1.3 %shard_map.106.lefts = bf16[2,512,512]{2,1,0:T(8,128)(2,1)S(1)} custom-call(s32[90]{0:T(128)S(1)} %copy-done.5, bf16[2,2,64,512]{3,2,1,0:T(8,128)(2,1)} %shard_map.105.refs_0_, bf16[2,2,64,512]{3,2,1,0:T(8,128)(2,1)} %collective-permute-done.4.refs_1_, bf16[2,2,64,512]{3,2,1,0:T(8,128)(2,1)} %collective-permute-done.5.refs_2_, ...), custom_call_target="tpu_custom_call" | custom-call | tf_op jit(solution)/shard_map/pallas_call | solution.py:194
  88.1 0.0 copy-done.2
  88.1 0.0 copy-start.4
  88.1 1.1 %copy-done.4 = bf16[8,2,48,512]{3,2,1,0:T(8,128)(2,1)S(1)} copy-done((bf16[8,2,48,512]{3,2,1,0:T(8,128)(2,1)S(1)}, bf16[8,2,48,512]{3,2,1,0:T(8,128)(2,1)}, u32[]{:S(2)}) %copy-start.4) | copy-done | bytes 786456
  89.3 8.9 %shard_map.110 = (bf16[8,512,512]{2,1,0:T(8,128)(2,1)}, bf16[8,48,512]{2,1,0:T(8,128)(2,1)}) custom-call(s32[90]{0:T(128)S(1)} %copy-done.5, bf16[8,512,512]{2,1,0:T(8,128)(2,1)S(1)} %copy-done.2, bf16[8,2,48,512]{3,2,1,0:T(8,128)(2,1)S(1)} %copy-done.4, bf16[2,512,512]{2,1,0:T(8,128)(2,1)S(1)} %shard_map.106.lefts, ...), custom_call_target="tpu_custom_call" | custom-call | flops 8999999488 | tf_op jit(solution)/shard_map/pallas_call | solution.py:273
  98.2 1.0 copy-done
  99.2 0.0 all-to-all-done.refs_0_
  99.2 1.2 %copy-done.1 = bf16[2,512,512]{2,1,0:T(8,128)(2,1)S(1)} copy-done((bf16[2,512,512]{2,1,0:T(8,128)(2,1)S(1)}, bf16[2,512,512]{2,1,0:T(8,128)(2,1)}, u32[]{:S(2)}) %copy-start.1) | copy-done | bytes 1048600
  100.4 0.9 copy-done.3
  101.4 4.6 %shard_map.111 = (bf16[8,512,512]{2,1,0:T(8,128)(2,1)}, bf16[8,48,512]{2,1,0:T(8,128)(2,1)}) custom-call(s32[90]{0:T(128)S(1)} %copy-done.5, bf16[2,512,512]{2,1,0:T(8,128)(2,1)S(1)} %constant_dynamic-slice_fusion.1.near_tile, bf16[2,2,48,512]{3,2,1,0:T(8,128)(2,1)S(1)} %copy-done.3, ...), custom_call_target="tpu_custom_call", output_to_operand_aliasing={{0}: (5, {}), {1}: (6, {})} | custom-call | flops 3000000000 | tf_op jit(solution)/shard_map/pallas_call | solution.py:273
  (8 shorter events, 0.0 us)
Async XLA Ops:
  6.0 10.3 %collective-permute-start.7 = (bf16[608,512]{1,0:T(8,128)(2,1)}, bf16[608,512]{1,0:T(8,128)(2,1)}, u32[]{:S(2)}, u32[]{:S(2)}) collective-permute-start(bf16[608,512]{1,0:T(8,128)(2,1)} %get-tuple-element.8), channel_id=1, source_target_pairs={{2,4},{4,2},{3,5},{5,3},{10,12},{12,10},{11,13},{13,11},{18,20},{2... | collective-permute-start | bytes 1867784 | tf_op jit(solution)/shard_map/ppermute | solution.py:320
  7.5 19.0 %collective-permute-start = (bf16[608,512]{1,0:T(8,128)(2,1)}, bf16[608,512]{1,0:T(8,128)(2,1)S(1)}, u32[]{:S(2)}, u32[]{:S(2)}) collective-permute-start(bf16[608,512]{1,0:T(8,128)(2,1)} %get-tuple-element.8), channel_id=1, source_target_pairs={{0,2},{2,0},{4,6},{6,4},{1,3},{3,1},{5,7},{7,5},{8,10},{10,8},{12,... | collective-permute-start | bytes 1867784 | tf_op jit(solution)/shard_map/ppermute | solution.py:320
  12.6 20.8 %all-to-all-start.1 = ((bf16[8,152,512]{2,1,0:T(8,128)(2,1)}), bf16[8,152,512]{2,1,0:T(8,128)(2,1)S(1)}, u32[]{:S(2)}, u32[]{:S(2)}) async-start(bf16[8,152,512]{2,1,0:T(8,128)(2,1)} %get-tuple-element.9), calls=%async_computation.1 | async-start | bytes 2490368 | tf_op jit(solution)/shard_map/all_to_all | solution.py:343
  16.3 25.4 %collective-permute-start.8 = (bf16[608,512]{1,0:T(8,128)(2,1)}, bf16[608,512]{1,0:T(8,128)(2,1)}, u32[]{:S(2)}, u32[]{:S(2)}) collective-permute-start(bf16[608,512]{1,0:T(8,128)(2,1)} %collective-permute-done.7.refs_0_), channel_id=1, source_target_pairs={{2,0},{4,6},{3,1},{5,7},{10,8},{12,14},{11,9},{13,15},{18,16},{20,... | collective-permute-start | bytes 1867784 | tf_op jit(solution)/shard_map/ppermute | solution.py:320
  26.5 1.5 %copy-start.8 = (bf16[608,512]{1,0:T(8,128)(2,1)}, bf16[608,512]{1,0:T(8,128)(2,1)S(1)}, u32[]{:S(2)}) copy-start(bf16[608,512]{1,0:T(8,128)(2,1)S(1)} %collective-permute-done.refs_0_) | copy-start | bytes 1867780
  26.5 12.3 %collective-permute-start.1 = (bf16[608,512]{1,0:T(8,128)(2,1)S(1)}, bf16[608,512]{1,0:T(8,128)(2,1)}, u32[]{:S(2)}, u32[]{:S(2)}) collective-permute-start(bf16[608,512]{1,0:T(8,128)(2,1)S(1)} %collective-permute-done.refs_0_), channel_id=1, source_target_pairs={{2,4},{4,2},{3,5},{5,3},{10,12},{12,10},{11,13},{13,11},{18,20},{2... | collective-permute-start | bytes 1867784 | tf_op jit(solution)/shard_map/ppermute | solution.py:320
  30.9 6.0 %copy-start.7 = (bf16[2,64,512]{2,1,0:T(8,128)(2,1)S(1)}, bf16[2,64,512]{2,1,0:T(8,128)(2,1)}, u32[]{:S(2)}) copy-start(bf16[2,64,512]{2,1,0:T(8,128)(2,1)} %refs_0_.1) | copy-start | bytes 393220
  33.3 20.5 %all-to-all-start.2 = ((bf16[8,152,512]{2,1,0:T(8,128)(2,1)}), bf16[8,152,512]{2,1,0:T(8,128)(2,1)S(1)}, u32[]{:S(2)}, u32[]{:S(2)}) async-start(bf16[8,152,512]{2,1,0:T(8,128)(2,1)} %shard_map.108), calls=%async_computation.2 | async-start | bytes 2490368 | tf_op jit(solution)/shard_map/all_to_all | solution.py:343
  36.9 21.2 %collective-permute-start.3 = (bf16[2,64,512]{2,1,0:T(8,128)(2,1)S(1)}, bf16[2,64,512]{2,1,0:T(8,128)(2,1)S(1)}, u32[]{:S(2)}, u32[]{:S(2)}) collective-permute-start(bf16[2,64,512]{2,1,0:T(8,128)(2,1)S(1)} %copy-done.7), channel_id=1, source_target_pairs={{1,0},{0,1},{3,2},{2,3},{5,4},{4,5},{7,6},{6,7},{9,8},{8,9},{11,10... | collective-permute-start | bytes 393224 | tf_op jit(solution)/shard_map/ppermute | solution.py:325
  38.8 20.9 %collective-permute-start.2 = (bf16[608,512]{1,0:T(8,128)(2,1)}, bf16[608,512]{1,0:T(8,128)(2,1)S(1)}, u32[]{:S(2)}, u32[]{:S(2)}) collective-permute-start(bf16[608,512]{1,0:T(8,128)(2,1)} %collective-permute-done.1.refs_0_.refs_2_), channel_id=1, source_target_pairs={{2,0},{4,6},{3,1},{5,7},{10,8},{12,14},{11,9},{13,15},{18,16},{20,... | collective-permute-start | bytes 1867784 | tf_op jit(solution)/shard_map/ppermute | solution.py:320
  53.8 21.3 %all-to-all-start.3 = ((bf16[8,152,512]{2,1,0:T(8,128)(2,1)}), bf16[8,152,512]{2,1,0:T(8,128)(2,1)}, u32[]{:S(2)}, u32[]{:S(2)}) async-start(bf16[8,152,512]{2,1,0:T(8,128)(2,1)} %shard_map.109), calls=%async_computation.3 | async-start | bytes 2490368 | tf_op jit(solution)/shard_map/all_to_all | solution.py:343
  59.7 0.9 copy-start.6
  60.6 21.9 %collective-permute-start.6 = (bf16[2,2,64,512]{3,2,1,0:T(8,128)(2,1)}, bf16[2,2,64,512]{3,2,1,0:T(8,128)(2,1)}, u32[]{:S(2)}, u32[]{:S(2)}) collective-permute-start(bf16[2,2,64,512]{3,2,1,0:T(8,128)(2,1)} %shard_map.105.refs_0_), channel_id=1, source_target_pairs={{0,6},{2,0},{4,2},{6,4},{1,7},{3,1},{5,3},{7,5},{8,14},{10,8},{12,... | collective-permute-start | bytes 786440 | tf_op jit(solution)/shard_map/ppermute | solution.py:320
  63.1 23.7 %collective-permute-start.5 = (bf16[2,2,64,512]{3,2,1,0:T(8,128)(2,1)}, bf16[2,2,64,512]{3,2,1,0:T(8,128)(2,1)}, u32[]{:S(2)}, u32[]{:S(2)}) collective-permute-start(bf16[2,2,64,512]{3,2,1,0:T(8,128)(2,1)} %shard_map.105.refs_0_), channel_id=1, source_target_pairs={{0,4},{2,6},{4,0},{6,2},{1,5},{3,7},{5,1},{7,3},{8,12},{10,14},{12... | collective-permute-start | bytes 786440 | tf_op jit(solution)/shard_map/ppermute | solution.py:320
  63.1 23.7 %collective-permute-start.4 = (bf16[2,2,64,512]{3,2,1,0:T(8,128)(2,1)}, bf16[2,2,64,512]{3,2,1,0:T(8,128)(2,1)}, u32[]{:S(2)}, u32[]{:S(2)}) collective-permute-start(bf16[2,2,64,512]{3,2,1,0:T(8,128)(2,1)} %shard_map.105.refs_0_), channel_id=1, source_target_pairs={{0,2},{2,4},{4,6},{6,0},{1,3},{3,5},{5,7},{7,1},{8,10},{10,12},{12... | collective-permute-start | bytes 786440 | tf_op jit(solution)/shard_map/ppermute | solution.py:320
  75.2 24.1 %all-to-all-start = ((bf16[8,152,512]{2,1,0:T(8,128)(2,1)}), bf16[8,152,512]{2,1,0:T(8,128)(2,1)}, u32[]{:S(2)}, u32[]{:S(2)}) async-start(bf16[8,152,512]{2,1,0:T(8,128)(2,1)} %shard_map.107), calls=%async_computation | async-start | bytes 2490368 | tf_op jit(solution)/shard_map/all_to_all | solution.py:343
  79.4 7.4 %copy-start.5 = (s32[90]{0:T(128)S(1)}, s32[90]{0:T(128)}, u32[]{:S(2)}) copy-start(s32[90]{0:T(128)} %get-tuple-element.7.table) | copy-start | bytes 1084
  81.1 7.0 %copy-start.2 = (bf16[8,512,512]{2,1,0:T(8,128)(2,1)S(1)}, bf16[8,512,512]{2,1,0:T(8,128)(2,1)}, u32[]{:S(2)}) copy-start(bf16[8,512,512]{2,1,0:T(8,128)(2,1)} %near_tile.1) | copy-start | bytes 12582916
  88.1 1.1 %copy-start.4 = (bf16[8,2,48,512]{3,2,1,0:T(8,128)(2,1)S(1)}, bf16[8,2,48,512]{3,2,1,0:T(8,128)(2,1)}, u32[]{:S(2)}) copy-start(bf16[8,2,48,512]{3,2,1,0:T(8,128)(2,1)} %far_tile.1) | copy-start | bytes 2359300
  98.2 1.0 copy-start
  99.2 1.2 %copy-start.1 = (bf16[2,512,512]{2,1,0:T(8,128)(2,1)S(1)}, bf16[2,512,512]{2,1,0:T(8,128)(2,1)}, u32[]{:S(2)}) copy-start(bf16[2,512,512]{2,1,0:T(8,128)(2,1)} %copy-done) | copy-start | bytes 3145732
  100.4 0.9 copy-start.3

commit v7 on v6

--- a/solution.py
+++ b/solution.py
@@ -14,6 +14,7 @@
 LANES = 128
 VMEM_LIMIT = 16 * 1024 * 1024
 WIDE_VMEM = 60 * 1024 * 1024
+LEFTS_VMEM = 24 * 1024 * 1024
 HBM = pl.BlockSpec(memory_space=pltpu.HBM)
 CHUNK_OWNER = ((0, 1, 2, 3), (1, 0, 3, 2), (2, 2, 1, 1), (3, 3, 0, 0))
 CHUNK_SOURCE = ((0, 0, 0, 0), (0, 0, 0, 0), (1, 0, 0, 1), (1, 0, 0, 1))
@@ -53,8 +54,8 @@
     return result
 
 
-def fill_table(sizes, place, near_cols, far_cols, near_rows, far_rows, table):
-    outer, inner = place[0], place[1]
+def fill_table(sizes, near_cols, far_cols, near_rows, far_rows, table):
+    outer, inner = lax.axis_index("outer"), lax.axis_index("inner")
     table[sizes.inner_at] = inner
     table[sizes.outer_at] = outer
     for n in range(OUTER):
@@ -100,14 +101,19 @@
     ]
 
 
-def first_kernel(sizes, place, near_cols, far_cols, near_rows, far_rows, near, pairs, *outs):
+def first_kernel(sizes, near_cols, far_cols, near_rows, far_rows, near, pairs, *outs):
     table, own, sent, out, sems = outs
-    fill_table(sizes, place, near_cols, far_cols, near_rows, far_rows, table)
+    fill_table(sizes, near_cols, far_cols, near_rows, far_rows, table)
     quarter, far = sizes.quarter, sizes.far
     far_at = sizes.per_bucket * quarter
     for j in range(sizes.per_bucket):
         own[j * quarter : (j + 1) * quarter, :] = near[j]
-        own[far_at + j * far : far_at + (j + 1) * far, :] = pairs[j]
+        at = far_at + j * far
+        count = 2 * pairs.shape[1]
+        for r in range(pairs.shape[1]):
+            own[at + 2 * r : at + 2 * r + 2, :] = pairs[j, r]
+        if count < far:
+            own[at + count : at + far, :] = jnp.zeros((far - count, own.shape[1]), own.dtype)
     pack_from(sizes, 0, table, own, out, sent, sems)
 
 
@@ -115,12 +121,12 @@
     return jax.ShapeDtypeStruct((sizes.wanted, sizes.quarter + sizes.far, order), jnp.bfloat16)
 
 
-def first(sizes, place, near_cols, far_cols, near_rows, far_rows, near, pairs):
+def first(sizes, near_cols, far_cols, near_rows, far_rows, near, pairs):
     order = near.shape[2]
     rows = sizes.per_bucket * (sizes.quarter + sizes.far)
     return pl.pallas_call(
         functools.partial(first_kernel, sizes),
-        in_specs=[SMEM] * 5 + [VMEM] * 2,
+        in_specs=[SMEM] * 4 + [VMEM] * 2,
         out_specs=[SMEM, VMEM, HBM],
         scratch_shapes=pack_scratch(sizes, order),
         out_shape=[
@@ -130,7 +136,7 @@
         ],
         compiler_params=pltpu.CompilerParams(vmem_limit_bytes=WIDE_VMEM),
         cost_estimate=pl.CostEstimate(flops=0, bytes_accessed=0, transcendentals=0),
-    )(place, near_cols.T, far_cols.T, near_rows, far_rows, near, pairs)
+    )(near_cols.T, far_cols.T, near_rows, far_rows, near, pairs)
 
 
 def pack_kernel(sizes, n, table, *refs):
@@ -176,8 +182,8 @@
     )(after, *parts)
 
 
-def lefts_kernel(sizes, table, *refs):
-    parts, lefts = refs[:-1], refs[-1]
+def lefts_kernel(sizes, table, far_tiles, *refs):
+    parts, (lefts, x_halves) = refs[:-2], refs[-2:]
     shard = sizes.shard
     inner, outer = table[sizes.inner_at], table[sizes.outer_at]
     for step, part in enumerate(parts):
@@ -187,68 +193,86 @@
             at = pl.multiple_of((z * sizes.inner + x) * shard, ROW_ALIGN)
             for r in range(lefts.shape[0]):
                 lefts[r, pl.ds(at, shard), :] = part[k, r]
-
-
-def make_lefts(sizes, table, parts):
+    rank = far_tiles.shape[2]
+    bases = jnp.concatenate([far_tiles[s, 0] for s in range(sizes.slots)], axis=0)
+    for r in range(lefts.shape[0]):
+        x_trans = jnp.dot(bases, lefts[r], preferred_element_type=jnp.float32)
+        for s in range(sizes.slots):
+
+            @pl.when(table[sizes.far_rows_at + s] == r)
+            def _(s=s, own=x_trans[s * rank : (s + 1) * rank]):
+                x_halves[s] = halves(own)
+
+
+def make_lefts(sizes, table, far_tiles, parts):
     row_group, shard, order = parts[0].shape[1:]
+    rank = far_tiles.shape[2]
     return pl.pallas_call(
         functools.partial(lefts_kernel, sizes),
-        in_specs=[SMEM] + [VMEM] * len(parts),
-        out_specs=VMEM,
-        out_shape=jax.ShapeDtypeStruct((row_group, order, order), jnp.bfloat16),
-        compiler_params=pltpu.CompilerParams(vmem_limit_bytes=VMEM_LIMIT),
+        in_specs=[SMEM, VMEM] + [VMEM] * len(parts),
+        out_specs=[VMEM, VMEM],
+        out_shape=[
+            jax.ShapeDtypeStruct((row_group, order, order), jnp.bfloat16),
+            jax.ShapeDtypeStruct((sizes.slots, 2 * rank, order), jnp.bfloat16),
+        ],
+        compiler_params=pltpu.CompilerParams(vmem_limit_bytes=LEFTS_VMEM),
         cost_estimate=pl.CostEstimate(flops=0, bytes_accessed=0, transcendentals=0),
-    )(table, *parts)
+    )(table, far_tiles, *parts)
 
 
 def halves(value):
     high = value.astype(jnp.bfloat16)
-    return high, (value - high.astype(jnp.float32)).astype(jnp.bfloat16)
-
-
-def update_kernel(sizes, chunks, table, near_tile, far_tile, lefts, *refs):
+    low = (value - high.astype(jnp.float32)).astype(jnp.bfloat16)
+    return jnp.concatenate([high, low], axis=0)
+
+
+ACROSS = (((1,), (1,)), ((), ()))
+
+
+def near_update(tile, left, panel):
+    product = lax.dot_general(left, panel, ACROSS, preferred_element_type=jnp.float32)
+    return (tile.astype(jnp.float32) - product).astype(jnp.bfloat16)
+
+
+def far_update(tile, x_halves, pairs):
+    rank = tile.shape[0]
+    both = lax.dot_general(x_halves, pairs, ACROSS, preferred_element_type=jnp.float32)
+    small = both[:rank] + both[rank:]
+    turned = pltpu.roll(small, small.shape[1] - 1, 1)
+    lane = lax.broadcasted_iota(jnp.int32, turned.shape, 1)
+    turned = jnp.where(lane % 2 == 0, turned, 0.0)
+    change = jnp.dot(halves(turned), pairs, preferred_element_type=jnp.float32)
+    return (tile.astype(jnp.float32) - (change[:rank] + change[rank:])).astype(jnp.bfloat16)
+
+
+def clear_rest(sizes, factors):
+    filled = sizes.groups * sizes.far
+    if filled < sizes.far_all:
+        factors[filled:, :] = jnp.zeros_like(factors[filled:, :])
+
+
+def take_part(sizes, g, part, panel, factors):
+    quarter, far = sizes.quarter, sizes.far
+    panel[g * quarter : (g + 1) * quarter, :] = part[0:quarter, :]
+    factors[g * far : (g + 1) * far, :] = part[quarter : quarter + far, :]
+
+
+def update_kernel(sizes, chunks, table, near_tile, far_tile, lefts, x_halves, *refs):
     got, (near_out, far_out, panel, factors) = refs[: len(chunks)], refs[-4:]
     step = pl.program_id(0)
     x = step % sizes.inner
     slot = slot_of(sizes, chunks, step, table)
-    quarter, far = sizes.quarter, sizes.far
     for k, part in enumerate(got):
 
         @pl.when(step // sizes.inner == k)
         def _(part=part):
             for g in range(sizes.groups):
-                at = g * sizes.inner + x
-                panel[g * quarter : (g + 1) * quarter, :] = part[at, 0:quarter, :]
-                factors[g * far : (g + 1) * far, :] = part[at, quarter : quarter + far, :]
-
-    filled = sizes.groups * far
-    if filled < sizes.far_all:
-        factors[filled:, :] = jnp.zeros_like(factors[filled:, :])
-    across = (((1,), (1,)), ((), ()))
-    product = lax.dot_general(
-        lefts[table[sizes.near_rows_at + slot]],
-        panel[...],
-        across,
-        preferred_element_type=jnp.float32,
-    )
-    near_out[0] = (near_tile[0].astype(jnp.float32) - product).astype(jnp.bfloat16)
-    x_trans = jnp.dot(
-        far_tile[0, 0],
-        lefts[table[sizes.far_rows_at + slot]],
-        preferred_element_type=jnp.float32,
-    )
-    pairs = factors[...]
-    small = sum(
-        lax.dot_general(part, pairs, across, preferred_element_type=jnp.float32)
-        for part in halves(x_trans)
-    )
-    turned = pltpu.roll(small, sizes.far_all - 1, 1)
-    lane = lax.broadcasted_iota(jnp.int32, turned.shape, 1)
-    turned = jnp.where(lane % 2 == 0, turned, 0.0)
-    change = sum(
-        jnp.dot(part, pairs, preferred_element_type=jnp.float32) for part in halves(turned)
-    )
-    far_out[0] = (far_tile[0, 1].astype(jnp.float32) - change).astype(jnp.bfloat16)
+                take_part(sizes, g, part.at[g * sizes.inner + x], panel, factors)
+
+    clear_rest(sizes, factors)
+    left = lefts[table[sizes.near_rows_at + slot]]
+    near_out[0] = near_update(near_tile[0], left, panel[...])
+    far_out[0] = far_update(far_tile[0, 1], x_halves[slot], factors[...])
 
 
 def slot_of(sizes, chunks, step, table):
@@ -259,29 +283,32 @@
     return owner * sizes.inner + step % sizes.inner
 
 
-def update(sizes, chunks, table, near_tiles, far_tiles, lefts, got, before):
+def out_shapes(sizes, near_tiles, far_tiles):
     order, rank = near_tiles.shape[1], far_tiles.shape[2]
-    steps = len(chunks) * sizes.inner
+    return [
+        jax.ShapeDtypeStruct((sizes.slots, order, order), jnp.bfloat16),
+        jax.ShapeDtypeStruct((sizes.slots, rank, order), jnp.bfloat16),
+    ]
+
+
+def update(sizes, chunks, table, near_tiles, far_tiles, lefts, x_halves, got):
+    order, rank = near_tiles.shape[1], far_tiles.shape[2]
 
     def at_slot(*rest):
         return lambda step, table: (slot_of(sizes, chunks, step, table),) + rest
 
-    def at_step(*rest):
-        return lambda step, table: (step,) + rest
-
-    place_in = at_slot if near_tiles.shape[0] == sizes.slots else at_step
     return pl.pallas_call(
         functools.partial(update_kernel, sizes, chunks),
         grid_spec=pltpu.PrefetchScalarGridSpec(
             num_scalar_prefetch=1,
-            grid=(steps,),
+            grid=(len(chunks) * sizes.inner,),
             in_specs=[
-                pl.BlockSpec((1, order, order), place_in(0, 0)),
-                pl.BlockSpec((1, 2, rank, order), place_in(0, 0, 0)),
+                pl.BlockSpec((1, order, order), at_slot(0, 0)),
+                pl.BlockSpec((1, 2, rank, order), at_slot(0, 0, 0)),
+                VMEM,
                 VMEM,
             ]
-            + [VMEM] * len(got)
-            + [KEPT] * len(before),
+            + [VMEM] * len(got),
             out_specs=[
                 pl.BlockSpec((1, order, order), at_slot(0, 0)),
                 pl.BlockSpec((1, rank, order), at_slot(0, 0)),
@@ -291,16 +318,82 @@
                 pltpu.VMEM((sizes.far_all, order), jnp.bfloat16),
             ],
         ),
-        out_shape=[
-            jax.ShapeDtypeStruct((sizes.slots, order, order), jnp.bfloat16),
-            jax.ShapeDtypeStruct((sizes.slots, rank, order), jnp.bfloat16),
-        ],
-        input_output_aliases={4 + len(got) + k: k for k in range(len(before))},
+        out_shape=out_shapes(sizes, near_tiles, far_tiles),
         compiler_params=pltpu.CompilerParams(vmem_limit_bytes=VMEM_LIMIT),
         cost_estimate=pl.CostEstimate(
             flops=UPDATE_FLOPS * len(chunks), bytes_accessed=0, transcendentals=0
         ),
-    )(table, near_tiles, far_tiles, lefts, *got, *before)
+    )(table, near_tiles, far_tiles, lefts, x_halves, *got)
+
+
+def last_kernel(sizes, n, table, near_tiles, far_tiles, lefts, x_halves, got, *refs):
+    near_out, far_out = refs[2:4]
+    tile, far_tile, left, x_half, parts, near_done, far_done, panel, factors, sems = refs[4:]
+    first = table[sizes.owner_at(n)] * sizes.inner
+    loads = []
+    for x in range(sizes.inner):
+        slot = first + x
+        pairs = [(got.at[g * sizes.inner + x], parts.at[x, g]) for g in range(sizes.groups)]
+        pairs += [
+            (lefts.at[table[sizes.near_rows_at + slot]], left.at[x]),
+            (near_tiles.at[slot], tile.at[x]),
+            (x_halves.at[slot], x_half.at[x]),
+            (far_tiles.at[slot, 1], far_tile.at[x]),
+        ]
+        loads.append(
+            [
+                pltpu.make_async_copy(source, to, sems.at[x, k])
+                for k, (source, to) in enumerate(pairs)
+            ]
+        )
+        for load in loads[x]:
+            load.start()
+    clear_rest(sizes, factors)
+    stores = []
+    at = sizes.groups + 4
+    for x in range(sizes.inner):
+        for load in loads[x]:
+            load.wait()
+        for g in range(sizes.groups):
+            take_part(sizes, g, parts.at[x, g], panel, factors)
+        near_done[x] = near_update(tile[x], left[x], panel[...])
+        stores.append(
+            pltpu.make_async_copy(near_done.at[x], near_out.at[first + x], sems.at[x, at])
+        )
+        stores[-1].start()
+        far_done[x] = far_update(far_tile[x], x_half[x], factors[...])
+        stores.append(
+            pltpu.make_async_copy(far_done.at[x], far_out.at[first + x], sems.at[x, at + 1])
+        )
+        stores[-1].start()
+    for store in stores:
+        store.wait()
+
+
+def last_update(sizes, n, table, near_tiles, far_tiles, lefts, x_halves, got, before):
+    order, rank = near_tiles.shape[1], far_tiles.shape[2]
+    inner, groups = sizes.inner, sizes.groups
+    return pl.pallas_call(
+        functools.partial(last_kernel, sizes, n),
+        in_specs=[SMEM] + [HBM] * 7,
+        out_specs=[HBM, HBM],
+        out_shape=out_shapes(sizes, near_tiles, far_tiles),
+        scratch_shapes=[
+            pltpu.VMEM((inner, order, order), jnp.bfloat16),
+            pltpu.VMEM((inner, rank, order), jnp.bfloat16),
+            pltpu.VMEM((inner, order, order), jnp.bfloat16),
+            pltpu.VMEM((inner, 2 * rank, order), jnp.bfloat16),
+            pltpu.VMEM((inner, groups, sizes.quarter + sizes.far, order), jnp.bfloat16),
+            pltpu.VMEM((inner, order, order), jnp.bfloat16),
+            pltpu.VMEM((inner, rank, order), jnp.bfloat16),
+            pltpu.VMEM((order, order), jnp.bfloat16),
+            pltpu.VMEM((sizes.far_all, order), jnp.bfloat16),
+            pltpu.SemaphoreType.DMA((inner, groups + 6)),
+        ],
+        input_output_aliases={6: 0, 7: 1},
+        compiler_params=pltpu.CompilerParams(vmem_limit_bytes=WIDE_VMEM),
+        cost_estimate=pl.CostEstimate(flops=UPDATE_FLOPS, bytes_accessed=0, transcendentals=0),
+    )(table, near_tiles, far_tiles, lefts, x_halves, got, *before)
 
 
 def shards(
@@ -308,12 +401,10 @@
 ):
     inner_size = lax.axis_size("inner")
     groups = lax.axis_size("gy") * lax.axis_size("core")
-    outer, inner = lax.axis_index("outer"), lax.axis_index("inner")
     per_bucket, quarter, order = col_near.shape
     row_group, shard = row_panel.shape[:2]
-    far_pairs = jnp.swapaxes(col_far, 1, 2).reshape(per_bucket, -1, order)
-    far = -(-far_pairs.shape[1] // FAR_ALIGN) * FAR_ALIGN
-    far_pairs = jnp.pad(far_pairs, ((0, 0), (0, far - far_pairs.shape[1]), (0, 0)))
+    far_pairs = jnp.swapaxes(col_far, 1, 2)
+    far = -(-2 * col_far.shape[2] // FAR_ALIGN) * FAR_ALIGN
     sizes = Sizes(groups, inner_size, per_bucket, quarter, far, shard)
 
     def along(value, pairs):
@@ -324,9 +415,8 @@
         turn = [((i + k) % inner_size, i) for i in range(inner_size)]
         rows.append(lax.ppermute(row_panel, "inner", turn))
 
-    place = jnp.stack([outer, inner])
     table, own, send = first(
-        sizes, place, near_cols, far_cols, near_rows, far_rows, col_near, far_pairs
+        sizes, near_cols, far_cols, near_rows, far_rows, col_near, far_pairs
     )
     held = {"own": own}
     held["pair"] = along(own, [(0, 1), (1, 0), (2, 3), (3, 2)])
@@ -346,12 +436,10 @@
     parts = [line]
     for k in range(1, OUTER):
         parts.append(along(line, [(i, (i + k) % OUTER) for i in range(OUTER)]))
-    lefts = make_lefts(sizes, table, parts)
-    outs = update(sizes, (0, 1, 2), table, near_tiles, far_tiles, lefts, got[:3], ())
-    at = by_position(CHUNK_OWNER[3], outer) * inner_size
-    near = lax.dynamic_slice_in_dim(near_tiles, at, inner_size, 0)
-    far_pair = lax.dynamic_slice_in_dim(far_tiles, at, inner_size, 0)
-    outs = update(sizes, (3,), table, near, far_pair, lefts, got[3:], outs)
+    lefts, x_halves = make_lefts(sizes, table, far_tiles, parts)
+    tiles = (near_tiles, far_tiles, lefts, x_halves)
+    outs = update(sizes, (0, 1, 2), table, *tiles, got[:3])
+    outs = last_update(sizes, 3, table, *tiles, got[3], outs)
     return tuple(outs)
 
 

time: 107 us -> 105 us (0.981)
  local copies, waits for them, and re-layouts: 9.12 us -> 6.44 us
  waiting for transfers between devices: 36.7 us -> 39 us
  Pallas kernels: 27.3 us -> 26 us
    pallas_call x2 -> x1, Pallas kernels: 13.5 us -> 7.59 us  [update(): pl.pallas_call(functools.partial(update_kernel, sizes, chunks), grid_spec...]
    pallas_call x1 -> x2, Pallas kernels: 1.27 us -> 6.61 us  [the longest x1 4.49 us: last_update(): pl.pallas_call(functools.partial(last_kernel, sizes, n), in_specs=[SMEM]...]
    ppermute x8, waiting for transfers between devices: 16.4 us -> 20.1 us  [along(): return lax.ppermute(value, 'outer', pairs)]
    dynamic_slice x2 -> x0, local copies, waits for them, and re-layouts: 3.08 us -> none  [the longest x1 1.63 us: shards(): far_pair = lax.dynamic_slice_in_dim(far_tiles, at, inner_size, 0)]
    unnamed x18 -> x20, local copies, waits for them, and re-layouts: 4.47 us -> 6.44 us
    reshape x1 -> x0, local copies, waits for them, and re-layouts: 1.58 us -> none  [shards(): far_pairs = jnp.swapaxes(col_far, 1, 2).reshape(per_bucket, -1, order)]
    all_to_all x4, waiting for transfers between devices: 20.3 us -> 18.9 us  [shards(): lax.all_to_all(send, PLANE, split_axis=0, concat_axis=0, tiled=True)]
  transfers between devices with their start and end apart: 13 -> 13, of which waited for: 7 -> 7; matrix products, arithmetic and copies ran while one was open for 3% -> 0% of each run, Pallas kernels for 18% -> 18%
where the time goes in v7:
time: 105 us; the launch traced here: 104 us
  waiting for transfers between devices  39 us (37%)
  starting transfers between devices  32 us (30%)
  Pallas kernels  26 us (25%)
  local copies, waits for them, and re-layouts  6.44 us (6%)
    ppermute x8, waiting for transfers between devices, along(): return lax.ppermute(value, 'outer', pairs)  20.1 us
    all_to_all x4, waiting for transfers between devices, shards(): lax.all_to_all(send, PLANE, split_axis=0, concat_axis=0, tiled=True)  18.9 us
    all_to_all x4, starting transfers between devices, shards(): lax.all_to_all(send, PLANE, split_axis=0, concat_axis=0, tiled=True)  15.8 us
    ppermute x8, starting transfers between devices, along(): return lax.ppermute(value, 'outer', pairs)  14.2 us
    pallas_call x3, Pallas kernels, pack(): pl.pallas_call(functools.partial(pack_kernel, sizes, n), in_specs=[SMEM]...  8.62 us
    pallas_call x1, Pallas kernels, update(): pl.pallas_call(functools.partial(update_kernel, sizes, chunks), grid_spec...  7.59 us
    unnamed x20, local copies, waits for them, and re-layouts  6.44 us
    pallas_call x1, Pallas kernels, last_update(): pl.pallas_call(functools.partial(last_kernel, sizes, n), in_specs=[SMEM]...  4.49 us
  transfers between devices with their start and end apart: 13, of which 7 were waited for; matrix products, arithmetic and copies ran while one was open for 0% of the time, Pallas kernels for 18%

profile of v7, /device:TPU:0, one launch (start us, length us, event | category | flops | bytes accessed | tf_op | source)
XLA Modules:
  0.0 104.2 jit_solution(10464310549586058746)
XLA Ops:
  0.6 3.1 %shard_map.104 = (s32[90]{0:T(128)}, bf16[608,512]{1,0:T(8,128)(2,1)}, bf16[8,152,512]{2,1,0:T(8,128)(2,1)}) custom-call(s32[8,32]{1,0:T(8,128)} %bitcast.4, s32[8,32]{1,0:T(8,128)} %bitcast.5, s32[1,8]{1,0:T(1,128)} %near_rows.1, s32[1,8]{1,0:T(1,128)} %far_rows.1, bf16[4,128,512]{2,1,0:T(8,128)(2,1)} %near.1, bf16[4,12,2,512]{3,2,1,0:T(2,128)(2,1)} %bitcast.3), custom_call_target="tpu_custom_call" | custom-call | tf_op jit(solution)/shard_map/pallas_call | solution.py:127
  3.8 1.5 %collective-permute-start.7 = (bf16[608,512]{1,0:T(8,128)(2,1)}, bf16[608,512]{1,0:T(8,128)(2,1)}, u32[]{:S(2)}, u32[]{:S(2)}) collective-permute-start(bf16[608,512]{1,0:T(8,128)(2,1)} %get-tuple-element.10), channel_id=1, source_target_pairs={{2,4},{4,2},{3,5},{5,3},{10,12},{12,10},{11,13},{13,11},{18,20},{2... | collective-permute-start | bytes 1867784 | tf_op jit(solution)/shard_map/ppermute | solution.py:411
  5.3 5.1 %collective-permute-start = (bf16[608,512]{1,0:T(8,128)(2,1)}, bf16[608,512]{1,0:T(8,128)(2,1)S(1)}, u32[]{:S(2)}, u32[]{:S(2)}) collective-permute-start(bf16[608,512]{1,0:T(8,128)(2,1)} %get-tuple-element.10), channel_id=1, source_target_pairs={{0,2},{2,0},{4,6},{6,4},{1,3},{3,1},{5,7},{7,5},{8,10},{10,8},{12,... | collective-permute-start | bytes 1867784 | tf_op jit(solution)/shard_map/ppermute | solution.py:411
  10.4 3.7 %all-to-all-start.1 = ((bf16[8,152,512]{2,1,0:T(8,128)(2,1)}), bf16[8,152,512]{2,1,0:T(8,128)(2,1)S(1)}, u32[]{:S(2)}, u32[]{:S(2)}) async-start(bf16[8,152,512]{2,1,0:T(8,128)(2,1)} %get-tuple-element.13), calls=%async_computation.1 | async-start | bytes 2490368 | tf_op jit(solution)/shard_map/all_to_all | solution.py:433
  14.1 0.0 collective-permute-done.7.refs_0_
  14.1 1.3 %collective-permute-start.8 = (bf16[608,512]{1,0:T(8,128)(2,1)}, bf16[608,512]{1,0:T(8,128)(2,1)}, u32[]{:S(2)}, u32[]{:S(2)}) collective-permute-start(bf16[608,512]{1,0:T(8,128)(2,1)} %collective-permute-done.7.refs_0_), channel_id=1, source_target_pairs={{2,0},{4,6},{3,1},{5,7},{10,8},{12,14},{11,9},{13,15},{18,16},{20,... | collective-permute-start | bytes 1867784 | tf_op jit(solution)/shard_map/ppermute | solution.py:411
  15.4 8.9 %collective-permute-done.refs_0_ = bf16[608,512]{1,0:T(8,128)(2,1)S(1)} collective-permute-done((bf16[608,512]{1,0:T(8,128)(2,1)}, bf16[608,512]{1,0:T(8,128)(2,1)S(1)}, u32[]{:S(2)}, u32[]{:S(2)}) %collective-permute-start) | collective-permute-done | bytes 622624 | tf_op jit(solution)/shard_map/ppermute | solution.py:411
  24.3 1.5 %collective-permute-start.1 = (bf16[608,512]{1,0:T(8,128)(2,1)S(1)}, bf16[608,512]{1,0:T(8,128)(2,1)}, u32[]{:S(2)}, u32[]{:S(2)}) collective-permute-start(bf16[608,512]{1,0:T(8,128)(2,1)S(1)} %collective-permute-done.refs_0_), channel_id=1, source_target_pairs={{2,4},{4,2},{3,5},{5,3},{10,12},{12,10},{11,13},{13,11},{18,20},{2... | collective-permute-start | bytes 1867784 | tf_op jit(solution)/shard_map/ppermute | solution.py:411
  25.8 0.0 copy-done.9
  25.8 2.9 %shard_map.108 = bf16[8,152,512]{2,1,0:T(8,128)(2,1)} custom-call(s32[90]{0:T(128)} %get-tuple-element.9.table, bf16[608,512]{1,0:T(8,128)(2,1)} %copy-done.9), custom_call_target="tpu_custom_call" | custom-call | flops 10000000000 | tf_op jit(solution)/shard_map/pallas_call | solution.py:157
  28.7 0.0 copy-start.6
  28.7 2.4 %all-to-all-done.1.refs_0_ = bf16[8,152,512]{2,1,0:T(8,128)(2,1)S(1)} async-done(((bf16[8,152,512]{2,1,0:T(8,128)(2,1)}), bf16[8,152,512]{2,1,0:T(8,128)(2,1)S(1)}, u32[]{:S(2)}, u32[]{:S(2)}) %all-to-all-start.1) | async-done | bytes 1245216 | tf_op jit(solution)/shard_map/all_to_all | solution.py:433
  31.1 3.6 %all-to-all-start.2 = ((bf16[8,152,512]{2,1,0:T(8,128)(2,1)}), bf16[8,152,512]{2,1,0:T(8,128)(2,1)S(1)}, u32[]{:S(2)}, u32[]{:S(2)}) async-start(bf16[8,152,512]{2,1,0:T(8,128)(2,1)} %shard_map.108), calls=%async_computation.2 | async-start | bytes 2490368 | tf_op jit(solution)/shard_map/all_to_all | solution.py:433
  34.7 0.0 copy-done.6
  34.7 1.9 %collective-permute-start.3 = (bf16[2,64,512]{2,1,0:T(8,128)(2,1)S(1)}, bf16[2,64,512]{2,1,0:T(8,128)(2,1)S(1)}, u32[]{:S(2)}, u32[]{:S(2)}) collective-permute-start(bf16[2,64,512]{2,1,0:T(8,128)(2,1)S(1)} %copy-done.6), channel_id=1, source_target_pairs={{1,0},{0,1},{3,2},{2,3},{5,4},{4,5},{7,6},{6,7},{9,8},{8,9},{11,10... | collective-permute-start | bytes 393224 | tf_op jit(solution)/shard_map/ppermute | solution.py:416
  36.6 0.0 collective-permute-done.1.refs_0_.refs_2_
  36.6 1.3 %collective-permute-start.2 = (bf16[608,512]{1,0:T(8,128)(2,1)}, bf16[608,512]{1,0:T(8,128)(2,1)S(1)}, u32[]{:S(2)}, u32[]{:S(2)}) collective-permute-start(bf16[608,512]{1,0:T(8,128)(2,1)} %collective-permute-done.1.refs_0_.refs_2_), channel_id=1, source_target_pairs={{2,0},{4,6},{3,1},{5,7},{10,8},{12,14},{11,9},{13,15},{18,16},{20,... | collective-permute-start | bytes 1867784 | tf_op jit(solution)/shard_map/ppermute | solution.py:411
  37.9 1.6 %collective-permute-done.8.refs_1_ = bf16[608,512]{1,0:T(8,128)(2,1)} collective-permute-done((bf16[608,512]{1,0:T(8,128)(2,1)}, bf16[608,512]{1,0:T(8,128)(2,1)}, u32[]{:S(2)}, u32[]{:S(2)}) %collective-permute-start.8) | collective-permute-done | bytes 622624 | tf_op jit(solution)/shard_map/ppermute | solution.py:411
  39.5 2.9 %shard_map.109 = bf16[8,152,512]{2,1,0:T(8,128)(2,1)} custom-call(s32[90]{0:T(128)} %get-tuple-element.9.table, bf16[608,512]{1,0:T(8,128)(2,1)} %collective-permute-done.7.refs_0_, bf16[608,512]{1,0:T(8,128)(2,1)} %collective-permute-done.8.refs_1_, bf16[608,512]{1,0:T(8,128)(2,1)} %collective-permute-done.1.refs_0_.refs_2_), custom_call_target="tpu_custom_call" | custom-call | flops 10000000000 | tf_op jit(solution)/shard_map/pallas_call | solution.py:157
  42.4 9.3 %all-to-all-done.2.refs_1_ = bf16[8,152,512]{2,1,0:T(8,128)(2,1)S(1)} async-done(((bf16[8,152,512]{2,1,0:T(8,128)(2,1)}), bf16[8,152,512]{2,1,0:T(8,128)(2,1)S(1)}, u32[]{:S(2)}, u32[]{:S(2)}) %all-to-all-start.2) | async-done | bytes 1245216 | tf_op jit(solution)/shard_map/all_to_all | solution.py:433
  51.6 4.3 %all-to-all-start.3 = ((bf16[8,152,512]{2,1,0:T(8,128)(2,1)}), bf16[8,152,512]{2,1,0:T(8,128)(2,1)}, u32[]{:S(2)}, u32[]{:S(2)}) async-start(bf16[8,152,512]{2,1,0:T(8,128)(2,1)} %shard_map.109), calls=%async_computation.3 | async-start | bytes 2490368 | tf_op jit(solution)/shard_map/all_to_all | solution.py:433
  55.9 0.0 collective-permute-done.3.refs_1_
  55.9 0.0 copy-start.7
  55.9 0.6 copy-done.7
  56.6 0.9 collective-permute-done.2.after.refs_1_
  57.5 0.9 copy-done.8
  58.4 0.8 copy-done.5
  59.2 2.5 %collective-permute-start.6 = (bf16[2,2,64,512]{3,2,1,0:T(8,128)(2,1)S(1)}, bf16[2,2,64,512]{3,2,1,0:T(8,128)(2,1)}, u32[]{:S(2)}, u32[]{:S(2)}) collective-permute-start(bf16[2,2,64,512]{3,2,1,0:T(8,128)(2,1)S(1)} %shard_map.105.refs_0_), channel_id=1, source_target_pairs={{0,6},{2,0},{4,2},{6,4},{1,7},{3,1},{5,3},{7,5},{8,14},{10,8},{12,... | collective-permute-start | bytes 786440 | tf_op jit(solution)/shard_map/ppermute | solution.py:411
  61.7 0.7 collective-permute-start.5
  62.4 0.4 collective-permute-start.4
  62.8 2.9 %shard_map.107 = bf16[8,152,512]{2,1,0:T(8,128)(2,1)} custom-call(s32[90]{0:T(128)} %get-tuple-element.9.table, bf16[608,512]{1,0:T(8,128)(2,1)} %collective-permute-done.1.refs_0_.refs_2_, bf16[608,512]{1,0:T(8,128)(2,1)} %copy-done.5), custom_call_target="tpu_custom_call" | custom-call | flops 10000000000 | tf_op jit(solution)/shard_map/pallas_call | solution.py:157
  65.7 0.0 copy-start.1
  65.7 0.0 copy-start.4
  65.7 7.2 %all-to-all-done.3.refs_2_ = bf16[8,152,512]{2,1,0:T(8,128)(2,1)} async-done(((bf16[8,152,512]{2,1,0:T(8,128)(2,1)}), bf16[8,152,512]{2,1,0:T(8,128)(2,1)}, u32[]{:S(2)}, u32[]{:S(2)}) %all-to-all-start.3) | async-done | bytes 1245216 | tf_op jit(solution)/shard_map/all_to_all | solution.py:433
  73.0 4.3 %all-to-all-start = ((bf16[8,152,512]{2,1,0:T(8,128)(2,1)}), bf16[8,152,512]{2,1,0:T(8,128)(2,1)}, u32[]{:S(2)}, u32[]{:S(2)}) async-start(bf16[8,152,512]{2,1,0:T(8,128)(2,1)} %shard_map.107), calls=%async_computation | async-start | bytes 2490368 | tf_op jit(solution)/shard_map/all_to_all | solution.py:433
  77.2 0.0 collective-permute-done.6.refs_3_
  77.3 8.6 %collective-permute-done.5.refs_2_ = bf16[2,2,64,512]{3,2,1,0:T(8,128)(2,1)} collective-permute-done((bf16[2,2,64,512]{3,2,1,0:T(8,128)(2,1)S(1)}, bf16[2,2,64,512]{3,2,1,0:T(8,128)(2,1)}, u32[]{:S(2)}, u32[]{:S(2)}) %collective-permute-start.5) | collective-permute-done | bytes 262176 | tf_op jit(solution)/shard_map/ppermute | solution.py:411
  85.9 0.0 collective-permute-done.4.refs_1_
  85.9 0.0 copy-done.1
  85.9 0.0 copy-done.4
  85.9 2.1 %shard_map.106 = (bf16[2,512,512]{2,1,0:T(8,128)(2,1)S(1)}, bf16[8,96,512]{2,1,0:T(8,128)(2,1)S(1)}) custom-call(s32[90]{0:T(128)S(1)} %copy-done.4, bf16[8,2,48,512]{3,2,1,0:T(8,128)(2,1)S(1)} %copy-done.1, bf16[2,2,64,512]{3,2,1,0:T(8,128)(2,1)S(1)} %shard_map.105.refs_0_, bf16[2,2,64,512]{3,2,1,0:T(8,128)(2,1)} %collective-permute-done.4.refs_1_, ...), custom_call_target="tpu_custom_call" | custom-call | tf_op jit(solution)/shard_map/pallas_call | solution.py:210
  88.0 0.0 copy-start
  88.0 2.2 %copy-done = bf16[8,512,512]{2,1,0:T(8,128)(2,1)S(1)} copy-done((bf16[8,512,512]{2,1,0:T(8,128)(2,1)S(1)}, bf16[8,512,512]{2,1,0:T(8,128)(2,1)}, u32[]{:S(2)}) %copy-start) | copy-done | bytes 4194328
  90.2 7.6 %shard_map.110 = (bf16[8,512,512]{2,1,0:T(8,128)(2,1)}, bf16[8,48,512]{2,1,0:T(8,128)(2,1)}) custom-call(s32[90]{0:T(128)S(1)} %copy-done.4, bf16[8,512,512]{2,1,0:T(8,128)(2,1)S(1)} %copy-done, bf16[8,2,48,512]{3,2,1,0:T(8,128)(2,1)S(1)} %copy-done.1, bf16[2,512,512]{2,1,0:T(8,128)(2,1)S(1)} %get-tuple-element.11.lefts, ...), custom_call_target="tpu_custom_call" | custom-call | flops 8999999488 | tf_op jit(solution)/shard_map/pallas_call | solution.py:300
  97.8 1.0 copy-done.2
  98.8 0.9 copy-done.3
  99.7 0.0 all-to-all-done.got
  99.7 4.5 %shard_map.111 = (bf16[8,512,512]{2,1,0:T(8,128)(2,1)}, bf16[8,48,512]{2,1,0:T(8,128)(2,1)}) custom-call(s32[90]{0:T(128)} %get-tuple-element.9.table, bf16[8,512,512]{2,1,0:T(8,128)(2,1)} %near_tiles.1, bf16[8,2,48,512]{3,2,1,0:T(8,128)(2,1)} %far_tiles.3, bf16[2,512,512]{2,1,0:T(8,128)(2,1)} %copy-done.2, ...), custom_call_target="tpu_custom_call", output_to_operand_aliasing={{0}: (6, {}), {1}: (7, {})} | custom-call | flops 3000000000 | tf_op jit(solution)/shard_map/pallas_call | solution.py:376
  (6 shorter events, 0.0 us)
Async XLA Ops:
  3.8 10.3 %collective-permute-start.7 = (bf16[608,512]{1,0:T(8,128)(2,1)}, bf16[608,512]{1,0:T(8,128)(2,1)}, u32[]{:S(2)}, u32[]{:S(2)}) collective-permute-start(bf16[608,512]{1,0:T(8,128)(2,1)} %get-tuple-element.10), channel_id=1, source_target_pairs={{2,4},{4,2},{3,5},{5,3},{10,12},{12,10},{11,13},{13,11},{18,20},{2... | collective-permute-start | bytes 1867784 | tf_op jit(solution)/shard_map/ppermute | solution.py:411
  5.3 19.0 %collective-permute-start = (bf16[608,512]{1,0:T(8,128)(2,1)}, bf16[608,512]{1,0:T(8,128)(2,1)S(1)}, u32[]{:S(2)}, u32[]{:S(2)}) collective-permute-start(bf16[608,512]{1,0:T(8,128)(2,1)} %get-tuple-element.10), channel_id=1, source_target_pairs={{0,2},{2,0},{4,6},{6,4},{1,3},{3,1},{5,7},{7,5},{8,10},{10,8},{12,... | collective-permute-start | bytes 1867784 | tf_op jit(solution)/shard_map/ppermute | solution.py:411
  10.4 20.8 %all-to-all-start.1 = ((bf16[8,152,512]{2,1,0:T(8,128)(2,1)}), bf16[8,152,512]{2,1,0:T(8,128)(2,1)S(1)}, u32[]{:S(2)}, u32[]{:S(2)}) async-start(bf16[8,152,512]{2,1,0:T(8,128)(2,1)} %get-tuple-element.13), calls=%async_computation.1 | async-start | bytes 2490368 | tf_op jit(solution)/shard_map/all_to_all | solution.py:433
  14.1 25.4 %collective-permute-start.8 = (bf16[608,512]{1,0:T(8,128)(2,1)}, bf16[608,512]{1,0:T(8,128)(2,1)}, u32[]{:S(2)}, u32[]{:S(2)}) collective-permute-start(bf16[608,512]{1,0:T(8,128)(2,1)} %collective-permute-done.7.refs_0_), channel_id=1, source_target_pairs={{2,0},{4,6},{3,1},{5,7},{10,8},{12,14},{11,9},{13,15},{18,16},{20,... | collective-permute-start | bytes 1867784 | tf_op jit(solution)/shard_map/ppermute | solution.py:411
  24.3 1.5 %copy-start.9 = (bf16[608,512]{1,0:T(8,128)(2,1)}, bf16[608,512]{1,0:T(8,128)(2,1)S(1)}, u32[]{:S(2)}) copy-start(bf16[608,512]{1,0:T(8,128)(2,1)S(1)} %collective-permute-done.refs_0_) | copy-start | bytes 1867780
  24.3 12.3 %collective-permute-start.1 = (bf16[608,512]{1,0:T(8,128)(2,1)S(1)}, bf16[608,512]{1,0:T(8,128)(2,1)}, u32[]{:S(2)}, u32[]{:S(2)}) collective-permute-start(bf16[608,512]{1,0:T(8,128)(2,1)S(1)} %collective-permute-done.refs_0_), channel_id=1, source_target_pairs={{2,4},{4,2},{3,5},{5,3},{10,12},{12,10},{11,13},{13,11},{18,20},{2... | collective-permute-start | bytes 1867784 | tf_op jit(solution)/shard_map/ppermute | solution.py:411
  28.7 6.0 %copy-start.6 = (bf16[2,64,512]{2,1,0:T(8,128)(2,1)S(1)}, bf16[2,64,512]{2,1,0:T(8,128)(2,1)}, u32[]{:S(2)}) copy-start(bf16[2,64,512]{2,1,0:T(8,128)(2,1)} %refs_0_.1) | copy-start | bytes 393220
  31.1 20.5 %all-to-all-start.2 = ((bf16[8,152,512]{2,1,0:T(8,128)(2,1)}), bf16[8,152,512]{2,1,0:T(8,128)(2,1)S(1)}, u32[]{:S(2)}, u32[]{:S(2)}) async-start(bf16[8,152,512]{2,1,0:T(8,128)(2,1)} %shard_map.108), calls=%async_computation.2 | async-start | bytes 2490368 | tf_op jit(solution)/shard_map/all_to_all | solution.py:433
  34.7 21.2 %collective-permute-start.3 = (bf16[2,64,512]{2,1,0:T(8,128)(2,1)S(1)}, bf16[2,64,512]{2,1,0:T(8,128)(2,1)S(1)}, u32[]{:S(2)}, u32[]{:S(2)}) collective-permute-start(bf16[2,64,512]{2,1,0:T(8,128)(2,1)S(1)} %copy-done.6), channel_id=1, source_target_pairs={{1,0},{0,1},{3,2},{2,3},{5,4},{4,5},{7,6},{6,7},{9,8},{8,9},{11,10... | collective-permute-start | bytes 393224 | tf_op jit(solution)/shard_map/ppermute | solution.py:416
  36.6 20.9 %collective-permute-start.2 = (bf16[608,512]{1,0:T(8,128)(2,1)}, bf16[608,512]{1,0:T(8,128)(2,1)S(1)}, u32[]{:S(2)}, u32[]{:S(2)}) collective-permute-start(bf16[608,512]{1,0:T(8,128)(2,1)} %collective-permute-done.1.refs_0_.refs_2_), channel_id=1, source_target_pairs={{2,0},{4,6},{3,1},{5,7},{10,8},{12,14},{11,9},{13,15},{18,16},{20,... | collective-permute-start | bytes 1867784 | tf_op jit(solution)/shard_map/ppermute | solution.py:411
  51.6 21.3 %all-to-all-start.3 = ((bf16[8,152,512]{2,1,0:T(8,128)(2,1)}), bf16[8,152,512]{2,1,0:T(8,128)(2,1)}, u32[]{:S(2)}, u32[]{:S(2)}) async-start(bf16[8,152,512]{2,1,0:T(8,128)(2,1)} %shard_map.109), calls=%async_computation.3 | async-start | bytes 2490368 | tf_op jit(solution)/shard_map/all_to_all | solution.py:433
  55.9 0.7 copy-start.7
  57.5 0.9 copy-start.8
  58.4 0.8 copy-start.5
  59.2 18.0 %collective-permute-start.6 = (bf16[2,2,64,512]{3,2,1,0:T(8,128)(2,1)S(1)}, bf16[2,2,64,512]{3,2,1,0:T(8,128)(2,1)}, u32[]{:S(2)}, u32[]{:S(2)}) collective-permute-start(bf16[2,2,64,512]{3,2,1,0:T(8,128)(2,1)S(1)} %shard_map.105.refs_0_), channel_id=1, source_target_pairs={{0,6},{2,0},{4,2},{6,4},{1,7},{3,1},{5,3},{7,5},{8,14},{10,8},{12,... | collective-permute-start | bytes 786440 | tf_op jit(solution)/shard_map/ppermute | solution.py:411
  61.7 24.2 %collective-permute-start.5 = (bf16[2,2,64,512]{3,2,1,0:T(8,128)(2,1)S(1)}, bf16[2,2,64,512]{3,2,1,0:T(8,128)(2,1)}, u32[]{:S(2)}, u32[]{:S(2)}) collective-permute-start(bf16[2,2,64,512]{3,2,1,0:T(8,128)(2,1)S(1)} %shard_map.105.refs_0_), channel_id=1, source_target_pairs={{0,4},{2,6},{4,0},{6,2},{1,5},{3,7},{5,1},{7,3},{8,12},{10,14},{12... | collective-permute-start | bytes 786440 | tf_op jit(solution)/shard_map/ppermute | solution.py:411
  62.4 23.5 %collective-permute-start.4 = (bf16[2,2,64,512]{3,2,1,0:T(8,128)(2,1)S(1)}, bf16[2,2,64,512]{3,2,1,0:T(8,128)(2,1)}, u32[]{:S(2)}, u32[]{:S(2)}) collective-permute-start(bf16[2,2,64,512]{3,2,1,0:T(8,128)(2,1)S(1)} %shard_map.105.refs_0_), channel_id=1, source_target_pairs={{0,2},{2,4},{4,6},{6,0},{1,3},{3,5},{5,7},{7,1},{8,10},{10,12},{12... | collective-permute-start | bytes 786440 | tf_op jit(solution)/shard_map/ppermute | solution.py:411
  65.7 20.2 %copy-start.1 = (bf16[8,2,48,512]{3,2,1,0:T(8,128)(2,1)S(1)}, bf16[8,2,48,512]{3,2,1,0:T(8,128)(2,1)}, u32[]{:S(2)}) copy-start(bf16[8,2,48,512]{3,2,1,0:T(8,128)(2,1)} %far_tiles.3) | copy-start | bytes 2359300
  65.7 20.2 %copy-start.4 = (s32[90]{0:T(128)S(1)}, s32[90]{0:T(128)}, u32[]{:S(2)}) copy-start(s32[90]{0:T(128)} %get-tuple-element.9.table) | copy-start | bytes 1084
  73.0 26.7 %all-to-all-start = ((bf16[8,152,512]{2,1,0:T(8,128)(2,1)}), bf16[8,152,512]{2,1,0:T(8,128)(2,1)}, u32[]{:S(2)}, u32[]{:S(2)}) async-start(bf16[8,152,512]{2,1,0:T(8,128)(2,1)} %shard_map.107), calls=%async_computation | async-start | bytes 2490368 | tf_op jit(solution)/shard_map/all_to_all | solution.py:433
  88.0 2.2 %copy-start = (bf16[8,512,512]{2,1,0:T(8,128)(2,1)S(1)}, bf16[8,512,512]{2,1,0:T(8,128)(2,1)}, u32[]{:S(2)}) copy-start(bf16[8,512,512]{2,1,0:T(8,128)(2,1)} %near_tiles.1) | copy-start | bytes 12582916
  97.8 1.0 copy-start.2
  98.8 0.9 copy-start.3

commit v8 on v7

--- a/solution.py
+++ b/solution.py
@@ -182,17 +182,23 @@
     )(after, *parts)
 
 
-def lefts_kernel(sizes, table, far_tiles, *refs):
-    parts, (lefts, x_halves) = refs[:-2], refs[-2:]
+def lefts_kernel(sizes, table, far_tiles, line, near1, near2, near3, relayed, lefts, x_halves):
     shard = sizes.shard
     inner, outer = table[sizes.inner_at], table[sizes.outer_at]
-    for step, part in enumerate(parts):
-        z = lax.rem(outer + OUTER - step, OUTER)
+
+    def place(z, part):
         for k in range(sizes.inner):
             x = lax.rem(inner + k, sizes.inner)
             at = pl.multiple_of((z * sizes.inner + x) * shard, ROW_ALIGN)
             for r in range(lefts.shape[0]):
                 lefts[r, pl.ds(at, shard), :] = part[k, r]
+
+    place(outer, line)
+    amid = (outer == 1) | (outer == 2)
+    for n, part in ((1, near1), (2, near2), (3, near3)):
+        owner = table[sizes.owner_at(n)]
+        pl.when(amid)(functools.partial(place, owner, part))
+        pl.when(jnp.logical_not(amid))(functools.partial(place, owner, relayed.at[n - 1]))
     rank = far_tiles.shape[2]
     bases = jnp.concatenate([far_tiles[s, 0] for s in range(sizes.slots)], axis=0)
     for r in range(lefts.shape[0]):
@@ -205,7 +211,7 @@
 
 
 def make_lefts(sizes, table, far_tiles, parts):
-    row_group, shard, order = parts[0].shape[1:]
+    row_group, _, order = parts[0].shape[1:]
     rank = far_tiles.shape[2]
     return pl.pallas_call(
         functools.partial(lefts_kernel, sizes),
@@ -257,32 +263,6 @@
     factors[g * far : (g + 1) * far, :] = part[quarter : quarter + far, :]
 
 
-def update_kernel(sizes, chunks, table, near_tile, far_tile, lefts, x_halves, *refs):
-    got, (near_out, far_out, panel, factors) = refs[: len(chunks)], refs[-4:]
-    step = pl.program_id(0)
-    x = step % sizes.inner
-    slot = slot_of(sizes, chunks, step, table)
-    for k, part in enumerate(got):
-
-        @pl.when(step // sizes.inner == k)
-        def _(part=part):
-            for g in range(sizes.groups):
-                take_part(sizes, g, part.at[g * sizes.inner + x], panel, factors)
-
-    clear_rest(sizes, factors)
-    left = lefts[table[sizes.near_rows_at + slot]]
-    near_out[0] = near_update(near_tile[0], left, panel[...])
-    far_out[0] = far_update(far_tile[0, 1], x_halves[slot], factors[...])
-
-
-def slot_of(sizes, chunks, step, table):
-    k = step // sizes.inner
-    owner = table[sizes.owner_at(chunks[0])]
-    for j in range(1, len(chunks)):
-        owner = jnp.where(k == j, table[sizes.owner_at(chunks[j])], owner)
-    return owner * sizes.inner + step % sizes.inner
-
-
 def out_shapes(sizes, near_tiles, far_tiles):
     order, rank = near_tiles.shape[1], far_tiles.shape[2]
     return [
@@ -291,109 +271,82 @@
     ]
 
 
-def update(sizes, chunks, table, near_tiles, far_tiles, lefts, x_halves, got):
+def update_kernel(sizes, chunks, table, near_tiles, far_tiles, lefts, x_halves, *refs):
+    got, (near_out, far_out) = refs[: len(chunks)], refs[-12:-10]
+    tile, far_tile, left, x_half, parts, near_done, far_done, panel, factors, sems = refs[-10:]
+    left_loads = [
+        pltpu.make_async_copy(lefts.at[r], left.at[r], sems.at[0, sizes.groups + 5 + r])
+        for r in range(left.shape[0])
+    ]
+    slots, loads = [], []
+    for k, n in enumerate(chunks):
+        for x in range(sizes.inner):
+            at = len(slots)
+            slot = table[sizes.owner_at(n)] * sizes.inner + x
+            pairs = [(got[k].at[g * sizes.inner + x], parts.at[at, g]) for g in range(sizes.groups)]
+            pairs += [
+                (near_tiles.at[slot], tile.at[at]),
+                (x_halves.at[slot], x_half.at[at]),
+                (far_tiles.at[slot, 1], far_tile.at[at]),
+            ]
+            slots.append(slot)
+            loads.append(
+                [
+                    pltpu.make_async_copy(source, to, sems.at[at, j])
+                    for j, (source, to) in enumerate(pairs)
+                ]
+            )
+    for load in loads[0] + left_loads + sum(loads[1:], []):
+        load.start()
+    clear_rest(sizes, factors)
+    for load in left_loads:
+        load.wait()
+    stores = []
+    for at, slot in enumerate(slots):
+        for load in loads[at]:
+            load.wait()
+        for g in range(sizes.groups):
+            take_part(sizes, g, parts.at[at, g], panel, factors)
+        own_left = left[table[sizes.near_rows_at + slot]]
+        near_done[at] = near_update(tile[at], own_left, panel[...])
+        far_done[at] = far_update(far_tile[at], x_half[at], factors[...])
+        for j, (done, out) in enumerate(((near_done, near_out), (far_done, far_out))):
+            copy = pltpu.make_async_copy(
+                done.at[at], out.at[slot], sems.at[at, sizes.groups + 3 + j]
+            )
+            copy.start()
+            stores.append(copy)
+    for store in stores:
+        store.wait()
+
+
+def update(sizes, chunks, table, near_tiles, far_tiles, lefts, x_halves, got, before):
     order, rank = near_tiles.shape[1], far_tiles.shape[2]
-
-    def at_slot(*rest):
-        return lambda step, table: (slot_of(sizes, chunks, step, table),) + rest
-
+    groups, row_group = sizes.groups, lefts.shape[0]
+    count = len(chunks) * sizes.inner
     return pl.pallas_call(
         functools.partial(update_kernel, sizes, chunks),
-        grid_spec=pltpu.PrefetchScalarGridSpec(
-            num_scalar_prefetch=1,
-            grid=(len(chunks) * sizes.inner,),
-            in_specs=[
-                pl.BlockSpec((1, order, order), at_slot(0, 0)),
-                pl.BlockSpec((1, 2, rank, order), at_slot(0, 0, 0)),
-                VMEM,
-                VMEM,
-            ]
-            + [VMEM] * len(got),
-            out_specs=[
-                pl.BlockSpec((1, order, order), at_slot(0, 0)),
-                pl.BlockSpec((1, rank, order), at_slot(0, 0)),
-            ],
-            scratch_shapes=[
-                pltpu.VMEM((order, order), jnp.bfloat16),
-                pltpu.VMEM((sizes.far_all, order), jnp.bfloat16),
-            ],
-        ),
+        in_specs=[SMEM] + [HBM] * (4 + len(got) + len(before)),
+        out_specs=[HBM, HBM],
         out_shape=out_shapes(sizes, near_tiles, far_tiles),
-        compiler_params=pltpu.CompilerParams(vmem_limit_bytes=VMEM_LIMIT),
+        scratch_shapes=[
+            pltpu.VMEM((count, order, order), jnp.bfloat16),
+            pltpu.VMEM((count, rank, order), jnp.bfloat16),
+            pltpu.VMEM((row_group, order, order), jnp.bfloat16),
+            pltpu.VMEM((count, 2 * rank, order), jnp.bfloat16),
+            pltpu.VMEM((count, groups, sizes.quarter + sizes.far, order), jnp.bfloat16),
+            pltpu.VMEM((count, order, order), jnp.bfloat16),
+            pltpu.VMEM((count, rank, order), jnp.bfloat16),
+            pltpu.VMEM((order, order), jnp.bfloat16),
+            pltpu.VMEM((sizes.far_all, order), jnp.bfloat16),
+            pltpu.SemaphoreType.DMA((count, groups + 5 + row_group)),
+        ],
+        input_output_aliases={5 + len(got) + k: k for k in range(len(before))},
+        compiler_params=pltpu.CompilerParams(vmem_limit_bytes=WIDE_VMEM),
         cost_estimate=pl.CostEstimate(
             flops=UPDATE_FLOPS * len(chunks), bytes_accessed=0, transcendentals=0
         ),
-    )(table, near_tiles, far_tiles, lefts, x_halves, *got)
-
-
-def last_kernel(sizes, n, table, near_tiles, far_tiles, lefts, x_halves, got, *refs):
-    near_out, far_out = refs[2:4]
-    tile, far_tile, left, x_half, parts, near_done, far_done, panel, factors, sems = refs[4:]
-    first = table[sizes.owner_at(n)] * sizes.inner
-    loads = []
-    for x in range(sizes.inner):
-        slot = first + x
-        pairs = [(got.at[g * sizes.inner + x], parts.at[x, g]) for g in range(sizes.groups)]
-        pairs += [
-            (lefts.at[table[sizes.near_rows_at + slot]], left.at[x]),
-            (near_tiles.at[slot], tile.at[x]),
-            (x_halves.at[slot], x_half.at[x]),
-            (far_tiles.at[slot, 1], far_tile.at[x]),
-        ]
-        loads.append(
-            [
-                pltpu.make_async_copy(source, to, sems.at[x, k])
-                for k, (source, to) in enumerate(pairs)
-            ]
-        )
-        for load in loads[x]:
-            load.start()
-    clear_rest(sizes, factors)
-    stores = []
-    at = sizes.groups + 4
-    for x in range(sizes.inner):
-        for load in loads[x]:
-            load.wait()
-        for g in range(sizes.groups):
-            take_part(sizes, g, parts.at[x, g], panel, factors)
-        near_done[x] = near_update(tile[x], left[x], panel[...])
-        stores.append(
-            pltpu.make_async_copy(near_done.at[x], near_out.at[first + x], sems.at[x, at])
-        )
-        stores[-1].start()
-        far_done[x] = far_update(far_tile[x], x_half[x], factors[...])
-        stores.append(
-            pltpu.make_async_copy(far_done.at[x], far_out.at[first + x], sems.at[x, at + 1])
-        )
-        stores[-1].start()
-    for store in stores:
-        store.wait()
-
-
-def last_update(sizes, n, table, near_tiles, far_tiles, lefts, x_halves, got, before):
-    order, rank = near_tiles.shape[1], far_tiles.shape[2]
-    inner, groups = sizes.inner, sizes.groups
-    return pl.pallas_call(
-        functools.partial(last_kernel, sizes, n),
-        in_specs=[SMEM] + [HBM] * 7,
-        out_specs=[HBM, HBM],
-        out_shape=out_shapes(sizes, near_tiles, far_tiles),
-        scratch_shapes=[
-            pltpu.VMEM((inner, order, order), jnp.bfloat16),
-            pltpu.VMEM((inner, rank, order), jnp.bfloat16),
-            pltpu.VMEM((inner, order, order), jnp.bfloat16),
-            pltpu.VMEM((inner, 2 * rank, order), jnp.bfloat16),
-            pltpu.VMEM((inner, groups, sizes.quarter + sizes.far, order), jnp.bfloat16),
-            pltpu.VMEM((inner, order, order), jnp.bfloat16),
-            pltpu.VMEM((inner, rank, order), jnp.bfloat16),
-            pltpu.VMEM((order, order), jnp.bfloat16),
-            pltpu.VMEM((sizes.far_all, order), jnp.bfloat16),
-            pltpu.SemaphoreType.DMA((inner, groups + 6)),
-        ],
-        input_output_aliases={6: 0, 7: 1},
-        compiler_params=pltpu.CompilerParams(vmem_limit_bytes=WIDE_VMEM),
-        cost_estimate=pl.CostEstimate(flops=UPDATE_FLOPS, bytes_accessed=0, transcendentals=0),
-    )(table, near_tiles, far_tiles, lefts, x_halves, got, *before)
+    )(table, near_tiles, far_tiles, lefts, x_halves, *got, *before)
 
 
 def shards(
@@ -422,8 +375,8 @@
     held["pair"] = along(own, [(0, 1), (1, 0), (2, 3), (3, 2)])
     held["middle"] = along(own, [(1, 2), (2, 1)])
     held["cross"] = along(held["pair"], [(1, 2), (2, 1)])
-    held["pass2"] = along(held["middle"], [(1, 0), (2, 3)])
-    held["pass3"] = along(held["cross"], [(1, 0), (2, 3)])
+    held["pass2"] = along(held["middle"], [(0, 1), (1, 0), (2, 3), (3, 2)])
+    held["pass3"] = along(held["cross"], [(0, 1), (1, 0), (2, 3), (3, 2)])
 
     got = []
     for n in range(OUTER):
@@ -432,14 +385,17 @@
             send = pack(sizes, n, table, [held[name] for name in CHUNK_SOURCES[n]], after)
         got.append(lax.all_to_all(send, PLANE, split_axis=0, concat_axis=0, tiled=True))
 
-    line = join_rows(rows, held["pass3"])
-    parts = [line]
-    for k in range(1, OUTER):
-        parts.append(along(line, [(i, (i + k) % OUTER) for i in range(OUTER)]))
+    line = join_rows(rows, held["cross"])
+    near1 = along(line, [(0, 1), (3, 2)])
+    near2 = along(line, [(1, 2), (2, 1)])
+    near3 = along(line, [(0, 2), (3, 1)])
+    relayed = join_rows([line, near2, near3], held["pass3"])
+    relayed = along(relayed, [(0, 1), (1, 0), (2, 3), (3, 2)])
+    parts = [line, near1, near2, near3, relayed]
     lefts, x_halves = make_lefts(sizes, table, far_tiles, parts)
     tiles = (near_tiles, far_tiles, lefts, x_halves)
-    outs = update(sizes, (0, 1, 2), table, *tiles, got[:3])
-    outs = last_update(sizes, 3, table, *tiles, got[3], outs)
+    outs = update(sizes, (0, 1, 2), table, *tiles, got[:3], ())
+    outs = update(sizes, (3,), table, *tiles, got[3:], outs)
     return tuple(outs)
 
 

time: 105 us -> 103 us (0.981)
  starting transfers between devices: 32 us -> 48.8 us
  waiting for transfers between devices: 39 us -> 23 us
  local copies, waits for them, and re-layouts: 6.44 us -> 3.78 us
    ppermute x8 -> x9, starting transfers between devices: 14.2 us -> 30.1 us  [along(): return lax.ppermute(value, 'outer', pairs)]
    all_to_all x4, waiting for transfers between devices: 18.9 us -> 6.15 us  [shards(): lax.all_to_all(send, PLANE, split_axis=0, concat_axis=0, tiled=True)]
    ppermute x8 -> x9, waiting for transfers between devices: 20.1 us -> 16.9 us  [along(): return lax.ppermute(value, 'outer', pairs)]
    unnamed x20 -> x18, local copies, waits for them, and re-layouts: 6.44 us -> 3.78 us
  transfers between devices with their start and end apart: 13 -> 14, of which waited for: 7 -> 5; matrix products, arithmetic and copies ran while one was open for 0% -> 0% of each run, Pallas kernels for 18% -> 18%
where the time goes in v8:
time: 103 us
  starting transfers between devices  48.8 us (47%)
  Pallas kernels  26.3 us (26%)
  waiting for transfers between devices  23 us (22%)
  local copies, waits for them, and re-layouts  3.78 us (4%)
    ppermute x9, starting transfers between devices, along(): return lax.ppermute(value, 'outer', pairs)  30.1 us
    ppermute x9, waiting for transfers between devices, along(): return lax.ppermute(value, 'outer', pairs)  16.9 us
    all_to_all x4, starting transfers between devices, shards(): lax.all_to_all(send, PLANE, split_axis=0, concat_axis=0, tiled=True)  16.7 us
    pallas_call x2, Pallas kernels, update(): pl.pallas_call(functools.partial(update_kernel, sizes, chunks), in_specs=...  12.9 us
    pallas_call x3, Pallas kernels, pack(): pl.pallas_call(functools.partial(pack_kernel, sizes, n), in_specs=[SMEM]...  8.6 us
    all_to_all x4, waiting for transfers between devices, shards(): lax.all_to_all(send, PLANE, split_axis=0, concat_axis=0, tiled=True)  6.15 us
    unnamed x18, local copies, waits for them, and re-layouts  3.78 us
    pallas_call x1, Pallas kernels, first(): pl.pallas_call(functools.partial(first_kernel, sizes), in_specs=[SMEM] *...  3.13 us
  transfers between devices with their start and end apart: 14, of which 5 were waited for; matrix products, arithmetic and copies ran while one was open for 0% of the time, Pallas kernels for 18%

profile of v8, /device:TPU:0, one launch (start us, length us, event | category | flops | bytes accessed | tf_op | source)
XLA Modules:
  0.0 102.8 jit_solution(13039038782431780607)
XLA Ops:
  0.6 3.1 %shard_map.104 = (s32[90]{0:T(128)}, bf16[608,512]{1,0:T(8,128)(2,1)}, bf16[8,152,512]{2,1,0:T(8,128)(2,1)}) custom-call(s32[8,32]{1,0:T(8,128)} %bitcast.4, s32[8,32]{1,0:T(8,128)} %bitcast.5, s32[1,8]{1,0:T(1,128)} %near_rows.1, s32[1,8]{1,0:T(1,128)} %far_rows.1, bf16[4,128,512]{2,1,0:T(8,128)(2,1)} %near.1, bf16[4,12,2,512]{3,2,1,0:T(2,128)(2,1)} %bitcast.3), custom_call_target="tpu_custom_call" | custom-call | tf_op jit(solution)/shard_map/pallas_call | solution.py:127
  3.8 0.7 collective-permute-start.8
  4.5 5.9 %collective-permute-start = (bf16[608,512]{1,0:T(8,128)(2,1)}, bf16[608,512]{1,0:T(8,128)(2,1)}, u32[]{:S(2)}, u32[]{:S(2)}) collective-permute-start(bf16[608,512]{1,0:T(8,128)(2,1)} %get-tuple-element.10), channel_id=1, source_target_pairs={{0,2},{2,0},{4,6},{6,4},{1,3},{3,1},{5,7},{7,5},{8,10},{10,8},{12,... | collective-permute-start | bytes 1867784 | tf_op jit(solution)/shard_map/ppermute | solution.py:364
  10.4 3.9 %all-to-all-start.1 = ((bf16[8,152,512]{2,1,0:T(8,128)(2,1)}), bf16[8,152,512]{2,1,0:T(8,128)(2,1)S(1)}, u32[]{:S(2)}, u32[]{:S(2)}) async-start(bf16[8,152,512]{2,1,0:T(8,128)(2,1)} %get-tuple-element.13), calls=%async_computation.1 | async-start | bytes 2490368 | tf_op jit(solution)/shard_map/all_to_all | solution.py:386
  14.2 0.0 copy-done.6
  14.2 2.0 %collective-permute-start.2 = (bf16[2,64,512]{2,1,0:T(8,128)(2,1)S(1)}, bf16[2,64,512]{2,1,0:T(8,128)(2,1)S(1)}, u32[]{:S(2)}, u32[]{:S(2)}) collective-permute-start(bf16[2,64,512]{2,1,0:T(8,128)(2,1)S(1)} %copy-done.6), channel_id=1, source_target_pairs={{1,0},{0,1},{3,2},{2,3},{5,4},{4,5},{7,6},{6,7},{9,8},{8,9},{11,10... | collective-permute-start | bytes 393224 | tf_op jit(solution)/shard_map/ppermute | solution.py:369
  16.2 0.0 collective-permute-done.8.refs_0_
  16.2 8.4 %collective-permute-start.9 = (bf16[608,512]{1,0:T(8,128)(2,1)S(1)}, bf16[608,512]{1,0:T(8,128)(2,1)}, u32[]{:S(2)}, u32[]{:S(2)}) collective-permute-start(bf16[608,512]{1,0:T(8,128)(2,1)S(1)} %collective-permute-done.8.refs_0_), channel_id=1, source_target_pairs={{0,2},{2,0},{4,6},{6,4},{1,3},{3,1},{5,7},{7,5},{8,10},{10,8},{12,... | collective-permute-start | bytes 1867784 | tf_op jit(solution)/shard_map/ppermute | solution.py:364
  24.7 0.0 collective-permute-done.refs_0_
  24.7 0.7 collective-permute-start.1
  25.4 2.9 %shard_map.109 = bf16[8,152,512]{2,1,0:T(8,128)(2,1)} custom-call(s32[90]{0:T(128)} %get-tuple-element.9.table, bf16[608,512]{1,0:T(8,128)(2,1)} %collective-permute-done.refs_0_), custom_call_target="tpu_custom_call" | custom-call | flops 10000000000 | tf_op jit(solution)/shard_map/pallas_call | solution.py:157
  28.3 0.0 copy-done.8
  28.3 3.0 %all-to-all-done.1.refs_0_ = bf16[8,152,512]{2,1,0:T(8,128)(2,1)S(1)} async-done(((bf16[8,152,512]{2,1,0:T(8,128)(2,1)}), bf16[8,152,512]{2,1,0:T(8,128)(2,1)S(1)}, u32[]{:S(2)}, u32[]{:S(2)}) %all-to-all-start.1) | async-done | bytes 1245216 | tf_op jit(solution)/shard_map/all_to_all | solution.py:386
  31.2 1.0 %copy-done.7 = bf16[8,152,512]{2,1,0:T(8,128)(2,1)} copy-done((bf16[8,152,512]{2,1,0:T(8,128)(2,1)}, bf16[8,152,512]{2,1,0:T(8,128)(2,1)S(1)}, u32[]{:S(2)}) %copy-start.7) | copy-done | bytes 1245208
  32.3 4.3 %all-to-all-start.2 = ((bf16[8,152,512]{2,1,0:T(8,128)(2,1)}), bf16[8,152,512]{2,1,0:T(8,128)(2,1)}, u32[]{:S(2)}, u32[]{:S(2)}) async-start(bf16[8,152,512]{2,1,0:T(8,128)(2,1)} %shard_map.109), calls=%async_computation.2 | async-start | bytes 2490368 | tf_op jit(solution)/shard_map/all_to_all | solution.py:386
  36.6 0.0 collective-permute-done.2.refs_1_
  36.6 0.0 collective-permute-done.1.after.refs_0_.refs_2_
  36.6 0.0 copy-start.4
  36.6 8.1 %collective-permute-start.5 = (bf16[2,2,64,512]{3,2,1,0:T(8,128)(2,1)S(1)}, bf16[2,2,64,512]{3,2,1,0:T(8,128)(2,1)S(1)}, u32[]{:S(2)}, u32[]{:S(2)}) collective-permute-start(bf16[2,2,64,512]{3,2,1,0:T(8,128)(2,1)S(1)} %shard_map.105.refs_0_.line), channel_id=1, source_target_pairs={{0,4},{6,2},{1,5},{7,3},{8,12},{14,10},{9,13},{15,11},{16,20},{22,... | collective-permute-start | bytes 786440 | tf_op jit(solution)/shard_map/ppermute | solution.py:364
  44.8 0.7 collective-permute-start.4
  45.4 3.1 %collective-permute-start.3 = (bf16[2,2,64,512]{3,2,1,0:T(8,128)(2,1)S(1)}, bf16[2,2,64,512]{3,2,1,0:T(8,128)(2,1)S(1)}, u32[]{:S(2)}, u32[]{:S(2)}) collective-permute-start(bf16[2,2,64,512]{3,2,1,0:T(8,128)(2,1)S(1)} %shard_map.105.refs_0_.line), channel_id=1, source_target_pairs={{0,2},{6,4},{1,3},{7,5},{8,10},{14,12},{9,11},{15,13},{16,18},{22,... | collective-permute-start | bytes 786440 | tf_op jit(solution)/shard_map/ppermute | solution.py:364
  48.5 0.0 copy-done.4
  48.5 0.1 collective-permute-start.6
  48.6 0.0 collective-permute-done.9.refs_1_
  48.6 2.9 %shard_map.110 = bf16[8,152,512]{2,1,0:T(8,128)(2,1)} custom-call(s32[90]{0:T(128)} %get-tuple-element.9.table, bf16[608,512]{1,0:T(8,128)(2,1)} %copy-done.8, bf16[608,512]{1,0:T(8,128)(2,1)} %collective-permute-done.9.refs_1_, bf16[608,512]{1,0:T(8,128)(2,1)} %copy-done.4), custom_call_target="tpu_custom_call" | custom-call | flops 10000000000 | tf_op jit(solution)/shard_map/pallas_call | solution.py:157
  51.5 2.1 %all-to-all-done.2.refs_1_ = bf16[8,152,512]{2,1,0:T(8,128)(2,1)} async-done(((bf16[8,152,512]{2,1,0:T(8,128)(2,1)}), bf16[8,152,512]{2,1,0:T(8,128)(2,1)}, u32[]{:S(2)}, u32[]{:S(2)}) %all-to-all-start.2) | async-done | bytes 1245216 | tf_op jit(solution)/shard_map/all_to_all | solution.py:386
  53.6 4.3 %all-to-all-start.3 = ((bf16[8,152,512]{2,1,0:T(8,128)(2,1)}), bf16[8,152,512]{2,1,0:T(8,128)(2,1)}, u32[]{:S(2)}, u32[]{:S(2)}) async-start(bf16[8,152,512]{2,1,0:T(8,128)(2,1)} %shard_map.110), calls=%async_computation.3 | async-start | bytes 2490368 | tf_op jit(solution)/shard_map/all_to_all | solution.py:386
  57.9 0.0 collective-permute-done.5.refs_2_.near3
  57.9 0.0 collective-permute-done.4.refs_1_.near2
  57.9 9.7 %collective-permute-done.6.after.refs_1_ = bf16[608,512]{1,0:T(8,128)(2,1)S(1)} collective-permute-done((bf16[608,512]{1,0:T(8,128)(2,1)S(1)}, bf16[608,512]{1,0:T(8,128)(2,1)S(1)}, u32[]{:S(2)}, u32[]{:S(2)}) %collective-permute-start.6) | collective-permute-done | bytes 622624 | tf_op jit(solution)/shard_map/ppermute | solution.py:364
  67.6 0.1 shard_map.106
  67.6 0.0 copy-start.5
  67.6 0.8 copy-done.5
  68.5 2.5 %collective-permute-start.7 = (bf16[3,2,2,64,512]{4,3,2,1,0:T(8,128)(2,1)S(1)}, bf16[3,2,2,64,512]{4,3,2,1,0:T(8,128)(2,1)S(1)}, u32[]{:S(2)}, u32[]{:S(2)}) collective-permute-start(bf16[3,2,2,64,512]{4,3,2,1,0:T(8,128)(2,1)S(1)} %shard_map.106), channel_id=1, source_target_pairs={{0,2},{2,0},{4,6},{6,4},{1,3},{3,1},{5,7},{7,5},{8,10},{10,8},{12,... | collective-permute-start | bytes 2359304 | tf_op jit(solution)/shard_map/ppermute | solution.py:364
  70.9 2.9 %shard_map.108 = bf16[8,152,512]{2,1,0:T(8,128)(2,1)} custom-call(s32[90]{0:T(128)} %get-tuple-element.9.table, bf16[608,512]{1,0:T(8,128)(2,1)} %copy-done.4, bf16[608,512]{1,0:T(8,128)(2,1)} %copy-done.5), custom_call_target="tpu_custom_call" | custom-call | flops 10000000000 | tf_op jit(solution)/shard_map/pallas_call | solution.py:157
  73.8 0.0 copy-start
  73.8 0.0 copy-start.3
  73.8 1.1 %all-to-all-done.3.refs_2_ = bf16[8,152,512]{2,1,0:T(8,128)(2,1)} async-done(((bf16[8,152,512]{2,1,0:T(8,128)(2,1)}), bf16[8,152,512]{2,1,0:T(8,128)(2,1)}, u32[]{:S(2)}, u32[]{:S(2)}) %all-to-all-start.3) | async-done | bytes 1245216 | tf_op jit(solution)/shard_map/all_to_all | solution.py:386
  74.9 4.3 %all-to-all-start = ((bf16[8,152,512]{2,1,0:T(8,128)(2,1)}), bf16[8,152,512]{2,1,0:T(8,128)(2,1)}, u32[]{:S(2)}, u32[]{:S(2)}) async-start(bf16[8,152,512]{2,1,0:T(8,128)(2,1)} %shard_map.108), calls=%async_computation | async-start | bytes 2490368 | tf_op jit(solution)/shard_map/all_to_all | solution.py:386
  79.2 0.0 collective-permute-done.3.near1
  79.2 7.2 %collective-permute-done.7.relayed = bf16[3,2,2,64,512]{4,3,2,1,0:T(8,128)(2,1)S(1)} collective-permute-done((bf16[3,2,2,64,512]{4,3,2,1,0:T(8,128)(2,1)S(1)}, bf16[3,2,2,64,512]{4,3,2,1,0:T(8,128)(2,1)S(1)}, u32[]{:S(2)}, u32[]{:S(2)}) %collective-permute-start.7) | collective-permute-done | bytes 786464 | tf_op jit(solution)/shard_map/ppermute | solution.py:364
  86.4 0.0 copy-done
  86.4 1.6 %shard_map.107 = (bf16[2,512,512]{2,1,0:T(8,128)(2,1)S(1)}, bf16[8,96,512]{2,1,0:T(8,128)(2,1)S(1)}) custom-call(s32[90]{0:T(128)S(1)} %copy-done.3, bf16[8,2,48,512]{3,2,1,0:T(8,128)(2,1)S(1)} %copy-done, bf16[2,2,64,512]{3,2,1,0:T(8,128)(2,1)S(1)} %shard_map.105.refs_0_.line, bf16[2,2,64,512]{3,2,1,0:T(8,128)(2,1)S(1)} %collective-permute-done.3.near1, ...), custom_call_target="tpu_custom_call" | custom-call | tf_op jit(solution)/shard_map/pallas_call | solution.py:216
  88.0 1.0 copy-done.1
  89.0 0.9 copy-done.2
  89.9 8.2 %shard_map.111 = (bf16[8,512,512]{2,1,0:T(8,128)(2,1)}, bf16[8,48,512]{2,1,0:T(8,128)(2,1)}) custom-call(s32[90]{0:T(128)} %get-tuple-element.9.table, bf16[8,512,512]{2,1,0:T(8,128)(2,1)} %near_tiles.3, bf16[8,2,48,512]{3,2,1,0:T(8,128)(2,1)} %far_tiles.5, bf16[2,512,512]{2,1,0:T(8,128)(2,1)} %copy-done.1, bf16[8,96,512]{2,1,0:T(8,128)(2,1)} %copy-done.2, ...), custom_call_target="tpu_custom_call" | custom-call | flops 8999999488 | tf_op jit(solution)/shard_map/pallas_call | solution.py:327
  98.1 0.0 all-to-all-done.refs_0_
  98.1 4.7 %shard_map.112 = (bf16[8,512,512]{2,1,0:T(8,128)(2,1)}, bf16[8,48,512]{2,1,0:T(8,128)(2,1)}) custom-call(s32[90]{0:T(128)} %get-tuple-element.9.table, bf16[8,512,512]{2,1,0:T(8,128)(2,1)} %near_tiles.3, bf16[8,2,48,512]{3,2,1,0:T(8,128)(2,1)} %far_tiles.5, bf16[2,512,512]{2,1,0:T(8,128)(2,1)} %copy-done.1, ...), custom_call_target="tpu_custom_call", output_to_operand_aliasing={{0}: (6, {}), {1}: (7, {})} | custom-call | flops 3000000000 | tf_op jit(solution)/shard_map/pallas_call | solution.py:327
  (7 shorter events, 0.0 us)
Async XLA Ops:
  3.8 12.5 %collective-permute-start.8 = (bf16[608,512]{1,0:T(8,128)(2,1)}, bf16[608,512]{1,0:T(8,128)(2,1)S(1)}, u32[]{:S(2)}, u32[]{:S(2)}) collective-permute-start(bf16[608,512]{1,0:T(8,128)(2,1)} %get-tuple-element.10), channel_id=1, source_target_pairs={{2,4},{4,2},{3,5},{5,3},{10,12},{12,10},{11,13},{13,11},{18,20},{2... | collective-permute-start | bytes 1867784 | tf_op jit(solution)/shard_map/ppermute | solution.py:364
  4.5 20.2 %collective-permute-start = (bf16[608,512]{1,0:T(8,128)(2,1)}, bf16[608,512]{1,0:T(8,128)(2,1)}, u32[]{:S(2)}, u32[]{:S(2)}) collective-permute-start(bf16[608,512]{1,0:T(8,128)(2,1)} %get-tuple-element.10), channel_id=1, source_target_pairs={{0,2},{2,0},{4,6},{6,4},{1,3},{3,1},{5,7},{7,5},{8,10},{10,8},{12,... | collective-permute-start | bytes 1867784 | tf_op jit(solution)/shard_map/ppermute | solution.py:364
  10.4 3.9 %copy-start.6 = (bf16[2,64,512]{2,1,0:T(8,128)(2,1)S(1)}, bf16[2,64,512]{2,1,0:T(8,128)(2,1)}, u32[]{:S(2)}) copy-start(bf16[2,64,512]{2,1,0:T(8,128)(2,1)} %refs_0_.1) | copy-start | bytes 393220
  10.4 20.9 %all-to-all-start.1 = ((bf16[8,152,512]{2,1,0:T(8,128)(2,1)}), bf16[8,152,512]{2,1,0:T(8,128)(2,1)S(1)}, u32[]{:S(2)}, u32[]{:S(2)}) async-start(bf16[8,152,512]{2,1,0:T(8,128)(2,1)} %get-tuple-element.13), calls=%async_computation.1 | async-start | bytes 2490368 | tf_op jit(solution)/shard_map/all_to_all | solution.py:386
  14.2 22.3 %collective-permute-start.2 = (bf16[2,64,512]{2,1,0:T(8,128)(2,1)S(1)}, bf16[2,64,512]{2,1,0:T(8,128)(2,1)S(1)}, u32[]{:S(2)}, u32[]{:S(2)}) collective-permute-start(bf16[2,64,512]{2,1,0:T(8,128)(2,1)S(1)} %copy-done.6), channel_id=1, source_target_pairs={{1,0},{0,1},{3,2},{2,3},{5,4},{4,5},{7,6},{6,7},{9,8},{8,9},{11,10... | collective-permute-start | bytes 393224 | tf_op jit(solution)/shard_map/ppermute | solution.py:369
  16.2 12.0 %copy-start.8 = (bf16[608,512]{1,0:T(8,128)(2,1)}, bf16[608,512]{1,0:T(8,128)(2,1)S(1)}, u32[]{:S(2)}) copy-start(bf16[608,512]{1,0:T(8,128)(2,1)S(1)} %collective-permute-done.8.refs_0_) | copy-start | bytes 1867780
  16.2 32.4 %collective-permute-start.9 = (bf16[608,512]{1,0:T(8,128)(2,1)S(1)}, bf16[608,512]{1,0:T(8,128)(2,1)}, u32[]{:S(2)}, u32[]{:S(2)}) collective-permute-start(bf16[608,512]{1,0:T(8,128)(2,1)S(1)} %collective-permute-done.8.refs_0_), channel_id=1, source_target_pairs={{0,2},{2,0},{4,6},{6,4},{1,3},{3,1},{5,7},{7,5},{8,10},{10,8},{12,... | collective-permute-start | bytes 1867784 | tf_op jit(solution)/shard_map/ppermute | solution.py:364
  24.7 11.9 %collective-permute-start.1 = (bf16[608,512]{1,0:T(8,128)(2,1)}, bf16[608,512]{1,0:T(8,128)(2,1)S(1)}, u32[]{:S(2)}, u32[]{:S(2)}) collective-permute-start(bf16[608,512]{1,0:T(8,128)(2,1)} %collective-permute-done.refs_0_), channel_id=1, source_target_pairs={{2,4},{4,2},{3,5},{5,3},{10,12},{12,10},{11,13},{13,11},{18,20},{2... | collective-permute-start | bytes 1867784 | tf_op jit(solution)/shard_map/ppermute | solution.py:364
  31.2 1.0 %copy-start.7 = (bf16[8,152,512]{2,1,0:T(8,128)(2,1)}, bf16[8,152,512]{2,1,0:T(8,128)(2,1)S(1)}, u32[]{:S(2)}) copy-start(bf16[8,152,512]{2,1,0:T(8,128)(2,1)S(1)} %all-to-all-done.1.refs_0_) | copy-start | bytes 3735556
  32.3 21.3 %all-to-all-start.2 = ((bf16[8,152,512]{2,1,0:T(8,128)(2,1)}), bf16[8,152,512]{2,1,0:T(8,128)(2,1)}, u32[]{:S(2)}, u32[]{:S(2)}) async-start(bf16[8,152,512]{2,1,0:T(8,128)(2,1)} %shard_map.109), calls=%async_computation.2 | async-start | bytes 2490368 | tf_op jit(solution)/shard_map/all_to_all | solution.py:386
  36.6 12.0 %copy-start.4 = (bf16[608,512]{1,0:T(8,128)(2,1)}, bf16[608,512]{1,0:T(8,128)(2,1)S(1)}, u32[]{:S(2)}) copy-start(bf16[608,512]{1,0:T(8,128)(2,1)S(1)} %collective-permute-done.1.after.refs_0_.refs_2_) | copy-start | bytes 1867780
  36.6 21.3 %collective-permute-start.5 = (bf16[2,2,64,512]{3,2,1,0:T(8,128)(2,1)S(1)}, bf16[2,2,64,512]{3,2,1,0:T(8,128)(2,1)S(1)}, u32[]{:S(2)}, u32[]{:S(2)}) collective-permute-start(bf16[2,2,64,512]{3,2,1,0:T(8,128)(2,1)S(1)} %shard_map.105.refs_0_.line), channel_id=1, source_target_pairs={{0,4},{6,2},{1,5},{7,3},{8,12},{14,10},{9,13},{15,11},{16,20},{22,... | collective-permute-start | bytes 786440 | tf_op jit(solution)/shard_map/ppermute | solution.py:364
  44.8 13.1 %collective-permute-start.4 = (bf16[2,2,64,512]{3,2,1,0:T(8,128)(2,1)S(1)}, bf16[2,2,64,512]{3,2,1,0:T(8,128)(2,1)S(1)}, u32[]{:S(2)}, u32[]{:S(2)}) collective-permute-start(bf16[2,2,64,512]{3,2,1,0:T(8,128)(2,1)S(1)} %shard_map.105.refs_0_.line), channel_id=1, source_target_pairs={{2,4},{4,2},{3,5},{5,3},{10,12},{12,10},{11,13},{13,11},{18,20},{2... | collective-permute-start | bytes 786440 | tf_op jit(solution)/shard_map/ppermute | solution.py:364
  45.4 33.8 %collective-permute-start.3 = (bf16[2,2,64,512]{3,2,1,0:T(8,128)(2,1)S(1)}, bf16[2,2,64,512]{3,2,1,0:T(8,128)(2,1)S(1)}, u32[]{:S(2)}, u32[]{:S(2)}) collective-permute-start(bf16[2,2,64,512]{3,2,1,0:T(8,128)(2,1)S(1)} %shard_map.105.refs_0_.line), channel_id=1, source_target_pairs={{0,2},{6,4},{1,3},{7,5},{8,10},{14,12},{9,11},{15,13},{16,18},{22,... | collective-permute-start | bytes 786440 | tf_op jit(solution)/shard_map/ppermute | solution.py:364
  48.5 19.0 %collective-permute-start.6 = (bf16[608,512]{1,0:T(8,128)(2,1)S(1)}, bf16[608,512]{1,0:T(8,128)(2,1)S(1)}, u32[]{:S(2)}, u32[]{:S(2)}) collective-permute-start(bf16[608,512]{1,0:T(8,128)(2,1)S(1)} %collective-permute-done.1.after.refs_0_.refs_2_), channel_id=1, source_target_pairs={{0,2},{2,0},{4,6},{6,4},{1,3},{3,1},{5,7},{7,5},{8,10},{10,8},{12,... | collective-permute-start | bytes 1867784 | tf_op jit(solution)/shard_map/ppermute | solution.py:364
  53.6 21.3 %all-to-all-start.3 = ((bf16[8,152,512]{2,1,0:T(8,128)(2,1)}), bf16[8,152,512]{2,1,0:T(8,128)(2,1)}, u32[]{:S(2)}, u32[]{:S(2)}) async-start(bf16[8,152,512]{2,1,0:T(8,128)(2,1)} %shard_map.110), calls=%async_computation.3 | async-start | bytes 2490368 | tf_op jit(solution)/shard_map/all_to_all | solution.py:386
  67.6 0.8 copy-start.5
  68.5 18.0 %collective-permute-start.7 = (bf16[3,2,2,64,512]{4,3,2,1,0:T(8,128)(2,1)S(1)}, bf16[3,2,2,64,512]{4,3,2,1,0:T(8,128)(2,1)S(1)}, u32[]{:S(2)}, u32[]{:S(2)}) collective-permute-start(bf16[3,2,2,64,512]{4,3,2,1,0:T(8,128)(2,1)S(1)} %shard_map.106), channel_id=1, source_target_pairs={{0,2},{2,0},{4,6},{6,4},{1,3},{3,1},{5,7},{7,5},{8,10},{10,8},{12,... | collective-permute-start | bytes 2359304 | tf_op jit(solution)/shard_map/ppermute | solution.py:364
  73.8 12.6 %copy-start = (bf16[8,2,48,512]{3,2,1,0:T(8,128)(2,1)S(1)}, bf16[8,2,48,512]{3,2,1,0:T(8,128)(2,1)}, u32[]{:S(2)}) copy-start(bf16[8,2,48,512]{3,2,1,0:T(8,128)(2,1)} %far_tiles.5) | copy-start | bytes 2359300
  73.8 12.6 %copy-start.3 = (s32[90]{0:T(128)S(1)}, s32[90]{0:T(128)}, u32[]{:S(2)}) copy-start(s32[90]{0:T(128)} %get-tuple-element.9.table) | copy-start | bytes 1084
  74.9 23.2 %all-to-all-start = ((bf16[8,152,512]{2,1,0:T(8,128)(2,1)}), bf16[8,152,512]{2,1,0:T(8,128)(2,1)}, u32[]{:S(2)}, u32[]{:S(2)}) async-start(bf16[8,152,512]{2,1,0:T(8,128)(2,1)} %shard_map.108), calls=%async_computation | async-start | bytes 2490368 | tf_op jit(solution)/shard_map/all_to_all | solution.py:386
  88.0 1.0 copy-start.1
  89.0 0.9 copy-start.2

commit v9 on v8

--- a/solution.py
+++ b/solution.py
@@ -19,7 +19,8 @@
 CHUNK_OWNER = ((0, 1, 2, 3), (1, 0, 3, 2), (2, 2, 1, 1), (3, 3, 0, 0))
 CHUNK_SOURCE = ((0, 0, 0, 0), (0, 0, 0, 0), (1, 0, 0, 1), (1, 0, 0, 1))
 CHUNK_SOURCES = (("own",), ("pair",), ("middle", "pass2"), ("cross", "pass3"))
-PACK_FLOPS = 10**10
+PACK_FLOPS = (0, 5 * 10**9, 10**10, 10**10)
+JOIN_FLOPS = 10**9
 UPDATE_FLOPS = 3 * 10**9
 VMEM = pl.BlockSpec(memory_space=pltpu.VMEM)
 SMEM = pl.BlockSpec(memory_space=pltpu.SMEM)
@@ -162,7 +163,7 @@
         scratch_shapes=pack_scratch(sizes, order)
         + [pltpu.VMEM(sources[0].shape, jnp.bfloat16), pltpu.SemaphoreType.DMA((1,))],
         compiler_params=pltpu.CompilerParams(vmem_limit_bytes=WIDE_VMEM),
-        cost_estimate=pl.CostEstimate(flops=PACK_FLOPS, bytes_accessed=0, transcendentals=0),
+        cost_estimate=pl.CostEstimate(flops=PACK_FLOPS[n], bytes_accessed=0, transcendentals=0),
     )(table, *sources, *after)
 
 
@@ -178,7 +179,7 @@
         out_specs=VMEM,
         out_shape=jax.ShapeDtypeStruct((len(parts),) + parts[0].shape, jnp.bfloat16),
         compiler_params=pltpu.CompilerParams(vmem_limit_bytes=VMEM_LIMIT),
-        cost_estimate=pl.CostEstimate(flops=PACK_FLOPS, bytes_accessed=0, transcendentals=0),
+        cost_estimate=pl.CostEstimate(flops=JOIN_FLOPS, bytes_accessed=0, transcendentals=0),
     )(after, *parts)
 
 

time: 103 us -> 101 us (0.981)
  starting transfers between devices: 48.8 us -> 40.8 us
  waiting for transfers between devices: 23 us -> 29 us
    all_to_all x4, waiting for transfers between devices: 6.15 us -> 13.7 us  [shards(): lax.all_to_all(send, PLANE, split_axis=0, concat_axis=0, tiled=True)]
    ppermute x9, starting transfers between devices: 30.1 us -> 22.6 us  [along(): return lax.ppermute(value, 'outer', pairs)]
    ppermute x9, waiting for transfers between devices: 16.9 us -> 15.2 us  [along(): return lax.ppermute(value, 'outer', pairs)]
  transfers between devices with their start and end apart: 14 -> 14, of which waited for: 5 -> 4; matrix products, arithmetic and copies ran while one was open for 0% -> 0% of each run, Pallas kernels for 18% -> 18%
where the time goes in v9:
time: 101 us
  starting transfers between devices  40.8 us (40%)
  waiting for transfers between devices  29 us (29%)
  Pallas kernels  26.3 us (26%)
  local copies, waits for them, and re-layouts  3.78 us (4%)
    ppermute x9, starting transfers between devices, along(): return lax.ppermute(value, 'outer', pairs)  22.6 us
    all_to_all x4, starting transfers between devices, shards(): lax.all_to_all(send, PLANE, split_axis=0, concat_axis=0, tiled=True)  16.7 us
    ppermute x9, waiting for transfers between devices, along(): return lax.ppermute(value, 'outer', pairs)  15.2 us
    all_to_all x4, waiting for transfers between devices, shards(): lax.all_to_all(send, PLANE, split_axis=0, concat_axis=0, tiled=True)  13.7 us
    pallas_call x2, Pallas kernels, update(): pl.pallas_call(functools.partial(update_kernel, sizes, chunks), in_specs=...  12.9 us
    pallas_call x3, Pallas kernels, pack(): pl.pallas_call(functools.partial(pack_kernel, sizes, n), in_specs=[SMEM]...  8.6 us
    unnamed x18, local copies, waits for them, and re-layouts  3.78 us
    pallas_call x1, Pallas kernels, first(): pl.pallas_call(functools.partial(first_kernel, sizes), in_specs=[SMEM] *...  3.13 us
  transfers between devices with their start and end apart: 14, of which 4 were waited for; matrix products, arithmetic and copies ran while one was open for 0% of the time, Pallas kernels for 18%

profile of v9, /device:TPU:0, one launch (start us, length us, event | category | flops | bytes accessed | tf_op | source)
XLA Modules:
  0.0 100.7 jit_solution(4011999304189607089)
XLA Ops:
  0.6 3.1 %shard_map.104 = (s32[90]{0:T(128)}, bf16[608,512]{1,0:T(8,128)(2,1)}, bf16[8,152,512]{2,1,0:T(8,128)(2,1)}) custom-call(s32[8,32]{1,0:T(8,128)} %bitcast.4, s32[8,32]{1,0:T(8,128)} %bitcast.5, s32[1,8]{1,0:T(1,128)} %near_rows.1, s32[1,8]{1,0:T(1,128)} %far_rows.1, bf16[4,128,512]{2,1,0:T(8,128)(2,1)} %near.1, bf16[4,12,2,512]{3,2,1,0:T(2,128)(2,1)} %bitcast.3), custom_call_target="tpu_custom_call" | custom-call | tf_op jit(solution)/shard_map/pallas_call | solution.py:128
  3.8 3.1 %collective-permute-start = (bf16[608,512]{1,0:T(8,128)(2,1)}, bf16[608,512]{1,0:T(8,128)(2,1)}, u32[]{:S(2)}, u32[]{:S(2)}) collective-permute-start(bf16[608,512]{1,0:T(8,128)(2,1)} %get-tuple-element.10), channel_id=1, source_target_pairs={{0,2},{2,0},{4,6},{6,4},{1,3},{3,1},{5,7},{7,5},{8,10},{10,8},{12,... | collective-permute-start | bytes 1867784 | tf_op jit(solution)/shard_map/ppermute | solution.py:365
  6.9 0.7 collective-permute-start.8
  7.6 0.0 copy-start.6
  7.6 3.9 %all-to-all-start.1 = ((bf16[8,152,512]{2,1,0:T(8,128)(2,1)}), bf16[8,152,512]{2,1,0:T(8,128)(2,1)S(1)}, u32[]{:S(2)}, u32[]{:S(2)}) async-start(bf16[8,152,512]{2,1,0:T(8,128)(2,1)} %get-tuple-element.13), calls=%async_computation.1 | async-start | bytes 2490368 | tf_op jit(solution)/shard_map/all_to_all | solution.py:387
  11.4 9.8 %collective-permute-done.refs_0_ = bf16[608,512]{1,0:T(8,128)(2,1)} collective-permute-done((bf16[608,512]{1,0:T(8,128)(2,1)}, bf16[608,512]{1,0:T(8,128)(2,1)}, u32[]{:S(2)}, u32[]{:S(2)}) %collective-permute-start) | collective-permute-done | bytes 622624 | tf_op jit(solution)/shard_map/ppermute | solution.py:365
  21.2 0.7 collective-permute-start.1
  21.9 0.0 collective-permute-done.8.refs_0_
  21.9 0.0 copy-start.8
  21.9 4.6 %collective-permute-start.9 = (bf16[608,512]{1,0:T(8,128)(2,1)S(1)}, bf16[608,512]{1,0:T(8,128)(2,1)}, u32[]{:S(2)}, u32[]{:S(2)}) collective-permute-start(bf16[608,512]{1,0:T(8,128)(2,1)S(1)} %collective-permute-done.8.refs_0_), channel_id=1, source_target_pairs={{0,2},{2,0},{4,6},{6,4},{1,3},{3,1},{5,7},{7,5},{8,10},{10,8},{12,... | collective-permute-start | bytes 1867784 | tf_op jit(solution)/shard_map/ppermute | solution.py:365
  26.5 0.0 copy-done.6
  26.5 1.5 %collective-permute-start.2 = (bf16[2,64,512]{2,1,0:T(8,128)(2,1)S(1)}, bf16[2,64,512]{2,1,0:T(8,128)(2,1)S(1)}, u32[]{:S(2)}, u32[]{:S(2)}) collective-permute-start(bf16[2,64,512]{2,1,0:T(8,128)(2,1)S(1)} %copy-done.6), channel_id=1, source_target_pairs={{1,0},{0,1},{3,2},{2,3},{5,4},{4,5},{7,6},{6,7},{9,8},{8,9},{11,10... | collective-permute-start | bytes 393224 | tf_op jit(solution)/shard_map/ppermute | solution.py:370
  28.0 2.9 %shard_map.109 = bf16[8,152,512]{2,1,0:T(8,128)(2,1)} custom-call(s32[90]{0:T(128)} %get-tuple-element.9.table, bf16[608,512]{1,0:T(8,128)(2,1)} %collective-permute-done.refs_0_), custom_call_target="tpu_custom_call" | custom-call | flops 5000000000 | tf_op jit(solution)/shard_map/pallas_call | solution.py:158
  30.9 0.0 copy-done.8
  30.9 0.0 all-to-all-done.1.refs_0_
  30.9 0.0 copy-start.7
  30.9 1.0 %copy-done.7 = bf16[8,152,512]{2,1,0:T(8,128)(2,1)} copy-done((bf16[8,152,512]{2,1,0:T(8,128)(2,1)}, bf16[8,152,512]{2,1,0:T(8,128)(2,1)S(1)}, u32[]{:S(2)}) %copy-start.7) | copy-done | bytes 1245208
  31.9 4.3 %all-to-all-start.2 = ((bf16[8,152,512]{2,1,0:T(8,128)(2,1)}), bf16[8,152,512]{2,1,0:T(8,128)(2,1)}, u32[]{:S(2)}, u32[]{:S(2)}) async-start(bf16[8,152,512]{2,1,0:T(8,128)(2,1)} %shard_map.109), calls=%async_computation.2 | async-start | bytes 2490368 | tf_op jit(solution)/shard_map/all_to_all | solution.py:387
  36.2 0.0 collective-permute-done.2.refs_1_
  36.2 0.0 collective-permute-done.1.after.refs_0_.refs_2_
  36.3 6.6 %collective-permute-start.5 = (bf16[2,2,64,512]{3,2,1,0:T(8,128)(2,1)S(1)}, bf16[2,2,64,512]{3,2,1,0:T(8,128)(2,1)S(1)}, u32[]{:S(2)}, u32[]{:S(2)}) collective-permute-start(bf16[2,2,64,512]{3,2,1,0:T(8,128)(2,1)S(1)} %shard_map.105.refs_0_.line), channel_id=1, source_target_pairs={{0,4},{6,2},{1,5},{7,3},{8,12},{14,10},{9,13},{15,11},{16,20},{22,... | collective-permute-start | bytes 786440 | tf_op jit(solution)/shard_map/ppermute | solution.py:365
  42.9 0.7 collective-permute-start.4
  43.6 1.2 %collective-permute-start.6 = (bf16[608,512]{1,0:T(8,128)(2,1)S(1)}, bf16[608,512]{1,0:T(8,128)(2,1)S(1)}, u32[]{:S(2)}, u32[]{:S(2)}) collective-permute-start(bf16[608,512]{1,0:T(8,128)(2,1)S(1)} %collective-permute-done.1.after.refs_0_.refs_2_), channel_id=1, source_target_pairs={{0,2},{2,0},{4,6},{6,4},{1,3},{3,1},{5,7},{7,5},{8,10},{10,8},{12,... | collective-permute-start | bytes 1867784 | tf_op jit(solution)/shard_map/ppermute | solution.py:365
  44.8 0.0 collective-permute-done.9.refs_1_
  44.8 2.9 %shard_map.110 = bf16[8,152,512]{2,1,0:T(8,128)(2,1)} custom-call(s32[90]{0:T(128)} %get-tuple-element.9.table, bf16[608,512]{1,0:T(8,128)(2,1)} %copy-done.8, bf16[608,512]{1,0:T(8,128)(2,1)} %collective-permute-done.9.refs_1_, bf16[608,512]{1,0:T(8,128)(2,1)} %copy-done.4), custom_call_target="tpu_custom_call" | custom-call | flops 10000000000 | tf_op jit(solution)/shard_map/pallas_call | solution.py:158
  47.7 5.6 %all-to-all-done.2.refs_1_ = bf16[8,152,512]{2,1,0:T(8,128)(2,1)} async-done(((bf16[8,152,512]{2,1,0:T(8,128)(2,1)}), bf16[8,152,512]{2,1,0:T(8,128)(2,1)}, u32[]{:S(2)}, u32[]{:S(2)}) %all-to-all-start.2) | async-done | bytes 1245216 | tf_op jit(solution)/shard_map/all_to_all | solution.py:387
  53.3 4.3 %all-to-all-start.3 = ((bf16[8,152,512]{2,1,0:T(8,128)(2,1)}), bf16[8,152,512]{2,1,0:T(8,128)(2,1)}, u32[]{:S(2)}, u32[]{:S(2)}) async-start(bf16[8,152,512]{2,1,0:T(8,128)(2,1)} %shard_map.110), calls=%async_computation.3 | async-start | bytes 2490368 | tf_op jit(solution)/shard_map/all_to_all | solution.py:387
  57.5 3.9 %collective-permute-start.3 = (bf16[2,2,64,512]{3,2,1,0:T(8,128)(2,1)S(1)}, bf16[2,2,64,512]{3,2,1,0:T(8,128)(2,1)S(1)}, u32[]{:S(2)}, u32[]{:S(2)}) collective-permute-start(bf16[2,2,64,512]{3,2,1,0:T(8,128)(2,1)S(1)} %shard_map.105.refs_0_.line), channel_id=1, source_target_pairs={{0,2},{6,4},{1,3},{7,5},{8,10},{14,12},{9,11},{15,13},{16,18},{22,... | collective-permute-start | bytes 786440 | tf_op jit(solution)/shard_map/ppermute | solution.py:365
  61.4 0.0 collective-permute-done.5.refs_2_.near3
  61.4 0.0 collective-permute-done.4.refs_1_.near2
  61.4 0.0 collective-permute-done.6.after.refs_1_
  61.4 0.1 shard_map.106
  61.5 0.8 copy-done.5
  62.3 1.2 %collective-permute-start.7 = (bf16[3,2,2,64,512]{4,3,2,1,0:T(8,128)(2,1)S(1)}, bf16[3,2,2,64,512]{4,3,2,1,0:T(8,128)(2,1)S(1)}, u32[]{:S(2)}, u32[]{:S(2)}) collective-permute-start(bf16[3,2,2,64,512]{4,3,2,1,0:T(8,128)(2,1)S(1)} %shard_map.106), channel_id=1, source_target_pairs={{0,2},{2,0},{4,6},{6,4},{1,3},{3,1},{5,7},{7,5},{8,10},{10,8},{12,... | collective-permute-start | bytes 2359304 | tf_op jit(solution)/shard_map/ppermute | solution.py:365
  63.5 2.9 %shard_map.108 = bf16[8,152,512]{2,1,0:T(8,128)(2,1)} custom-call(s32[90]{0:T(128)} %get-tuple-element.9.table, bf16[608,512]{1,0:T(8,128)(2,1)} %copy-done.4, bf16[608,512]{1,0:T(8,128)(2,1)} %copy-done.5), custom_call_target="tpu_custom_call" | custom-call | flops 10000000000 | tf_op jit(solution)/shard_map/pallas_call | solution.py:158
  66.4 0.0 copy-start
  66.4 0.0 copy-start.3
  66.4 8.2 %all-to-all-done.3.refs_2_ = bf16[8,152,512]{2,1,0:T(8,128)(2,1)} async-done(((bf16[8,152,512]{2,1,0:T(8,128)(2,1)}), bf16[8,152,512]{2,1,0:T(8,128)(2,1)}, u32[]{:S(2)}, u32[]{:S(2)}) %all-to-all-start.3) | async-done | bytes 1245216 | tf_op jit(solution)/shard_map/all_to_all | solution.py:387
  74.6 4.3 %all-to-all-start = ((bf16[8,152,512]{2,1,0:T(8,128)(2,1)}), bf16[8,152,512]{2,1,0:T(8,128)(2,1)}, u32[]{:S(2)}, u32[]{:S(2)}) async-start(bf16[8,152,512]{2,1,0:T(8,128)(2,1)} %shard_map.108), calls=%async_computation | async-start | bytes 2490368 | tf_op jit(solution)/shard_map/all_to_all | solution.py:387
  78.9 0.0 collective-permute-done.3.near1
  78.9 5.4 %collective-permute-done.7.relayed = bf16[3,2,2,64,512]{4,3,2,1,0:T(8,128)(2,1)S(1)} collective-permute-done((bf16[3,2,2,64,512]{4,3,2,1,0:T(8,128)(2,1)S(1)}, bf16[3,2,2,64,512]{4,3,2,1,0:T(8,128)(2,1)S(1)}, u32[]{:S(2)}, u32[]{:S(2)}) %collective-permute-start.7) | collective-permute-done | bytes 786464 | tf_op jit(solution)/shard_map/ppermute | solution.py:365
  84.3 1.6 %shard_map.107 = (bf16[2,512,512]{2,1,0:T(8,128)(2,1)S(1)}, bf16[8,96,512]{2,1,0:T(8,128)(2,1)S(1)}) custom-call(s32[90]{0:T(128)S(1)} %copy-done.3, bf16[8,2,48,512]{3,2,1,0:T(8,128)(2,1)S(1)} %copy-done, bf16[2,2,64,512]{3,2,1,0:T(8,128)(2,1)S(1)} %shard_map.105.refs_0_.line, bf16[2,2,64,512]{3,2,1,0:T(8,128)(2,1)S(1)} %collective-permute-done.3.near1, ...), custom_call_target="tpu_custom_call" | custom-call | tf_op jit(solution)/shard_map/pallas_call | solution.py:217
  85.9 0.0 copy-start.1
  85.9 1.0 copy-done.1
  86.9 0.9 copy-done.2
  87.8 8.2 %shard_map.111 = (bf16[8,512,512]{2,1,0:T(8,128)(2,1)}, bf16[8,48,512]{2,1,0:T(8,128)(2,1)}) custom-call(s32[90]{0:T(128)} %get-tuple-element.9.table, bf16[8,512,512]{2,1,0:T(8,128)(2,1)} %near_tiles.3, bf16[8,2,48,512]{3,2,1,0:T(8,128)(2,1)} %far_tiles.5, bf16[2,512,512]{2,1,0:T(8,128)(2,1)} %copy-done.1, bf16[8,96,512]{2,1,0:T(8,128)(2,1)} %copy-done.2, ...), custom_call_target="tpu_custom_call" | custom-call | flops 8999999488 | tf_op jit(solution)/shard_map/pallas_call | solution.py:328
  96.0 0.0 all-to-all-done.refs_0_
  96.0 4.7 %shard_map.112 = (bf16[8,512,512]{2,1,0:T(8,128)(2,1)}, bf16[8,48,512]{2,1,0:T(8,128)(2,1)}) custom-call(s32[90]{0:T(128)} %get-tuple-element.9.table, bf16[8,512,512]{2,1,0:T(8,128)(2,1)} %near_tiles.3, bf16[8,2,48,512]{3,2,1,0:T(8,128)(2,1)} %far_tiles.5, bf16[2,512,512]{2,1,0:T(8,128)(2,1)} %copy-done.1, ...), custom_call_target="tpu_custom_call", output_to_operand_aliasing={{0}: (6, {}), {1}: (7, {})} | custom-call | flops 3000000000 | tf_op jit(solution)/shard_map/pallas_call | solution.py:328
  (7 shorter events, 0.0 us)
Async XLA Ops:
  3.8 17.4 %collective-permute-start = (bf16[608,512]{1,0:T(8,128)(2,1)}, bf16[608,512]{1,0:T(8,128)(2,1)}, u32[]{:S(2)}, u32[]{:S(2)}) collective-permute-start(bf16[608,512]{1,0:T(8,128)(2,1)} %get-tuple-element.10), channel_id=1, source_target_pairs={{0,2},{2,0},{4,6},{6,4},{1,3},{3,1},{5,7},{7,5},{8,10},{10,8},{12,... | collective-permute-start | bytes 1867784 | tf_op jit(solution)/shard_map/ppermute | solution.py:365
  6.9 15.0 %collective-permute-start.8 = (bf16[608,512]{1,0:T(8,128)(2,1)}, bf16[608,512]{1,0:T(8,128)(2,1)S(1)}, u32[]{:S(2)}, u32[]{:S(2)}) collective-permute-start(bf16[608,512]{1,0:T(8,128)(2,1)} %get-tuple-element.10), channel_id=1, source_target_pairs={{2,4},{4,2},{3,5},{5,3},{10,12},{12,10},{11,13},{13,11},{18,20},{2... | collective-permute-start | bytes 1867784 | tf_op jit(solution)/shard_map/ppermute | solution.py:365
  7.6 19.0 %copy-start.6 = (bf16[2,64,512]{2,1,0:T(8,128)(2,1)S(1)}, bf16[2,64,512]{2,1,0:T(8,128)(2,1)}, u32[]{:S(2)}) copy-start(bf16[2,64,512]{2,1,0:T(8,128)(2,1)} %refs_0_.1) | copy-start | bytes 393220
  7.6 23.3 %all-to-all-start.1 = ((bf16[8,152,512]{2,1,0:T(8,128)(2,1)}), bf16[8,152,512]{2,1,0:T(8,128)(2,1)S(1)}, u32[]{:S(2)}, u32[]{:S(2)}) async-start(bf16[8,152,512]{2,1,0:T(8,128)(2,1)} %get-tuple-element.13), calls=%async_computation.1 | async-start | bytes 2490368 | tf_op jit(solution)/shard_map/all_to_all | solution.py:387
  21.2 15.0 %collective-permute-start.1 = (bf16[608,512]{1,0:T(8,128)(2,1)}, bf16[608,512]{1,0:T(8,128)(2,1)S(1)}, u32[]{:S(2)}, u32[]{:S(2)}) collective-permute-start(bf16[608,512]{1,0:T(8,128)(2,1)} %collective-permute-done.refs_0_), channel_id=1, source_target_pairs={{2,4},{4,2},{3,5},{5,3},{10,12},{12,10},{11,13},{13,11},{18,20},{2... | collective-permute-start | bytes 1867784 | tf_op jit(solution)/shard_map/ppermute | solution.py:365
  21.9 9.0 %copy-start.8 = (bf16[608,512]{1,0:T(8,128)(2,1)}, bf16[608,512]{1,0:T(8,128)(2,1)S(1)}, u32[]{:S(2)}) copy-start(bf16[608,512]{1,0:T(8,128)(2,1)S(1)} %collective-permute-done.8.refs_0_) | copy-start | bytes 1867780
  21.9 22.9 %collective-permute-start.9 = (bf16[608,512]{1,0:T(8,128)(2,1)S(1)}, bf16[608,512]{1,0:T(8,128)(2,1)}, u32[]{:S(2)}, u32[]{:S(2)}) collective-permute-start(bf16[608,512]{1,0:T(8,128)(2,1)S(1)} %collective-permute-done.8.refs_0_), channel_id=1, source_target_pairs={{0,2},{2,0},{4,6},{6,4},{1,3},{3,1},{5,7},{7,5},{8,10},{10,8},{12,... | collective-permute-start | bytes 1867784 | tf_op jit(solution)/shard_map/ppermute | solution.py:365
  26.5 9.7 %collective-permute-start.2 = (bf16[2,64,512]{2,1,0:T(8,128)(2,1)S(1)}, bf16[2,64,512]{2,1,0:T(8,128)(2,1)S(1)}, u32[]{:S(2)}, u32[]{:S(2)}) collective-permute-start(bf16[2,64,512]{2,1,0:T(8,128)(2,1)S(1)} %copy-done.6), channel_id=1, source_target_pairs={{1,0},{0,1},{3,2},{2,3},{5,4},{4,5},{7,6},{6,7},{9,8},{8,9},{11,10... | collective-permute-start | bytes 393224 | tf_op jit(solution)/shard_map/ppermute | solution.py:370
  30.9 1.0 %copy-start.7 = (bf16[8,152,512]{2,1,0:T(8,128)(2,1)}, bf16[8,152,512]{2,1,0:T(8,128)(2,1)S(1)}, u32[]{:S(2)}) copy-start(bf16[8,152,512]{2,1,0:T(8,128)(2,1)S(1)} %all-to-all-done.1.refs_0_) | copy-start | bytes 3735556
  31.9 21.3 %all-to-all-start.2 = ((bf16[8,152,512]{2,1,0:T(8,128)(2,1)}), bf16[8,152,512]{2,1,0:T(8,128)(2,1)}, u32[]{:S(2)}, u32[]{:S(2)}) async-start(bf16[8,152,512]{2,1,0:T(8,128)(2,1)} %shard_map.109), calls=%async_computation.2 | async-start | bytes 2490368 | tf_op jit(solution)/shard_map/all_to_all | solution.py:387
  36.2 7.3 %copy-start.4 = (bf16[608,512]{1,0:T(8,128)(2,1)}, bf16[608,512]{1,0:T(8,128)(2,1)S(1)}, u32[]{:S(2)}) copy-start(bf16[608,512]{1,0:T(8,128)(2,1)S(1)} %collective-permute-done.1.after.refs_0_.refs_2_) | copy-start | bytes 1867780
  36.3 25.1 %collective-permute-start.5 = (bf16[2,2,64,512]{3,2,1,0:T(8,128)(2,1)S(1)}, bf16[2,2,64,512]{3,2,1,0:T(8,128)(2,1)S(1)}, u32[]{:S(2)}, u32[]{:S(2)}) collective-permute-start(bf16[2,2,64,512]{3,2,1,0:T(8,128)(2,1)S(1)} %shard_map.105.refs_0_.line), channel_id=1, source_target_pairs={{0,4},{6,2},{1,5},{7,3},{8,12},{14,10},{9,13},{15,11},{16,20},{22,... | collective-permute-start | bytes 786440 | tf_op jit(solution)/shard_map/ppermute | solution.py:365
  42.9 18.5 %collective-permute-start.4 = (bf16[2,2,64,512]{3,2,1,0:T(8,128)(2,1)S(1)}, bf16[2,2,64,512]{3,2,1,0:T(8,128)(2,1)S(1)}, u32[]{:S(2)}, u32[]{:S(2)}) collective-permute-start(bf16[2,2,64,512]{3,2,1,0:T(8,128)(2,1)S(1)} %shard_map.105.refs_0_.line), channel_id=1, source_target_pairs={{2,4},{4,2},{3,5},{5,3},{10,12},{12,10},{11,13},{13,11},{18,20},{2... | collective-permute-start | bytes 786440 | tf_op jit(solution)/shard_map/ppermute | solution.py:365
  43.6 17.8 %collective-permute-start.6 = (bf16[608,512]{1,0:T(8,128)(2,1)S(1)}, bf16[608,512]{1,0:T(8,128)(2,1)S(1)}, u32[]{:S(2)}, u32[]{:S(2)}) collective-permute-start(bf16[608,512]{1,0:T(8,128)(2,1)S(1)} %collective-permute-done.1.after.refs_0_.refs_2_), channel_id=1, source_target_pairs={{0,2},{2,0},{4,6},{6,4},{1,3},{3,1},{5,7},{7,5},{8,10},{10,8},{12,... | collective-permute-start | bytes 1867784 | tf_op jit(solution)/shard_map/ppermute | solution.py:365
  53.3 21.3 %all-to-all-start.3 = ((bf16[8,152,512]{2,1,0:T(8,128)(2,1)}), bf16[8,152,512]{2,1,0:T(8,128)(2,1)}, u32[]{:S(2)}, u32[]{:S(2)}) async-start(bf16[8,152,512]{2,1,0:T(8,128)(2,1)} %shard_map.110), calls=%async_computation.3 | async-start | bytes 2490368 | tf_op jit(solution)/shard_map/all_to_all | solution.py:387
  57.5 21.3 %collective-permute-start.3 = (bf16[2,2,64,512]{3,2,1,0:T(8,128)(2,1)S(1)}, bf16[2,2,64,512]{3,2,1,0:T(8,128)(2,1)S(1)}, u32[]{:S(2)}, u32[]{:S(2)}) collective-permute-start(bf16[2,2,64,512]{3,2,1,0:T(8,128)(2,1)S(1)} %shard_map.105.refs_0_.line), channel_id=1, source_target_pairs={{0,2},{6,4},{1,3},{7,5},{8,10},{14,12},{9,11},{15,13},{16,18},{22,... | collective-permute-start | bytes 786440 | tf_op jit(solution)/shard_map/ppermute | solution.py:365
  61.5 0.8 copy-start.5
  62.3 22.0 %collective-permute-start.7 = (bf16[3,2,2,64,512]{4,3,2,1,0:T(8,128)(2,1)S(1)}, bf16[3,2,2,64,512]{4,3,2,1,0:T(8,128)(2,1)S(1)}, u32[]{:S(2)}, u32[]{:S(2)}) collective-permute-start(bf16[3,2,2,64,512]{4,3,2,1,0:T(8,128)(2,1)S(1)} %shard_map.106), channel_id=1, source_target_pairs={{0,2},{2,0},{4,6},{6,4},{1,3},{3,1},{5,7},{7,5},{8,10},{10,8},{12,... | collective-permute-start | bytes 2359304 | tf_op jit(solution)/shard_map/ppermute | solution.py:365
  66.4 17.9 %copy-start = (bf16[8,2,48,512]{3,2,1,0:T(8,128)(2,1)S(1)}, bf16[8,2,48,512]{3,2,1,0:T(8,128)(2,1)}, u32[]{:S(2)}) copy-start(bf16[8,2,48,512]{3,2,1,0:T(8,128)(2,1)} %far_tiles.5) | copy-start | bytes 2359300
  66.4 17.9 %copy-start.3 = (s32[90]{0:T(128)S(1)}, s32[90]{0:T(128)}, u32[]{:S(2)}) copy-start(s32[90]{0:T(128)} %get-tuple-element.9.table) | copy-start | bytes 1084
  74.6 21.4 %all-to-all-start = ((bf16[8,152,512]{2,1,0:T(8,128)(2,1)}), bf16[8,152,512]{2,1,0:T(8,128)(2,1)}, u32[]{:S(2)}, u32[]{:S(2)}) async-start(bf16[8,152,512]{2,1,0:T(8,128)(2,1)} %shard_map.108), calls=%async_computation | async-start | bytes 2490368 | tf_op jit(solution)/shard_map/all_to_all | solution.py:387
  85.9 1.0 copy-start.1
  86.9 0.9 copy-start.2

commit v10 on v9

--- a/solution.py
+++ b/solution.py
@@ -19,7 +19,7 @@
 CHUNK_OWNER = ((0, 1, 2, 3), (1, 0, 3, 2), (2, 2, 1, 1), (3, 3, 0, 0))
 CHUNK_SOURCE = ((0, 0, 0, 0), (0, 0, 0, 0), (1, 0, 0, 1), (1, 0, 0, 1))
 CHUNK_SOURCES = (("own",), ("pair",), ("middle", "pass2"), ("cross", "pass3"))
-PACK_FLOPS = (0, 5 * 10**9, 10**10, 10**10)
+PACK_FLOPS = (0, 2 * 10**9, 10**10, 10**10)
 JOIN_FLOPS = 10**9
 UPDATE_FLOPS = 3 * 10**9
 VMEM = pl.BlockSpec(memory_space=pltpu.VMEM)
@@ -276,7 +276,7 @@
     got, (near_out, far_out) = refs[: len(chunks)], refs[-12:-10]
     tile, far_tile, left, x_half, parts, near_done, far_done, panel, factors, sems = refs[-10:]
     left_loads = [
-        pltpu.make_async_copy(lefts.at[r], left.at[r], sems.at[0, sizes.groups + 5 + r])
+        pltpu.make_async_copy(lefts.at[r], left.at[r], sems.at[0, sizes.groups + 6 + r])
         for r in range(left.shape[0])
     ]
     slots, loads = [], []
@@ -308,15 +308,23 @@
             load.wait()
         for g in range(sizes.groups):
             take_part(sizes, g, parts.at[at, g], panel, factors)
-        own_left = left[table[sizes.near_rows_at + slot]]
-        near_done[at] = near_update(tile[at], own_left, panel[...])
+        own_row = table[sizes.near_rows_at + slot]
         far_done[at] = far_update(far_tile[at], x_half[at], factors[...])
-        for j, (done, out) in enumerate(((near_done, near_out), (far_done, far_out))):
-            copy = pltpu.make_async_copy(
-                done.at[at], out.at[slot], sems.at[at, sizes.groups + 3 + j]
+        store_at = sizes.groups + 3
+        stores.append(
+            pltpu.make_async_copy(far_done.at[at], far_out.at[slot], sems.at[at, store_at])
+        )
+        stores[-1].start()
+        half = tile.shape[1] // 2
+        for h in range(2):
+            rows = pl.ds(h * half, half)
+            near_done[at, rows, :] = near_update(tile[at, rows, :], left[own_row, rows, :], panel[...])
+            stores.append(
+                pltpu.make_async_copy(
+                    near_done.at[at, rows], near_out.at[slot, rows], sems.at[at, store_at + 1 + h]
+                )
             )
-            copy.start()
-            stores.append(copy)
+            stores[-1].start()
     for store in stores:
         store.wait()
 
@@ -340,7 +348,7 @@
             pltpu.VMEM((count, rank, order), jnp.bfloat16),
             pltpu.VMEM((order, order), jnp.bfloat16),
             pltpu.VMEM((sizes.far_all, order), jnp.bfloat16),
-            pltpu.SemaphoreType.DMA((count, groups + 5 + row_group)),
+            pltpu.SemaphoreType.DMA((count, groups + 6 + row_group)),
         ],
         input_output_aliases={5 + len(got) + k: k for k in range(len(before))},
         compiler_params=pltpu.CompilerParams(vmem_limit_bytes=WIDE_VMEM),

time: 101 us -> 101 us (level)
  waiting for transfers between devices: 29 us -> 26.9 us
  starting transfers between devices: 40.8 us -> 42.8 us
  local copies, waits for them, and re-layouts: 3.78 us -> 2.75 us
    all_to_all x4, waiting for transfers between devices: 13.7 us -> 11.7 us  [shards(): lax.all_to_all(send, PLANE, split_axis=0, concat_axis=0, tiled=True)]
    ppermute x9, starting transfers between devices: 22.6 us -> 24.6 us  [along(): return lax.ppermute(value, 'outer', pairs)]
    unnamed x18, local copies, waits for them, and re-layouts: 3.78 us -> 2.75 us
  transfers between devices with their start and end apart: 14 -> 14, of which waited for: 4 -> 4; matrix products, arithmetic and copies ran while one was open for 0% -> 0% of each run, Pallas kernels for 18% -> 19%
where the time goes in v10:
time: 101 us; the launch traced here: 100 us
  starting transfers between devices  42.8 us (42%)
  waiting for transfers between devices  26.9 us (27%)
  Pallas kernels  26.6 us (26%)
  local copies, waits for them, and re-layouts  2.75 us (3%)
    ppermute x9, starting transfers between devices, along(): return lax.ppermute(value, 'outer', pairs)  24.6 us
    all_to_all x4, starting transfers between devices, shards(): lax.all_to_all(send, PLANE, split_axis=0, concat_axis=0, tiled=True)  16.7 us
    ppermute x9, waiting for transfers between devices, along(): return lax.ppermute(value, 'outer', pairs)  15.2 us
    pallas_call x2, Pallas kernels, update(): pl.pallas_call(functools.partial(update_kernel, sizes, chunks), in_specs=...  13.2 us
    all_to_all x4, waiting for transfers between devices, shards(): lax.all_to_all(send, PLANE, split_axis=0, concat_axis=0, tiled=True)  11.7 us
    pallas_call x3, Pallas kernels, pack(): pl.pallas_call(functools.partial(pack_kernel, sizes, n), in_specs=[SMEM]...  8.6 us
    pallas_call x1, Pallas kernels, first(): pl.pallas_call(functools.partial(first_kernel, sizes), in_specs=[SMEM] *...  3.13 us
    unnamed x18, local copies, waits for them, and re-layouts  2.75 us
  transfers between devices with their start and end apart: 14, of which 4 were waited for; matrix products, arithmetic and copies ran while one was open for 0% of the time, Pallas kernels for 19%

profile of v10, /device:TPU:0, one launch (start us, length us, event | category | flops | bytes accessed | tf_op | source)
XLA Modules:
  0.0 100.0 jit_solution(6827552020590778232)
XLA Ops:
  0.6 3.1 %shard_map.104 = (s32[90]{0:T(128)}, bf16[608,512]{1,0:T(8,128)(2,1)}, bf16[8,152,512]{2,1,0:T(8,128)(2,1)}) custom-call(s32[8,32]{1,0:T(8,128)} %bitcast.4, s32[8,32]{1,0:T(8,128)} %bitcast.5, s32[1,8]{1,0:T(1,128)} %near_rows.1, s32[1,8]{1,0:T(1,128)} %far_rows.1, bf16[4,128,512]{2,1,0:T(8,128)(2,1)} %near.1, bf16[4,12,2,512]{3,2,1,0:T(2,128)(2,1)} %bitcast.3), custom_call_target="tpu_custom_call" | custom-call | tf_op jit(solution)/shard_map/pallas_call | solution.py:128
  3.8 3.1 %collective-permute-start = (bf16[608,512]{1,0:T(8,128)(2,1)}, bf16[608,512]{1,0:T(8,128)(2,1)}, u32[]{:S(2)}, u32[]{:S(2)}) collective-permute-start(bf16[608,512]{1,0:T(8,128)(2,1)} %get-tuple-element.10), channel_id=1, source_target_pairs={{0,2},{2,0},{4,6},{6,4},{1,3},{3,1},{5,7},{7,5},{8,10},{10,8},{12,... | collective-permute-start | bytes 1867784 | tf_op jit(solution)/shard_map/ppermute | solution.py:373
  6.9 0.7 collective-permute-start.8
  7.6 0.0 copy-start.6
  7.6 3.9 %all-to-all-start.1 = ((bf16[8,152,512]{2,1,0:T(8,128)(2,1)}), bf16[8,152,512]{2,1,0:T(8,128)(2,1)S(1)}, u32[]{:S(2)}, u32[]{:S(2)}) async-start(bf16[8,152,512]{2,1,0:T(8,128)(2,1)} %get-tuple-element.13), calls=%async_computation.1 | async-start | bytes 2490368 | tf_op jit(solution)/shard_map/all_to_all | solution.py:395
  11.4 9.8 %collective-permute-done.refs_0_ = bf16[608,512]{1,0:T(8,128)(2,1)} collective-permute-done((bf16[608,512]{1,0:T(8,128)(2,1)}, bf16[608,512]{1,0:T(8,128)(2,1)}, u32[]{:S(2)}, u32[]{:S(2)}) %collective-permute-start) | collective-permute-done | bytes 622624 | tf_op jit(solution)/shard_map/ppermute | solution.py:373
  21.2 0.7 collective-permute-start.1
  21.9 0.0 collective-permute-done.8.refs_0_
  21.9 0.0 copy-start.8
  21.9 4.6 %collective-permute-start.9 = (bf16[608,512]{1,0:T(8,128)(2,1)S(1)}, bf16[608,512]{1,0:T(8,128)(2,1)}, u32[]{:S(2)}, u32[]{:S(2)}) collective-permute-start(bf16[608,512]{1,0:T(8,128)(2,1)S(1)} %collective-permute-done.8.refs_0_), channel_id=1, source_target_pairs={{0,2},{2,0},{4,6},{6,4},{1,3},{3,1},{5,7},{7,5},{8,10},{10,8},{12,... | collective-permute-start | bytes 1867784 | tf_op jit(solution)/shard_map/ppermute | solution.py:373
  26.5 0.0 copy-done.6
  26.5 1.5 %collective-permute-start.2 = (bf16[2,64,512]{2,1,0:T(8,128)(2,1)S(1)}, bf16[2,64,512]{2,1,0:T(8,128)(2,1)S(1)}, u32[]{:S(2)}, u32[]{:S(2)}) collective-permute-start(bf16[2,64,512]{2,1,0:T(8,128)(2,1)S(1)} %copy-done.6), channel_id=1, source_target_pairs={{1,0},{0,1},{3,2},{2,3},{5,4},{4,5},{7,6},{6,7},{9,8},{8,9},{11,10... | collective-permute-start | bytes 393224 | tf_op jit(solution)/shard_map/ppermute | solution.py:378
  28.0 2.9 %shard_map.109 = bf16[8,152,512]{2,1,0:T(8,128)(2,1)} custom-call(s32[90]{0:T(128)} %get-tuple-element.9.table, bf16[608,512]{1,0:T(8,128)(2,1)} %collective-permute-done.refs_0_), custom_call_target="tpu_custom_call" | custom-call | flops 2000000000 | tf_op jit(solution)/shard_map/pallas_call | solution.py:158
  30.9 0.0 copy-done.8
  30.9 0.0 all-to-all-done.1.refs_0_
  30.9 0.0 copy-start.7
  30.9 4.3 %all-to-all-start.2 = ((bf16[8,152,512]{2,1,0:T(8,128)(2,1)}), bf16[8,152,512]{2,1,0:T(8,128)(2,1)}, u32[]{:S(2)}, u32[]{:S(2)}) async-start(bf16[8,152,512]{2,1,0:T(8,128)(2,1)} %shard_map.109), calls=%async_computation.2 | async-start | bytes 2490368 | tf_op jit(solution)/shard_map/all_to_all | solution.py:395
  35.2 0.0 collective-permute-done.2.refs_1_
  35.2 0.0 copy-done.7
  35.2 0.0 collective-permute-done.1.after.refs_0_.refs_2_
  35.3 7.6 %collective-permute-start.5 = (bf16[2,2,64,512]{3,2,1,0:T(8,128)(2,1)S(1)}, bf16[2,2,64,512]{3,2,1,0:T(8,128)(2,1)S(1)}, u32[]{:S(2)}, u32[]{:S(2)}) collective-permute-start(bf16[2,2,64,512]{3,2,1,0:T(8,128)(2,1)S(1)} %shard_map.105.refs_0_.line), channel_id=1, source_target_pairs={{0,4},{6,2},{1,5},{7,3},{8,12},{14,10},{9,13},{15,11},{16,20},{22,... | collective-permute-start | bytes 786440 | tf_op jit(solution)/shard_map/ppermute | solution.py:373
  42.9 0.7 collective-permute-start.4
  43.6 0.0 copy-done.4
  43.6 1.2 %collective-permute-start.6 = (bf16[608,512]{1,0:T(8,128)(2,1)S(1)}, bf16[608,512]{1,0:T(8,128)(2,1)S(1)}, u32[]{:S(2)}, u32[]{:S(2)}) collective-permute-start(bf16[608,512]{1,0:T(8,128)(2,1)S(1)} %collective-permute-done.1.after.refs_0_.refs_2_), channel_id=1, source_target_pairs={{0,2},{2,0},{4,6},{6,4},{1,3},{3,1},{5,7},{7,5},{8,10},{10,8},{12,... | collective-permute-start | bytes 1867784 | tf_op jit(solution)/shard_map/ppermute | solution.py:373
  44.8 0.0 collective-permute-done.9.refs_1_
  44.8 2.9 %shard_map.110 = bf16[8,152,512]{2,1,0:T(8,128)(2,1)} custom-call(s32[90]{0:T(128)} %get-tuple-element.9.table, bf16[608,512]{1,0:T(8,128)(2,1)} %copy-done.8, bf16[608,512]{1,0:T(8,128)(2,1)} %collective-permute-done.9.refs_1_, bf16[608,512]{1,0:T(8,128)(2,1)} %copy-done.4), custom_call_target="tpu_custom_call" | custom-call | flops 10000000000 | tf_op jit(solution)/shard_map/pallas_call | solution.py:158
  47.7 4.5 %all-to-all-done.2.refs_1_ = bf16[8,152,512]{2,1,0:T(8,128)(2,1)} async-done(((bf16[8,152,512]{2,1,0:T(8,128)(2,1)}), bf16[8,152,512]{2,1,0:T(8,128)(2,1)}, u32[]{:S(2)}, u32[]{:S(2)}) %all-to-all-start.2) | async-done | bytes 1245216 | tf_op jit(solution)/shard_map/all_to_all | solution.py:395
  52.2 4.3 %all-to-all-start.3 = ((bf16[8,152,512]{2,1,0:T(8,128)(2,1)}), bf16[8,152,512]{2,1,0:T(8,128)(2,1)}, u32[]{:S(2)}, u32[]{:S(2)}) async-start(bf16[8,152,512]{2,1,0:T(8,128)(2,1)} %shard_map.110), calls=%async_computation.3 | async-start | bytes 2490368 | tf_op jit(solution)/shard_map/all_to_all | solution.py:395
  56.5 3.8 %collective-permute-start.3 = (bf16[2,2,64,512]{3,2,1,0:T(8,128)(2,1)S(1)}, bf16[2,2,64,512]{3,2,1,0:T(8,128)(2,1)S(1)}, u32[]{:S(2)}, u32[]{:S(2)}) collective-permute-start(bf16[2,2,64,512]{3,2,1,0:T(8,128)(2,1)S(1)} %shard_map.105.refs_0_.line), channel_id=1, source_target_pairs={{0,2},{6,4},{1,3},{7,5},{8,10},{14,12},{9,11},{15,13},{16,18},{22,... | collective-permute-start | bytes 786440 | tf_op jit(solution)/shard_map/ppermute | solution.py:373
  60.4 0.0 collective-permute-done.5.refs_2_.near3
  60.4 0.0 collective-permute-done.4.refs_1_.near2
  60.4 0.0 collective-permute-done.6.after.refs_1_
  60.4 0.1 shard_map.106
  60.5 0.8 copy-done.5
  61.3 2.2 %collective-permute-start.7 = (bf16[3,2,2,64,512]{4,3,2,1,0:T(8,128)(2,1)S(1)}, bf16[3,2,2,64,512]{4,3,2,1,0:T(8,128)(2,1)S(1)}, u32[]{:S(2)}, u32[]{:S(2)}) collective-permute-start(bf16[3,2,2,64,512]{4,3,2,1,0:T(8,128)(2,1)S(1)} %shard_map.106), channel_id=1, source_target_pairs={{0,2},{2,0},{4,6},{6,4},{1,3},{3,1},{5,7},{7,5},{8,10},{10,8},{12,... | collective-permute-start | bytes 2359304 | tf_op jit(solution)/shard_map/ppermute | solution.py:373
  63.5 2.9 %shard_map.108 = bf16[8,152,512]{2,1,0:T(8,128)(2,1)} custom-call(s32[90]{0:T(128)} %get-tuple-element.9.table, bf16[608,512]{1,0:T(8,128)(2,1)} %copy-done.4, bf16[608,512]{1,0:T(8,128)(2,1)} %copy-done.5), custom_call_target="tpu_custom_call" | custom-call | flops 10000000000 | tf_op jit(solution)/shard_map/pallas_call | solution.py:158
  66.4 0.0 copy-start
  66.4 7.2 %all-to-all-done.3.refs_2_ = bf16[8,152,512]{2,1,0:T(8,128)(2,1)} async-done(((bf16[8,152,512]{2,1,0:T(8,128)(2,1)}), bf16[8,152,512]{2,1,0:T(8,128)(2,1)}, u32[]{:S(2)}, u32[]{:S(2)}) %all-to-all-start.3) | async-done | bytes 1245216 | tf_op jit(solution)/shard_map/all_to_all | solution.py:395
  73.6 4.3 %all-to-all-start = ((bf16[8,152,512]{2,1,0:T(8,128)(2,1)}), bf16[8,152,512]{2,1,0:T(8,128)(2,1)}, u32[]{:S(2)}, u32[]{:S(2)}) async-start(bf16[8,152,512]{2,1,0:T(8,128)(2,1)} %shard_map.108), calls=%async_computation | async-start | bytes 2490368 | tf_op jit(solution)/shard_map/all_to_all | solution.py:395
  77.8 0.0 collective-permute-done.3.near1
  77.9 5.4 %collective-permute-done.7.relayed = bf16[3,2,2,64,512]{4,3,2,1,0:T(8,128)(2,1)S(1)} collective-permute-done((bf16[3,2,2,64,512]{4,3,2,1,0:T(8,128)(2,1)S(1)}, bf16[3,2,2,64,512]{4,3,2,1,0:T(8,128)(2,1)S(1)}, u32[]{:S(2)}, u32[]{:S(2)}) %collective-permute-start.7) | collective-permute-done | bytes 786464 | tf_op jit(solution)/shard_map/ppermute | solution.py:373
  83.3 0.0 copy-done.3
  83.3 1.6 %shard_map.107 = (bf16[2,512,512]{2,1,0:T(8,128)(2,1)S(1)}, bf16[8,96,512]{2,1,0:T(8,128)(2,1)S(1)}) custom-call(s32[90]{0:T(128)S(1)} %copy-done.3, bf16[8,2,48,512]{3,2,1,0:T(8,128)(2,1)S(1)} %copy-done, bf16[2,2,64,512]{3,2,1,0:T(8,128)(2,1)S(1)} %shard_map.105.refs_0_.line, bf16[2,2,64,512]{3,2,1,0:T(8,128)(2,1)S(1)} %collective-permute-done.3.near1, ...), custom_call_target="tpu_custom_call" | custom-call | tf_op jit(solution)/shard_map/pallas_call | solution.py:217
  84.9 1.0 copy-done.1
  85.8 0.9 copy-done.2
  86.7 8.4 %shard_map.111 = (bf16[8,512,512]{2,1,0:T(8,128)(2,1)}, bf16[8,48,512]{2,1,0:T(8,128)(2,1)}) custom-call(s32[90]{0:T(128)} %get-tuple-element.9.table, bf16[8,512,512]{2,1,0:T(8,128)(2,1)} %near_tiles.3, bf16[8,2,48,512]{3,2,1,0:T(8,128)(2,1)} %far_tiles.5, bf16[2,512,512]{2,1,0:T(8,128)(2,1)} %copy-done.1, bf16[8,96,512]{2,1,0:T(8,128)(2,1)} %copy-done.2, ...), custom_call_target="tpu_custom_call" | custom-call | flops 8999999488 | tf_op jit(solution)/shard_map/pallas_call | solution.py:336
  95.1 0.0 all-to-all-done.refs_0_
  95.1 4.8 %shard_map.112 = (bf16[8,512,512]{2,1,0:T(8,128)(2,1)}, bf16[8,48,512]{2,1,0:T(8,128)(2,1)}) custom-call(s32[90]{0:T(128)} %get-tuple-element.9.table, bf16[8,512,512]{2,1,0:T(8,128)(2,1)} %near_tiles.3, bf16[8,2,48,512]{3,2,1,0:T(8,128)(2,1)} %far_tiles.5, bf16[2,512,512]{2,1,0:T(8,128)(2,1)} %copy-done.1, ...), custom_call_target="tpu_custom_call", output_to_operand_aliasing={{0}: (6, {}), {1}: (7, {})} | custom-call | flops 3000000000 | tf_op jit(solution)/shard_map/pallas_call | solution.py:336
  (7 shorter events, 0.0 us)
Async XLA Ops:
  3.8 17.4 %collective-permute-start = (bf16[608,512]{1,0:T(8,128)(2,1)}, bf16[608,512]{1,0:T(8,128)(2,1)}, u32[]{:S(2)}, u32[]{:S(2)}) collective-permute-start(bf16[608,512]{1,0:T(8,128)(2,1)} %get-tuple-element.10), channel_id=1, source_target_pairs={{0,2},{2,0},{4,6},{6,4},{1,3},{3,1},{5,7},{7,5},{8,10},{10,8},{12,... | collective-permute-start | bytes 1867784 | tf_op jit(solution)/shard_map/ppermute | solution.py:373
  6.9 15.0 %collective-permute-start.8 = (bf16[608,512]{1,0:T(8,128)(2,1)}, bf16[608,512]{1,0:T(8,128)(2,1)S(1)}, u32[]{:S(2)}, u32[]{:S(2)}) collective-permute-start(bf16[608,512]{1,0:T(8,128)(2,1)} %get-tuple-element.10), channel_id=1, source_target_pairs={{2,4},{4,2},{3,5},{5,3},{10,12},{12,10},{11,13},{13,11},{18,20},{2... | collective-permute-start | bytes 1867784 | tf_op jit(solution)/shard_map/ppermute | solution.py:373
  7.6 19.0 %copy-start.6 = (bf16[2,64,512]{2,1,0:T(8,128)(2,1)S(1)}, bf16[2,64,512]{2,1,0:T(8,128)(2,1)}, u32[]{:S(2)}) copy-start(bf16[2,64,512]{2,1,0:T(8,128)(2,1)} %refs_0_.1) | copy-start | bytes 393220
  7.6 23.3 %all-to-all-start.1 = ((bf16[8,152,512]{2,1,0:T(8,128)(2,1)}), bf16[8,152,512]{2,1,0:T(8,128)(2,1)S(1)}, u32[]{:S(2)}, u32[]{:S(2)}) async-start(bf16[8,152,512]{2,1,0:T(8,128)(2,1)} %get-tuple-element.13), calls=%async_computation.1 | async-start | bytes 2490368 | tf_op jit(solution)/shard_map/all_to_all | solution.py:395
  21.2 14.0 %collective-permute-start.1 = (bf16[608,512]{1,0:T(8,128)(2,1)}, bf16[608,512]{1,0:T(8,128)(2,1)S(1)}, u32[]{:S(2)}, u32[]{:S(2)}) collective-permute-start(bf16[608,512]{1,0:T(8,128)(2,1)} %collective-permute-done.refs_0_), channel_id=1, source_target_pairs={{2,4},{4,2},{3,5},{5,3},{10,12},{12,10},{11,13},{13,11},{18,20},{2... | collective-permute-start | bytes 1867784 | tf_op jit(solution)/shard_map/ppermute | solution.py:373
  21.9 9.0 %copy-start.8 = (bf16[608,512]{1,0:T(8,128)(2,1)}, bf16[608,512]{1,0:T(8,128)(2,1)S(1)}, u32[]{:S(2)}) copy-start(bf16[608,512]{1,0:T(8,128)(2,1)S(1)} %collective-permute-done.8.refs_0_) | copy-start | bytes 1867780
  21.9 22.9 %collective-permute-start.9 = (bf16[608,512]{1,0:T(8,128)(2,1)S(1)}, bf16[608,512]{1,0:T(8,128)(2,1)}, u32[]{:S(2)}, u32[]{:S(2)}) collective-permute-start(bf16[608,512]{1,0:T(8,128)(2,1)S(1)} %collective-permute-done.8.refs_0_), channel_id=1, source_target_pairs={{0,2},{2,0},{4,6},{6,4},{1,3},{3,1},{5,7},{7,5},{8,10},{10,8},{12,... | collective-permute-start | bytes 1867784 | tf_op jit(solution)/shard_map/ppermute | solution.py:373
  26.5 8.7 %collective-permute-start.2 = (bf16[2,64,512]{2,1,0:T(8,128)(2,1)S(1)}, bf16[2,64,512]{2,1,0:T(8,128)(2,1)S(1)}, u32[]{:S(2)}, u32[]{:S(2)}) collective-permute-start(bf16[2,64,512]{2,1,0:T(8,128)(2,1)S(1)} %copy-done.6), channel_id=1, source_target_pairs={{1,0},{0,1},{3,2},{2,3},{5,4},{4,5},{7,6},{6,7},{9,8},{8,9},{11,10... | collective-permute-start | bytes 393224 | tf_op jit(solution)/shard_map/ppermute | solution.py:378
  30.9 4.3 %copy-start.7 = (bf16[8,152,512]{2,1,0:T(8,128)(2,1)}, bf16[8,152,512]{2,1,0:T(8,128)(2,1)S(1)}, u32[]{:S(2)}) copy-start(bf16[8,152,512]{2,1,0:T(8,128)(2,1)S(1)} %all-to-all-done.1.refs_0_) | copy-start | bytes 3735556
  30.9 21.3 %all-to-all-start.2 = ((bf16[8,152,512]{2,1,0:T(8,128)(2,1)}), bf16[8,152,512]{2,1,0:T(8,128)(2,1)}, u32[]{:S(2)}, u32[]{:S(2)}) async-start(bf16[8,152,512]{2,1,0:T(8,128)(2,1)} %shard_map.109), calls=%async_computation.2 | async-start | bytes 2490368 | tf_op jit(solution)/shard_map/all_to_all | solution.py:395
  35.2 8.4 %copy-start.4 = (bf16[608,512]{1,0:T(8,128)(2,1)}, bf16[608,512]{1,0:T(8,128)(2,1)S(1)}, u32[]{:S(2)}) copy-start(bf16[608,512]{1,0:T(8,128)(2,1)S(1)} %collective-permute-done.1.after.refs_0_.refs_2_) | copy-start | bytes 1867780
  35.3 25.1 %collective-permute-start.5 = (bf16[2,2,64,512]{3,2,1,0:T(8,128)(2,1)S(1)}, bf16[2,2,64,512]{3,2,1,0:T(8,128)(2,1)S(1)}, u32[]{:S(2)}, u32[]{:S(2)}) collective-permute-start(bf16[2,2,64,512]{3,2,1,0:T(8,128)(2,1)S(1)} %shard_map.105.refs_0_.line), channel_id=1, source_target_pairs={{0,4},{6,2},{1,5},{7,3},{8,12},{14,10},{9,13},{15,11},{16,20},{22,... | collective-permute-start | bytes 786440 | tf_op jit(solution)/shard_map/ppermute | solution.py:373
  42.9 17.5 %collective-permute-start.4 = (bf16[2,2,64,512]{3,2,1,0:T(8,128)(2,1)S(1)}, bf16[2,2,64,512]{3,2,1,0:T(8,128)(2,1)S(1)}, u32[]{:S(2)}, u32[]{:S(2)}) collective-permute-start(bf16[2,2,64,512]{3,2,1,0:T(8,128)(2,1)S(1)} %shard_map.105.refs_0_.line), channel_id=1, source_target_pairs={{2,4},{4,2},{3,5},{5,3},{10,12},{12,10},{11,13},{13,11},{18,20},{2... | collective-permute-start | bytes 786440 | tf_op jit(solution)/shard_map/ppermute | solution.py:373
  43.6 16.8 %collective-permute-start.6 = (bf16[608,512]{1,0:T(8,128)(2,1)S(1)}, bf16[608,512]{1,0:T(8,128)(2,1)S(1)}, u32[]{:S(2)}, u32[]{:S(2)}) collective-permute-start(bf16[608,512]{1,0:T(8,128)(2,1)S(1)} %collective-permute-done.1.after.refs_0_.refs_2_), channel_id=1, source_target_pairs={{0,2},{2,0},{4,6},{6,4},{1,3},{3,1},{5,7},{7,5},{8,10},{10,8},{12,... | collective-permute-start | bytes 1867784 | tf_op jit(solution)/shard_map/ppermute | solution.py:373
  52.2 21.3 %all-to-all-start.3 = ((bf16[8,152,512]{2,1,0:T(8,128)(2,1)}), bf16[8,152,512]{2,1,0:T(8,128)(2,1)}, u32[]{:S(2)}, u32[]{:S(2)}) async-start(bf16[8,152,512]{2,1,0:T(8,128)(2,1)} %shard_map.110), calls=%async_computation.3 | async-start | bytes 2490368 | tf_op jit(solution)/shard_map/all_to_all | solution.py:395
  56.5 21.3 %collective-permute-start.3 = (bf16[2,2,64,512]{3,2,1,0:T(8,128)(2,1)S(1)}, bf16[2,2,64,512]{3,2,1,0:T(8,128)(2,1)S(1)}, u32[]{:S(2)}, u32[]{:S(2)}) collective-permute-start(bf16[2,2,64,512]{3,2,1,0:T(8,128)(2,1)S(1)} %shard_map.105.refs_0_.line), channel_id=1, source_target_pairs={{0,2},{6,4},{1,3},{7,5},{8,10},{14,12},{9,11},{15,13},{16,18},{22,... | collective-permute-start | bytes 786440 | tf_op jit(solution)/shard_map/ppermute | solution.py:373
  60.5 0.8 copy-start.5
  61.3 22.0 %collective-permute-start.7 = (bf16[3,2,2,64,512]{4,3,2,1,0:T(8,128)(2,1)S(1)}, bf16[3,2,2,64,512]{4,3,2,1,0:T(8,128)(2,1)S(1)}, u32[]{:S(2)}, u32[]{:S(2)}) collective-permute-start(bf16[3,2,2,64,512]{4,3,2,1,0:T(8,128)(2,1)S(1)} %shard_map.106), channel_id=1, source_target_pairs={{0,2},{2,0},{4,6},{6,4},{1,3},{3,1},{5,7},{7,5},{8,10},{10,8},{12,... | collective-permute-start | bytes 2359304 | tf_op jit(solution)/shard_map/ppermute | solution.py:373
  66.4 16.9 %copy-start = (bf16[8,2,48,512]{3,2,1,0:T(8,128)(2,1)S(1)}, bf16[8,2,48,512]{3,2,1,0:T(8,128)(2,1)}, u32[]{:S(2)}) copy-start(bf16[8,2,48,512]{3,2,1,0:T(8,128)(2,1)} %far_tiles.5) | copy-start | bytes 2359300
  66.4 16.9 %copy-start.3 = (s32[90]{0:T(128)S(1)}, s32[90]{0:T(128)}, u32[]{:S(2)}) copy-start(s32[90]{0:T(128)} %get-tuple-element.9.table) | copy-start | bytes 1084
  73.6 21.6 %all-to-all-start = ((bf16[8,152,512]{2,1,0:T(8,128)(2,1)}), bf16[8,152,512]{2,1,0:T(8,128)(2,1)}, u32[]{:S(2)}, u32[]{:S(2)}) async-start(bf16[8,152,512]{2,1,0:T(8,128)(2,1)} %shard_map.108), calls=%async_computation | async-start | bytes 2490368 | tf_op jit(solution)/shard_map/all_to_all | solution.py:395
  84.8 1.0 copy-start.1
  85.8 0.9 copy-start.2

commit v11 on v9

--- a/solution.py
+++ b/solution.py
@@ -13,13 +13,12 @@
 FAR_ALIGN = 8
 LANES = 128
 VMEM_LIMIT = 16 * 1024 * 1024
-WIDE_VMEM = 60 * 1024 * 1024
-LEFTS_VMEM = 24 * 1024 * 1024
+WIDE_VMEM = 63 * 1024 * 1024
 HBM = pl.BlockSpec(memory_space=pltpu.HBM)
 CHUNK_OWNER = ((0, 1, 2, 3), (1, 0, 3, 2), (2, 2, 1, 1), (3, 3, 0, 0))
 CHUNK_SOURCE = ((0, 0, 0, 0), (0, 0, 0, 0), (1, 0, 0, 1), (1, 0, 0, 1))
 CHUNK_SOURCES = (("own",), ("pair",), ("middle", "pass2"), ("cross", "pass3"))
-PACK_FLOPS = (0, 5 * 10**9, 10**10, 10**10)
+PACK_FLOPS = (0, 2 * 10**9, 10**10, 10**10)
 JOIN_FLOPS = 10**9
 UPDATE_FLOPS = 3 * 10**9
 VMEM = pl.BlockSpec(memory_space=pltpu.VMEM)
@@ -183,7 +182,8 @@
     )(after, *parts)
 
 
-def lefts_kernel(sizes, table, far_tiles, line, near1, near2, near3, relayed, lefts, x_halves):
+def fill_lefts(sizes, table, far_tiles, parts, lefts, x_halves):
+    line, near1, near2, near3, relayed = parts
     shard = sizes.shard
     inner, outer = table[sizes.inner_at], table[sizes.outer_at]
 
@@ -211,22 +211,6 @@
                 x_halves[s] = halves(own)
 
 
-def make_lefts(sizes, table, far_tiles, parts):
-    row_group, _, order = parts[0].shape[1:]
-    rank = far_tiles.shape[2]
-    return pl.pallas_call(
-        functools.partial(lefts_kernel, sizes),
-        in_specs=[SMEM, VMEM] + [VMEM] * len(parts),
-        out_specs=[VMEM, VMEM],
-        out_shape=[
-            jax.ShapeDtypeStruct((row_group, order, order), jnp.bfloat16),
-            jax.ShapeDtypeStruct((sizes.slots, 2 * rank, order), jnp.bfloat16),
-        ],
-        compiler_params=pltpu.CompilerParams(vmem_limit_bytes=LEFTS_VMEM),
-        cost_estimate=pl.CostEstimate(flops=0, bytes_accessed=0, transcendentals=0),
-    )(table, far_tiles, *parts)
-
-
 def halves(value):
     high = value.astype(jnp.bfloat16)
     low = (value - high.astype(jnp.float32)).astype(jnp.bfloat16)
@@ -272,53 +256,144 @@
     ]
 
 
-def update_kernel(sizes, chunks, table, near_tiles, far_tiles, lefts, x_halves, *refs):
-    got, (near_out, far_out) = refs[: len(chunks)], refs[-12:-10]
-    tile, far_tile, left, x_half, parts, near_done, far_done, panel, factors, sems = refs[-10:]
-    left_loads = [
-        pltpu.make_async_copy(lefts.at[r], left.at[r], sems.at[0, sizes.groups + 5 + r])
-        for r in range(left.shape[0])
-    ]
+def slot_loads(sizes, chunks, table, got, near_tiles, parts, tile, sems):
     slots, loads = [], []
     for k, n in enumerate(chunks):
         for x in range(sizes.inner):
             at = len(slots)
-            slot = table[sizes.owner_at(n)] * sizes.inner + x
+            slots.append(table[sizes.owner_at(n)] * sizes.inner + x)
             pairs = [(got[k].at[g * sizes.inner + x], parts.at[at, g]) for g in range(sizes.groups)]
-            pairs += [
-                (near_tiles.at[slot], tile.at[at]),
-                (x_halves.at[slot], x_half.at[at]),
-                (far_tiles.at[slot, 1], far_tile.at[at]),
-            ]
-            slots.append(slot)
+            pairs.append((near_tiles.at[slots[at]], tile.at[at]))
             loads.append(
                 [
                     pltpu.make_async_copy(source, to, sems.at[at, j])
                     for j, (source, to) in enumerate(pairs)
                 ]
             )
+    return slots, loads
+
+
+def slot_update(
+    sizes, at, slot, table, tile, v_tile, left, x_half, parts, done, outs, panel, factors, sems
+):
+    (near_done, far_done), (near_out, far_out) = done, outs
+    for g in range(sizes.groups):
+        take_part(sizes, g, parts.at[at, g], panel, factors)
+    far_done[at] = far_update(v_tile, x_half, factors[...])
+    store_at = sizes.groups + 3
+    stores = [pltpu.make_async_copy(far_done.at[at], far_out.at[slot], sems.at[at, store_at])]
+    stores[0].start()
+    own_row = table[sizes.near_rows_at + slot]
+    half = tile.shape[1] // 2
+    for h in range(2):
+        rows = pl.ds(h * half, half)
+        near_done[at, rows, :] = near_update(tile[at, rows, :], left[own_row, rows, :], panel[...])
+        stores.append(
+            pltpu.make_async_copy(
+                near_done.at[at, rows], near_out.at[slot, rows], sems.at[at, store_at + 1 + h]
+            )
+        )
+        stores[-1].start()
+    return stores
+
+
+def first_update_kernel(sizes, chunks, table, near_tiles, far_tiles, *refs):
+    rows_in, got = refs[:5], refs[5 : 5 + len(chunks)]
+    near_out, far_out, lefts, x_halves = refs[5 + len(chunks) : 9 + len(chunks)]
+    rows, (far_all, left, x_all, tile, parts, near_done, far_done, panel, factors, sems, few) = (
+        refs[-16:-11],
+        refs[-11:],
+    )
+    early = [pltpu.make_async_copy(part, to, few.at[j]) for j, (part, to) in enumerate(zip(rows_in, rows))]
+    early.append(pltpu.make_async_copy(far_tiles, far_all, few.at[5]))
+    slots, loads = slot_loads(sizes, chunks, table, got, near_tiles, parts, tile, sems)
+    for load in early + sum(loads, []):
+        load.start()
+    clear_rest(sizes, factors)
+    for load in early:
+        load.wait()
+    fill_lefts(sizes, table, far_all, rows, left, x_all)
+    stores = [
+        pltpu.make_async_copy(left, lefts, few.at[6]),
+        pltpu.make_async_copy(x_all, x_halves, few.at[7]),
+    ]
+    for store in stores:
+        store.start()
+    done, outs = (near_done, far_done), (near_out, far_out)
+    for at, slot in enumerate(slots):
+        for load in loads[at]:
+            load.wait()
+        stores += slot_update(
+            sizes, at, slot, table, tile, far_all[slot, 1], left, x_all[slot], parts, done, outs,
+            panel, factors, sems,
+        )
+    for store in stores:
+        store.wait()
+
+
+def update_kernel(sizes, chunks, table, near_tiles, far_tiles, lefts, x_halves, *refs):
+    got, (near_out, far_out) = refs[: len(chunks)], refs[-12:-10]
+    tile, far_tile, left, x_half, parts, near_done, far_done, panel, factors, sems = refs[-10:]
+    slots, loads = slot_loads(sizes, chunks, table, got, near_tiles, parts, tile, sems)
+    for at, slot in enumerate(slots):
+        j = sizes.groups + 1
+        loads[at] += [
+            pltpu.make_async_copy(x_halves.at[slot], x_half.at[at], sems.at[at, j]),
+            pltpu.make_async_copy(far_tiles.at[slot, 1], far_tile.at[at], sems.at[at, j + 1]),
+        ]
+    left_loads = [
+        pltpu.make_async_copy(lefts.at[r], left.at[r], sems.at[0, sizes.groups + 6 + r])
+        for r in range(left.shape[0])
+    ]
     for load in loads[0] + left_loads + sum(loads[1:], []):
         load.start()
     clear_rest(sizes, factors)
     for load in left_loads:
         load.wait()
     stores = []
+    done, outs = (near_done, far_done), (near_out, far_out)
     for at, slot in enumerate(slots):
         for load in loads[at]:
             load.wait()
-        for g in range(sizes.groups):
-            take_part(sizes, g, parts.at[at, g], panel, factors)
-        own_left = left[table[sizes.near_rows_at + slot]]
-        near_done[at] = near_update(tile[at], own_left, panel[...])
-        far_done[at] = far_update(far_tile[at], x_half[at], factors[...])
-        for j, (done, out) in enumerate(((near_done, near_out), (far_done, far_out))):
-            copy = pltpu.make_async_copy(
-                done.at[at], out.at[slot], sems.at[at, sizes.groups + 3 + j]
-            )
-            copy.start()
-            stores.append(copy)
+        stores += slot_update(
+            sizes, at, slot, table, tile, far_tile[at], left, x_half[at], parts, done, outs,
+            panel, factors, sems,
+        )
     for store in stores:
         store.wait()
+
+
+def first_update(sizes, chunks, table, near_tiles, far_tiles, rows, got):
+    order, rank = near_tiles.shape[1], far_tiles.shape[2]
+    groups, row_group = sizes.groups, rows[0].shape[1]
+    count = len(chunks) * sizes.inner
+    lefts = (row_group, order, order)
+    x_halves = (sizes.slots, 2 * rank, order)
+    return pl.pallas_call(
+        functools.partial(first_update_kernel, sizes, chunks),
+        in_specs=[SMEM] + [HBM] * (2 + len(rows) + len(got)),
+        out_specs=[HBM] * 4,
+        out_shape=out_shapes(sizes, near_tiles, far_tiles)
+        + [jax.ShapeDtypeStruct(shape, jnp.bfloat16) for shape in (lefts, x_halves)],
+        scratch_shapes=[pltpu.VMEM(part.shape, jnp.bfloat16) for part in rows]
+        + [
+            pltpu.VMEM(far_tiles.shape, jnp.bfloat16),
+            pltpu.VMEM(lefts, jnp.bfloat16),
+            pltpu.VMEM(x_halves, jnp.bfloat16),
+            pltpu.VMEM((count, order, order), jnp.bfloat16),
+            pltpu.VMEM((count, groups, sizes.quarter + sizes.far, order), jnp.bfloat16),
+            pltpu.VMEM((count, order, order), jnp.bfloat16),
+            pltpu.VMEM((count, rank, order), jnp.bfloat16),
+            pltpu.VMEM((order, order), jnp.bfloat16),
+            pltpu.VMEM((sizes.far_all, order), jnp.bfloat16),
+            pltpu.SemaphoreType.DMA((count, groups + 6)),
+            pltpu.SemaphoreType.DMA((8,)),
+        ],
+        compiler_params=pltpu.CompilerParams(vmem_limit_bytes=WIDE_VMEM),
+        cost_estimate=pl.CostEstimate(
+            flops=UPDATE_FLOPS * len(chunks), bytes_accessed=0, transcendentals=0
+        ),
+    )(table, near_tiles, far_tiles, *rows, *got)
 
 
 def update(sizes, chunks, table, near_tiles, far_tiles, lefts, x_halves, got, before):
@@ -340,7 +415,7 @@
             pltpu.VMEM((count, rank, order), jnp.bfloat16),
             pltpu.VMEM((order, order), jnp.bfloat16),
             pltpu.VMEM((sizes.far_all, order), jnp.bfloat16),
-            pltpu.SemaphoreType.DMA((count, groups + 5 + row_group)),
+            pltpu.SemaphoreType.DMA((count, groups + 6 + row_group)),
         ],
         input_output_aliases={5 + len(got) + k: k for k in range(len(before))},
         compiler_params=pltpu.CompilerParams(vmem_limit_bytes=WIDE_VMEM),
@@ -393,10 +468,10 @@
     relayed = join_rows([line, near2, near3], held["pass3"])
     relayed = along(relayed, [(0, 1), (1, 0), (2, 3), (3, 2)])
     parts = [line, near1, near2, near3, relayed]
-    lefts, x_halves = make_lefts(sizes, table, far_tiles, parts)
-    tiles = (near_tiles, far_tiles, lefts, x_halves)
-    outs = update(sizes, (0, 1, 2), table, *tiles, got[:3], ())
-    outs = update(sizes, (3,), table, *tiles, got[3:], outs)
+    *outs, lefts, x_halves = first_update(
+        sizes, (0, 1, 2), table, near_tiles, far_tiles, parts, got[:3]
+    )
+    outs = update(sizes, (3,), table, near_tiles, far_tiles, lefts, x_halves, got[3:], outs)
     return tuple(outs)
 
 

time: 101 us -> 101 us (level)
  waiting for transfers between devices: 29 us -> 23.3 us
  starting transfers between devices: 40.8 us -> 44.7 us
  Pallas kernels: 26.3 us -> 29.7 us
  local copies, waits for them, and re-layouts: 3.78 us -> 1.66 us
    pallas_call x1, Pallas kernels: 1.55 us -> 11.3 us  [first_update(): pl.pallas_call(functools.partial(first_update_kernel, sizes, chunks), in_...]
    pallas_call x2 -> x1, Pallas kernels: 12.9 us -> 4.82 us  [update(): pl.pallas_call(functools.partial(update_kernel, sizes, chunks), in_specs=...]
    all_to_all x4, waiting for transfers between devices: 13.7 us -> 8.56 us  [shards(): lax.all_to_all(send, PLANE, split_axis=0, concat_axis=0, tiled=True)]
    ppermute x9, starting transfers between devices: 22.6 us -> 26 us  [along(): return lax.ppermute(value, 'outer', pairs)]
    unnamed x18 -> x8, local copies, waits for them, and re-layouts: 3.78 us -> 1.66 us
    pallas_call x2, Pallas kernels: 0.07 us -> 1.89 us  [join_rows(): pl.pallas_call(rows_kernel, in_specs=[KEPT] + [VMEM] * len(parts), out_sp...]
  transfers between devices with their start and end apart: 14 -> 14, of which waited for: 4 -> 4; matrix products, arithmetic and copies ran while one was open for 0% -> 0% of each run, Pallas kernels for 18% -> 22%
where the time goes in v11:
time: 101 us; the launch traced here: 100 us
  starting transfers between devices  44.7 us (44%)
  Pallas kernels  29.7 us (29%)
  waiting for transfers between devices  23.3 us (23%)
  local copies, waits for them, and re-layouts  1.66 us (2%)
    ppermute x9, starting transfers between devices, along(): return lax.ppermute(value, 'outer', pairs)  26 us
    all_to_all x4, starting transfers between devices, shards(): lax.all_to_all(send, PLANE, split_axis=0, concat_axis=0, tiled=True)  17.2 us
    ppermute x9, waiting for transfers between devices, along(): return lax.ppermute(value, 'outer', pairs)  14.7 us
    pallas_call x1, Pallas kernels, first_update(): pl.pallas_call(functools.partial(first_update_kernel, sizes, chunks), in_...  11.3 us
    pallas_call x3, Pallas kernels, pack(): pl.pallas_call(functools.partial(pack_kernel, sizes, n), in_specs=[SMEM]...  8.59 us
    all_to_all x4, waiting for transfers between devices, shards(): lax.all_to_all(send, PLANE, split_axis=0, concat_axis=0, tiled=True)  8.56 us
    pallas_call x1, Pallas kernels, update(): pl.pallas_call(functools.partial(update_kernel, sizes, chunks), in_specs=...  4.82 us
    pallas_call x1, Pallas kernels, first(): pl.pallas_call(functools.partial(first_kernel, sizes), in_specs=[SMEM] *...  3.13 us
  transfers between devices with their start and end apart: 14, of which 4 were waited for; matrix products, arithmetic and copies ran while one was open for 0% of the time, Pallas kernels for 22%

profile of v11, /device:TPU:0, one launch (start us, length us, event | category | flops | bytes accessed | tf_op | source)
XLA Modules:
  0.0 100.2 jit_solution(8973697499064218842)
XLA Ops:
  0.6 3.1 %shard_map.104 = (s32[90]{0:T(128)}, bf16[608,512]{1,0:T(8,128)(2,1)}, bf16[8,152,512]{2,1,0:T(8,128)(2,1)}) custom-call(s32[8,32]{1,0:T(8,128)} %bitcast.4, s32[8,32]{1,0:T(8,128)} %bitcast.5, s32[1,8]{1,0:T(1,128)} %near_rows.1, s32[1,8]{1,0:T(1,128)} %far_rows.1, bf16[4,128,512]{2,1,0:T(8,128)(2,1)} %near.1, bf16[4,12,2,512]{3,2,1,0:T(2,128)(2,1)} %bitcast.3), custom_call_target="tpu_custom_call" | custom-call | tf_op jit(solution)/shard_map/pallas_call | solution.py:127
  3.8 3.1 %collective-permute-start = (bf16[608,512]{1,0:T(8,128)(2,1)}, bf16[608,512]{1,0:T(8,128)(2,1)}, u32[]{:S(2)}, u32[]{:S(2)}) collective-permute-start(bf16[608,512]{1,0:T(8,128)(2,1)} %get-tuple-element.10), channel_id=1, source_target_pairs={{0,2},{2,0},{4,6},{6,4},{1,3},{3,1},{5,7},{7,5},{8,10},{10,8},{12,... | collective-permute-start | bytes 1867784 | tf_op jit(solution)/shard_map/ppermute | solution.py:440
  6.9 1.5 %collective-permute-start.8 = (bf16[608,512]{1,0:T(8,128)(2,1)}, bf16[608,512]{1,0:T(8,128)(2,1)}, u32[]{:S(2)}, u32[]{:S(2)}) collective-permute-start(bf16[608,512]{1,0:T(8,128)(2,1)} %get-tuple-element.10), channel_id=1, source_target_pairs={{2,4},{4,2},{3,5},{5,3},{10,12},{12,10},{11,13},{13,11},{18,20},{2... | collective-permute-start | bytes 1867784 | tf_op jit(solution)/shard_map/ppermute | solution.py:440
  8.3 0.0 copy-start.3
  8.3 4.4 %all-to-all-start = ((bf16[8,152,512]{2,1,0:T(8,128)(2,1)}), bf16[8,152,512]{2,1,0:T(8,128)(2,1)}, u32[]{:S(2)}, u32[]{:S(2)}) async-start(bf16[8,152,512]{2,1,0:T(8,128)(2,1)} %get-tuple-element.11), calls=%async_computation | async-start | bytes 2490368 | tf_op jit(solution)/shard_map/all_to_all | solution.py:462
  12.7 8.5 %collective-permute-done.refs_0_ = bf16[608,512]{1,0:T(8,128)(2,1)} collective-permute-done((bf16[608,512]{1,0:T(8,128)(2,1)}, bf16[608,512]{1,0:T(8,128)(2,1)}, u32[]{:S(2)}, u32[]{:S(2)}) %collective-permute-start) | collective-permute-done | bytes 622624 | tf_op jit(solution)/shard_map/ppermute | solution.py:440
  21.2 0.7 collective-permute-start.1
  21.9 0.0 collective-permute-done.8.refs_0_
  21.9 4.6 %collective-permute-start.9 = (bf16[608,512]{1,0:T(8,128)(2,1)}, bf16[608,512]{1,0:T(8,128)(2,1)}, u32[]{:S(2)}, u32[]{:S(2)}) collective-permute-start(bf16[608,512]{1,0:T(8,128)(2,1)} %collective-permute-done.8.refs_0_), channel_id=1, source_target_pairs={{0,2},{2,0},{4,6},{6,4},{1,3},{3,1},{5,7},{7,5},{8,10},{10,8},{12,... | collective-permute-start | bytes 1867784 | tf_op jit(solution)/shard_map/ppermute | solution.py:440
  26.5 0.0 copy-done.3
  26.5 1.5 %collective-permute-start.2 = (bf16[2,64,512]{2,1,0:T(8,128)(2,1)S(1)}, bf16[2,64,512]{2,1,0:T(8,128)(2,1)S(1)}, u32[]{:S(2)}, u32[]{:S(2)}) collective-permute-start(bf16[2,64,512]{2,1,0:T(8,128)(2,1)S(1)} %copy-done.3), channel_id=1, source_target_pairs={{1,0},{0,1},{3,2},{2,3},{5,4},{4,5},{7,6},{6,7},{9,8},{8,9},{11,10... | collective-permute-start | bytes 393224 | tf_op jit(solution)/shard_map/ppermute | solution.py:445
  28.0 2.9 %shard_map.107 = bf16[8,152,512]{2,1,0:T(8,128)(2,1)} custom-call(s32[90]{0:T(128)} %get-tuple-element.9.table, bf16[608,512]{1,0:T(8,128)(2,1)} %collective-permute-done.refs_0_), custom_call_target="tpu_custom_call" | custom-call | flops 2000000000 | tf_op jit(solution)/shard_map/pallas_call | solution.py:157
  30.9 0.0 all-to-all-done.refs_5_
  30.9 4.3 %all-to-all-start.1 = ((bf16[8,152,512]{2,1,0:T(8,128)(2,1)}), bf16[8,152,512]{2,1,0:T(8,128)(2,1)}, u32[]{:S(2)}, u32[]{:S(2)}) async-start(bf16[8,152,512]{2,1,0:T(8,128)(2,1)} %shard_map.107), calls=%async_computation.1 | async-start | bytes 2490368 | tf_op jit(solution)/shard_map/all_to_all | solution.py:462
  35.2 0.0 collective-permute-done.2.refs_1_
  35.2 0.0 collective-permute-done.1.after.refs_2_.refs_0_
  35.2 0.0 copy-start
  35.2 0.8 shard_map.105.refs_0_
  36.0 7.7 %collective-permute-start.5 = (bf16[2,2,64,512]{3,2,1,0:T(8,128)(2,1)}, bf16[2,2,64,512]{3,2,1,0:T(8,128)(2,1)S(1)}, u32[]{:S(2)}, u32[]{:S(2)}) collective-permute-start(bf16[2,2,64,512]{3,2,1,0:T(8,128)(2,1)} %shard_map.105.refs_0_), channel_id=1, source_target_pairs={{0,4},{6,2},{1,5},{7,3},{8,12},{14,10},{9,13},{15,11},{16,20},{22,... | collective-permute-start | bytes 786440 | tf_op jit(solution)/shard_map/ppermute | solution.py:440
  43.7 1.4 %collective-permute-start.4 = (bf16[2,2,64,512]{3,2,1,0:T(8,128)(2,1)}, bf16[2,2,64,512]{3,2,1,0:T(8,128)(2,1)}, u32[]{:S(2)}, u32[]{:S(2)}) collective-permute-start(bf16[2,2,64,512]{3,2,1,0:T(8,128)(2,1)} %shard_map.105.refs_0_), channel_id=1, source_target_pairs={{2,4},{4,2},{3,5},{5,3},{10,12},{12,10},{11,13},{13,11},{18,20},{2... | collective-permute-start | bytes 786440 | tf_op jit(solution)/shard_map/ppermute | solution.py:440
  45.0 0.0 copy-done
  45.0 0.6 collective-permute-start.6
  45.6 0.0 collective-permute-done.9.refs_1_
  45.6 2.9 %shard_map.108 = bf16[8,152,512]{2,1,0:T(8,128)(2,1)} custom-call(s32[90]{0:T(128)} %get-tuple-element.9.table, bf16[608,512]{1,0:T(8,128)(2,1)} %collective-permute-done.8.refs_0_, bf16[608,512]{1,0:T(8,128)(2,1)} %collective-permute-done.9.refs_1_, bf16[608,512]{1,0:T(8,128)(2,1)} %copy-done), custom_call_target="tpu_custom_call" | custom-call | flops 10000000000 | tf_op jit(solution)/shard_map/pallas_call | solution.py:157
  48.5 3.7 %all-to-all-done.1.refs_6_ = bf16[8,152,512]{2,1,0:T(8,128)(2,1)} async-done(((bf16[8,152,512]{2,1,0:T(8,128)(2,1)}), bf16[8,152,512]{2,1,0:T(8,128)(2,1)}, u32[]{:S(2)}, u32[]{:S(2)}) %all-to-all-start.1) | async-done | bytes 1245216 | tf_op jit(solution)/shard_map/all_to_all | solution.py:462
  52.2 4.3 %all-to-all-start.2 = ((bf16[8,152,512]{2,1,0:T(8,128)(2,1)}), bf16[8,152,512]{2,1,0:T(8,128)(2,1)}, u32[]{:S(2)}, u32[]{:S(2)}) async-start(bf16[8,152,512]{2,1,0:T(8,128)(2,1)} %shard_map.108), calls=%async_computation.2 | async-start | bytes 2490368 | tf_op jit(solution)/shard_map/all_to_all | solution.py:462
  56.5 5.1 %collective-permute-start.3 = (bf16[2,2,64,512]{3,2,1,0:T(8,128)(2,1)}, bf16[2,2,64,512]{3,2,1,0:T(8,128)(2,1)}, u32[]{:S(2)}, u32[]{:S(2)}) collective-permute-start(bf16[2,2,64,512]{3,2,1,0:T(8,128)(2,1)} %shard_map.105.refs_0_), channel_id=1, source_target_pairs={{0,2},{6,4},{1,3},{7,5},{8,10},{14,12},{9,11},{15,13},{16,18},{22,... | collective-permute-start | bytes 786440 | tf_op jit(solution)/shard_map/ppermute | solution.py:440
  61.6 0.0 collective-permute-done.5.refs_2_.refs_3_
  61.6 0.0 copy-start.1
  61.6 0.7 copy-done.1
  62.3 0.0 collective-permute-done.4.refs_1_.refs_2_
  62.3 0.0 collective-permute-done.6.after.refs_1_
  62.3 0.0 copy-start.2
  62.3 0.9 copy-done.2
  63.3 1.1 %shard_map.106 = bf16[3,2,2,64,512]{4,3,2,1,0:T(8,128)(2,1)S(1)} custom-call(bf16[608,512]{1,0:T(8,128)(2,1)} %collective-permute-done.6.after.refs_1_, bf16[2,2,64,512]{3,2,1,0:T(8,128)(2,1)} %shard_map.105.refs_0_, bf16[2,2,64,512]{3,2,1,0:T(8,128)(2,1)} %collective-permute-done.4.refs_1_.refs_2_, bf16[2,2,64,512]{3,2,1,0:T(8,128)(2,1)S(1)} %copy-done.2), custom_call_target="tpu_custom_call" | custom-call | flops 1000000000 | tf_op jit(solution)/shard_map/pallas_call | solution.py:175
  64.3 1.5 %collective-permute-start.7 = (bf16[3,2,2,64,512]{4,3,2,1,0:T(8,128)(2,1)S(1)}, bf16[3,2,2,64,512]{4,3,2,1,0:T(8,128)(2,1)}, u32[]{:S(2)}, u32[]{:S(2)}) collective-permute-start(bf16[3,2,2,64,512]{4,3,2,1,0:T(8,128)(2,1)S(1)} %shard_map.106), channel_id=1, source_target_pairs={{0,2},{2,0},{4,6},{6,4},{1,3},{3,1},{5,7},{7,5},{8,10},{10,8},{12,... | collective-permute-start | bytes 2359304 | tf_op jit(solution)/shard_map/ppermute | solution.py:440
  65.8 2.9 %shard_map.110 = bf16[8,152,512]{2,1,0:T(8,128)(2,1)} custom-call(s32[90]{0:T(128)} %get-tuple-element.9.table, bf16[608,512]{1,0:T(8,128)(2,1)} %copy-done, bf16[608,512]{1,0:T(8,128)(2,1)} %collective-permute-done.6.after.refs_1_), custom_call_target="tpu_custom_call" | custom-call | flops 10000000000 | tf_op jit(solution)/shard_map/pallas_call | solution.py:157
  68.7 4.8 %all-to-all-done.2.refs_7_ = bf16[8,152,512]{2,1,0:T(8,128)(2,1)} async-done(((bf16[8,152,512]{2,1,0:T(8,128)(2,1)}), bf16[8,152,512]{2,1,0:T(8,128)(2,1)}, u32[]{:S(2)}, u32[]{:S(2)}) %all-to-all-start.2) | async-done | bytes 1245216 | tf_op jit(solution)/shard_map/all_to_all | solution.py:462
  73.5 4.3 %all-to-all-start.3 = ((bf16[8,152,512]{2,1,0:T(8,128)(2,1)}), bf16[8,152,512]{2,1,0:T(8,128)(2,1)}, u32[]{:S(2)}, u32[]{:S(2)}) async-start(bf16[8,152,512]{2,1,0:T(8,128)(2,1)} %shard_map.110), calls=%async_computation.3 | async-start | bytes 2490368 | tf_op jit(solution)/shard_map/all_to_all | solution.py:462
  77.8 0.0 collective-permute-done.3.refs_1_
  77.8 6.2 %collective-permute-done.7.refs_4_ = bf16[3,2,2,64,512]{4,3,2,1,0:T(8,128)(2,1)} collective-permute-done((bf16[3,2,2,64,512]{4,3,2,1,0:T(8,128)(2,1)S(1)}, bf16[3,2,2,64,512]{4,3,2,1,0:T(8,128)(2,1)}, u32[]{:S(2)}, u32[]{:S(2)}) %collective-permute-start.7) | collective-permute-done | bytes 786464 | tf_op jit(solution)/shard_map/ppermute | solution.py:440
  84.0 11.3 %shard_map.109 = (bf16[8,512,512]{2,1,0:T(8,128)(2,1)}, bf16[8,48,512]{2,1,0:T(8,128)(2,1)}, bf16[2,512,512]{2,1,0:T(8,128)(2,1)}, bf16[8,96,512]{2,1,0:T(8,128)(2,1)}) custom-call(s32[90]{0:T(128)} %get-tuple-element.9.table, bf16[8,512,512]{2,1,0:T(8,128)(2,1)} %near_tiles.3, bf16[8,2,48,512]{3,2,1,0:T(8,128)(2,1)} %far_tiles.3, ...), custom_call_target="tpu_custom_call" | custom-call | flops 8999999488 | tf_op jit(solution)/shard_map/pallas_call | solution.py:372
  95.3 0.0 all-to-all-done.3.refs_0_
  95.3 4.8 %shard_map.111 = (bf16[8,512,512]{2,1,0:T(8,128)(2,1)}, bf16[8,48,512]{2,1,0:T(8,128)(2,1)}) custom-call(s32[90]{0:T(128)} %get-tuple-element.9.table, bf16[8,512,512]{2,1,0:T(8,128)(2,1)} %near_tiles.3, bf16[8,2,48,512]{3,2,1,0:T(8,128)(2,1)} %far_tiles.3, ...), custom_call_target="tpu_custom_call", output_to_operand_aliasing={{0}: (6, {}), {1}: (7, {})} | custom-call | flops 3000000000 | tf_op jit(solution)/shard_map/pallas_call | solution.py:403
Async XLA Ops:
  3.8 17.4 %collective-permute-start = (bf16[608,512]{1,0:T(8,128)(2,1)}, bf16[608,512]{1,0:T(8,128)(2,1)}, u32[]{:S(2)}, u32[]{:S(2)}) collective-permute-start(bf16[608,512]{1,0:T(8,128)(2,1)} %get-tuple-element.10), channel_id=1, source_target_pairs={{0,2},{2,0},{4,6},{6,4},{1,3},{3,1},{5,7},{7,5},{8,10},{10,8},{12,... | collective-permute-start | bytes 1867784 | tf_op jit(solution)/shard_map/ppermute | solution.py:440
  6.9 15.0 %collective-permute-start.8 = (bf16[608,512]{1,0:T(8,128)(2,1)}, bf16[608,512]{1,0:T(8,128)(2,1)}, u32[]{:S(2)}, u32[]{:S(2)}) collective-permute-start(bf16[608,512]{1,0:T(8,128)(2,1)} %get-tuple-element.10), channel_id=1, source_target_pairs={{2,4},{4,2},{3,5},{5,3},{10,12},{12,10},{11,13},{13,11},{18,20},{2... | collective-permute-start | bytes 1867784 | tf_op jit(solution)/shard_map/ppermute | solution.py:440
  8.3 18.2 %copy-start.3 = (bf16[2,64,512]{2,1,0:T(8,128)(2,1)S(1)}, bf16[2,64,512]{2,1,0:T(8,128)(2,1)}, u32[]{:S(2)}) copy-start(bf16[2,64,512]{2,1,0:T(8,128)(2,1)} %refs_0_.1) | copy-start | bytes 393220
  8.3 22.5 %all-to-all-start = ((bf16[8,152,512]{2,1,0:T(8,128)(2,1)}), bf16[8,152,512]{2,1,0:T(8,128)(2,1)}, u32[]{:S(2)}, u32[]{:S(2)}) async-start(bf16[8,152,512]{2,1,0:T(8,128)(2,1)} %get-tuple-element.11), calls=%async_computation | async-start | bytes 2490368 | tf_op jit(solution)/shard_map/all_to_all | solution.py:462
  21.2 14.0 %collective-permute-start.1 = (bf16[608,512]{1,0:T(8,128)(2,1)}, bf16[608,512]{1,0:T(8,128)(2,1)S(1)}, u32[]{:S(2)}, u32[]{:S(2)}) collective-permute-start(bf16[608,512]{1,0:T(8,128)(2,1)} %collective-permute-done.refs_0_), channel_id=1, source_target_pairs={{2,4},{4,2},{3,5},{5,3},{10,12},{12,10},{11,13},{13,11},{18,20},{2... | collective-permute-start | bytes 1867784 | tf_op jit(solution)/shard_map/ppermute | solution.py:440
  21.9 23.7 %collective-permute-start.9 = (bf16[608,512]{1,0:T(8,128)(2,1)}, bf16[608,512]{1,0:T(8,128)(2,1)}, u32[]{:S(2)}, u32[]{:S(2)}) collective-permute-start(bf16[608,512]{1,0:T(8,128)(2,1)} %collective-permute-done.8.refs_0_), channel_id=1, source_target_pairs={{0,2},{2,0},{4,6},{6,4},{1,3},{3,1},{5,7},{7,5},{8,10},{10,8},{12,... | collective-permute-start | bytes 1867784 | tf_op jit(solution)/shard_map/ppermute | solution.py:440
  26.5 8.7 %collective-permute-start.2 = (bf16[2,64,512]{2,1,0:T(8,128)(2,1)S(1)}, bf16[2,64,512]{2,1,0:T(8,128)(2,1)S(1)}, u32[]{:S(2)}, u32[]{:S(2)}) collective-permute-start(bf16[2,64,512]{2,1,0:T(8,128)(2,1)S(1)} %copy-done.3), channel_id=1, source_target_pairs={{1,0},{0,1},{3,2},{2,3},{5,4},{4,5},{7,6},{6,7},{9,8},{8,9},{11,10... | collective-permute-start | bytes 393224 | tf_op jit(solution)/shard_map/ppermute | solution.py:445
  30.9 21.3 %all-to-all-start.1 = ((bf16[8,152,512]{2,1,0:T(8,128)(2,1)}), bf16[8,152,512]{2,1,0:T(8,128)(2,1)}, u32[]{:S(2)}, u32[]{:S(2)}) async-start(bf16[8,152,512]{2,1,0:T(8,128)(2,1)} %shard_map.107), calls=%async_computation.1 | async-start | bytes 2490368 | tf_op jit(solution)/shard_map/all_to_all | solution.py:462
  35.2 9.9 %copy-start = (bf16[608,512]{1,0:T(8,128)(2,1)}, bf16[608,512]{1,0:T(8,128)(2,1)S(1)}, u32[]{:S(2)}) copy-start(bf16[608,512]{1,0:T(8,128)(2,1)S(1)} %collective-permute-done.1.after.refs_2_.refs_0_) | copy-start | bytes 1867780
  36.0 25.6 %collective-permute-start.5 = (bf16[2,2,64,512]{3,2,1,0:T(8,128)(2,1)}, bf16[2,2,64,512]{3,2,1,0:T(8,128)(2,1)S(1)}, u32[]{:S(2)}, u32[]{:S(2)}) collective-permute-start(bf16[2,2,64,512]{3,2,1,0:T(8,128)(2,1)} %shard_map.105.refs_0_), channel_id=1, source_target_pairs={{0,4},{6,2},{1,5},{7,3},{8,12},{14,10},{9,13},{15,11},{16,20},{22,... | collective-permute-start | bytes 786440 | tf_op jit(solution)/shard_map/ppermute | solution.py:440
  43.7 18.6 %collective-permute-start.4 = (bf16[2,2,64,512]{3,2,1,0:T(8,128)(2,1)}, bf16[2,2,64,512]{3,2,1,0:T(8,128)(2,1)}, u32[]{:S(2)}, u32[]{:S(2)}) collective-permute-start(bf16[2,2,64,512]{3,2,1,0:T(8,128)(2,1)} %shard_map.105.refs_0_), channel_id=1, source_target_pairs={{2,4},{4,2},{3,5},{5,3},{10,12},{12,10},{11,13},{13,11},{18,20},{2... | collective-permute-start | bytes 786440 | tf_op jit(solution)/shard_map/ppermute | solution.py:440
  45.0 17.3 %collective-permute-start.6 = (bf16[608,512]{1,0:T(8,128)(2,1)S(1)}, bf16[608,512]{1,0:T(8,128)(2,1)}, u32[]{:S(2)}, u32[]{:S(2)}) collective-permute-start(bf16[608,512]{1,0:T(8,128)(2,1)S(1)} %collective-permute-done.1.after.refs_2_.refs_0_), channel_id=1, source_target_pairs={{0,2},{2,0},{4,6},{6,4},{1,3},{3,1},{5,7},{7,5},{8,10},{10,8},{12,... | collective-permute-start | bytes 1867784 | tf_op jit(solution)/shard_map/ppermute | solution.py:440
  52.2 21.3 %all-to-all-start.2 = ((bf16[8,152,512]{2,1,0:T(8,128)(2,1)}), bf16[8,152,512]{2,1,0:T(8,128)(2,1)}, u32[]{:S(2)}, u32[]{:S(2)}) async-start(bf16[8,152,512]{2,1,0:T(8,128)(2,1)} %shard_map.108), calls=%async_computation.2 | async-start | bytes 2490368 | tf_op jit(solution)/shard_map/all_to_all | solution.py:462
  56.5 21.3 %collective-permute-start.3 = (bf16[2,2,64,512]{3,2,1,0:T(8,128)(2,1)}, bf16[2,2,64,512]{3,2,1,0:T(8,128)(2,1)}, u32[]{:S(2)}, u32[]{:S(2)}) collective-permute-start(bf16[2,2,64,512]{3,2,1,0:T(8,128)(2,1)} %shard_map.105.refs_0_), channel_id=1, source_target_pairs={{0,2},{6,4},{1,3},{7,5},{8,10},{14,12},{9,11},{15,13},{16,18},{22,... | collective-permute-start | bytes 786440 | tf_op jit(solution)/shard_map/ppermute | solution.py:440
  61.6 0.7 copy-start.1
  62.3 1.0 copy-start.2
  64.3 19.7 %collective-permute-start.7 = (bf16[3,2,2,64,512]{4,3,2,1,0:T(8,128)(2,1)S(1)}, bf16[3,2,2,64,512]{4,3,2,1,0:T(8,128)(2,1)}, u32[]{:S(2)}, u32[]{:S(2)}) collective-permute-start(bf16[3,2,2,64,512]{4,3,2,1,0:T(8,128)(2,1)S(1)} %shard_map.106), channel_id=1, source_target_pairs={{0,2},{2,0},{4,6},{6,4},{1,3},{3,1},{5,7},{7,5},{8,10},{10,8},{12,... | collective-permute-start | bytes 2359304 | tf_op jit(solution)/shard_map/ppermute | solution.py:440
  73.5 21.8 %all-to-all-start.3 = ((bf16[8,152,512]{2,1,0:T(8,128)(2,1)}), bf16[8,152,512]{2,1,0:T(8,128)(2,1)}, u32[]{:S(2)}, u32[]{:S(2)}) async-start(bf16[8,152,512]{2,1,0:T(8,128)(2,1)} %shard_map.110), calls=%async_computation.3 | async-start | bytes 2490368 | tf_op jit(solution)/shard_map/all_to_all | solution.py:462

commit v12 on v11

--- a/solution.py
+++ b/solution.py
@@ -13,7 +13,8 @@
 FAR_ALIGN = 8
 LANES = 128
 VMEM_LIMIT = 16 * 1024 * 1024
-WIDE_VMEM = 63 * 1024 * 1024
+WIDE_VMEM = 60 * 1024 * 1024
+FULL_VMEM = 63 * 1024 * 1024
 HBM = pl.BlockSpec(memory_space=pltpu.HBM)
 CHUNK_OWNER = ((0, 1, 2, 3), (1, 0, 3, 2), (2, 2, 1, 1), (3, 3, 0, 0))
 CHUNK_SOURCE = ((0, 0, 0, 0), (0, 0, 0, 0), (1, 0, 0, 1), (1, 0, 0, 1))
@@ -389,7 +390,7 @@
             pltpu.SemaphoreType.DMA((count, groups + 6)),
             pltpu.SemaphoreType.DMA((8,)),
         ],
-        compiler_params=pltpu.CompilerParams(vmem_limit_bytes=WIDE_VMEM),
+        compiler_params=pltpu.CompilerParams(vmem_limit_bytes=FULL_VMEM),
         cost_estimate=pl.CostEstimate(
             flops=UPDATE_FLOPS * len(chunks), bytes_accessed=0, transcendentals=0
         ),
@@ -418,7 +419,7 @@
             pltpu.SemaphoreType.DMA((count, groups + 6 + row_group)),
         ],
         input_output_aliases={5 + len(got) + k: k for k in range(len(before))},
-        compiler_params=pltpu.CompilerParams(vmem_limit_bytes=WIDE_VMEM),
+        compiler_params=pltpu.CompilerParams(vmem_limit_bytes=FULL_VMEM),
         cost_estimate=pl.CostEstimate(
             flops=UPDATE_FLOPS * len(chunks), bytes_accessed=0, transcendentals=0
         ),
@@ -465,7 +466,7 @@
     near1 = along(line, [(0, 1), (3, 2)])
     near2 = along(line, [(1, 2), (2, 1)])
     near3 = along(line, [(0, 2), (3, 1)])
-    relayed = join_rows([line, near2, near3], held["pass3"])
+    relayed = join_rows([line, near2, near3], held["pass2"])
     relayed = along(relayed, [(0, 1), (1, 0), (2, 3), (3, 2)])
     parts = [line, near1, near2, near3, relayed]
     *outs, lefts, x_halves = first_update(

time: 101 us -> 101 us (level)
  waiting for transfers between devices: 23.3 us -> 27.7 us
  starting transfers between devices: 44.7 us -> 42 us
  Pallas kernels: 29.7 us -> 28 us
    ppermute x9, waiting for transfers between devices: 14.7 us -> 17.2 us  [along(): return lax.ppermute(value, 'outer', pairs)]
    ppermute x9, starting transfers between devices: 26 us -> 23.8 us  [along(): return lax.ppermute(value, 'outer', pairs)]
    all_to_all x4, waiting for transfers between devices: 8.56 us -> 10.5 us  [shards(): lax.all_to_all(send, PLANE, split_axis=0, concat_axis=0, tiled=True)]
    pallas_call x2, Pallas kernels: 1.89 us -> 0.07 us  [join_rows(): pl.pallas_call(rows_kernel, in_specs=[KEPT] + [VMEM] * len(parts), out_sp...]
    unnamed x8 -> x18, local copies, waits for them, and re-layouts: 1.66 us -> 2.26 us
  transfers between devices with their start and end apart: 14 -> 14, of which waited for: 4 -> 5; matrix products, arithmetic and copies ran while one was open for 0% -> 0% of each run, Pallas kernels for 22% -> 20%
where the time goes in v12:
time: 101 us
  starting transfers between devices  42 us (42%)
  Pallas kernels  28 us (28%)
  waiting for transfers between devices  27.7 us (27%)
  local copies, waits for them, and re-layouts  2.26 us (2%)
    ppermute x9, starting transfers between devices, along(): return lax.ppermute(value, 'outer', pairs)  23.8 us
    ppermute x9, waiting for transfers between devices, along(): return lax.ppermute(value, 'outer', pairs)  17.2 us
    all_to_all x4, starting transfers between devices, shards(): lax.all_to_all(send, PLANE, split_axis=0, concat_axis=0, tiled=True)  16.7 us
    pallas_call x1, Pallas kernels, first_update(): pl.pallas_call(functools.partial(first_update_kernel, sizes, chunks), in_...  11.3 us
    all_to_all x4, waiting for transfers between devices, shards(): lax.all_to_all(send, PLANE, split_axis=0, concat_axis=0, tiled=True)  10.5 us
    pallas_call x3, Pallas kernels, pack(): pl.pallas_call(functools.partial(pack_kernel, sizes, n), in_specs=[SMEM]...  8.6 us
    pallas_call x1, Pallas kernels, update(): pl.pallas_call(functools.partial(update_kernel, sizes, chunks), in_specs=...  4.82 us
    pallas_call x1, Pallas kernels, first(): pl.pallas_call(functools.partial(first_kernel, sizes), in_specs=[SMEM] *...  3.15 us
  transfers between devices with their start and end apart: 14, of which 5 were waited for; matrix products, arithmetic and copies ran while one was open for 0% of the time, Pallas kernels for 20%

profile of v12, /device:TPU:0, one launch (start us, length us, event | category | flops | bytes accessed | tf_op | source)
XLA Modules:
  0.0 100.8 jit_solution(4995225594603639714)
XLA Ops:
  0.6 3.2 %shard_map.104 = (s32[90]{0:T(128)}, bf16[608,512]{1,0:T(8,128)(2,1)}, bf16[8,152,512]{2,1,0:T(8,128)(2,1)}) custom-call(s32[8,32]{1,0:T(8,128)} %bitcast.4, s32[8,32]{1,0:T(8,128)} %bitcast.5, s32[1,8]{1,0:T(1,128)} %near_rows.1, s32[1,8]{1,0:T(1,128)} %far_rows.1, bf16[4,128,512]{2,1,0:T(8,128)(2,1)} %near.1, bf16[4,12,2,512]{3,2,1,0:T(2,128)(2,1)} %bitcast.3), custom_call_target="tpu_custom_call" | custom-call | tf_op jit(solution)/shard_map/pallas_call | solution.py:128
  3.8 3.1 %collective-permute-start = (bf16[608,512]{1,0:T(8,128)(2,1)}, bf16[608,512]{1,0:T(8,128)(2,1)}, u32[]{:S(2)}, u32[]{:S(2)}) collective-permute-start(bf16[608,512]{1,0:T(8,128)(2,1)} %get-tuple-element.10), channel_id=1, source_target_pairs={{0,2},{2,0},{4,6},{6,4},{1,3},{3,1},{5,7},{7,5},{8,10},{10,8},{12,... | collective-permute-start | bytes 1867784 | tf_op jit(solution)/shard_map/ppermute | solution.py:441
  6.9 1.5 %collective-permute-start.6 = (bf16[608,512]{1,0:T(8,128)(2,1)}, bf16[608,512]{1,0:T(8,128)(2,1)}, u32[]{:S(2)}, u32[]{:S(2)}) collective-permute-start(bf16[608,512]{1,0:T(8,128)(2,1)} %get-tuple-element.10), channel_id=1, source_target_pairs={{2,4},{4,2},{3,5},{5,3},{10,12},{12,10},{11,13},{13,11},{18,20},{2... | collective-permute-start | bytes 1867784 | tf_op jit(solution)/shard_map/ppermute | solution.py:441
  8.4 3.9 %all-to-all-start = ((bf16[8,152,512]{2,1,0:T(8,128)(2,1)}), bf16[8,152,512]{2,1,0:T(8,128)(2,1)S(1)}, u32[]{:S(2)}, u32[]{:S(2)}) async-start(bf16[8,152,512]{2,1,0:T(8,128)(2,1)} %get-tuple-element.11), calls=%async_computation | async-start | bytes 2490368 | tf_op jit(solution)/shard_map/all_to_all | solution.py:463
  12.2 9.0 %collective-permute-done.refs_0_ = bf16[608,512]{1,0:T(8,128)(2,1)} collective-permute-done((bf16[608,512]{1,0:T(8,128)(2,1)}, bf16[608,512]{1,0:T(8,128)(2,1)}, u32[]{:S(2)}, u32[]{:S(2)}) %collective-permute-start) | collective-permute-done | bytes 622624 | tf_op jit(solution)/shard_map/ppermute | solution.py:441
  21.2 0.7 collective-permute-start.1
  21.9 0.0 collective-permute-done.6.refs_0_
  21.9 4.6 %collective-permute-start.7 = (bf16[608,512]{1,0:T(8,128)(2,1)}, bf16[608,512]{1,0:T(8,128)(2,1)S(1)}, u32[]{:S(2)}, u32[]{:S(2)}) collective-permute-start(bf16[608,512]{1,0:T(8,128)(2,1)} %collective-permute-done.6.refs_0_), channel_id=1, source_target_pairs={{0,2},{2,0},{4,6},{6,4},{1,3},{3,1},{5,7},{7,5},{8,10},{10,8},{12,... | collective-permute-start | bytes 1867784 | tf_op jit(solution)/shard_map/ppermute | solution.py:441
  26.5 0.0 copy-done.6
  26.5 1.5 %collective-permute-start.2 = (bf16[2,64,512]{2,1,0:T(8,128)(2,1)S(1)}, bf16[2,64,512]{2,1,0:T(8,128)(2,1)S(1)}, u32[]{:S(2)}, u32[]{:S(2)}) collective-permute-start(bf16[2,64,512]{2,1,0:T(8,128)(2,1)S(1)} %copy-done.6), channel_id=1, source_target_pairs={{1,0},{0,1},{3,2},{2,3},{5,4},{4,5},{7,6},{6,7},{9,8},{8,9},{11,10... | collective-permute-start | bytes 393224 | tf_op jit(solution)/shard_map/ppermute | solution.py:446
  28.0 2.9 %shard_map.107 = bf16[8,152,512]{2,1,0:T(8,128)(2,1)} custom-call(s32[90]{0:T(128)} %get-tuple-element.9.table, bf16[608,512]{1,0:T(8,128)(2,1)} %collective-permute-done.refs_0_), custom_call_target="tpu_custom_call" | custom-call | flops 2000000000 | tf_op jit(solution)/shard_map/pallas_call | solution.py:158
  30.9 0.0 all-to-all-done.refs_5_
  30.9 0.0 copy-start.7
  30.9 4.3 %all-to-all-start.1 = ((bf16[8,152,512]{2,1,0:T(8,128)(2,1)}), bf16[8,152,512]{2,1,0:T(8,128)(2,1)}, u32[]{:S(2)}, u32[]{:S(2)}) async-start(bf16[8,152,512]{2,1,0:T(8,128)(2,1)} %shard_map.107), calls=%async_computation.1 | async-start | bytes 2490368 | tf_op jit(solution)/shard_map/all_to_all | solution.py:463
  35.2 0.0 collective-permute-done.2.refs_1_
  35.2 0.0 copy-done.7
  35.2 0.0 collective-permute-done.1.after.refs_2_.refs_0_
  35.2 0.0 copy-start
  35.3 0.7 collective-permute-start.4
  36.0 9.3 %collective-permute-start.5 = (bf16[2,2,64,512]{3,2,1,0:T(8,128)(2,1)S(1)}, bf16[2,2,64,512]{3,2,1,0:T(8,128)(2,1)S(1)}, u32[]{:S(2)}, u32[]{:S(2)}) collective-permute-start(bf16[2,2,64,512]{3,2,1,0:T(8,128)(2,1)S(1)} %shard_map.105.refs_0_), channel_id=1, source_target_pairs={{0,4},{6,2},{1,5},{7,3},{8,12},{14,10},{9,13},{15,11},{16,20},{22,... | collective-permute-start | bytes 786440 | tf_op jit(solution)/shard_map/ppermute | solution.py:441
  45.3 0.0 copy-done
  45.3 0.1 collective-permute-start.9
  45.4 0.0 collective-permute-done.7.after.refs_1_
  45.4 0.0 copy-start.1
  45.4 0.8 copy-done.1
  46.2 2.9 %shard_map.108 = bf16[8,152,512]{2,1,0:T(8,128)(2,1)} custom-call(s32[90]{0:T(128)} %get-tuple-element.9.table, bf16[608,512]{1,0:T(8,128)(2,1)} %collective-permute-done.6.refs_0_, bf16[608,512]{1,0:T(8,128)(2,1)} %copy-done.1, bf16[608,512]{1,0:T(8,128)(2,1)} %copy-done), custom_call_target="tpu_custom_call" | custom-call | flops 10000000000 | tf_op jit(solution)/shard_map/pallas_call | solution.py:158
  49.1 3.1 %all-to-all-done.1.refs_6_ = bf16[8,152,512]{2,1,0:T(8,128)(2,1)} async-done(((bf16[8,152,512]{2,1,0:T(8,128)(2,1)}), bf16[8,152,512]{2,1,0:T(8,128)(2,1)}, u32[]{:S(2)}, u32[]{:S(2)}) %all-to-all-start.1) | async-done | bytes 1245216 | tf_op jit(solution)/shard_map/all_to_all | solution.py:463
  52.3 4.3 %all-to-all-start.2 = ((bf16[8,152,512]{2,1,0:T(8,128)(2,1)}), bf16[8,152,512]{2,1,0:T(8,128)(2,1)}, u32[]{:S(2)}, u32[]{:S(2)}) async-start(bf16[8,152,512]{2,1,0:T(8,128)(2,1)} %shard_map.108), calls=%async_computation.2 | async-start | bytes 2490368 | tf_op jit(solution)/shard_map/all_to_all | solution.py:463
  56.5 3.9 %collective-permute-start.3 = (bf16[2,2,64,512]{3,2,1,0:T(8,128)(2,1)S(1)}, bf16[2,2,64,512]{3,2,1,0:T(8,128)(2,1)S(1)}, u32[]{:S(2)}, u32[]{:S(2)}) collective-permute-start(bf16[2,2,64,512]{3,2,1,0:T(8,128)(2,1)S(1)} %shard_map.105.refs_0_), channel_id=1, source_target_pairs={{0,2},{6,4},{1,3},{7,5},{8,10},{14,12},{9,11},{15,13},{16,18},{22,... | collective-permute-start | bytes 786440 | tf_op jit(solution)/shard_map/ppermute | solution.py:441
  60.4 0.0 collective-permute-done.4.refs_1_.refs_2_
  60.4 0.0 copy-start.4
  60.4 0.0 collective-permute-done.5.refs_2_.refs_3_
  60.4 0.1 shard_map.106
  60.5 0.6 copy-done.4
  61.1 0.1 copy-done.5
  61.2 0.7 copy-done.3
  61.9 0.0 collective-permute-start.8
  61.9 1.5 %collective-permute-done.9.refs_1_ = bf16[608,512]{1,0:T(8,128)(2,1)} collective-permute-done((bf16[608,512]{1,0:T(8,128)(2,1)S(1)}, bf16[608,512]{1,0:T(8,128)(2,1)}, u32[]{:S(2)}, u32[]{:S(2)}) %collective-permute-start.9) | collective-permute-done | bytes 622624 | tf_op jit(solution)/shard_map/ppermute | solution.py:441
  63.4 2.9 %shard_map.110 = bf16[8,152,512]{2,1,0:T(8,128)(2,1)} custom-call(s32[90]{0:T(128)} %get-tuple-element.9.table, bf16[608,512]{1,0:T(8,128)(2,1)} %copy-done, bf16[608,512]{1,0:T(8,128)(2,1)} %collective-permute-done.9.refs_1_), custom_call_target="tpu_custom_call" | custom-call | flops 10000000000 | tf_op jit(solution)/shard_map/pallas_call | solution.py:158
  66.2 7.3 %all-to-all-done.2.refs_7_ = bf16[8,152,512]{2,1,0:T(8,128)(2,1)} async-done(((bf16[8,152,512]{2,1,0:T(8,128)(2,1)}), bf16[8,152,512]{2,1,0:T(8,128)(2,1)}, u32[]{:S(2)}, u32[]{:S(2)}) %all-to-all-start.2) | async-done | bytes 1245216 | tf_op jit(solution)/shard_map/all_to_all | solution.py:463
  73.6 4.3 %all-to-all-start.3 = ((bf16[8,152,512]{2,1,0:T(8,128)(2,1)}), bf16[8,152,512]{2,1,0:T(8,128)(2,1)}, u32[]{:S(2)}, u32[]{:S(2)}) async-start(bf16[8,152,512]{2,1,0:T(8,128)(2,1)} %shard_map.110), calls=%async_computation.3 | async-start | bytes 2490368 | tf_op jit(solution)/shard_map/all_to_all | solution.py:463
  77.9 0.0 collective-permute-done.3.refs_1_
  77.9 0.0 copy-start.8
  77.9 6.7 %collective-permute-done.8.refs_4_ = bf16[3,2,2,64,512]{4,3,2,1,0:T(8,128)(2,1)} collective-permute-done((bf16[3,2,2,64,512]{4,3,2,1,0:T(8,128)(2,1)S(1)}, bf16[3,2,2,64,512]{4,3,2,1,0:T(8,128)(2,1)}, u32[]{:S(2)}, u32[]{:S(2)}) %collective-permute-start.8) | collective-permute-done | bytes 786464 | tf_op jit(solution)/shard_map/ppermute | solution.py:441
  84.6 0.0 copy-done.8
  84.6 11.3 %shard_map.109 = (bf16[8,512,512]{2,1,0:T(8,128)(2,1)}, bf16[8,48,512]{2,1,0:T(8,128)(2,1)}, bf16[2,512,512]{2,1,0:T(8,128)(2,1)}, bf16[8,96,512]{2,1,0:T(8,128)(2,1)}) custom-call(s32[90]{0:T(128)} %get-tuple-element.9.table, bf16[8,512,512]{2,1,0:T(8,128)(2,1)} %near_tiles.3, bf16[8,2,48,512]{3,2,1,0:T(8,128)(2,1)} %far_tiles.3, ...), custom_call_target="tpu_custom_call" | custom-call | flops 8999999488 | tf_op jit(solution)/shard_map/pallas_call | solution.py:373
  95.9 0.0 all-to-all-done.3.refs_0_
  95.9 4.8 %shard_map.111 = (bf16[8,512,512]{2,1,0:T(8,128)(2,1)}, bf16[8,48,512]{2,1,0:T(8,128)(2,1)}) custom-call(s32[90]{0:T(128)} %get-tuple-element.9.table, bf16[8,512,512]{2,1,0:T(8,128)(2,1)} %near_tiles.3, bf16[8,2,48,512]{3,2,1,0:T(8,128)(2,1)} %far_tiles.3, ...), custom_call_target="tpu_custom_call", output_to_operand_aliasing={{0}: (6, {}), {1}: (7, {})} | custom-call | flops 3000000000 | tf_op jit(solution)/shard_map/pallas_call | solution.py:404
  (6 shorter events, 0.0 us)
Async XLA Ops:
  3.8 17.4 %collective-permute-start = (bf16[608,512]{1,0:T(8,128)(2,1)}, bf16[608,512]{1,0:T(8,128)(2,1)}, u32[]{:S(2)}, u32[]{:S(2)}) collective-permute-start(bf16[608,512]{1,0:T(8,128)(2,1)} %get-tuple-element.10), channel_id=1, source_target_pairs={{0,2},{2,0},{4,6},{6,4},{1,3},{3,1},{5,7},{7,5},{8,10},{10,8},{12,... | collective-permute-start | bytes 1867784 | tf_op jit(solution)/shard_map/ppermute | solution.py:441
  6.9 15.0 %collective-permute-start.6 = (bf16[608,512]{1,0:T(8,128)(2,1)}, bf16[608,512]{1,0:T(8,128)(2,1)}, u32[]{:S(2)}, u32[]{:S(2)}) collective-permute-start(bf16[608,512]{1,0:T(8,128)(2,1)} %get-tuple-element.10), channel_id=1, source_target_pairs={{2,4},{4,2},{3,5},{5,3},{10,12},{12,10},{11,13},{13,11},{18,20},{2... | collective-permute-start | bytes 1867784 | tf_op jit(solution)/shard_map/ppermute | solution.py:441
  8.4 18.1 %copy-start.6 = (bf16[2,64,512]{2,1,0:T(8,128)(2,1)S(1)}, bf16[2,64,512]{2,1,0:T(8,128)(2,1)}, u32[]{:S(2)}) copy-start(bf16[2,64,512]{2,1,0:T(8,128)(2,1)} %refs_0_.1) | copy-start | bytes 393220
  8.4 22.5 %all-to-all-start = ((bf16[8,152,512]{2,1,0:T(8,128)(2,1)}), bf16[8,152,512]{2,1,0:T(8,128)(2,1)S(1)}, u32[]{:S(2)}, u32[]{:S(2)}) async-start(bf16[8,152,512]{2,1,0:T(8,128)(2,1)} %get-tuple-element.11), calls=%async_computation | async-start | bytes 2490368 | tf_op jit(solution)/shard_map/all_to_all | solution.py:463
  21.2 14.0 %collective-permute-start.1 = (bf16[608,512]{1,0:T(8,128)(2,1)}, bf16[608,512]{1,0:T(8,128)(2,1)S(1)}, u32[]{:S(2)}, u32[]{:S(2)}) collective-permute-start(bf16[608,512]{1,0:T(8,128)(2,1)} %collective-permute-done.refs_0_), channel_id=1, source_target_pairs={{2,4},{4,2},{3,5},{5,3},{10,12},{12,10},{11,13},{13,11},{18,20},{2... | collective-permute-start | bytes 1867784 | tf_op jit(solution)/shard_map/ppermute | solution.py:441
  21.9 23.4 %collective-permute-start.7 = (bf16[608,512]{1,0:T(8,128)(2,1)}, bf16[608,512]{1,0:T(8,128)(2,1)S(1)}, u32[]{:S(2)}, u32[]{:S(2)}) collective-permute-start(bf16[608,512]{1,0:T(8,128)(2,1)} %collective-permute-done.6.refs_0_), channel_id=1, source_target_pairs={{0,2},{2,0},{4,6},{6,4},{1,3},{3,1},{5,7},{7,5},{8,10},{10,8},{12,... | collective-permute-start | bytes 1867784 | tf_op jit(solution)/shard_map/ppermute | solution.py:441
  26.5 8.7 %collective-permute-start.2 = (bf16[2,64,512]{2,1,0:T(8,128)(2,1)S(1)}, bf16[2,64,512]{2,1,0:T(8,128)(2,1)S(1)}, u32[]{:S(2)}, u32[]{:S(2)}) collective-permute-start(bf16[2,64,512]{2,1,0:T(8,128)(2,1)S(1)} %copy-done.6), channel_id=1, source_target_pairs={{1,0},{0,1},{3,2},{2,3},{5,4},{4,5},{7,6},{6,7},{9,8},{8,9},{11,10... | collective-permute-start | bytes 393224 | tf_op jit(solution)/shard_map/ppermute | solution.py:446
  30.9 4.3 %copy-start.7 = (bf16[8,152,512]{2,1,0:T(8,128)(2,1)}, bf16[8,152,512]{2,1,0:T(8,128)(2,1)S(1)}, u32[]{:S(2)}) copy-start(bf16[8,152,512]{2,1,0:T(8,128)(2,1)S(1)} %all-to-all-done.refs_5_) | copy-start | bytes 3735556
  30.9 21.3 %all-to-all-start.1 = ((bf16[8,152,512]{2,1,0:T(8,128)(2,1)}), bf16[8,152,512]{2,1,0:T(8,128)(2,1)}, u32[]{:S(2)}, u32[]{:S(2)}) async-start(bf16[8,152,512]{2,1,0:T(8,128)(2,1)} %shard_map.107), calls=%async_computation.1 | async-start | bytes 2490368 | tf_op jit(solution)/shard_map/all_to_all | solution.py:463
  35.2 10.0 %copy-start = (bf16[608,512]{1,0:T(8,128)(2,1)}, bf16[608,512]{1,0:T(8,128)(2,1)S(1)}, u32[]{:S(2)}) copy-start(bf16[608,512]{1,0:T(8,128)(2,1)S(1)} %collective-permute-done.1.after.refs_2_.refs_0_) | copy-start | bytes 1867780
  35.3 25.1 %collective-permute-start.4 = (bf16[2,2,64,512]{3,2,1,0:T(8,128)(2,1)S(1)}, bf16[2,2,64,512]{3,2,1,0:T(8,128)(2,1)S(1)}, u32[]{:S(2)}, u32[]{:S(2)}) collective-permute-start(bf16[2,2,64,512]{3,2,1,0:T(8,128)(2,1)S(1)} %shard_map.105.refs_0_), channel_id=1, source_target_pairs={{2,4},{4,2},{3,5},{5,3},{10,12},{12,10},{11,13},{13,11},{18,20},{2... | collective-permute-start | bytes 786440 | tf_op jit(solution)/shard_map/ppermute | solution.py:441
  36.0 24.4 %collective-permute-start.5 = (bf16[2,2,64,512]{3,2,1,0:T(8,128)(2,1)S(1)}, bf16[2,2,64,512]{3,2,1,0:T(8,128)(2,1)S(1)}, u32[]{:S(2)}, u32[]{:S(2)}) collective-permute-start(bf16[2,2,64,512]{3,2,1,0:T(8,128)(2,1)S(1)} %shard_map.105.refs_0_), channel_id=1, source_target_pairs={{0,4},{6,2},{1,5},{7,3},{8,12},{14,10},{9,13},{15,11},{16,20},{22,... | collective-permute-start | bytes 786440 | tf_op jit(solution)/shard_map/ppermute | solution.py:441
  45.3 18.1 %collective-permute-start.9 = (bf16[608,512]{1,0:T(8,128)(2,1)S(1)}, bf16[608,512]{1,0:T(8,128)(2,1)}, u32[]{:S(2)}, u32[]{:S(2)}) collective-permute-start(bf16[608,512]{1,0:T(8,128)(2,1)S(1)} %collective-permute-done.1.after.refs_2_.refs_0_), channel_id=1, source_target_pairs={{0,2},{2,0},{4,6},{6,4},{1,3},{3,1},{5,7},{7,5},{8,10},{10,8},{12,... | collective-permute-start | bytes 1867784 | tf_op jit(solution)/shard_map/ppermute | solution.py:441
  45.4 0.8 copy-start.1
  49.1 11.3 %copy-start.2 = (bf16[608,512]{1,0:T(8,128)(2,1)S(1)}, bf16[608,512]{1,0:T(8,128)(2,1)}, u32[]{:S(2)}) copy-start(bf16[608,512]{1,0:T(8,128)(2,1)} %copy-done.1) | copy-start | bytes 1867780
  52.3 21.3 %all-to-all-start.2 = ((bf16[8,152,512]{2,1,0:T(8,128)(2,1)}), bf16[8,152,512]{2,1,0:T(8,128)(2,1)}, u32[]{:S(2)}, u32[]{:S(2)}) async-start(bf16[8,152,512]{2,1,0:T(8,128)(2,1)} %shard_map.108), calls=%async_computation.2 | async-start | bytes 2490368 | tf_op jit(solution)/shard_map/all_to_all | solution.py:463
  56.5 21.3 %collective-permute-start.3 = (bf16[2,2,64,512]{3,2,1,0:T(8,128)(2,1)S(1)}, bf16[2,2,64,512]{3,2,1,0:T(8,128)(2,1)S(1)}, u32[]{:S(2)}, u32[]{:S(2)}) collective-permute-start(bf16[2,2,64,512]{3,2,1,0:T(8,128)(2,1)S(1)} %shard_map.105.refs_0_), channel_id=1, source_target_pairs={{0,2},{6,4},{1,3},{7,5},{8,10},{14,12},{9,11},{15,13},{16,18},{22,... | collective-permute-start | bytes 786440 | tf_op jit(solution)/shard_map/ppermute | solution.py:441
  60.4 0.7 copy-start.4
  60.4 0.8 copy-start.5
  61.2 0.7 copy-start.3
  61.9 22.7 %collective-permute-start.8 = (bf16[3,2,2,64,512]{4,3,2,1,0:T(8,128)(2,1)S(1)}, bf16[3,2,2,64,512]{4,3,2,1,0:T(8,128)(2,1)}, u32[]{:S(2)}, u32[]{:S(2)}) collective-permute-start(bf16[3,2,2,64,512]{4,3,2,1,0:T(8,128)(2,1)S(1)} %shard_map.106), channel_id=1, source_target_pairs={{0,2},{2,0},{4,6},{6,4},{1,3},{3,1},{5,7},{7,5},{8,10},{10,8},{12,... | collective-permute-start | bytes 2359304 | tf_op jit(solution)/shard_map/ppermute | solution.py:441
  73.6 22.4 %all-to-all-start.3 = ((bf16[8,152,512]{2,1,0:T(8,128)(2,1)}), bf16[8,152,512]{2,1,0:T(8,128)(2,1)}, u32[]{:S(2)}, u32[]{:S(2)}) async-start(bf16[8,152,512]{2,1,0:T(8,128)(2,1)} %shard_map.110), calls=%async_computation.3 | async-start | bytes 2490368 | tf_op jit(solution)/shard_map/all_to_all | solution.py:463
  77.9 6.7 %copy-start.8 = (bf16[2,2,64,512]{3,2,1,0:T(8,128)(2,1)}, bf16[2,2,64,512]{3,2,1,0:T(8,128)(2,1)S(1)}, u32[]{:S(2)}) copy-start(bf16[2,2,64,512]{3,2,1,0:T(8,128)(2,1)S(1)} %collective-permute-done.3.refs_1_) | copy-start | bytes 786436

commit v13 on v9

--- a/solution.py
+++ b/solution.py
@@ -19,7 +19,7 @@
 CHUNK_OWNER = ((0, 1, 2, 3), (1, 0, 3, 2), (2, 2, 1, 1), (3, 3, 0, 0))
 CHUNK_SOURCE = ((0, 0, 0, 0), (0, 0, 0, 0), (1, 0, 0, 1), (1, 0, 0, 1))
 CHUNK_SOURCES = (("own",), ("pair",), ("middle", "pass2"), ("cross", "pass3"))
-PACK_FLOPS = (0, 5 * 10**9, 10**10, 10**10)
+PACK_FLOPS = (0, 2 * 10**9, 10**10, 10**10)
 JOIN_FLOPS = 10**9
 UPDATE_FLOPS = 3 * 10**9
 VMEM = pl.BlockSpec(memory_space=pltpu.VMEM)
@@ -390,7 +390,7 @@
     near1 = along(line, [(0, 1), (3, 2)])
     near2 = along(line, [(1, 2), (2, 1)])
     near3 = along(line, [(0, 2), (3, 1)])
-    relayed = join_rows([line, near2, near3], held["pass3"])
+    relayed = join_rows([line, near2, near3], held["pass2"])
     relayed = along(relayed, [(0, 1), (1, 0), (2, 3), (3, 2)])
     parts = [line, near1, near2, near3, relayed]
     lefts, x_halves = make_lefts(sizes, table, far_tiles, parts)

time: 101 us -> 100 us (0.990)
    unnamed x18 -> x20, local copies, waits for them, and re-layouts: 3.78 us -> 2.78 us
where the time goes in v13:
time: 100 us; the launch traced here: 99.7 us
  starting transfers between devices  40.7 us (41%)
  waiting for transfers between devices  29 us (29%)
  Pallas kernels  26.3 us (26%)
  local copies, waits for them, and re-layouts  2.78 us (3%)
    ppermute x9, starting transfers between devices, along(): return lax.ppermute(value, 'outer', pairs)  22.5 us
    all_to_all x4, starting transfers between devices, shards(): lax.all_to_all(send, PLANE, split_axis=0, concat_axis=0, tiled=True)  16.7 us
    ppermute x9, waiting for transfers between devices, along(): return lax.ppermute(value, 'outer', pairs)  15.2 us
    all_to_all x4, waiting for transfers between devices, shards(): lax.all_to_all(send, PLANE, split_axis=0, concat_axis=0, tiled=True)  13.8 us
    pallas_call x2, Pallas kernels, update(): pl.pallas_call(functools.partial(update_kernel, sizes, chunks), in_specs=...  12.9 us
    pallas_call x3, Pallas kernels, pack(): pl.pallas_call(functools.partial(pack_kernel, sizes, n), in_specs=[SMEM]...  8.62 us
    pallas_call x1, Pallas kernels, first(): pl.pallas_call(functools.partial(first_kernel, sizes), in_specs=[SMEM] *...  3.14 us
    unnamed x20, local copies, waits for them, and re-layouts  2.78 us
  transfers between devices with their start and end apart: 14, of which 4 were waited for; matrix products, arithmetic and copies ran while one was open for 0% of the time, Pallas kernels for 18%

profile of v13, /device:TPU:0, one launch (start us, length us, event | category | flops | bytes accessed | tf_op | source)
XLA Modules:
  0.0 99.7 jit_solution(2305511365571590063)
XLA Ops:
  0.6 3.1 %shard_map.104 = (s32[90]{0:T(128)}, bf16[608,512]{1,0:T(8,128)(2,1)}, bf16[8,152,512]{2,1,0:T(8,128)(2,1)}) custom-call(s32[8,32]{1,0:T(8,128)} %bitcast.4, s32[8,32]{1,0:T(8,128)} %bitcast.5, s32[1,8]{1,0:T(1,128)} %near_rows.1, s32[1,8]{1,0:T(1,128)} %far_rows.1, bf16[4,128,512]{2,1,0:T(8,128)(2,1)} %near.1, bf16[4,12,2,512]{3,2,1,0:T(2,128)(2,1)} %bitcast.3), custom_call_target="tpu_custom_call" | custom-call | tf_op jit(solution)/shard_map/pallas_call | solution.py:128
  3.8 3.1 %collective-permute-start = (bf16[608,512]{1,0:T(8,128)(2,1)}, bf16[608,512]{1,0:T(8,128)(2,1)}, u32[]{:S(2)}, u32[]{:S(2)}) collective-permute-start(bf16[608,512]{1,0:T(8,128)(2,1)} %get-tuple-element.10), channel_id=1, source_target_pairs={{0,2},{2,0},{4,6},{6,4},{1,3},{3,1},{5,7},{7,5},{8,10},{10,8},{12,... | collective-permute-start | bytes 1867784 | tf_op jit(solution)/shard_map/ppermute | solution.py:365
  6.9 0.7 collective-permute-start.6
  7.6 0.0 copy-start.7
  7.6 3.9 %all-to-all-start.1 = ((bf16[8,152,512]{2,1,0:T(8,128)(2,1)}), bf16[8,152,512]{2,1,0:T(8,128)(2,1)S(1)}, u32[]{:S(2)}, u32[]{:S(2)}) async-start(bf16[8,152,512]{2,1,0:T(8,128)(2,1)} %get-tuple-element.13), calls=%async_computation.1 | async-start | bytes 2490368 | tf_op jit(solution)/shard_map/all_to_all | solution.py:387
  11.4 9.8 %collective-permute-done.refs_0_ = bf16[608,512]{1,0:T(8,128)(2,1)} collective-permute-done((bf16[608,512]{1,0:T(8,128)(2,1)}, bf16[608,512]{1,0:T(8,128)(2,1)}, u32[]{:S(2)}, u32[]{:S(2)}) %collective-permute-start) | collective-permute-done | bytes 622624 | tf_op jit(solution)/shard_map/ppermute | solution.py:365
  21.2 0.7 collective-permute-start.1
  21.9 0.0 collective-permute-done.6.refs_0_
  21.9 0.0 copy-start.9
  21.9 4.6 %collective-permute-start.7 = (bf16[608,512]{1,0:T(8,128)(2,1)S(1)}, bf16[608,512]{1,0:T(8,128)(2,1)S(1)}, u32[]{:S(2)}, u32[]{:S(2)}) collective-permute-start(bf16[608,512]{1,0:T(8,128)(2,1)S(1)} %collective-permute-done.6.refs_0_), channel_id=1, source_target_pairs={{0,2},{2,0},{4,6},{6,4},{1,3},{3,1},{5,7},{7,5},{8,10},{10,8},{12,... | collective-permute-start | bytes 1867784 | tf_op jit(solution)/shard_map/ppermute | solution.py:365
  26.5 0.0 copy-done.7
  26.5 1.5 %collective-permute-start.2 = (bf16[2,64,512]{2,1,0:T(8,128)(2,1)S(1)}, bf16[2,64,512]{2,1,0:T(8,128)(2,1)S(1)}, u32[]{:S(2)}, u32[]{:S(2)}) collective-permute-start(bf16[2,64,512]{2,1,0:T(8,128)(2,1)S(1)} %copy-done.7), channel_id=1, source_target_pairs={{1,0},{0,1},{3,2},{2,3},{5,4},{4,5},{7,6},{6,7},{9,8},{8,9},{11,10... | collective-permute-start | bytes 393224 | tf_op jit(solution)/shard_map/ppermute | solution.py:370
  28.0 2.9 %shard_map.109 = bf16[8,152,512]{2,1,0:T(8,128)(2,1)} custom-call(s32[90]{0:T(128)} %get-tuple-element.9.table, bf16[608,512]{1,0:T(8,128)(2,1)} %collective-permute-done.refs_0_), custom_call_target="tpu_custom_call" | custom-call | flops 2000000000 | tf_op jit(solution)/shard_map/pallas_call | solution.py:158
  30.9 0.0 copy-done.9
  30.9 0.0 all-to-all-done.1.refs_0_
  30.9 0.0 copy-start.8
  30.9 4.3 %all-to-all-start.2 = ((bf16[8,152,512]{2,1,0:T(8,128)(2,1)}), bf16[8,152,512]{2,1,0:T(8,128)(2,1)}, u32[]{:S(2)}, u32[]{:S(2)}) async-start(bf16[8,152,512]{2,1,0:T(8,128)(2,1)} %shard_map.109), calls=%async_computation.2 | async-start | bytes 2490368 | tf_op jit(solution)/shard_map/all_to_all | solution.py:387
  35.2 0.0 collective-permute-done.2.refs_1_
  35.2 0.0 copy-done.8
  35.2 0.0 collective-permute-done.1.after.refs_0_.refs_2_
  35.2 0.0 copy-start.4
  35.3 7.6 %collective-permute-start.5 = (bf16[2,2,64,512]{3,2,1,0:T(8,128)(2,1)S(1)}, bf16[2,2,64,512]{3,2,1,0:T(8,128)(2,1)S(1)}, u32[]{:S(2)}, u32[]{:S(2)}) collective-permute-start(bf16[2,2,64,512]{3,2,1,0:T(8,128)(2,1)S(1)} %shard_map.105.refs_0_.line), channel_id=1, source_target_pairs={{0,4},{6,2},{1,5},{7,3},{8,12},{14,10},{9,13},{15,11},{16,20},{22,... | collective-permute-start | bytes 786440 | tf_op jit(solution)/shard_map/ppermute | solution.py:365
  42.9 0.7 collective-permute-start.4
  43.6 1.2 %collective-permute-start.9 = (bf16[608,512]{1,0:T(8,128)(2,1)S(1)}, bf16[608,512]{1,0:T(8,128)(2,1)}, u32[]{:S(2)}, u32[]{:S(2)}) collective-permute-start(bf16[608,512]{1,0:T(8,128)(2,1)S(1)} %collective-permute-done.1.after.refs_0_.refs_2_), channel_id=1, source_target_pairs={{0,2},{2,0},{4,6},{6,4},{1,3},{3,1},{5,7},{7,5},{8,10},{10,8},{12,... | collective-permute-start | bytes 1867784 | tf_op jit(solution)/shard_map/ppermute | solution.py:365
  44.8 0.0 collective-permute-done.7.after.refs_1_
  44.8 0.8 copy-done.5
  45.7 2.9 %shard_map.110 = bf16[8,152,512]{2,1,0:T(8,128)(2,1)} custom-call(s32[90]{0:T(128)} %get-tuple-element.9.table, bf16[608,512]{1,0:T(8,128)(2,1)} %copy-done.9, bf16[608,512]{1,0:T(8,128)(2,1)} %copy-done.5, bf16[608,512]{1,0:T(8,128)(2,1)} %copy-done.4), custom_call_target="tpu_custom_call" | custom-call | flops 10000000000 | tf_op jit(solution)/shard_map/pallas_call | solution.py:158
  48.6 3.7 %all-to-all-done.2.refs_1_ = bf16[8,152,512]{2,1,0:T(8,128)(2,1)} async-done(((bf16[8,152,512]{2,1,0:T(8,128)(2,1)}), bf16[8,152,512]{2,1,0:T(8,128)(2,1)}, u32[]{:S(2)}, u32[]{:S(2)}) %all-to-all-start.2) | async-done | bytes 1245216 | tf_op jit(solution)/shard_map/all_to_all | solution.py:387
  52.3 4.3 %all-to-all-start.3 = ((bf16[8,152,512]{2,1,0:T(8,128)(2,1)}), bf16[8,152,512]{2,1,0:T(8,128)(2,1)}, u32[]{:S(2)}, u32[]{:S(2)}) async-start(bf16[8,152,512]{2,1,0:T(8,128)(2,1)} %shard_map.110), calls=%async_computation.3 | async-start | bytes 2490368 | tf_op jit(solution)/shard_map/all_to_all | solution.py:387
  56.6 3.8 %collective-permute-start.3 = (bf16[2,2,64,512]{3,2,1,0:T(8,128)(2,1)S(1)}, bf16[2,2,64,512]{3,2,1,0:T(8,128)(2,1)S(1)}, u32[]{:S(2)}, u32[]{:S(2)}) collective-permute-start(bf16[2,2,64,512]{3,2,1,0:T(8,128)(2,1)S(1)} %shard_map.105.refs_0_.line), channel_id=1, source_target_pairs={{0,2},{6,4},{1,3},{7,5},{8,10},{14,12},{9,11},{15,13},{16,18},{22,... | collective-permute-start | bytes 786440 | tf_op jit(solution)/shard_map/ppermute | solution.py:365
  60.4 0.0 collective-permute-done.5.refs_2_.near3
  60.4 0.0 collective-permute-done.4.refs_1_.near2
  60.4 0.1 shard_map.106
  60.5 0.1 collective-permute-start.8
  60.6 0.0 collective-permute-done.9.refs_1_
  60.6 2.9 %shard_map.108 = bf16[8,152,512]{2,1,0:T(8,128)(2,1)} custom-call(s32[90]{0:T(128)} %get-tuple-element.9.table, bf16[608,512]{1,0:T(8,128)(2,1)} %copy-done.4, bf16[608,512]{1,0:T(8,128)(2,1)} %collective-permute-done.9.refs_1_), custom_call_target="tpu_custom_call" | custom-call | flops 10000000000 | tf_op jit(solution)/shard_map/pallas_call | solution.py:158
  63.4 0.0 copy-start
  63.5 10.1 %all-to-all-done.3.refs_2_ = bf16[8,152,512]{2,1,0:T(8,128)(2,1)} async-done(((bf16[8,152,512]{2,1,0:T(8,128)(2,1)}), bf16[8,152,512]{2,1,0:T(8,128)(2,1)}, u32[]{:S(2)}, u32[]{:S(2)}) %all-to-all-start.3) | async-done | bytes 1245216 | tf_op jit(solution)/shard_map/all_to_all | solution.py:387
  73.6 4.3 %all-to-all-start = ((bf16[8,152,512]{2,1,0:T(8,128)(2,1)}), bf16[8,152,512]{2,1,0:T(8,128)(2,1)}, u32[]{:S(2)}, u32[]{:S(2)}) async-start(bf16[8,152,512]{2,1,0:T(8,128)(2,1)} %shard_map.108), calls=%async_computation | async-start | bytes 2490368 | tf_op jit(solution)/shard_map/all_to_all | solution.py:387
  77.9 0.0 collective-permute-done.3.near1
  77.9 5.4 %collective-permute-done.8.relayed = bf16[3,2,2,64,512]{4,3,2,1,0:T(8,128)(2,1)S(1)} collective-permute-done((bf16[3,2,2,64,512]{4,3,2,1,0:T(8,128)(2,1)S(1)}, bf16[3,2,2,64,512]{4,3,2,1,0:T(8,128)(2,1)S(1)}, u32[]{:S(2)}, u32[]{:S(2)}) %collective-permute-start.8) | collective-permute-done | bytes 786464 | tf_op jit(solution)/shard_map/ppermute | solution.py:365
  83.3 0.0 copy-done
  83.3 1.6 %shard_map.107 = (bf16[2,512,512]{2,1,0:T(8,128)(2,1)S(1)}, bf16[8,96,512]{2,1,0:T(8,128)(2,1)S(1)}) custom-call(s32[90]{0:T(128)S(1)} %copy-done.3, bf16[8,2,48,512]{3,2,1,0:T(8,128)(2,1)S(1)} %copy-done, bf16[2,2,64,512]{3,2,1,0:T(8,128)(2,1)S(1)} %shard_map.105.refs_0_.line, bf16[2,2,64,512]{3,2,1,0:T(8,128)(2,1)S(1)} %collective-permute-done.3.near1, ...), custom_call_target="tpu_custom_call" | custom-call | tf_op jit(solution)/shard_map/pallas_call | solution.py:217
  84.9 0.9 copy-done.1
  85.8 0.9 copy-done.2
  86.8 8.2 %shard_map.111 = (bf16[8,512,512]{2,1,0:T(8,128)(2,1)}, bf16[8,48,512]{2,1,0:T(8,128)(2,1)}) custom-call(s32[90]{0:T(128)} %get-tuple-element.9.table, bf16[8,512,512]{2,1,0:T(8,128)(2,1)} %near_tiles.3, bf16[8,2,48,512]{3,2,1,0:T(8,128)(2,1)} %far_tiles.5, bf16[2,512,512]{2,1,0:T(8,128)(2,1)} %copy-done.1, bf16[8,96,512]{2,1,0:T(8,128)(2,1)} %copy-done.2, ...), custom_call_target="tpu_custom_call" | custom-call | flops 8999999488 | tf_op jit(solution)/shard_map/pallas_call | solution.py:328
  95.0 0.0 all-to-all-done.refs_0_
  95.0 4.7 %shard_map.112 = (bf16[8,512,512]{2,1,0:T(8,128)(2,1)}, bf16[8,48,512]{2,1,0:T(8,128)(2,1)}) custom-call(s32[90]{0:T(128)} %get-tuple-element.9.table, bf16[8,512,512]{2,1,0:T(8,128)(2,1)} %near_tiles.3, bf16[8,2,48,512]{3,2,1,0:T(8,128)(2,1)} %far_tiles.5, bf16[2,512,512]{2,1,0:T(8,128)(2,1)} %copy-done.1, ...), custom_call_target="tpu_custom_call", output_to_operand_aliasing={{0}: (6, {}), {1}: (7, {})} | custom-call | flops 3000000000 | tf_op jit(solution)/shard_map/pallas_call | solution.py:328
  (9 shorter events, 0.0 us)
Async XLA Ops:
  3.8 17.4 %collective-permute-start = (bf16[608,512]{1,0:T(8,128)(2,1)}, bf16[608,512]{1,0:T(8,128)(2,1)}, u32[]{:S(2)}, u32[]{:S(2)}) collective-permute-start(bf16[608,512]{1,0:T(8,128)(2,1)} %get-tuple-element.10), channel_id=1, source_target_pairs={{0,2},{2,0},{4,6},{6,4},{1,3},{3,1},{5,7},{7,5},{8,10},{10,8},{12,... | collective-permute-start | bytes 1867784 | tf_op jit(solution)/shard_map/ppermute | solution.py:365
  6.9 15.0 %collective-permute-start.6 = (bf16[608,512]{1,0:T(8,128)(2,1)}, bf16[608,512]{1,0:T(8,128)(2,1)S(1)}, u32[]{:S(2)}, u32[]{:S(2)}) collective-permute-start(bf16[608,512]{1,0:T(8,128)(2,1)} %get-tuple-element.10), channel_id=1, source_target_pairs={{2,4},{4,2},{3,5},{5,3},{10,12},{12,10},{11,13},{13,11},{18,20},{2... | collective-permute-start | bytes 1867784 | tf_op jit(solution)/shard_map/ppermute | solution.py:365
  7.6 19.0 %copy-start.7 = (bf16[2,64,512]{2,1,0:T(8,128)(2,1)S(1)}, bf16[2,64,512]{2,1,0:T(8,128)(2,1)}, u32[]{:S(2)}) copy-start(bf16[2,64,512]{2,1,0:T(8,128)(2,1)} %refs_0_.1) | copy-start | bytes 393220
  7.6 23.3 %all-to-all-start.1 = ((bf16[8,152,512]{2,1,0:T(8,128)(2,1)}), bf16[8,152,512]{2,1,0:T(8,128)(2,1)S(1)}, u32[]{:S(2)}, u32[]{:S(2)}) async-start(bf16[8,152,512]{2,1,0:T(8,128)(2,1)} %get-tuple-element.13), calls=%async_computation.1 | async-start | bytes 2490368 | tf_op jit(solution)/shard_map/all_to_all | solution.py:387
  21.2 14.0 %collective-permute-start.1 = (bf16[608,512]{1,0:T(8,128)(2,1)}, bf16[608,512]{1,0:T(8,128)(2,1)S(1)}, u32[]{:S(2)}, u32[]{:S(2)}) collective-permute-start(bf16[608,512]{1,0:T(8,128)(2,1)} %collective-permute-done.refs_0_), channel_id=1, source_target_pairs={{2,4},{4,2},{3,5},{5,3},{10,12},{12,10},{11,13},{13,11},{18,20},{2... | collective-permute-start | bytes 1867784 | tf_op jit(solution)/shard_map/ppermute | solution.py:365
  21.9 9.0 %copy-start.9 = (bf16[608,512]{1,0:T(8,128)(2,1)}, bf16[608,512]{1,0:T(8,128)(2,1)S(1)}, u32[]{:S(2)}) copy-start(bf16[608,512]{1,0:T(8,128)(2,1)S(1)} %collective-permute-done.6.refs_0_) | copy-start | bytes 1867780
  21.9 22.9 %collective-permute-start.7 = (bf16[608,512]{1,0:T(8,128)(2,1)S(1)}, bf16[608,512]{1,0:T(8,128)(2,1)S(1)}, u32[]{:S(2)}, u32[]{:S(2)}) collective-permute-start(bf16[608,512]{1,0:T(8,128)(2,1)S(1)} %collective-permute-done.6.refs_0_), channel_id=1, source_target_pairs={{0,2},{2,0},{4,6},{6,4},{1,3},{3,1},{5,7},{7,5},{8,10},{10,8},{12,... | collective-permute-start | bytes 1867784 | tf_op jit(solution)/shard_map/ppermute | solution.py:365
  26.5 8.7 %collective-permute-start.2 = (bf16[2,64,512]{2,1,0:T(8,128)(2,1)S(1)}, bf16[2,64,512]{2,1,0:T(8,128)(2,1)S(1)}, u32[]{:S(2)}, u32[]{:S(2)}) collective-permute-start(bf16[2,64,512]{2,1,0:T(8,128)(2,1)S(1)} %copy-done.7), channel_id=1, source_target_pairs={{1,0},{0,1},{3,2},{2,3},{5,4},{4,5},{7,6},{6,7},{9,8},{8,9},{11,10... | collective-permute-start | bytes 393224 | tf_op jit(solution)/shard_map/ppermute | solution.py:370
  30.9 4.3 %copy-start.8 = (bf16[8,152,512]{2,1,0:T(8,128)(2,1)}, bf16[8,152,512]{2,1,0:T(8,128)(2,1)S(1)}, u32[]{:S(2)}) copy-start(bf16[8,152,512]{2,1,0:T(8,128)(2,1)S(1)} %all-to-all-done.1.refs_0_) | copy-start | bytes 3735556
  30.9 21.3 %all-to-all-start.2 = ((bf16[8,152,512]{2,1,0:T(8,128)(2,1)}), bf16[8,152,512]{2,1,0:T(8,128)(2,1)}, u32[]{:S(2)}, u32[]{:S(2)}) async-start(bf16[8,152,512]{2,1,0:T(8,128)(2,1)} %shard_map.109), calls=%async_computation.2 | async-start | bytes 2490368 | tf_op jit(solution)/shard_map/all_to_all | solution.py:387
  35.2 8.4 %copy-start.4 = (bf16[608,512]{1,0:T(8,128)(2,1)}, bf16[608,512]{1,0:T(8,128)(2,1)S(1)}, u32[]{:S(2)}) copy-start(bf16[608,512]{1,0:T(8,128)(2,1)S(1)} %collective-permute-done.1.after.refs_0_.refs_2_) | copy-start | bytes 1867780
  35.3 25.1 %collective-permute-start.5 = (bf16[2,2,64,512]{3,2,1,0:T(8,128)(2,1)S(1)}, bf16[2,2,64,512]{3,2,1,0:T(8,128)(2,1)S(1)}, u32[]{:S(2)}, u32[]{:S(2)}) collective-permute-start(bf16[2,2,64,512]{3,2,1,0:T(8,128)(2,1)S(1)} %shard_map.105.refs_0_.line), channel_id=1, source_target_pairs={{0,4},{6,2},{1,5},{7,3},{8,12},{14,10},{9,13},{15,11},{16,20},{22,... | collective-permute-start | bytes 786440 | tf_op jit(solution)/shard_map/ppermute | solution.py:365
  42.9 17.5 %collective-permute-start.4 = (bf16[2,2,64,512]{3,2,1,0:T(8,128)(2,1)S(1)}, bf16[2,2,64,512]{3,2,1,0:T(8,128)(2,1)S(1)}, u32[]{:S(2)}, u32[]{:S(2)}) collective-permute-start(bf16[2,2,64,512]{3,2,1,0:T(8,128)(2,1)S(1)} %shard_map.105.refs_0_.line), channel_id=1, source_target_pairs={{2,4},{4,2},{3,5},{5,3},{10,12},{12,10},{11,13},{13,11},{18,20},{2... | collective-permute-start | bytes 786440 | tf_op jit(solution)/shard_map/ppermute | solution.py:365
  43.6 17.0 %collective-permute-start.9 = (bf16[608,512]{1,0:T(8,128)(2,1)S(1)}, bf16[608,512]{1,0:T(8,128)(2,1)}, u32[]{:S(2)}, u32[]{:S(2)}) collective-permute-start(bf16[608,512]{1,0:T(8,128)(2,1)S(1)} %collective-permute-done.1.after.refs_0_.refs_2_), channel_id=1, source_target_pairs={{0,2},{2,0},{4,6},{6,4},{1,3},{3,1},{5,7},{7,5},{8,10},{10,8},{12,... | collective-permute-start | bytes 1867784 | tf_op jit(solution)/shard_map/ppermute | solution.py:365
  44.8 0.8 copy-start.5
  48.6 11.9 %copy-start.6 = (bf16[608,512]{1,0:T(8,128)(2,1)S(1)}, bf16[608,512]{1,0:T(8,128)(2,1)}, u32[]{:S(2)}) copy-start(bf16[608,512]{1,0:T(8,128)(2,1)} %copy-done.5) | copy-start | bytes 1867780
  52.3 21.3 %all-to-all-start.3 = ((bf16[8,152,512]{2,1,0:T(8,128)(2,1)}), bf16[8,152,512]{2,1,0:T(8,128)(2,1)}, u32[]{:S(2)}, u32[]{:S(2)}) async-start(bf16[8,152,512]{2,1,0:T(8,128)(2,1)} %shard_map.110), calls=%async_computation.3 | async-start | bytes 2490368 | tf_op jit(solution)/shard_map/all_to_all | solution.py:387
  56.6 21.3 %collective-permute-start.3 = (bf16[2,2,64,512]{3,2,1,0:T(8,128)(2,1)S(1)}, bf16[2,2,64,512]{3,2,1,0:T(8,128)(2,1)S(1)}, u32[]{:S(2)}, u32[]{:S(2)}) collective-permute-start(bf16[2,2,64,512]{3,2,1,0:T(8,128)(2,1)S(1)} %shard_map.105.refs_0_.line), channel_id=1, source_target_pairs={{0,2},{6,4},{1,3},{7,5},{8,10},{14,12},{9,11},{15,13},{16,18},{22,... | collective-permute-start | bytes 786440 | tf_op jit(solution)/shard_map/ppermute | solution.py:365
  60.5 22.8 %collective-permute-start.8 = (bf16[3,2,2,64,512]{4,3,2,1,0:T(8,128)(2,1)S(1)}, bf16[3,2,2,64,512]{4,3,2,1,0:T(8,128)(2,1)S(1)}, u32[]{:S(2)}, u32[]{:S(2)}) collective-permute-start(bf16[3,2,2,64,512]{4,3,2,1,0:T(8,128)(2,1)S(1)} %shard_map.106), channel_id=1, source_target_pairs={{0,2},{2,0},{4,6},{6,4},{1,3},{3,1},{5,7},{7,5},{8,10},{10,8},{12,... | collective-permute-start | bytes 2359304 | tf_op jit(solution)/shard_map/ppermute | solution.py:365
  63.4 19.8 %copy-start = (bf16[8,2,48,512]{3,2,1,0:T(8,128)(2,1)S(1)}, bf16[8,2,48,512]{3,2,1,0:T(8,128)(2,1)}, u32[]{:S(2)}) copy-start(bf16[8,2,48,512]{3,2,1,0:T(8,128)(2,1)} %far_tiles.5) | copy-start | bytes 2359300
  63.5 19.8 %copy-start.3 = (s32[90]{0:T(128)S(1)}, s32[90]{0:T(128)}, u32[]{:S(2)}) copy-start(s32[90]{0:T(128)} %get-tuple-element.9.table) | copy-start | bytes 1084
  73.6 21.4 %all-to-all-start = ((bf16[8,152,512]{2,1,0:T(8,128)(2,1)}), bf16[8,152,512]{2,1,0:T(8,128)(2,1)}, u32[]{:S(2)}, u32[]{:S(2)}) async-start(bf16[8,152,512]{2,1,0:T(8,128)(2,1)} %shard_map.108), calls=%async_computation | async-start | bytes 2490368 | tf_op jit(solution)/shard_map/all_to_all | solution.py:387
  84.9 1.0 copy-start.1
  85.8 0.9 copy-start.2
